TPU v7x, 32 devices: a whole 2x2x4 slice. The times are simulated.
32 devices in a mesh: groups: 2 (over x), serve: 16 (over z, y, core).
Axes of the slice: x: 2, y: 2, z: 4, core: 2. Of those that a mesh axis runs over, the one named last changes fastest.
Arguments:
- queries: bfloat16 [4096, 2560], P(('groups', 'serve')), parts along dimension 0, may hold values from -9 to 9
- new_kv: bfloat16 [32, 1, 2, 128, 512], P(('groups', 'serve')), parts along dimension 0, may hold values from -9 to 9
- pool: bfloat16 [512, 2, 128, 512], P(('groups', 'serve')), parts along dimension 0, may hold values from -9 to 9
- page_owner: int32 [32, 48], P(('groups', 'serve')), parts along dimension 0, may hold values from 0 to 15, as said below
- page_slot: int32 [32, 48], P(('groups', 'serve')), parts along dimension 0, may hold values from 0 to 15, as said below
- prefix_len: int32 [32], P(('groups', 'serve')), parts along dimension 0, may hold values from 3713 to 6144, as said below
- store_slot: int32 [32, 1], P(('groups', 'serve')), parts along dimension 0, may hold values from 0 to 15, as said below
Outputs:
- attended: bfloat16 [4096, 2560], P(('groups', 'serve')), parts along dimension 0
- pool_out: bfloat16 [512, 2, 128, 512], P(('groups', 'serve')), parts along dimension 0
There are 2 independent parts, one for each index of `groups`. A program takes and returns all parts, laid end to end along the dimension named above; each array names one. Nothing has to cross between parts.
Inputs may be any that keep to these rules, and one draw needn't show every extreme that they name: `page_owner`: no request names its own index as owner, and a request names one owner at most 4 times among its first ceil(prefix_len / 128) entries; entries past those are 0 and are not read. `page_slot`: entries past a request's pages are 0 and are not read. `prefix_len`: some request has exactly 6144 cached tokens. `store_slot`: the 1 slots of a row are distinct.
All inputs are finite; a program needn't handle non-finite values.
Results may differ from a plain program's by a relative error of at most 0.0047.
Values may be sent and summed in bfloat16 or wider, within the bound.
No kernel may reach another device: no remote copies, remote signals or barrier semaphores. Data moves between devices by JAX's collectives and lax.ppermute only.
A program may use at most 128 MiB of HBM per device.

v0:
```python
import jax
import jax.numpy as jnp
from jax import lax
from jax.sharding import PartitionSpec as P

PAGE = 128
KVH = 4
GQ = 5
HD = 128
MAXP = 48


def shifted(array, axis, by):
    size = lax.axis_size(axis)
    return lax.ppermute(array, axis, [(i, (i + by) % size) for i in range(size)])


def heads_major(rows, heads):
    return rows.reshape(rows.shape[0], heads, HD).transpose(1, 0, 2)


def partial_attend(query_heads, key_heads, value_heads, valid):
    scale = HD ** (-0.5)

    def one_head(operands):
        query, keys, values = operands
        scores = jnp.einsum("qd,kd->qk", query, keys, preferred_element_type=jnp.float32) * scale
        scores = jnp.where(valid, scores, -1e30)
        top = jnp.max(scores, axis=1)
        expo = jnp.exp(scores - top[:, None])
        total = jnp.sum(expo, axis=1)
        accum = jnp.dot(expo.astype(jnp.bfloat16), values, preferred_element_type=jnp.float32)
        return (top, total, accum)

    return lax.map(one_head, (query_heads, key_heads, value_heads))


def prefix_part(query_heads, pages, heads, valid):
    key_heads = heads_major(pages[:, 0].reshape(MAXP * PAGE, heads * HD), heads)
    value_heads = heads_major(pages[:, 1].reshape(MAXP * PAGE, heads * HD), heads)
    return partial_attend(query_heads, key_heads, value_heads, valid)


def per_device(queries, new_kv, pool, page_owner, page_slot, prefix_len, store_slot):
    width = lax.axis_size("serve")
    capacity = (MAXP + width - 2) // (width - 1)
    span = queries.shape[0]
    rows = GQ * span
    kv_cols = KVH * HD
    owners = page_owner[0]
    slots = page_slot[0]
    length = prefix_len[0]
    used = jnp.arange(MAXP) < (length + PAGE - 1) // PAGE
    hits = ((owners[:, None] == jnp.arange(width)[None, :]) & used[:, None]).astype(jnp.int32)
    before = jnp.cumsum(hits, axis=0) - hits
    place = jnp.sum(before * hits, axis=1)
    spots = jnp.arange(capacity)
    picked = hits[:, :, None] * (place[:, None, None] == spots[None, None, :]).astype(jnp.int32)
    outgoing = jnp.sum(picked * (slots + 1)[:, None, None], axis=0) - 1
    wanted = lax.all_to_all(outgoing, "serve", split_axis=0, concat_axis=0, tiled=True)
    looked = jnp.take(pool, jnp.maximum(wanted, 0).reshape(-1), axis=0)
    looked = looked.reshape(width, capacity, 2, PAGE, kv_cols)
    query_heads = queries.reshape(span, KVH, GQ, HD).transpose(1, 2, 0, 3).reshape(KVH, rows, HD)
    fresh = new_kv[0]
    span_keys = heads_major(fresh[:, 0].reshape(span, kv_cols), KVH)
    span_values = heads_major(fresh[:, 1].reshape(span, kv_cols), KVH)
    span_valid = jnp.arange(span)[None, :] <= (jnp.arange(rows) % span)[:, None]
    second = partial_attend(query_heads, span_keys, span_values, span_valid)
    position = jnp.where(used, owners * capacity + place, 0)
    prefix_valid = (jnp.arange(MAXP * PAGE) < length)[None, :]
    received = lax.all_to_all(looked, "serve", split_axis=0, concat_axis=0, tiled=True)
    flat = received.reshape((width * capacity,) + received.shape[2:])
    first = prefix_part(query_heads, jnp.take(flat, position, axis=0), KVH, prefix_valid)
    top = jnp.maximum(first[0], second[0])
    scale_one = jnp.exp(first[0] - top)
    scale_two = jnp.exp(second[0] - top)
    denom = scale_one * first[1] + scale_two * second[1]
    merged = (scale_one[..., None] * first[2] + scale_two[..., None] * second[2]) / denom[..., None]
    attended = merged.reshape(KVH, GQ, span, HD).transpose(2, 0, 1, 3).reshape(span, KVH * GQ * HD)
    incoming = shifted(fresh, "serve", 1)
    pool_out = pool.at[store_slot[0]].set(incoming)
    return (attended.astype(jnp.bfloat16), pool_out)


def solution(mesh):
    return jax.shard_map(
        per_device,
        mesh=mesh,
        in_specs=(
            P(("groups", "serve"), None),
            P(("groups", "serve"), None, None, None, None),
            P(("groups", "serve"), None, None, None),
            P(("groups", "serve"), None),
            P(("groups", "serve"), None),
            P(("groups", "serve")),
            P(("groups", "serve"), None),
        ),
        out_specs=(P(("groups", "serve"), None), P(("groups", "serve"), None, None, None)),
        check_vma=False,
    )
```

profile of v0, /device:TPU:18, one launch (start us, length us, event | category | flops | bytes accessed | tf_op | source)
XLA Modules:
  0.0 571.5 jit_solution(14561713764879130084)
XLA Ops:
  0.7 4.7 copy.104
  6.7 10.1 %all_to_all.11 = s32[16,1,4]{2,1,0:T(1,128)S(1)} all-to-all(s32[16,1,4]{2,1,0:T(1,128)S(1)} %copy.51), channel_id=1, replica_groups=mesh['groups'=2,'serve'=16] {'serve'}, dimensions={0} | all-to-all | bytes 512 | tf_op jit(solution)/shard_map/all_to_all | solution.py:60
  17.1 9.6 %gather_fusion = bf16[64,2,128,512]{3,2,1,0:T(8,128)(2,1)} fusion(bf16[16,2,128,512]{3,2,1,0:T(8,128)(2,1)} %copy.104, s32[1024]{0:T(1024)S(1)} %pad_clamp_fusion.1), kind=kCustom, calls=%fused_computation | custom fusion | bytes 33554688 | tf_op jit(solution)/shard_map/jit(_take)/gather | solution.py:61
  26.7 14.2 %broadcast_select_fusion = bf16[16,4,2,128,512]{4,3,2,1,0:T(8,128)(2,1)} fusion(bf16[16,4,2,128,512]{4,3,2,1,0:T(8,128)(2,1)} %bitcast.109, pred[16,4]{1,0:T(8,128)(4,1)S(1)} %copy.53), kind=kLoop, calls=%fused_computation.42 | loop fusion | flops 8388608 | bytes 33554496 | tf_op jit(solution)/shard_map/jit(_take)/select_n | solution.py:61
  40.9 7.5 %all-to-all-start.1 = ((bf16[16,4,2,128,512]{4,3,2,1,0:T(8,128)(2,1)}), bf16[16,4,2,128,512]{4,3,2,1,0:T(8,128)(2,1)}, u32[]{:S(2)}, u32[]{:S(2)}) async-start(bf16[16,4,2,128,512]{4,3,2,1,0:T(8,128)(2,1)} %broadcast_select_fusion), calls=%async_computation.1 | async-start | bytes 33554432 | tf_op jit(solution)/shard_map/all_to_all | solution.py:71
  48.6 0.3 copy.48
  49.0 0.3 copy.49
  50.1 0.7 and_reduce_fusion
  51.0 2.8 while.32
  51.0 0.2 fusion.76
  51.2 0.2 fusion.78
  51.7 0.2 fusion.76
  51.9 0.2 fusion.78
  52.6 0.2 fusion.78
  53.1 0.2 fusion.76
  53.3 0.2 fusion.78
  53.8 359.6 %collective-permute-done = bf16[1,2,128,512]{3,2,1,0:T(8,128)(2,1)S(1)} collective-permute-done((bf16[1,2,128,512]{3,2,1,0:T(8,128)(2,1)S(1)}, bf16[1,2,128,512]{3,2,1,0:T(8,128)(2,1)S(1)}, u32[]{:S(2)}, u32[]{:S(2)}) %collective-permute-start) | collective-permute-done | bytes 262176 | tf_op jit(solution)/shard_map/ppermute | solution.py:15
  413.5 2.3 select_dynamic-update-slice_fusion
  415.8 12.1 %gather_fusion.1 = bf16[48,2,128,512]{3,2,1,0:T(8,128)(2,1)} fusion(bf16[64,2,128,512]{3,2,1,0:T(8,128)(2,1)} %bitcast.9, s32[1024]{0:T(1024)S(1)} %pad_clamp_fusion), kind=kCustom, calls=%fused_computation.1 | custom fusion | bytes 25166016 | tf_op jit(solution)/shard_map/jit(_take)/gather | solution.py:73
  427.9 6.5 %broadcast_select_fusion.1 = bf16[48,2,128,512]{3,2,1,0:T(8,128)(2,1)S(1)} fusion(bf16[48,2,128,512]{3,2,1,0:T(8,128)(2,1)} %gather_fusion.1, pred[48]{0:T(512)(128)(4,1)S(1)} %compare_and_fusion), kind=kLoop, calls=%fused_computation.43 | loop fusion | flops 6291456 | bytes 25165872 | tf_op jit(solution)/shard_map/jit(_take)/select_n | solution.py:73
  434.4 4.8 fusion.57
  439.3 9.7 %reshape.253 = bf16[6144,4,128]{2,1,0:T(4,128)(2,1)} reshape(bf16[48,1,128,512]{3,2,1,0:T(8,128)(2,1)} %get-tuple-element.226) | data formatting | bytes 12582912 | tf_op jit(solution)/shard_map/reshape;reshape;squeeze | solution.py:19
  449.0 9.8 %reshape.254 = bf16[6144,4,128]{2,1,0:T(4,128)(2,1)} reshape(bf16[48,1,128,512]{3,2,1,0:T(8,128)(2,1)} %get-tuple-element.225) | data formatting | bytes 12582912 | tf_op jit(solution)/shard_map/reshape;reshape;squeeze | solution.py:19
  458.7 11.6 %copy_bitcast_fusion = (bf16[4,6144,128]{2,1,0:T(8,128)(2,1)}, bf16[4,6144,128]{2,1,0:T(8,128)(2,1)}) fusion(bf16[6144,4,128]{2,1,0:T(4,128)(2,1)} %reshape.254, bf16[6144,4,128]{2,1,0:T(4,128)(2,1)} %reshape.253), kind=kLoop, calls=%fused_computation.44 | loop fusion | bytes 25165824
  470.5 96.2 %while.31 = (s32[]{:T(128)}, f32[4,640]{1,0:T(4,128)S(1)}, f32[4,640]{1,0:T(4,128)S(1)}, f32[4,640,128]{2,1,0:T(8,128)S(1)}, bf16[4,640,128]{2,1,0:T(8,128)(2,1)...) while((s32[]{:T(128)}, f32[4,640]{1,0:T(4,128)S(1)}, ...), condition=%wide.region_6.7_spmd.clone, body=%wide.region_3.6_spmd.clone.sunk | while | flops 2056524544 | bytes 113796744 | solution.py:35
  470.7 0.7 compare_reduce_fusion.2
  471.4 4.0 fusion.71
  475.4 5.5 copy-done
  480.9 4.6 fusion.73
  485.5 9.0 %fusion.72 = f32[640]{0:T(1024)S(1)} fusion(f32[640,6144]{1,0:T(8,128)} %copy-done, f32[640]{0:T(1024)S(1)} %get-tuple-element.327, pred[6144]{0:T(1024)(128)(4,1)S(1)} %compare_reduce_fusion.2), kind=kLoop, calls=%fused_computation.25.clone.1 | loop fusion | flops 15728000 | bytes 15739904 | tf_op jit(solution)/shard_map/while/body/eval_jaxpr/reduce_sum | solution.py:31
  494.7 0.7 compare_reduce_fusion.2
  495.4 4.0 fusion.71
  499.4 5.5 copy-done
  504.9 4.6 fusion.73
  509.6 9.0 %fusion.72 = f32[640]{0:T(1024)S(1)} fusion(f32[640,6144]{1,0:T(8,128)} %copy-done, f32[640]{0:T(1024)S(1)} %get-tuple-element.327, pred[6144]{0:T(1024)(128)(4,1)S(1)} %compare_reduce_fusion.2), kind=kLoop, calls=%fused_computation.25.clone.1 | loop fusion | flops 15728000 | bytes 15739904 | tf_op jit(solution)/shard_map/while/body/eval_jaxpr/reduce_sum | solution.py:31
  518.7 0.7 compare_reduce_fusion.2
  519.4 4.0 fusion.71
  523.4 5.5 copy-done
  528.9 4.6 fusion.73
  533.6 9.0 %fusion.72 = f32[640]{0:T(1024)S(1)} fusion(f32[640,6144]{1,0:T(8,128)} %copy-done, f32[640]{0:T(1024)S(1)} %get-tuple-element.327, pred[6144]{0:T(1024)(128)(4,1)S(1)} %compare_reduce_fusion.2), kind=kLoop, calls=%fused_computation.25.clone.1 | loop fusion | flops 15728000 | bytes 15739904 | tf_op jit(solution)/shard_map/while/body/eval_jaxpr/reduce_sum | solution.py:31
  542.7 0.7 compare_reduce_fusion.2
  543.4 4.0 fusion.71
  547.4 5.5 copy-done
  552.9 4.6 fusion.73
  557.6 9.0 %fusion.72 = f32[640]{0:T(1024)S(1)} fusion(f32[640,6144]{1,0:T(8,128)} %copy-done, f32[640]{0:T(1024)S(1)} %get-tuple-element.327, pred[6144]{0:T(1024)(128)(4,1)S(1)} %compare_reduce_fusion.2), kind=kLoop, calls=%fused_computation.25.clone.1 | loop fusion | flops 15728000 | bytes 15739904 | tf_op jit(solution)/shard_map/while/body/eval_jaxpr/reduce_sum | solution.py:31
  566.7 2.2 divide_convert_fusion
  569.0 1.4 copy.60
  570.4 1.1 copy.61
  (84 shorter events, 3.0 us)
Async XLA Ops:
  0.6 5.4 copy-start.3
  0.6 5.8 %copy-start.5 = (s32[1,48]{1,0:T(1,128)S(1)}, s32[1,48]{1,0:T(1,128)}, u32[]{:S(2)}) copy-start(s32[1,48]{1,0:T(1,128)} %param.17) | copy-start | bytes 580
  40.9 7.5 %copy-start.2 = (bf16[1,1,2,128,512]{4,3,2,1,0:T(8,128)(2,1)S(1)}, bf16[1,1,2,128,512]{4,3,2,1,0:T(8,128)(2,1)}, u32[]{:S(2)}) copy-start(bf16[1,1,2,128,512]{4,3,2,1,0:T(8,128)(2,1)} %param.14) | copy-start | bytes 786436
  40.9 7.7 %copy-start.1 = (bf16[128,2560]{1,0:T(8,128)(2,1)S(1)}, bf16[128,2560]{1,0:T(8,128)(2,1)}, u32[]{:S(2)}) copy-start(bf16[128,2560]{1,0:T(8,128)(2,1)} %param.13) | copy-start | bytes 1966084
  40.9 9.1 %copy-start.4 = (s32[4]{0:T(128)S(1)}, s32[4]{0:T(128)}, u32[]{:S(2)}) copy-start(s32[4]{0:T(128)} %constant.144.clone.1) | copy-start | bytes 52
  40.9 374.9 %all-to-all-start.1 = ((bf16[16,4,2,128,512]{4,3,2,1,0:T(8,128)(2,1)}), bf16[16,4,2,128,512]{4,3,2,1,0:T(8,128)(2,1)}, u32[]{:S(2)}, u32[]{:S(2)}) async-start(bf16[16,4,2,128,512]{4,3,2,1,0:T(8,128)(2,1)} %broadcast_select_fusion), calls=%async_computation.1 | async-start | bytes 33554432 | tf_op jit(solution)/shard_map/all_to_all | solution.py:71
  48.4 365.0 %collective-permute-start = (bf16[1,2,128,512]{3,2,1,0:T(8,128)(2,1)S(1)}, bf16[1,2,128,512]{3,2,1,0:T(8,128)(2,1)S(1)}, u32[]{:S(2)}, u32[]{:S(2)}) collective-permute-start(bf16[1,2,128,512]{3,2,1,0:T(8,128)(2,1)S(1)} %bitcast.114), channel_id=1, source_target_pairs={{0,1},{1,2},{2,3},{3,4},{4,5},{5,6},{6,7},{7,8},{8,9},{9,10},{10,1... | collective-permute-start | bytes 786440 | tf_op jit(solution)/shard_map/ppermute | solution.py:15
  475.4 5.5 copy-start
  499.4 5.5 copy-start
  523.4 5.5 copy-start
  547.4 5.5 copy-start
where the time goes:
time: 573 us; the launch traced here: 571 us
  waiting for transfers between devices  360 us (63%)
  local copies, waits for them, and re-layouts  89.2 us (16%)
  other arithmetic  65.8 us (11%)
  matrix products  36.4 us (6%)
  blocking collectives  10.1 us (2%)
  starting transfers between devices  7.69 us (1%)
    ppermute x1, waiting for transfers between devices, shifted(): lax.ppermute(array, axis, [(i, (i + by) % size) for i in range(size)])  360 us
    reduce_sum x8, other arithmetic, one_head(): total = jnp.sum(expo, axis=1)  36.3 us
    while x8, local copies, waits for them, and re-layouts  22 us
    another operation x4, local copies, waits for them, and re-layouts, heads_major(): return rows.reshape(rows.shape[0], heads, HD).transpose(1, 0, 2)  19.5 us
    dot_general x8, matrix products, one_head(): jnp.dot(expo.astype(jnp.bfloat16), values, preferred_element_type=jnp.flo...  19.5 us
    unnamed x14, local copies, waits for them, and re-layouts  17.7 us
    dot_general x8, matrix products, one_head(): jnp.einsum('qd,kd->qk', query, keys, preferred_element_type=jnp.float32)  16.9 us
    select_n x1, other arithmetic, per_device(): looked = jnp.take(pool, jnp.maximum(wanted, 0).reshape(-1), axis=0)  14.2 us
  transfers between devices with their start and end apart: 2, of which 1 were waited for; matrix products, arithmetic and copies ran while one was open for 1% of the time, Pallas kernels for 0%

commit v1 on v0

v1 whole, which is shorter than its diff:
```python
import functools

import jax
import jax.numpy as jnp
from jax import lax
from jax.experimental import pallas as pl
from jax.experimental.pallas import tpu as pltpu
from jax.sharding import PartitionSpec as P

PAGE = 128
KVH = 4
GQ = 5
HD = 128
MAXP = 48
SCALE = HD ** (-0.5)
LOG2E = 1.4426950408889634
LOW = -1e30
CLUSTER = 4
BLOCK = 4
STAT = 16
ROWS = GQ * PAGE + STAT
CHUNK = GQ * HD
CONTRACT_LAST = (((1,), (1,)), ((), ()))


def swapped(array, axis, bit):
    size = lax.axis_size(axis)
    return lax.ppermute(array, axis, [(i, i ^ bit) for i in range(size)])


def shifted(array, axis, by):
    size = lax.axis_size(axis)
    return lax.ppermute(array, axis, [(i, (i + by) % size) for i in range(size)])


def attend_kernel(lines, head, q_head, picks, counts, lasts, mine, *refs):
    own_q, *other_q = refs[:lines]
    own, twin, side, both, fresh = refs[lines:lines + 5]
    outs = refs[lines + 5:2 * lines + 5]
    pages, queries, results, tops, acc, q_sems, page_sems, out_sems = refs[2 * lines + 5:]
    slots = own.shape[0]
    columns = pl.ds(head * HD, HD)
    extra = pages.shape[1] - 1

    q_copies = [pltpu.make_async_copy(own_q.at[:, pl.ds(head * CHUNK, CHUNK)], queries.at[0], q_sems.at[0])]
    for t in range(1, lines):
        q_copies.append(
            pltpu.make_async_copy(other_q[t - 1].at[:, pl.ds(q_head * CHUNK, CHUNK)], queries.at[t], q_sems.at[t])
        )
    for copy in q_copies:
        copy.start()
    pages[...] = jnp.zeros(pages.shape, pages.dtype)
    fresh_copy = pltpu.make_async_copy(fresh.at[:, :, columns], pages.at[0, extra], page_sems.at[0, extra])
    fresh_copy.start()

    def request_of(t):
        return lax.rem(mine[0] - t + lines, lines)

    def page_copy(source, slot, buffer, place):
        if source.shape[-1] == HD:
            origin = source.at[slot]
        else:
            origin = source.at[slot, :, :, columns]
        return pltpu.make_async_copy(origin, pages.at[buffer, place], page_sems.at[buffer, place])

    def fetch(t):
        request = request_of(t)
        buffer = lax.rem(t, 2)

        @pl.loop(0, counts[request])
        def _(place):
            code = picks[request, place]
            rank = lax.div(code, slots)
            slot = lax.rem(code, slots)
            for index, source in enumerate((own, twin, side, both)):
                @pl.when(rank == index)
                def _():
                    page_copy(source, slot, buffer, place).start()

    def arrive(t):
        buffer = lax.rem(t, 2)

        @pl.loop(0, counts[request_of(t)])
        def _(place):
            page_copy(own, 0, buffer, place).wait()

    def update(h, s, values):
        old = tops[h]
        new = jnp.maximum(old, jnp.max(s, axis=1, keepdims=True))
        tops[h] = new
        factor = SCALE * LOG2E
        fade = jnp.exp2((old - new) * factor)
        wide = jnp.concatenate([new] * (s.shape[1] // PAGE), axis=1)
        expo = jnp.exp2((s - wide) * factor).astype(jnp.bfloat16)
        fresh_acc = jnp.dot(expo, values, preferred_element_type=jnp.float32)
        acc[h] = acc[h] * jnp.concatenate([fade, fade], axis=1) + fresh_acc

    def with_ones(values):
        return jnp.concatenate([values, jnp.ones_like(values)], axis=1)

    def attend_block(t, buffer, index, limit):
        block = pages[buffer, pl.ds(index * BLOCK, BLOCK)]
        keys = block[:, 0].reshape(BLOCK * PAGE, HD)
        values = with_ones(block[:, 1].reshape(BLOCK * PAGE, HD))
        for h in range(GQ):
            query = queries[t, :, h * HD:(h + 1) * HD]
            s = lax.dot_general(query, keys, CONTRACT_LAST, preferred_element_type=jnp.float32)
            if limit is not None:
                s = jnp.where(lax.broadcasted_iota(jnp.int32, s.shape, 1) < limit, s, LOW)
            update(h, s, values)

    fetch(0)
    for copy in q_copies:
        copy.wait()
    fresh_copy.wait()

    @pl.loop(0, lines)
    def _(t):
        buffer = lax.rem(t, 2)
        request = request_of(t)
        count = counts[request]
        blocks = lax.div(count + BLOCK - 1, BLOCK)

        @pl.when(t + 1 < lines)
        def _():
            fetch(t + 1)

        tops[...] = jnp.full(tops.shape, LOW, jnp.float32)
        acc[...] = jnp.zeros(acc.shape, jnp.float32)

        @pl.when(t == 0)
        def _():
            keys = pages[0, extra, 0]
            values = with_ones(pages[0, extra, 1])
            for h in range(GQ):
                query = queries[0, :, h * HD:(h + 1) * HD]
                s = lax.dot_general(query, keys, CONTRACT_LAST, preferred_element_type=jnp.float32)
                seen = lax.broadcasted_iota(jnp.int32, s.shape, 1) <= lax.broadcasted_iota(jnp.int32, s.shape, 0)
                update(h, jnp.where(seen, s, LOW), values)

        arrive(t)

        @pl.loop(0, jnp.maximum(blocks - 1, 0))
        def _(index):
            attend_block(t, buffer, index, None)

        @pl.when(blocks > 0)
        def _():
            last = blocks - 1
            attend_block(t, buffer, last, (count - 1 - last * BLOCK) * PAGE + lasts[request])

        lane = lax.broadcasted_iota(jnp.int32, (PAGE, PAGE), 1)
        stat = jnp.zeros((PAGE, PAGE), jnp.float32)
        for h in range(GQ):
            total = acc[h, :, HD:]
            some = total > 0.0
            total = jnp.where(some, total, 1.0)
            results[t, h * PAGE:(h + 1) * PAGE, :] = (acc[h, :, :HD] / total).astype(jnp.bfloat16)
            level = jnp.where(some, tops[h] * SCALE + jnp.log(total), LOW)
            high = level.astype(jnp.bfloat16).astype(jnp.float32)
            middle = (level - high).astype(jnp.bfloat16).astype(jnp.float32)
            low = level - high - middle
            stat = jnp.where(lane == h, high, stat)
            stat = jnp.where(lane == GQ + h, middle, stat)
            stat = jnp.where(lane == 2 * GQ + h, low, stat)
        results[t, GQ * PAGE:, :] = stat.T[:STAT].astype(jnp.bfloat16)
        for index in range(lines):
            @pl.when(t == index)
            def _():
                pltpu.make_async_copy(results.at[index], outs[index], out_sems.at[index]).start()

    for index in range(lines):
        pltpu.make_async_copy(results.at[index], outs[index], out_sems.at[index]).wait()


def attend(head, q_head, tables, queries, pools, fresh):
    picks, counts, lasts, mine = tables
    lines = len(queries)
    places = picks.shape[1]
    keys = places * PAGE * 5 // 8
    grid_spec = pltpu.PrefetchScalarGridSpec(
        num_scalar_prefetch=4,
        grid=(),
        in_specs=[pl.BlockSpec(memory_space=pl.ANY)] * (lines + 5),
        out_specs=[pl.BlockSpec(memory_space=pl.ANY)] * lines,
        scratch_shapes=[
            pltpu.VMEM((2, places + 1, 2, PAGE, HD), jnp.bfloat16),
            pltpu.VMEM((lines, PAGE, CHUNK), jnp.bfloat16),
            pltpu.VMEM((lines, ROWS, HD), jnp.bfloat16),
            pltpu.VMEM((GQ, PAGE, PAGE), jnp.float32),
            pltpu.VMEM((GQ, PAGE, 2 * HD), jnp.float32),
            pltpu.SemaphoreType.DMA((lines,)),
            pltpu.SemaphoreType.DMA((2, places + 1)),
            pltpu.SemaphoreType.DMA((lines,)),
        ],
    )
    return pl.pallas_call(
        functools.partial(attend_kernel, lines, head, q_head),
        grid_spec=grid_spec,
        out_shape=[jax.ShapeDtypeStruct((ROWS, HD), jnp.bfloat16)] * lines,
        compiler_params=pltpu.CompilerParams(vmem_limit_bytes=24 * 2**20),
        cost_estimate=pl.CostEstimate(
            flops=lines * 4 * GQ * PAGE * keys * HD,
            bytes_accessed=lines * keys * 4 * HD + lines * 2 * (CHUNK * PAGE + ROWS * HD),
            transcendentals=lines * GQ * PAGE * keys,
        ),
    )(picks, counts, lasts, mine, *queries, *pools, fresh)


def merge_kernel(lines, head, *refs):
    parts = refs[:lines]
    out, result, sem = refs[-3:]
    levels = []
    for part in parts:
        block = part[GQ * PAGE:, :].astype(jnp.float32)
        levels.append(block[:GQ] + block[GQ:2 * GQ] + block[2 * GQ:3 * GQ])
    top = functools.reduce(jnp.maximum, levels)
    weights = [jnp.exp(level - top) for level in levels]
    total = functools.reduce(jnp.add, weights)
    weights = [weight / total for weight in weights]
    filler = PAGE - lines * GQ
    table = jnp.concatenate(weights + [jnp.zeros((filler, PAGE), jnp.float32)], axis=0).T
    for h in range(GQ):
        merged = jnp.zeros((PAGE, HD), jnp.float32)
        for i, part in enumerate(parts):
            column = i * GQ + h
            merged += table[:, column:column + 1] * part[h * PAGE:(h + 1) * PAGE, :].astype(jnp.float32)
        result[:, h * HD:(h + 1) * HD] = merged.astype(jnp.bfloat16)
    copy = pltpu.make_async_copy(result, out.at[:, pl.ds(head * CHUNK, CHUNK)], sem)
    copy.start()
    copy.wait()


def merge(head, parts, whole):
    lines = len(parts)
    before = [] if whole is None else [whole]
    return pl.pallas_call(
        functools.partial(merge_kernel, lines, head),
        in_specs=[pl.BlockSpec(memory_space=pltpu.VMEM)] * lines + [pl.BlockSpec(memory_space=pl.ANY)] * len(before),
        out_specs=pl.BlockSpec(memory_space=pl.ANY),
        out_shape=jax.ShapeDtypeStruct((PAGE, KVH * CHUNK), jnp.bfloat16),
        scratch_shapes=[pltpu.VMEM((PAGE, CHUNK), jnp.bfloat16), pltpu.SemaphoreType.DMA],
        input_output_aliases={lines: 0} if before else {},
        cost_estimate=pl.CostEstimate(
            flops=2 * lines * ROWS * HD, bytes_accessed=2 * (lines + 1) * ROWS * HD, transcendentals=0
        ),
    )(*parts, *before)


def page_tables(me, width, slots, page_owner, page_slot, prefix_len):
    lines = width // CLUSTER
    capacity = (MAXP + width - 2) // (width - 1)
    limit = min(MAXP, CLUSTER * capacity)
    groups = [[c * CLUSTER + i for c in range(lines)] for i in range(CLUSTER)]
    table = jnp.concatenate([page_owner[0], page_slot[0], prefix_len])[None]
    tables = lax.all_gather(table, "serve", axis_index_groups=groups, tiled=True)
    owners = tables[:, :MAXP]
    places = tables[:, MAXP:2 * MAXP]
    length = tables[:, 2 * MAXP]
    used = (length + PAGE - 1) // PAGE
    spot = jnp.arange(MAXP)
    here = (spot[None] < used[:, None]) & (owners // CLUSTER == me // CLUSTER)
    hits = here.astype(jnp.int32)
    before = jnp.sum(hits[:, None, :] * (spot[None, None, :] < spot[None, :, None]), axis=2)
    local = ((owners % CLUSTER) ^ (me % CLUSTER)) * slots + places
    chosen = here[:, :, None] & (before[:, :, None] == jnp.arange(limit)[None, None, :])
    picks = jnp.sum(jnp.where(chosen, local[:, :, None], 0), axis=1)
    counts = jnp.sum(hits, axis=1)
    tail = jnp.sum(jnp.where(here & (spot[None] == used[:, None] - 1), 1, 0), axis=1)
    lasts = jnp.where(tail > 0, length - (used - 1) * PAGE, PAGE)
    return picks, counts, lasts, (me // CLUSTER)[None]


def per_device(queries, new_kv, pool, page_owner, page_slot, prefix_len, store_slot):
    width = lax.axis_size("serve")
    lines = width // CLUSTER
    me = lax.axis_index("serve")
    slots = pool.shape[0]
    tables = page_tables(me, width, slots, page_owner, page_slot, prefix_len)
    fresh = new_kv[0, 0]
    sides = [swapped(pool[:, :, :, g * HD:(g + 1) * HD], "serve", 2) for g in range(KVH)]
    early = [shifted(queries[:, :CHUNK], "serve", t * CLUSTER) for t in range(1, lines)]
    twin = swapped(pool, "serve", 1)
    later = [shifted(queries[:, CHUNK:], "serve", t * CLUSTER) for t in range(1, lines)]
    incoming = shifted(new_kv[0], "serve", 1)
    attended = None
    for g in range(KVH):
        both = swapped(sides[g], "serve", 1)
        others = early if g == 0 else later
        parts = attend(g, max(g - 1, 0), tables, [queries] + others, (pool, twin, sides[g], both), fresh)
        parts = [part if t == 0 else shifted(part, "serve", -t * CLUSTER) for t, part in enumerate(parts)]
        attended = merge(g, parts, attended)
    pool_out = pool.at[store_slot[0]].set(incoming)
    return (attended, pool_out)


def solution(mesh):
    return jax.shard_map(
        per_device,
        mesh=mesh,
        in_specs=(
            P(("groups", "serve"), None),
            P(("groups", "serve"), None, None, None, None),
            P(("groups", "serve"), None, None, None),
            P(("groups", "serve"), None),
            P(("groups", "serve"), None),
            P(("groups", "serve")),
            P(("groups", "serve"), None),
        ),
        out_specs=(P(("groups", "serve"), None), P(("groups", "serve"), None, None, None)),
        check_vma=False,
    )
```

time: 573 us -> 233 us (0.41)
  the two profiles are of different devices: /device:TPU:18 before, /device:TPU:0 now
where the time goes in v1:
time: 233 us; the launch traced here: 232 us
  waiting for transfers between devices  86.3 us (37%)
  Pallas kernels  68.7 us (29%)
  starting transfers between devices  44.3 us (19%)
  local copies, waits for them, and re-layouts  18.7 us (8%)
  blocking collectives  7.15 us (3%)
  other arithmetic  4.18 us (2%)
  between operations  2.98 us (1%)
    pallas_call x4, Pallas kernels, attend(): pl.pallas_call(functools.partial(attend_kernel, lines, head, q_head), gri...  59.1 us
    ppermute x9, waiting for transfers between devices, swapped(): return lax.ppermute(array, axis, [(i, i ^ bit) for i in range(size)])  46.3 us
    ppermute x19, waiting for transfers between devices, shifted(): lax.ppermute(array, axis, [(i, (i + by) % size) for i in range(size)])  40 us
    ppermute x19, starting transfers between devices, shifted(): lax.ppermute(array, axis, [(i, (i + by) % size) for i in range(size)])  38.8 us
    unnamed x61, local copies, waits for them, and re-layouts  14.1 us
    pallas_call x4, Pallas kernels, merge(): pl.pallas_call(functools.partial(merge_kernel, lines, head), in_specs=[pl...  9.67 us
    unnamed x1, blocking collectives  7.15 us
    ppermute x9, starting transfers between devices, swapped(): return lax.ppermute(array, axis, [(i, i ^ bit) for i in range(size)])  5.48 us
  transfers between devices with their start and end apart: 28, of which 9 were waited for; matrix products, arithmetic and copies ran while one was open for 4% of the time, Pallas kernels for 29%

profile of v1, /device:TPU:0, one launch (start us, length us, event | category | flops | bytes accessed | tf_op | source)
XLA Modules:
  0.0 232.3 jit_solution(14737903178427263017)
XLA Ops:
  0.6 4.6 %copy.23.refs_4_ = bf16[16,2,128,512]{3,2,1,0:T(8,128)(2,1)} copy(bf16[16,2,128,512]{3,2,1,0:T(8,128)(2,1)} %param.11) | data formatting | bytes 8388608
  5.8 4.4 %fusion.12 = (bf16[16,2,128,128]{3,2,1,0:T(8,128)(2,1)}, bf16[16,2,128,128]{3,2,1,0:T(8,128)(2,1)}, bf16[16,2,128,128]{3,2,1,0:T(8,128)(2,1)}, bf16[16,2,128,128]{3,2,1,0:T(8,128)(2,1)}) fusion(bf16[16,2,128,512]{3,2,1,0:T(8,128)(2,1)} %copy.23.refs_4_), kind=kLoop, calls=%fused_computation.42 | loop fusion | bytes 8388608 | tf_op jit(solution)/shard_map/slice | solution.py:281
  10.2 2.6 %collective-permute-start.22 = (bf16[16,2,128,128]{3,2,1,0:T(8,128)(2,1)}, bf16[16,2,128,128]{3,2,1,0:T(8,128)(2,1)}, u32[]{:S(2)}, u32[]{:S(2)}) collective-permute-start(bf16[16,2,128,128]{3,2,1,0:T(8,128)(2,1)} %get-tuple-element.52), channel_id=1, source_target_pairs={{0,2},{1,3},{2,0},{3,1},{4,6},{5,7},{6,4},{7,5},{8,10},{9,11},{10,... | collective-permute-start | bytes 3145736 | tf_op jit(solution)/shard_map/ppermute | solution.py:28
  12.8 1.6 collective-permute-start.19
  14.5 1.6 collective-permute-start
  16.1 1.2 collective-permute-start.20
  17.4 4.4 %collective-permute-done.19.refs_1_ = bf16[128,640]{1,0:T(8,128)(2,1)S(1)} collective-permute-done((bf16[128,640]{1,0:T(8,128)(2,1)S(1)}, bf16[128,640]{1,0:T(8,128)(2,1)S(1)}, u32[]{:S(2)}, u32[]{:S(2)}) %collective-permute-start.19) | collective-permute-done | bytes 163872 | tf_op jit(solution)/shard_map/ppermute | solution.py:33
  21.8 0.7 copy-done.6
  22.7 15.8 %collective-permute-done.20.refs_2_ = bf16[128,640]{1,0:T(8,128)(2,1)S(1)} collective-permute-done((bf16[128,640]{1,0:T(8,128)(2,1)S(1)}, bf16[128,640]{1,0:T(8,128)(2,1)S(1)}, u32[]{:S(2)}, u32[]{:S(2)}) %collective-permute-start.20) | collective-permute-done | bytes 163872 | tf_op jit(solution)/shard_map/ppermute | solution.py:33
  38.6 0.7 copy-done.8
  39.2 1.6 collective-permute-start.21
  40.8 4.5 %collective-permute-done.21.refs_3_ = bf16[128,640]{1,0:T(8,128)(2,1)S(1)} collective-permute-done((bf16[128,640]{1,0:T(8,128)(2,1)S(1)}, bf16[128,640]{1,0:T(8,128)(2,1)S(1)}, u32[]{:S(2)}, u32[]{:S(2)}) %collective-permute-start.21) | collective-permute-done | bytes 163872 | tf_op jit(solution)/shard_map/ppermute | solution.py:33
  45.3 0.7 copy-done.10
  46.5 1.5 collective-permute-start.4
  50.1 7.2 %all-reduce = s32[388]{0:T(512)S(1)} all-reduce(s32[388]{0:T(512)S(1)} %add_dynamic-update-slice_fusion), channel_id=2, replica_groups={{0,4,8,12},{1,5,9,13},{2,6,10,14},{3,7,11,15},{16,20,24,28},{17,21,25,2..., use_global_device_ids=true, to_apply=%add | all-reduce | flops 388 | bytes 3104
  57.7 1.8 collective-permute-done.14.refs_6_
  59.7 22.3 %collective-permute-done.9.refs_6_ = bf16[16,2,128,128]{3,2,1,0:T(8,128)(2,1)} collective-permute-done((bf16[16,2,128,128]{3,2,1,0:T(8,128)(2,1)}, bf16[16,2,128,128]{3,2,1,0:T(8,128)(2,1)}, u32[]{:S(2)}, u32[]{:S(2)}) %collective-permute-start.9) | collective-permute-done | bytes 1048608 | tf_op jit(solution)/shard_map/ppermute | solution.py:28
  82.1 22.1 %collective-permute-done.4.refs_6_ = bf16[16,2,128,128]{3,2,1,0:T(8,128)(2,1)S(1)} collective-permute-done((bf16[16,2,128,128]{3,2,1,0:T(8,128)(2,1)}, bf16[16,2,128,128]{3,2,1,0:T(8,128)(2,1)S(1)}, u32[]{:S(2)}, u32[]{:S(2)}) %collective-permute-start.4) | collective-permute-done | bytes 1048608 | tf_op jit(solution)/shard_map/ppermute | solution.py:28
  105.1 2.8 %collective-permute-start.1 = (bf16[128,1920]{1,0:T(8,128)(2,1)}, bf16[128,1920]{1,0:T(8,128)(2,1)S(1)}, u32[]{:S(2)}, u32[]{:S(2)}) collective-permute-start(bf16[128,1920]{1,0:T(8,128)(2,1)} %copy-done.12), channel_id=1, source_target_pairs={{0,8},{1,9},{2,10},{3,11},{4,12},{5,13},{6,14},{7,15},{8,0},{9,1},... | collective-permute-start | bytes 1474568 | tf_op jit(solution)/shard_map/ppermute | solution.py:33
  107.9 1.3 collective-permute-start.2
  109.4 0.9 copy-done.7
  110.3 0.9 copy-done.9
  111.3 0.9 copy-done.11
  112.2 14.7 %shard_map.89 = (bf16[656,128]{1,0:T(8,128)(2,1)S(1)}, bf16[656,128]{1,0:T(8,128)(2,1)S(1)}, bf16[656,128]{1,0:T(8,128)(2,1)S(1)}, bf16[656,128]{1,0:T(8,128)(2,1)S(1)}) custom-call(s32[4,16]{1,0:T(4,128)S(1)} %select_reduce_fusion.picks, s32[4]{0:T(128)S(1)} %get-tuple-element.49.counts, s32[4]{0:T(128)S(1)} %compare_select_fusion.lasts, s32[1]{0:T(128)} %bitcast.3.mine, ...), custom_call_target="tpu_custom_call" | custom-call | flops 1677721600 | bytes 3948544 | tf_op jit(solution)/shard_map/pallas_call | solution.py:197
  126.9 0.7 copy-done.2
  127.6 3.2 %collective-permute-done.1.refs_2_ = bf16[128,1920]{1,0:T(8,128)(2,1)S(1)} collective-permute-done((bf16[128,1920]{1,0:T(8,128)(2,1)}, bf16[128,1920]{1,0:T(8,128)(2,1)S(1)}, u32[]{:S(2)}, u32[]{:S(2)}) %collective-permute-start.1) | collective-permute-done | bytes 491552 | tf_op jit(solution)/shard_map/ppermute | solution.py:33
  130.9 13.8 %collective-permute-start.24 = (bf16[656,128]{1,0:T(8,128)(2,1)S(1)}, bf16[656,128]{1,0:T(8,128)(2,1)S(1)}, u32[]{:S(2)}, u32[]{:S(2)}) collective-permute-start(bf16[656,128]{1,0:T(8,128)(2,1)S(1)} %get-tuple-element.43), channel_id=1, source_target_pairs={{0,12},{1,13},{2,14},{3,15},{4,0},{5,1},{6,2},{7,3},{8,4},{9,5},{1... | collective-permute-start | bytes 503816 | tf_op jit(solution)/shard_map/ppermute | solution.py:33
  144.7 15.1 %shard_map.88 = (bf16[656,128]{1,0:T(8,128)(2,1)S(1)}, bf16[656,128]{1,0:T(8,128)(2,1)S(1)}, bf16[656,128]{1,0:T(8,128)(2,1)S(1)}, bf16[656,128]{1,0:T(8,128)(2,1)S(1)}) custom-call(s32[4,16]{1,0:T(4,128)S(1)} %select_reduce_fusion.picks, s32[4]{0:T(128)S(1)} %get-tuple-element.49.counts, s32[4]{0:T(128)S(1)} %compare_select_fusion.lasts, s32[1]{0:T(128)} %bitcast.3.mine, ...), custom_call_target="tpu_custom_call" | custom-call | flops 1677721600 | bytes 3948544 | tf_op jit(solution)/shard_map/pallas_call | solution.py:197
  159.8 0.7 copy-done.4
  160.5 0.7 collective-permute-start.26
  161.1 14.1 %shard_map.87 = (bf16[656,128]{1,0:T(8,128)(2,1)S(1)}, bf16[656,128]{1,0:T(8,128)(2,1)S(1)}, bf16[656,128]{1,0:T(8,128)(2,1)S(1)}, bf16[656,128]{1,0:T(8,128)(2,1)S(1)}) custom-call(s32[4,16]{1,0:T(4,128)S(1)} %select_reduce_fusion.picks, s32[4]{0:T(128)S(1)} %get-tuple-element.49.counts, s32[4]{0:T(128)S(1)} %compare_select_fusion.lasts, s32[1]{0:T(128)} %bitcast.3.mine, ...), custom_call_target="tpu_custom_call" | custom-call | flops 1677721600 | bytes 3948544 | tf_op jit(solution)/shard_map/pallas_call | solution.py:197
  175.3 0.7 copy-done.3
  176.0 3.2 %collective-permute-start.16 = (bf16[656,128]{1,0:T(8,128)(2,1)S(1)}, bf16[656,128]{1,0:T(8,128)(2,1)S(1)}, u32[]{:S(2)}, u32[]{:S(2)}) collective-permute-start(bf16[656,128]{1,0:T(8,128)(2,1)S(1)} %get-tuple-element.39), channel_id=1, source_target_pairs={{0,12},{1,13},{2,14},{3,15},{4,0},{5,1},{6,2},{7,3},{8,4},{9,5},{1... | collective-permute-start | bytes 503816 | tf_op jit(solution)/shard_map/ppermute | solution.py:33
  179.1 2.0 collective-permute-start.17
  181.2 0.8 collective-permute-start.18
  181.9 3.1 %collective-permute-start.11 = (bf16[656,128]{1,0:T(8,128)(2,1)S(1)}, bf16[656,128]{1,0:T(8,128)(2,1)S(1)}, u32[]{:S(2)}, u32[]{:S(2)}) collective-permute-start(bf16[656,128]{1,0:T(8,128)(2,1)S(1)} %get-tuple-element.35), channel_id=1, source_target_pairs={{0,12},{1,13},{2,14},{3,15},{4,0},{5,1},{6,2},{7,3},{8,4},{9,5},{1... | collective-permute-start | bytes 503816 | tf_op jit(solution)/shard_map/ppermute | solution.py:33
  185.0 0.7 and_reduce_fusion
  185.7 15.1 %shard_map.86 = (bf16[656,128]{1,0:T(8,128)(2,1)S(1)}, bf16[656,128]{1,0:T(8,128)(2,1)S(1)}, bf16[656,128]{1,0:T(8,128)(2,1)S(1)}, bf16[656,128]{1,0:T(8,128)(2,1)S(1)}) custom-call(s32[4,16]{1,0:T(4,128)S(1)} %select_reduce_fusion.picks, s32[4]{0:T(128)S(1)} %get-tuple-element.49.counts, s32[4]{0:T(128)S(1)} %compare_select_fusion.lasts, s32[1]{0:T(128)} %bitcast.3.mine, ...), custom_call_target="tpu_custom_call" | custom-call | flops 1677721600 | bytes 3948544 | tf_op jit(solution)/shard_map/pallas_call | solution.py:197
  202.2 3.3 %collective-permute-start.6 = (bf16[656,128]{1,0:T(8,128)(2,1)S(1)}, bf16[656,128]{1,0:T(8,128)(2,1)S(1)}, u32[]{:S(2)}, u32[]{:S(2)}) collective-permute-start(bf16[656,128]{1,0:T(8,128)(2,1)S(1)} %get-tuple-element.31), channel_id=1, source_target_pairs={{0,12},{1,13},{2,14},{3,15},{4,0},{5,1},{6,2},{7,3},{8,4},{9,5},{1... | collective-permute-start | bytes 503816 | tf_op jit(solution)/shard_map/ppermute | solution.py:33
  205.4 1.1 collective-permute-start.7
  206.6 2.4 %select_dynamic-update-slice_fusion = bf16[16,2,128,512]{3,2,1,0:T(8,128)(2,1)} fusion(bf16[16,2,128,512]{3,2,1,0:T(8,128)(2,1)} %copy.23.refs_4_, s32[]{:T(128)} %bitcast.7, bf16[1,2,128,512]{3,2,1,0:T(8,128)(2,1)S(1)} %collective-permute-done.27, pred[]{:T(512)} %and_reduce_fusion), kind=kLoop, calls=%fused_computation | loop fusion | flops 131072 | bytes 787456 | tf_op jit(solution)/shard_map/scatter | solution.py:293
  209.0 2.4 %shard_map.90.refs_4_ = bf16[128,2560]{1,0:T(8,128)(2,1)} custom-call(bf16[656,128]{1,0:T(8,128)(2,1)} %copy-done.2, bf16[656,128]{1,0:T(8,128)(2,1)} %copy-done.13, bf16[656,128]{1,0:T(8,128)(2,1)} %copy-done.14, bf16[656,128]{1,0:T(8,128)(2,1)} %copy-done.15), custom_call_target="tpu_custom_call" | custom-call | flops 671744 | bytes 839680 | tf_op jit(solution)/shard_map/pallas_call | solution.py:237
  211.4 2.4 %shard_map.91.refs_4_ = bf16[128,2560]{1,0:T(8,128)(2,1)} custom-call(bf16[656,128]{1,0:T(8,128)(2,1)} %copy-done.4, bf16[656,128]{1,0:T(8,128)(2,1)} %copy-done.16, bf16[656,128]{1,0:T(8,128)(2,1)} %copy-done.17, bf16[656,128]{1,0:T(8,128)(2,1)} %copy-done.19, bf16[128,2560]{1,0:T(8,128)(2,1)} %shard_map.90.refs_4_), custom_call_target="tpu_custom_call", output_to_operand_aliasing={{}: (4, {})} | custom-call | flops 671744 | bytes 839680 | tf_op jit(solution)/shard_map/pallas_call | solution.py:237
  213.8 1.4 collective-permute-done.12.refs_2_
  215.3 0.7 copy-done.21
  216.0 2.4 %shard_map.92.refs_4_ = bf16[128,2560]{1,0:T(8,128)(2,1)} custom-call(bf16[656,128]{1,0:T(8,128)(2,1)} %copy-done.3, bf16[656,128]{1,0:T(8,128)(2,1)} %copy-done.18, bf16[656,128]{1,0:T(8,128)(2,1)} %copy-done.21, bf16[656,128]{1,0:T(8,128)(2,1)} %copy-done.23, bf16[128,2560]{1,0:T(8,128)(2,1)} %shard_map.91.refs_4_), custom_call_target="tpu_custom_call", output_to_operand_aliasing={{}: (4, {})} | custom-call | flops 671744 | bytes 839680 | tf_op jit(solution)/shard_map/pallas_call | solution.py:237
  218.4 10.6 %collective-permute-done.7.refs_2_ = bf16[656,128]{1,0:T(8,128)(2,1)S(1)} collective-permute-done((bf16[656,128]{1,0:T(8,128)(2,1)S(1)}, bf16[656,128]{1,0:T(8,128)(2,1)S(1)}, u32[]{:S(2)}, u32[]{:S(2)}) %collective-permute-start.7) | collective-permute-done | bytes 167968 | tf_op jit(solution)/shard_map/ppermute | solution.py:33
  229.7 2.4 %shard_map.93 = bf16[128,2560]{1,0:T(8,128)(2,1)} custom-call(bf16[656,128]{1,0:T(8,128)(2,1)} %copy-done.5, bf16[656,128]{1,0:T(8,128)(2,1)} %copy-done.20, bf16[656,128]{1,0:T(8,128)(2,1)} %copy-done.22, bf16[656,128]{1,0:T(8,128)(2,1)} %copy-done.24, bf16[128,2560]{1,0:T(8,128)(2,1)} %shard_map.92.refs_4_), custom_call_target="tpu_custom_call", output_to_operand_aliasing={{}: (4, {})} | custom-call | flops 671744 | bytes 839680 | tf_op jit(solution)/shard_map/pallas_call | solution.py:237
  (94 shorter events, 5.5 us)
Async XLA Ops:
  5.3 7.5 %copy-start = (bf16[128,2560]{1,0:T(8,128)(2,1)S(1)}, bf16[128,2560]{1,0:T(8,128)(2,1)}, u32[]{:S(2)}) copy-start(bf16[128,2560]{1,0:T(8,128)(2,1)} %refs_0_.7) | copy-start | bytes 1966084
  5.3 43.4 %copy-start.28 = (u32[32]{0:T(128)S(1)}, u32[32]{0:T(128)}, u32[]{:S(2)}) copy-start(u32[32]{0:T(128)} %constant.110) | copy-start | bytes 388
  5.3 44.6 %copy-start.25 = (s32[1,48]{1,0:T(1,128)S(1)}, s32[1,48]{1,0:T(1,128)}, u32[]{:S(2)}) copy-start(s32[1,48]{1,0:T(1,128)} %param.13) | copy-start | bytes 580
  5.3 44.6 %copy-start.26 = (s32[1,48]{1,0:T(1,128)S(1)}, s32[1,48]{1,0:T(1,128)}, u32[]{:S(2)}) copy-start(s32[1,48]{1,0:T(1,128)} %param.12) | copy-start | bytes 580
  5.3 104.1 %copy-start.1 = (bf16[1,1,2,128,512]{4,3,2,1,0:T(8,128)(2,1)S(1)}, bf16[1,1,2,128,512]{4,3,2,1,0:T(8,128)(2,1)}, u32[]{:S(2)}) copy-start(bf16[1,1,2,128,512]{4,3,2,1,0:T(8,128)(2,1)} %param.10) | copy-start | bytes 786436
  5.3 102.6 %collective-permute-start.3 = (bf16[16,2,128,512]{3,2,1,0:T(8,128)(2,1)}, bf16[16,2,128,512]{3,2,1,0:T(8,128)(2,1)}, u32[]{:S(2)}, u32[]{:S(2)}) collective-permute-start(bf16[16,2,128,512]{3,2,1,0:T(8,128)(2,1)} %copy.23.refs_4_), channel_id=1, source_target_pairs={{0,1},{1,0},{2,3},{3,2},{4,5},{5,4},{6,7},{7,6},{8,9},{9,8},{10,11... | collective-permute-start | bytes 12582920 | tf_op jit(solution)/shard_map/ppermute | solution.py:28
  10.2 39.6 %collective-permute-start.22 = (bf16[16,2,128,128]{3,2,1,0:T(8,128)(2,1)}, bf16[16,2,128,128]{3,2,1,0:T(8,128)(2,1)}, u32[]{:S(2)}, u32[]{:S(2)}) collective-permute-start(bf16[16,2,128,128]{3,2,1,0:T(8,128)(2,1)} %get-tuple-element.52), channel_id=1, source_target_pairs={{0,2},{1,3},{2,0},{3,1},{4,6},{5,7},{6,4},{7,5},{8,10},{9,11},{10,... | collective-permute-start | bytes 3145736 | tf_op jit(solution)/shard_map/ppermute | solution.py:28
  12.8 9.0 %collective-permute-start.19 = (bf16[128,640]{1,0:T(8,128)(2,1)S(1)}, bf16[128,640]{1,0:T(8,128)(2,1)S(1)}, u32[]{:S(2)}, u32[]{:S(2)}) collective-permute-start(bf16[128,640]{1,0:T(8,128)(2,1)S(1)} %slice.62), channel_id=1, source_target_pairs={{0,4},{1,5},{2,6},{3,7},{4,8},{5,9},{6,10},{7,11},{8,12},{9,13},{1... | collective-permute-start | bytes 491528 | tf_op jit(solution)/shard_map/ppermute | solution.py:33
  14.5 32.0 %copy-start.12 = (bf16[128,1920]{1,0:T(8,128)(2,1)}, bf16[128,1920]{1,0:T(8,128)(2,1)S(1)}, u32[]{:S(2)}) copy-start(bf16[128,1920]{1,0:T(8,128)(2,1)S(1)} %slice.58) | copy-start | bytes 1474564
  14.5 32.0 %collective-permute-start = (bf16[128,1920]{1,0:T(8,128)(2,1)S(1)}, bf16[128,1920]{1,0:T(8,128)(2,1)S(1)}, u32[]{:S(2)}, u32[]{:S(2)}) collective-permute-start(bf16[128,1920]{1,0:T(8,128)(2,1)S(1)} %slice.58), channel_id=1, source_target_pairs={{0,4},{1,5},{2,6},{3,7},{4,8},{5,9},{6,10},{7,11},{8,12},{9,13},{1... | collective-permute-start | bytes 1474568 | tf_op jit(solution)/shard_map/ppermute | solution.py:33
  16.1 22.4 %collective-permute-start.20 = (bf16[128,640]{1,0:T(8,128)(2,1)S(1)}, bf16[128,640]{1,0:T(8,128)(2,1)S(1)}, u32[]{:S(2)}, u32[]{:S(2)}) collective-permute-start(bf16[128,640]{1,0:T(8,128)(2,1)S(1)} %slice.62), channel_id=1, source_target_pairs={{0,8},{1,9},{2,10},{3,11},{4,12},{5,13},{6,14},{7,15},{8,0},{9,1},... | collective-permute-start | bytes 491528 | tf_op jit(solution)/shard_map/ppermute | solution.py:33
  22.5 37.0 %collective-permute-start.14 = (bf16[16,2,128,128]{3,2,1,0:T(8,128)(2,1)}, bf16[16,2,128,128]{3,2,1,0:T(8,128)(2,1)S(1)}, u32[]{:S(2)}, u32[]{:S(2)}) collective-permute-start(bf16[16,2,128,128]{3,2,1,0:T(8,128)(2,1)} %get-tuple-element.53), channel_id=1, source_target_pairs={{0,2},{1,3},{2,0},{3,1},{4,6},{5,7},{6,4},{7,5},{8,10},{9,11},{10,... | collective-permute-start | bytes 3145736 | tf_op jit(solution)/shard_map/ppermute | solution.py:28
  39.2 6.1 %collective-permute-start.21 = (bf16[128,640]{1,0:T(8,128)(2,1)S(1)}, bf16[128,640]{1,0:T(8,128)(2,1)S(1)}, u32[]{:S(2)}, u32[]{:S(2)}) collective-permute-start(bf16[128,640]{1,0:T(8,128)(2,1)S(1)} %slice.62), channel_id=1, source_target_pairs={{0,12},{1,13},{2,14},{3,15},{4,0},{5,1},{6,2},{7,3},{8,4},{9,5},{1... | collective-permute-start | bytes 491528 | tf_op jit(solution)/shard_map/ppermute | solution.py:33
  46.0 36.1 %collective-permute-start.9 = (bf16[16,2,128,128]{3,2,1,0:T(8,128)(2,1)}, bf16[16,2,128,128]{3,2,1,0:T(8,128)(2,1)}, u32[]{:S(2)}, u32[]{:S(2)}) collective-permute-start(bf16[16,2,128,128]{3,2,1,0:T(8,128)(2,1)} %get-tuple-element.54), channel_id=1, source_target_pairs={{0,2},{1,3},{2,0},{3,1},{4,6},{5,7},{6,4},{7,5},{8,10},{9,11},{10,... | collective-permute-start | bytes 3145736 | tf_op jit(solution)/shard_map/ppermute | solution.py:28
  46.5 57.7 %collective-permute-start.4 = (bf16[16,2,128,128]{3,2,1,0:T(8,128)(2,1)}, bf16[16,2,128,128]{3,2,1,0:T(8,128)(2,1)S(1)}, u32[]{:S(2)}, u32[]{:S(2)}) collective-permute-start(bf16[16,2,128,128]{3,2,1,0:T(8,128)(2,1)} %get-tuple-element.55), channel_id=1, source_target_pairs={{0,2},{1,3},{2,0},{3,1},{4,6},{5,7},{6,4},{7,5},{8,10},{9,11},{10,... | collective-permute-start | bytes 3145736 | tf_op jit(solution)/shard_map/ppermute | solution.py:28
  49.8 55.2 %collective-permute-start.23 = (bf16[16,2,128,128]{3,2,1,0:T(8,128)(2,1)}, bf16[16,2,128,128]{3,2,1,0:T(8,128)(2,1)}, u32[]{:S(2)}, u32[]{:S(2)}) collective-permute-start(bf16[16,2,128,128]{3,2,1,0:T(8,128)(2,1)} %collective-permute-done.22.refs_6_), channel_id=1, source_target_pairs={{0,1},{1,0},{2,3},{3,2},{4,5},{5,4},{6,7},{7,6},{8,9},{9,8},{10,11... | collective-permute-start | bytes 3145736 | tf_op jit(solution)/shard_map/ppermute | solution.py:28
  59.5 85.2 %collective-permute-start.15 = (bf16[16,2,128,128]{3,2,1,0:T(8,128)(2,1)S(1)}, bf16[16,2,128,128]{3,2,1,0:T(8,128)(2,1)}, u32[]{:S(2)}, u32[]{:S(2)}) collective-permute-start(bf16[16,2,128,128]{3,2,1,0:T(8,128)(2,1)S(1)} %collective-permute-done.14.refs_6_), channel_id=1, source_target_pairs={{0,1},{1,0},{2,3},{3,2},{4,5},{5,4},{6,7},{7,6},{8,9},{9,8},{10,11... | collective-permute-start | bytes 3145736 | tf_op jit(solution)/shard_map/ppermute | solution.py:28
  82.1 78.4 %collective-permute-start.10 = (bf16[16,2,128,128]{3,2,1,0:T(8,128)(2,1)}, bf16[16,2,128,128]{3,2,1,0:T(8,128)(2,1)}, u32[]{:S(2)}, u32[]{:S(2)}) collective-permute-start(bf16[16,2,128,128]{3,2,1,0:T(8,128)(2,1)} %collective-permute-done.9.refs_6_), channel_id=1, source_target_pairs={{0,1},{1,0},{2,3},{3,2},{4,5},{5,4},{6,7},{7,6},{8,9},{9,8},{10,11... | collective-permute-start | bytes 3145736 | tf_op jit(solution)/shard_map/ppermute | solution.py:28
  104.2 75.0 %collective-permute-start.5 = (bf16[16,2,128,128]{3,2,1,0:T(8,128)(2,1)S(1)}, bf16[16,2,128,128]{3,2,1,0:T(8,128)(2,1)}, u32[]{:S(2)}, u32[]{:S(2)}) collective-permute-start(bf16[16,2,128,128]{3,2,1,0:T(8,128)(2,1)S(1)} %collective-permute-done.4.refs_6_), channel_id=1, source_target_pairs={{0,1},{1,0},{2,3},{3,2},{4,5},{5,4},{6,7},{7,6},{8,9},{9,8},{10,11... | collective-permute-start | bytes 3145736 | tf_op jit(solution)/shard_map/ppermute | solution.py:28
  105.1 25.8 %collective-permute-start.1 = (bf16[128,1920]{1,0:T(8,128)(2,1)}, bf16[128,1920]{1,0:T(8,128)(2,1)S(1)}, u32[]{:S(2)}, u32[]{:S(2)}) collective-permute-start(bf16[128,1920]{1,0:T(8,128)(2,1)} %copy-done.12), channel_id=1, source_target_pairs={{0,8},{1,9},{2,10},{3,11},{4,12},{5,13},{6,14},{7,15},{8,0},{9,1},... | collective-permute-start | bytes 1474568 | tf_op jit(solution)/shard_map/ppermute | solution.py:33
  107.9 23.0 %collective-permute-start.2 = (bf16[128,1920]{1,0:T(8,128)(2,1)}, bf16[128,1920]{1,0:T(8,128)(2,1)S(1)}, u32[]{:S(2)}, u32[]{:S(2)}) collective-permute-start(bf16[128,1920]{1,0:T(8,128)(2,1)} %copy-done.12), channel_id=1, source_target_pairs={{0,12},{1,13},{2,14},{3,15},{4,0},{5,1},{6,2},{7,3},{8,4},{9,5},{1... | collective-permute-start | bytes 1474568 | tf_op jit(solution)/shard_map/ppermute | solution.py:33
  109.4 0.9 copy-start.7
  110.3 0.9 copy-start.9
  111.3 0.9 copy-start.11
  130.9 45.1 %collective-permute-start.27 = (bf16[1,2,128,512]{3,2,1,0:T(8,128)(2,1)S(1)}, bf16[1,2,128,512]{3,2,1,0:T(8,128)(2,1)S(1)}, u32[]{:S(2)}, u32[]{:S(2)}) collective-permute-start(bf16[1,2,128,512]{3,2,1,0:T(8,128)(2,1)S(1)} %bitcast.12), channel_id=1, source_target_pairs={{0,1},{1,2},{2,3},{3,4},{4,5},{5,6},{6,7},{7,8},{8,9},{9,10},{10,1... | collective-permute-start | bytes 786440 | tf_op jit(solution)/shard_map/ppermute | solution.py:33
  130.9 50.3 %collective-permute-start.24 = (bf16[656,128]{1,0:T(8,128)(2,1)S(1)}, bf16[656,128]{1,0:T(8,128)(2,1)S(1)}, u32[]{:S(2)}, u32[]{:S(2)}) collective-permute-start(bf16[656,128]{1,0:T(8,128)(2,1)S(1)} %get-tuple-element.43), channel_id=1, source_target_pairs={{0,12},{1,13},{2,14},{3,15},{4,0},{5,1},{6,2},{7,3},{8,4},{9,5},{1... | collective-permute-start | bytes 503816 | tf_op jit(solution)/shard_map/ppermute | solution.py:33
  144.7 37.3 %collective-permute-start.25 = (bf16[656,128]{1,0:T(8,128)(2,1)S(1)}, bf16[656,128]{1,0:T(8,128)(2,1)S(1)}, u32[]{:S(2)}, u32[]{:S(2)}) collective-permute-start(bf16[656,128]{1,0:T(8,128)(2,1)S(1)} %get-tuple-element.44), channel_id=1, source_target_pairs={{0,8},{1,9},{2,10},{3,11},{4,12},{5,13},{6,14},{7,15},{8,0},{9,1},... | collective-permute-start | bytes 503816 | tf_op jit(solution)/shard_map/ppermute | solution.py:33
  160.5 24.5 %copy-start.27 = (s32[4]{0:T(128)S(1)}, s32[4]{0:T(128)}, u32[]{:S(2)}) copy-start(s32[4]{0:T(128)} %constant.100.clone.1) | copy-start | bytes 52
  160.5 41.0 %collective-permute-start.26 = (bf16[656,128]{1,0:T(8,128)(2,1)S(1)}, bf16[656,128]{1,0:T(8,128)(2,1)S(1)}, u32[]{:S(2)}, u32[]{:S(2)}) collective-permute-start(bf16[656,128]{1,0:T(8,128)(2,1)S(1)} %get-tuple-element.45), channel_id=1, source_target_pairs={{0,4},{1,5},{2,6},{3,7},{4,8},{5,9},{6,10},{7,11},{8,12},{9,13},{1... | collective-permute-start | bytes 503816 | tf_op jit(solution)/shard_map/ppermute | solution.py:33
  176.0 25.5 %collective-permute-start.16 = (bf16[656,128]{1,0:T(8,128)(2,1)S(1)}, bf16[656,128]{1,0:T(8,128)(2,1)S(1)}, u32[]{:S(2)}, u32[]{:S(2)}) collective-permute-start(bf16[656,128]{1,0:T(8,128)(2,1)S(1)} %get-tuple-element.39), channel_id=1, source_target_pairs={{0,12},{1,13},{2,14},{3,15},{4,0},{5,1},{6,2},{7,3},{8,4},{9,5},{1... | collective-permute-start | bytes 503816 | tf_op jit(solution)/shard_map/ppermute | solution.py:33
  179.1 23.0 %collective-permute-start.17 = (bf16[656,128]{1,0:T(8,128)(2,1)S(1)}, bf16[656,128]{1,0:T(8,128)(2,1)S(1)}, u32[]{:S(2)}, u32[]{:S(2)}) collective-permute-start(bf16[656,128]{1,0:T(8,128)(2,1)S(1)} %get-tuple-element.40), channel_id=1, source_target_pairs={{0,8},{1,9},{2,10},{3,11},{4,12},{5,13},{6,14},{7,15},{8,0},{9,1},... | collective-permute-start | bytes 503816 | tf_op jit(solution)/shard_map/ppermute | solution.py:33
  181.2 19.7 %copy-start.13 = (bf16[656,128]{1,0:T(8,128)(2,1)}, bf16[656,128]{1,0:T(8,128)(2,1)S(1)}, u32[]{:S(2)}) copy-start(bf16[656,128]{1,0:T(8,128)(2,1)S(1)} %collective-permute-done.24.refs_1_) | copy-start | bytes 503812
  181.2 24.3 %collective-permute-start.18 = (bf16[656,128]{1,0:T(8,128)(2,1)S(1)}, bf16[656,128]{1,0:T(8,128)(2,1)S(1)}, u32[]{:S(2)}, u32[]{:S(2)}) collective-permute-start(bf16[656,128]{1,0:T(8,128)(2,1)S(1)} %get-tuple-element.41), channel_id=1, source_target_pairs={{0,4},{1,5},{2,6},{3,7},{4,8},{5,9},{6,10},{7,11},{8,12},{9,13},{1... | collective-permute-start | bytes 503816 | tf_op jit(solution)/shard_map/ppermute | solution.py:33
  181.9 18.9 %copy-start.14 = (bf16[656,128]{1,0:T(8,128)(2,1)}, bf16[656,128]{1,0:T(8,128)(2,1)S(1)}, u32[]{:S(2)}) copy-start(bf16[656,128]{1,0:T(8,128)(2,1)S(1)} %collective-permute-done.25.refs_2_) | copy-start | bytes 503812
  181.9 24.5 %collective-permute-start.11 = (bf16[656,128]{1,0:T(8,128)(2,1)S(1)}, bf16[656,128]{1,0:T(8,128)(2,1)S(1)}, u32[]{:S(2)}, u32[]{:S(2)}) collective-permute-start(bf16[656,128]{1,0:T(8,128)(2,1)S(1)} %get-tuple-element.35), channel_id=1, source_target_pairs={{0,12},{1,13},{2,14},{3,15},{4,0},{5,1},{6,2},{7,3},{8,4},{9,5},{1... | collective-permute-start | bytes 503816 | tf_op jit(solution)/shard_map/ppermute | solution.py:33
  201.5 7.4 %copy-start.15 = (bf16[656,128]{1,0:T(8,128)(2,1)}, bf16[656,128]{1,0:T(8,128)(2,1)S(1)}, u32[]{:S(2)}) copy-start(bf16[656,128]{1,0:T(8,128)(2,1)S(1)} %collective-permute-done.26.refs_3_) | copy-start | bytes 503812
  201.5 13.8 %collective-permute-start.12 = (bf16[656,128]{1,0:T(8,128)(2,1)S(1)}, bf16[656,128]{1,0:T(8,128)(2,1)S(1)}, u32[]{:S(2)}, u32[]{:S(2)}) collective-permute-start(bf16[656,128]{1,0:T(8,128)(2,1)S(1)} %get-tuple-element.36), channel_id=1, source_target_pairs={{0,8},{1,9},{2,10},{3,11},{4,12},{5,13},{6,14},{7,15},{8,0},{9,1},... | collective-permute-start | bytes 503816 | tf_op jit(solution)/shard_map/ppermute | solution.py:33
  201.5 7.4 %copy-start.16 = (bf16[656,128]{1,0:T(8,128)(2,1)}, bf16[656,128]{1,0:T(8,128)(2,1)S(1)}, u32[]{:S(2)}) copy-start(bf16[656,128]{1,0:T(8,128)(2,1)S(1)} %collective-permute-done.16.refs_1_) | copy-start | bytes 503812
  201.5 13.7 %collective-permute-start.13 = (bf16[656,128]{1,0:T(8,128)(2,1)S(1)}, bf16[656,128]{1,0:T(8,128)(2,1)S(1)}, u32[]{:S(2)}, u32[]{:S(2)}) collective-permute-start(bf16[656,128]{1,0:T(8,128)(2,1)S(1)} %get-tuple-element.37), channel_id=1, source_target_pairs={{0,4},{1,5},{2,6},{3,7},{4,8},{5,9},{6,10},{7,11},{8,12},{9,13},{1... | collective-permute-start | bytes 503816 | tf_op jit(solution)/shard_map/ppermute | solution.py:33
  202.2 6.8 %copy-start.17 = (bf16[656,128]{1,0:T(8,128)(2,1)}, bf16[656,128]{1,0:T(8,128)(2,1)S(1)}, u32[]{:S(2)}) copy-start(bf16[656,128]{1,0:T(8,128)(2,1)S(1)} %collective-permute-done.17.refs_2_) | copy-start | bytes 503812
  202.2 16.2 %collective-permute-start.6 = (bf16[656,128]{1,0:T(8,128)(2,1)S(1)}, bf16[656,128]{1,0:T(8,128)(2,1)S(1)}, u32[]{:S(2)}, u32[]{:S(2)}) collective-permute-start(bf16[656,128]{1,0:T(8,128)(2,1)S(1)} %get-tuple-element.31), channel_id=1, source_target_pairs={{0,12},{1,13},{2,14},{3,15},{4,0},{5,1},{6,2},{7,3},{8,4},{9,5},{1... | collective-permute-start | bytes 503816 | tf_op jit(solution)/shard_map/ppermute | solution.py:33
  205.4 3.5 %copy-start.19 = (bf16[656,128]{1,0:T(8,128)(2,1)}, bf16[656,128]{1,0:T(8,128)(2,1)S(1)}, u32[]{:S(2)}) copy-start(bf16[656,128]{1,0:T(8,128)(2,1)S(1)} %collective-permute-done.18.refs_3_) | copy-start | bytes 503812
  205.4 23.5 %collective-permute-start.7 = (bf16[656,128]{1,0:T(8,128)(2,1)S(1)}, bf16[656,128]{1,0:T(8,128)(2,1)S(1)}, u32[]{:S(2)}, u32[]{:S(2)}) collective-permute-start(bf16[656,128]{1,0:T(8,128)(2,1)S(1)} %get-tuple-element.32), channel_id=1, source_target_pairs={{0,8},{1,9},{2,10},{3,11},{4,12},{5,13},{6,14},{7,15},{8,0},{9,1},... | collective-permute-start | bytes 503816 | tf_op jit(solution)/shard_map/ppermute | solution.py:33
  206.5 2.5 %copy-start.18 = (bf16[656,128]{1,0:T(8,128)(2,1)}, bf16[656,128]{1,0:T(8,128)(2,1)S(1)}, u32[]{:S(2)}) copy-start(bf16[656,128]{1,0:T(8,128)(2,1)S(1)} %collective-permute-done.11.refs_1_) | copy-start | bytes 503812
  206.5 22.5 %collective-permute-start.8 = (bf16[656,128]{1,0:T(8,128)(2,1)S(1)}, bf16[656,128]{1,0:T(8,128)(2,1)S(1)}, u32[]{:S(2)}, u32[]{:S(2)}) collective-permute-start(bf16[656,128]{1,0:T(8,128)(2,1)S(1)} %get-tuple-element.33), channel_id=1, source_target_pairs={{0,4},{1,5},{2,6},{3,7},{4,8},{5,9},{6,10},{7,11},{8,12},{9,13},{1... | collective-permute-start | bytes 503816 | tf_op jit(solution)/shard_map/ppermute | solution.py:33
  215.3 0.7 copy-start.23
  218.4 10.6 %copy-start.20 = (bf16[656,128]{1,0:T(8,128)(2,1)}, bf16[656,128]{1,0:T(8,128)(2,1)S(1)}, u32[]{:S(2)}) copy-start(bf16[656,128]{1,0:T(8,128)(2,1)S(1)} %collective-permute-done.6.refs_1_) | copy-start | bytes 503812
  229.0 0.7 copy-start.24
  (9 other events, 6.0 us)

commit v2 on v1

v2 whole, which is shorter than its diff:
```python
import functools

import jax
import jax.numpy as jnp
from jax import lax
from jax.experimental import pallas as pl
from jax.experimental.pallas import tpu as pltpu
from jax.sharding import PartitionSpec as P

PAGE = 128
KVH = 4
GQ = 5
HD = 128
MAXP = 48
SCALE = HD ** (-0.5)
LOG2E = 1.4426950408889634
LOW = -1e30
CLUSTER = 4
BLOCK = 4
STAT = 16
ROWS = GQ * PAGE + STAT
CHUNK = GQ * HD
CONTRACT_LAST = (((1,), (1,)), ((), ()))


def swapped(array, axis, bit):
    size = lax.axis_size(axis)
    return lax.ppermute(array, axis, [(i, i ^ bit) for i in range(size)])


def shifted(array, axis, by):
    size = lax.axis_size(axis)
    return lax.ppermute(array, axis, [(i, (i + by) % size) for i in range(size)])


def attend_kernel(lines, head, q_head, picks, counts, lasts, mine, store, *refs):
    q_all, own, twin, side, both, fresh = refs[:6]
    stores = len(refs) == 19
    if stores:
        incoming, out, pool_out = refs[6:9]
        store_sems = refs[-1]
        scratch = refs[9:-1]
    else:
        out = refs[6]
        scratch = refs[7:]
    pages, queries, results, scores, tops, acc, q_sems, page_sems, out_sems = scratch
    slots = own.shape[0]
    columns = pl.ds(head * HD, HD)
    extra = pages.shape[1] - 1

    def request_of(t):
        return lax.rem(mine[0] - t + lines, lines)

    def q_copy(t):
        origin = q_all.at[request_of(t), :, pl.ds(q_head * CHUNK, CHUNK)]
        return pltpu.make_async_copy(origin, queries.at[t], q_sems.at[t])

    def out_copy(t):
        return pltpu.make_async_copy(results.at[t], out.at[request_of(t)], out_sems.at[t])

    def page_copy(source, slot, buffer, place):
        if source.shape[-1] == HD:
            origin = source.at[slot]
        else:
            origin = source.at[slot, :, :, columns]
        return pltpu.make_async_copy(origin, pages.at[buffer, place], page_sems.at[buffer, place])

    def fetch(t):
        request = request_of(t)
        buffer = lax.rem(t, 2)

        @pl.loop(0, counts[request])
        def _(place):
            code = picks[request, place]
            rank = lax.div(code, slots)
            slot = lax.rem(code, slots)
            for index, source in enumerate((own, twin, side, both)):
                @pl.when(rank == index)
                def _():
                    page_copy(source, slot, buffer, place).start()

    def arrive(t):
        buffer = lax.rem(t, 2)

        @pl.loop(0, counts[request_of(t)])
        def _(place):
            page_copy(own, 0, buffer, place).wait()

    def store_copy(slot):
        return pltpu.make_async_copy(own.at[slot], pool_out.at[slot], store_sems.at[slot])

    fresh_copy = pltpu.make_async_copy(fresh.at[:, :, columns], pages.at[0, extra], page_sems.at[0, extra])
    for t in range(lines):
        q_copy(t).start()
    for buffer in range(2):
        pages[buffer, :extra] = jnp.zeros((extra,) + pages.shape[2:], pages.dtype)
    fresh_copy.start()
    fetch(0)
    if lines > 1:
        fetch(1)
    if stores:
        @pl.loop(0, slots)
        def _(slot):
            @pl.when(slot != store[0])
            def _():
                store_copy(slot).start()

        pltpu.make_async_copy(incoming.at[0], pool_out.at[store[0]], store_sems.at[store[0]]).start()

    def soften(h, s, values):
        old = tops[h]
        new = jnp.maximum(old, jnp.max(s, axis=1, keepdims=True))
        tops[h] = new
        factor = SCALE * LOG2E
        fade = jnp.exp2((old - new) * factor)
        wide = jnp.concatenate([new] * (s.shape[1] // PAGE), axis=1)
        expo = jnp.exp2((s - wide) * factor).astype(jnp.bfloat16)
        added = jnp.dot(expo, values, preferred_element_type=jnp.float32)
        acc[h] = acc[h] * jnp.concatenate([fade, fade], axis=1) + added

    def with_ones(values):
        return jnp.concatenate([values, jnp.ones_like(values)], axis=1)

    def score(t, h, keys):
        query = queries[t, :, h * HD:(h + 1) * HD]
        return lax.dot_general(query, keys, CONTRACT_LAST, preferred_element_type=jnp.float32)

    def keys_of(t, index):
        return pages[lax.rem(t, 2), pl.ds(index * BLOCK, BLOCK), 0].reshape(BLOCK * PAGE, HD)

    def values_of(t, index):
        return with_ones(pages[lax.rem(t, 2), pl.ds(index * BLOCK, BLOCK), 1].reshape(BLOCK * PAGE, HD))

    def blocks_of(t):
        return jnp.maximum(lax.div(counts[request_of(t)] + BLOCK - 1, BLOCK), 1)

    def reset():
        tops[...] = jnp.full(tops.shape, LOW, jnp.float32)
        acc[...] = jnp.zeros(acc.shape, jnp.float32)

    def finish(t):
        some = (counts[request_of(t)] > 0) | (t == 0)
        lane = lax.broadcasted_iota(jnp.int32, (PAGE, PAGE), 1)
        stat = jnp.zeros((PAGE, PAGE), jnp.float32)
        for h in range(GQ):
            total = acc[h, :, HD:]
            results[t, h * PAGE:(h + 1) * PAGE, :] = (acc[h, :, :HD] * (1.0 / total)).astype(jnp.bfloat16)
            level = jnp.where(some, tops[h] * SCALE + jnp.log(total), LOW)
            high = level.astype(jnp.bfloat16).astype(jnp.float32)
            middle = (level - high).astype(jnp.bfloat16).astype(jnp.float32)
            low = level - high - middle
            stat = jnp.where(lane == h, high, stat)
            stat = jnp.where(lane == GQ + h, middle, stat)
            stat = jnp.where(lane == 2 * GQ + h, low, stat)
        results[t, GQ * PAGE:, :] = stat.T[:STAT].astype(jnp.bfloat16)
        out_copy(t).start()

    for t in range(lines):
        q_copy(t).wait()
    fresh_copy.wait()
    reset()
    span_values = with_ones(pages[0, extra, 1])
    for h in range(GQ):
        s = score(0, h, pages[0, extra, 0])
        seen = lax.broadcasted_iota(jnp.int32, s.shape, 1) <= lax.broadcasted_iota(jnp.int32, s.shape, 0)
        soften(h, jnp.where(seen, s, LOW), span_values)
    arrive(0)
    first = keys_of(0, 0)
    for h in range(GQ):
        scores[h] = score(0, h, first)

    def step(_, carry):
        t, index = carry
        request = request_of(t)
        ends = index + 1 >= blocks_of(t)
        later_t = jnp.where(ends, t + 1, t)
        later_index = jnp.where(ends, 0, index + 1)
        ahead_t = jnp.minimum(later_t, lines - 1)

        @pl.when(ends & (t + 1 < lines))
        def _():
            arrive(t + 1)

        limit = (counts[request] - 1 - index * BLOCK) * PAGE + lasts[request]
        column = lax.broadcasted_iota(jnp.int32, (PAGE, BLOCK * PAGE), 1)
        values = values_of(t, index)
        keys = keys_of(ahead_t, later_index)
        for h in range(GQ):
            soften(h, jnp.where(column < limit, scores[h], LOW), values)
            scores[h] = score(ahead_t, h, keys)

        @pl.when(ends)
        def _():
            finish(t)
            reset()

            @pl.when(t + 2 < lines)
            def _():
                fetch(t + 2)

        return later_t, later_index

    steps = blocks_of(0)
    for t in range(1, lines):
        steps += blocks_of(t)
    lax.fori_loop(0, steps, step, (jnp.int32(0), jnp.int32(0)))
    for t in range(lines):
        out_copy(t).wait()
    if stores:
        @pl.loop(0, slots)
        def _(slot):
            store_copy(slot).wait()


def attend(head, q_head, tables, q_all, pools, fresh, incoming=None):
    picks, counts, lasts, mine, store = tables
    lines = q_all.shape[0]
    places = picks.shape[1]
    keys = places * PAGE * 5 // 8
    pool = pools[0]
    out_shape = [jax.ShapeDtypeStruct((lines, ROWS, HD), jnp.bfloat16)]
    scratch = [
        pltpu.VMEM((2, places + 1, 2, PAGE, HD), jnp.bfloat16),
        pltpu.VMEM((lines, PAGE, CHUNK), jnp.bfloat16),
        pltpu.VMEM((lines, ROWS, HD), jnp.bfloat16),
        pltpu.VMEM((GQ, PAGE, BLOCK * PAGE), jnp.float32),
        pltpu.VMEM((GQ, PAGE, PAGE), jnp.float32),
        pltpu.VMEM((GQ, PAGE, 2 * HD), jnp.float32),
        pltpu.SemaphoreType.DMA((lines,)),
        pltpu.SemaphoreType.DMA((2, places + 1)),
        pltpu.SemaphoreType.DMA((lines,)),
    ]
    operands = [q_all, *pools, fresh]
    if incoming is not None:
        operands.append(incoming)
        out_shape.append(jax.ShapeDtypeStruct(pool.shape, pool.dtype))
        scratch.append(pltpu.SemaphoreType.DMA((pool.shape[0],)))
    grid_spec = pltpu.PrefetchScalarGridSpec(
        num_scalar_prefetch=5,
        grid=(),
        in_specs=[pl.BlockSpec(memory_space=pl.ANY)] * len(operands),
        out_specs=[pl.BlockSpec(memory_space=pl.ANY)] * len(out_shape),
        scratch_shapes=scratch,
    )
    return pl.pallas_call(
        functools.partial(attend_kernel, lines, head, q_head),
        grid_spec=grid_spec,
        out_shape=out_shape,
        compiler_params=pltpu.CompilerParams(vmem_limit_bytes=24 * 2**20),
        cost_estimate=pl.CostEstimate(
            flops=lines * 4 * GQ * PAGE * keys * HD,
            bytes_accessed=lines * keys * 4 * HD + lines * 2 * (CHUNK * PAGE + ROWS * HD),
            transcendentals=lines * GQ * PAGE * keys,
        ),
    )(picks, counts, lasts, mine, store, *operands)


def merge_kernel(head, parts, *refs):
    lines = parts.shape[0]
    out, result, sem = refs[-3:]
    levels = []
    for i in range(lines):
        block = parts[i, GQ * PAGE:, :].astype(jnp.float32)
        levels.append(block[:GQ] + block[GQ:2 * GQ] + block[2 * GQ:3 * GQ])
    top = functools.reduce(jnp.maximum, levels)
    weights = [jnp.exp(level - top) for level in levels]
    total = functools.reduce(jnp.add, weights)
    weights = [weight / total for weight in weights]
    filler = PAGE - lines * GQ
    table = jnp.concatenate(weights + [jnp.zeros((filler, PAGE), jnp.float32)], axis=0).T
    for h in range(GQ):
        merged = jnp.zeros((PAGE, HD), jnp.float32)
        for i in range(lines):
            column = i * GQ + h
            merged += table[:, column:column + 1] * parts[i, h * PAGE:(h + 1) * PAGE, :].astype(jnp.float32)
        result[:, h * HD:(h + 1) * HD] = merged.astype(jnp.bfloat16)
    copy = pltpu.make_async_copy(result, out.at[:, pl.ds(head * CHUNK, CHUNK)], sem)
    copy.start()
    copy.wait()


def merge(head, parts, whole):
    before = [] if whole is None else [whole]
    return pl.pallas_call(
        functools.partial(merge_kernel, head),
        in_specs=[pl.BlockSpec(memory_space=pltpu.VMEM)] + [pl.BlockSpec(memory_space=pl.ANY)] * len(before),
        out_specs=pl.BlockSpec(memory_space=pl.ANY),
        out_shape=jax.ShapeDtypeStruct((PAGE, KVH * CHUNK), jnp.bfloat16),
        scratch_shapes=[pltpu.VMEM((PAGE, CHUNK), jnp.bfloat16), pltpu.SemaphoreType.DMA],
        input_output_aliases={1: 0} if before else {},
        cost_estimate=pl.CostEstimate(
            flops=2 * parts.size, bytes_accessed=2 * parts.size + 2 * PAGE * CHUNK, transcendentals=0
        ),
    )(parts, *before)


def page_tables(me, width, slots, page_owner, page_slot, prefix_len):
    lines = width // CLUSTER
    capacity = (MAXP + width - 2) // (width - 1)
    limit = min(MAXP, CLUSTER * capacity)
    groups = [[c * CLUSTER + i for c in range(lines)] for i in range(CLUSTER)]
    table = jnp.concatenate([page_owner[0], page_slot[0], prefix_len])[None]
    tables = lax.all_gather(table, "serve", axis_index_groups=groups, tiled=True)
    owners = tables[:, :MAXP]
    places = tables[:, MAXP:2 * MAXP]
    length = tables[:, 2 * MAXP]
    used = (length + PAGE - 1) // PAGE
    spot = jnp.arange(MAXP)
    here = (spot[None] < used[:, None]) & (owners // CLUSTER == me // CLUSTER)
    hits = here.astype(jnp.int32)
    before = jnp.sum(hits[:, None, :] * (spot[None, None, :] < spot[None, :, None]), axis=2)
    local = ((owners % CLUSTER) ^ (me % CLUSTER)) * slots + places
    chosen = here[:, :, None] & (before[:, :, None] == jnp.arange(limit)[None, None, :])
    picks = jnp.sum(jnp.where(chosen, local[:, :, None], 0), axis=1)
    counts = jnp.sum(hits, axis=1)
    tail = jnp.sum(jnp.where(here & (spot[None] == used[:, None] - 1), 1, 0), axis=1)
    lasts = jnp.where(tail > 0, length - (used - 1) * PAGE, PAGE)
    return picks, counts, lasts, (me // CLUSTER)[None]


def exchanged(array, groups):
    return lax.all_to_all(array, "serve", 0, 0, axis_index_groups=groups, tiled=True)


def per_device(queries, new_kv, pool, page_owner, page_slot, prefix_len, store_slot):
    width = lax.axis_size("serve")
    lines = width // CLUSTER
    groups = [[c * CLUSTER + i for c in range(lines)] for i in range(CLUSTER)]
    me = lax.axis_index("serve")
    slots = pool.shape[0]
    first = pool[:, :, :, :HD]
    rest, first = lax.optimization_barrier((pool, first))
    sides = [swapped(first, "serve", 2)]
    sides += [swapped(rest[:, :, :, g * HD:(g + 1) * HD], "serve", 2) for g in range(1, KVH)]
    twin = swapped(pool, "serve", 1)
    early = exchanged(jnp.broadcast_to(queries[None, :, :CHUNK], (lines, PAGE, CHUNK)), groups)
    rest_q, early = lax.optimization_barrier((queries, early))
    later = exchanged(jnp.broadcast_to(rest_q[None, :, CHUNK:], (lines, PAGE, 3 * CHUNK)), groups)
    tables = page_tables(me, width, slots, page_owner, page_slot, prefix_len) + (store_slot[0],)
    fresh = new_kv[0, 0]
    incoming = shifted(new_kv[0], "serve", 1)
    attended = None
    for g in range(KVH):
        both = swapped(sides[g], "serve", 1)
        pools = (pool, twin, sides[g], both)
        q_all = early if g == 0 else later
        if g == 1:
            parts, pool_out = attend(g, max(g - 1, 0), tables, q_all, pools, fresh, incoming)
        else:
            parts = attend(g, max(g - 1, 0), tables, q_all, pools, fresh)[0]
        attended = merge(g, exchanged(parts, groups), attended)
    return (attended, pool_out)


def solution(mesh):
    return jax.shard_map(
        per_device,
        mesh=mesh,
        in_specs=(
            P(("groups", "serve"), None),
            P(("groups", "serve"), None, None, None, None),
            P(("groups", "serve"), None, None, None),
            P(("groups", "serve"), None),
            P(("groups", "serve"), None),
            P(("groups", "serve")),
            P(("groups", "serve"), None),
        ),
        out_specs=(P(("groups", "serve"), None), P(("groups", "serve"), None, None, None)),
        check_vma=False,
    )
```

time: 233 us -> 222 us (0.953)
  blocking collectives: 7.15 us -> 57.2 us
  waiting for transfers between devices: 86.3 us -> 48.1 us
  starting transfers between devices: 44.3 us -> 27.2 us
  Pallas kernels: 68.7 us -> 63 us
  other arithmetic: 4.18 us -> 1.1 us
    ppermute x19 -> x1, waiting for transfers between devices: 40 us -> 0.01 us  [shifted(): lax.ppermute(array, axis, [(i, (i + by) % size) for i in range(size)])]
    ppermute x19 -> x1, starting transfers between devices: 38.8 us -> 0.01 us  [shifted(): lax.ppermute(array, axis, [(i, (i + by) % size) for i in range(size)])]
    unnamed x1, blocking collectives: 7.15 us -> 33.6 us
    all_to_all x0 -> x1, blocking collectives: none -> 23.6 us  [exchanged(): lax.all_to_all(array, 'serve', 0, 0, axis_index_groups=groups, tiled=True)]
    all_to_all x0 -> x5, starting transfers between devices: none -> 21.1 us  [exchanged(): lax.all_to_all(array, 'serve', 0, 0, axis_index_groups=groups, tiled=True)]
    all_to_all x0 -> x5, waiting for transfers between devices: none -> 13.1 us  [exchanged(): lax.all_to_all(array, 'serve', 0, 0, axis_index_groups=groups, tiled=True)]
    ppermute x9, waiting for transfers between devices: 46.3 us -> 35 us  [swapped(): return lax.ppermute(array, axis, [(i, i ^ bit) for i in range(size)])]
    pallas_call x4, Pallas kernels: 59.1 us -> 53.6 us  [attend(): pl.pallas_call(functools.partial(attend_kernel, lines, head, q_head), gri...]
  transfers between devices with their start and end apart: 28 -> 15, of which waited for: 9 -> 5; matrix products, arithmetic and copies ran while one was open for 4% -> 5% of each run, Pallas kernels for 29% -> 28%
where the time goes in v2:
time: 222 us; the launch traced here: 219 us
  Pallas kernels  63 us (28%)
  blocking collectives  57.2 us (26%)
  waiting for transfers between devices  48.1 us (22%)
  starting transfers between devices  27.2 us (12%)
  local copies, waits for them, and re-layouts  19.9 us (9%)
  between operations  2.87 us (1%)
    pallas_call x4, Pallas kernels, attend(): pl.pallas_call(functools.partial(attend_kernel, lines, head, q_head), gri...  53.6 us
    ppermute x9, waiting for transfers between devices, swapped(): return lax.ppermute(array, axis, [(i, i ^ bit) for i in range(size)])  35 us
    unnamed x1, blocking collectives  33.6 us
    all_to_all x1, blocking collectives, exchanged(): lax.all_to_all(array, 'serve', 0, 0, axis_index_groups=groups, tiled=True)  23.6 us
    all_to_all x5, starting transfers between devices, exchanged(): lax.all_to_all(array, 'serve', 0, 0, axis_index_groups=groups, tiled=True)  21.1 us
    all_to_all x5, waiting for transfers between devices, exchanged(): lax.all_to_all(array, 'serve', 0, 0, axis_index_groups=groups, tiled=True)  13.1 us
    unnamed x20, local copies, waits for them, and re-layouts  10.2 us
    pallas_call x4, Pallas kernels, merge(): pl.pallas_call(functools.partial(merge_kernel, head), in_specs=[pl.BlockS...  9.4 us
  transfers between devices with their start and end apart: 15, of which 5 were waited for; matrix products, arithmetic and copies ran while one was open for 5% of the time, Pallas kernels for 28%

profile of v2, /device:TPU:0, one launch (start us, length us, event | category | flops | bytes accessed | tf_op | source)
XLA Modules:
  0.0 219.3 jit_solution(7758217904961492319)
XLA Ops:
  0.6 0.5 collective-permute-start
  1.1 0.9 slice.30
  2.1 0.1 broadcast_in_dim.27
  2.1 23.6 %all_to_all.30.refs_0_ = bf16[4,128,640]{2,1,0:T(8,128)(2,1)S(1)} all-to-all(bf16[4,128,640]{2,1,0:T(8,128)(2,1)S(1)} %broadcast_in_dim.27), channel_id=1, replica_groups={{0,4,8,12},{1,5,9,13},{2,6,10,14},{3,7,11,15},{16,20,24,28},{17,21,25,2..., dimensions={0} | all-to-all | bytes 1310720 | tf_op jit(solution)/shard_map/all_to_all | solution.py:322
  25.8 1.1 slice.31
  26.9 1.4 broadcast_in_dim.28
  28.3 3.6 %all-to-all-start.1 = ((bf16[4,128,1920]{2,1,0:T(8,128)(2,1)}), bf16[4,128,1920]{2,1,0:T(8,128)(2,1)S(1)}, u32[]{:S(2)}, u32[]{:S(2)}) async-start(bf16[4,128,1920]{2,1,0:T(8,128)(2,1)} %broadcast_in_dim.28), calls=%async_computation.1 | async-start | bytes 3932160 | tf_op jit(solution)/shard_map/all_to_all | solution.py:322
  31.9 0.0 copy-start.8
  31.9 0.0 copy-start.6
  31.9 2.4 %slice.32 = bf16[16,2,128,128]{3,2,1,0:T(8,128)(2,1)} slice(bf16[16,2,128,512]{3,2,1,0:T(8,128)(2,1)} %refs_1_.7), slice={[0:16], [0:2], [0:128], [0:128]} | slice | bytes 2097152 | tf_op jit(solution)/shard_map/slice | solution.py:331
  34.3 3.7 %fusion.12 = (bf16[16,2,128,128]{3,2,1,0:T(8,128)(2,1)}, bf16[16,2,128,128]{3,2,1,0:T(8,128)(2,1)}, bf16[16,2,128,128]{3,2,1,0:T(8,128)(2,1)}) fusion(bf16[16,2,128,512]{3,2,1,0:T(8,128)(2,1)} %refs_1_.7), kind=kLoop, calls=%fused_computation.40 | loop fusion | bytes 6291456 | tf_op jit(solution)/shard_map/slice | solution.py:334
  38.0 1.5 collective-permute-start.5
  39.5 0.5 collective-permute-start.8
  40.1 1.5 collective-permute-start.3
  42.2 0.6 dynamic-slice
  43.5 0.2 add_dynamic-update-slice_fusion
  43.7 33.6 %all-reduce = s32[388]{0:T(512)S(1)} all-reduce(s32[388]{0:T(512)S(1)} %add_dynamic-update-slice_fusion), channel_id=2, replica_groups={{0,4,8,12},{1,5,9,13},{2,6,10,14},{3,7,11,15},{16,20,24,28},{17,21,25,2..., use_global_device_ids=true, to_apply=%add | all-reduce | flops 388 | bytes 3104
  77.2 0.1 reshape.28
  77.3 0.2 slice_reduce_fusion
  77.5 0.1 collective-permute-start.6
  77.6 0.1 add_reduce_fusion
  77.8 0.2 select_reduce_fusion.1
  78.0 0.1 fusion.6
  78.1 0.1 multiply_reduce_fusion
  78.2 32.3 %collective-permute-done.3.refs_3_ = bf16[16,2,128,128]{3,2,1,0:T(8,128)(2,1)} collective-permute-done((bf16[16,2,128,128]{3,2,1,0:T(8,128)(2,1)}, bf16[16,2,128,128]{3,2,1,0:T(8,128)(2,1)}, u32[]{:S(2)}, u32[]{:S(2)}) %collective-permute-start.3) | collective-permute-done | bytes 1048608 | tf_op jit(solution)/shard_map/ppermute | solution.py:28
  110.5 0.1 select_reduce_fusion.picks
  111.4 2.2 copy-done
  113.6 13.4 %shard_map.88 = (bf16[4,656,128]{2,1,0:T(8,128)(2,1)}, bf16[16,2,128,512]{3,2,1,0:T(8,128)(2,1)}) custom-call(s32[4,16]{1,0:T(4,128)S(1)} %select_reduce_fusion.picks, s32[4]{0:T(128)S(1)} %get-tuple-element.17.counts, s32[4]{0:T(128)S(1)} %compare_select_fusion.lasts, s32[1]{0:T(128)} %bitcast.3.mine, s32[1]{0:T(128)} %bitcast.9.store, ...), custom_call_target="tpu_custom_call" | custom-call | flops 1677721600 | bytes 3948544 | tf_op jit(solution)/shard_map/pallas_call | solution.py:245
  127.0 4.7 %all-to-all-start.4 = ((bf16[4,656,128]{2,1,0:T(8,128)(2,1)}), bf16[4,656,128]{2,1,0:T(8,128)(2,1)}, u32[]{:S(2)}, u32[]{:S(2)}) async-start(bf16[4,656,128]{2,1,0:T(8,128)(2,1)} %get-tuple-element.10), calls=%async_computation.4 | async-start | bytes 1343488 | tf_op jit(solution)/shard_map/all_to_all | solution.py:322
  131.8 2.0 collective-permute-start.1
  133.8 2.2 copy-done.1
  135.9 13.1 %shard_map.87 = bf16[4,656,128]{2,1,0:T(8,128)(2,1)} custom-call(s32[4,16]{1,0:T(4,128)S(1)} %select_reduce_fusion.picks, s32[4]{0:T(128)S(1)} %get-tuple-element.17.counts, s32[4]{0:T(128)S(1)} %compare_select_fusion.lasts, s32[1]{0:T(128)} %bitcast.3.mine, s32[1]{0:T(128)} %bitcast.8.store, bf16[4,128,1920]{2,1,0:T(8,128)(2,1)S(1)} %all-to-all-done.1.refs_0_, ...), custom_call_target="tpu_custom_call" | custom-call | flops 1677721600 | bytes 3948544 | tf_op jit(solution)/shard_map/pallas_call | solution.py:245
  149.1 0.5 all-to-all-done.4.parts
  149.6 4.5 %all-to-all-start.3 = ((bf16[4,656,128]{2,1,0:T(8,128)(2,1)}), bf16[4,656,128]{2,1,0:T(8,128)(2,1)}, u32[]{:S(2)}, u32[]{:S(2)}) async-start(bf16[4,656,128]{2,1,0:T(8,128)(2,1)} %shard_map.87), calls=%async_computation.3 | async-start | bytes 1343488 | tf_op jit(solution)/shard_map/all_to_all | solution.py:322
  154.1 2.7 %collective-permute-done.1.refs_3_ = bf16[16,2,128,128]{3,2,1,0:T(8,128)(2,1)} collective-permute-done((bf16[16,2,128,128]{3,2,1,0:T(8,128)(2,1)}, bf16[16,2,128,128]{3,2,1,0:T(8,128)(2,1)}, u32[]{:S(2)}, u32[]{:S(2)}) %collective-permute-start.1) | collective-permute-done | bytes 1048608 | tf_op jit(solution)/shard_map/ppermute | solution.py:28
  156.8 2.2 copy-done.2
  159.0 13.9 %shard_map.89 = bf16[4,656,128]{2,1,0:T(8,128)(2,1)} custom-call(s32[4,16]{1,0:T(4,128)S(1)} %select_reduce_fusion.picks, s32[4]{0:T(128)S(1)} %get-tuple-element.17.counts, s32[4]{0:T(128)S(1)} %compare_select_fusion.lasts, s32[1]{0:T(128)} %bitcast.3.mine, s32[1]{0:T(128)} %bitcast.10.store, bf16[4,128,640]{2,1,0:T(8,128)(2,1)S(1)} %all_to_all.30.refs_0_, ...), custom_call_target="tpu_custom_call" | custom-call | flops 1677721600 | bytes 3948544 | tf_op jit(solution)/shard_map/pallas_call | solution.py:245
  172.9 4.7 %all-to-all-start.5 = ((bf16[4,656,128]{2,1,0:T(8,128)(2,1)}), bf16[4,656,128]{2,1,0:T(8,128)(2,1)}, u32[]{:S(2)}, u32[]{:S(2)}) async-start(bf16[4,656,128]{2,1,0:T(8,128)(2,1)} %shard_map.89), calls=%async_computation.5 | async-start | bytes 1343488 | tf_op jit(solution)/shard_map/all_to_all | solution.py:322
  177.7 2.2 copy-done.3
  179.9 13.1 %shard_map.86 = bf16[4,656,128]{2,1,0:T(8,128)(2,1)} custom-call(s32[4,16]{1,0:T(4,128)S(1)} %select_reduce_fusion.picks, s32[4]{0:T(128)S(1)} %get-tuple-element.17.counts, s32[4]{0:T(128)S(1)} %compare_select_fusion.lasts, s32[1]{0:T(128)} %bitcast.3.mine, s32[1]{0:T(128)} %bitcast.7.store, bf16[4,128,1920]{2,1,0:T(8,128)(2,1)S(1)} %all-to-all-done.1.refs_0_, ...), custom_call_target="tpu_custom_call" | custom-call | flops 1677721600 | bytes 3948544 | tf_op jit(solution)/shard_map/pallas_call | solution.py:245
  193.0 2.5 %all-to-all-done.5.parts = bf16[4,656,128]{2,1,0:T(8,128)(2,1)} async-done(((bf16[4,656,128]{2,1,0:T(8,128)(2,1)}), bf16[4,656,128]{2,1,0:T(8,128)(2,1)}, u32[]{:S(2)}, u32[]{:S(2)}) %all-to-all-start.5) | async-done | bytes 671776 | tf_op jit(solution)/shard_map/all_to_all | solution.py:322
  195.5 3.5 %all-to-all-start.2 = ((bf16[4,656,128]{2,1,0:T(8,128)(2,1)}), bf16[4,656,128]{2,1,0:T(8,128)(2,1)S(1)}, u32[]{:S(2)}, u32[]{:S(2)}) async-start(bf16[4,656,128]{2,1,0:T(8,128)(2,1)} %shard_map.86), calls=%async_computation.2 | async-start | bytes 1343488 | tf_op jit(solution)/shard_map/all_to_all | solution.py:322
  199.0 2.3 %shard_map.90.refs_0_ = bf16[128,2560]{1,0:T(8,128)(2,1)} custom-call(bf16[4,656,128]{2,1,0:T(8,128)(2,1)} %all-to-all-done.5.parts), custom_call_target="tpu_custom_call" | custom-call | flops 671744 | bytes 835584 | tf_op jit(solution)/shard_map/pallas_call | solution.py:284
  201.4 2.4 %shard_map.91.refs_0_ = bf16[128,2560]{1,0:T(8,128)(2,1)} custom-call(bf16[4,656,128]{2,1,0:T(8,128)(2,1)} %all-to-all-done.4.parts, bf16[128,2560]{1,0:T(8,128)(2,1)} %shard_map.90.refs_0_), custom_call_target="tpu_custom_call", output_to_operand_aliasing={{}: (1, {})} | custom-call | flops 671744 | bytes 835584 | tf_op jit(solution)/shard_map/pallas_call | solution.py:284
  203.7 2.4 %shard_map.92.refs_0_ = bf16[128,2560]{1,0:T(8,128)(2,1)} custom-call(bf16[4,656,128]{2,1,0:T(8,128)(2,1)} %all-to-all-done.3.parts, bf16[128,2560]{1,0:T(8,128)(2,1)} %shard_map.91.refs_0_), custom_call_target="tpu_custom_call", output_to_operand_aliasing={{}: (1, {})} | custom-call | flops 671744 | bytes 835584 | tf_op jit(solution)/shard_map/pallas_call | solution.py:284
  206.1 10.1 %all-to-all-done.2.parts = bf16[4,656,128]{2,1,0:T(8,128)(2,1)S(1)} async-done(((bf16[4,656,128]{2,1,0:T(8,128)(2,1)}), bf16[4,656,128]{2,1,0:T(8,128)(2,1)S(1)}, u32[]{:S(2)}, u32[]{:S(2)}) %all-to-all-start.2) | async-done | bytes 671776 | tf_op jit(solution)/shard_map/all_to_all | solution.py:322
  216.1 0.8 copy-done.5
  217.0 2.3 %shard_map.93 = bf16[128,2560]{1,0:T(8,128)(2,1)} custom-call(bf16[4,656,128]{2,1,0:T(8,128)(2,1)} %copy-done.5, bf16[128,2560]{1,0:T(8,128)(2,1)} %shard_map.92.refs_0_), custom_call_target="tpu_custom_call", output_to_operand_aliasing={{}: (1, {})} | custom-call | flops 671744 | bytes 835584 | tf_op jit(solution)/shard_map/pallas_call | solution.py:284
  (29 shorter events, 0.1 us)
Async XLA Ops:
  0.6 110.8 %collective-permute-start = (bf16[16,2,128,512]{3,2,1,0:T(8,128)(2,1)}, bf16[16,2,128,512]{3,2,1,0:T(8,128)(2,1)}, u32[]{:S(2)}, u32[]{:S(2)}) collective-permute-start(bf16[16,2,128,512]{3,2,1,0:T(8,128)(2,1)} %refs_1_.7), channel_id=1, source_target_pairs={{0,1},{1,0},{2,3},{3,2},{4,5},{5,4},{6,7},{7,6},{8,9},{9,8},{10,11... | collective-permute-start | bytes 12582920 | tf_op jit(solution)/shard_map/ppermute | solution.py:28
  28.3 83.1 %all-to-all-start.1 = ((bf16[4,128,1920]{2,1,0:T(8,128)(2,1)}), bf16[4,128,1920]{2,1,0:T(8,128)(2,1)S(1)}, u32[]{:S(2)}, u32[]{:S(2)}) async-start(bf16[4,128,1920]{2,1,0:T(8,128)(2,1)} %broadcast_in_dim.28), calls=%async_computation.1 | async-start | bytes 3932160 | tf_op jit(solution)/shard_map/all_to_all | solution.py:322
  31.9 7.7 %copy-start.4 = (bf16[1,1,2,128,512]{4,3,2,1,0:T(8,128)(2,1)S(1)}, bf16[1,1,2,128,512]{4,3,2,1,0:T(8,128)(2,1)}, u32[]{:S(2)}) copy-start(bf16[1,1,2,128,512]{4,3,2,1,0:T(8,128)(2,1)} %param.8) | copy-start | bytes 786436
  31.9 10.3 %copy-start.8 = (u32[32]{0:T(128)S(1)}, u32[32]{0:T(128)}, u32[]{:S(2)}) copy-start(u32[32]{0:T(128)} %constant.84) | copy-start | bytes 388
  31.9 11.6 %copy-start.6 = (s32[1,48]{1,0:T(1,128)S(1)}, s32[1,48]{1,0:T(1,128)}, u32[]{:S(2)}) copy-start(s32[1,48]{1,0:T(1,128)} %param.11) | copy-start | bytes 580
  31.9 11.6 %copy-start.7 = (s32[1,48]{1,0:T(1,128)S(1)}, s32[1,48]{1,0:T(1,128)}, u32[]{:S(2)}) copy-start(s32[1,48]{1,0:T(1,128)} %param.10) | copy-start | bytes 580
  38.0 39.5 %collective-permute-start.5 = (bf16[16,2,128,128]{3,2,1,0:T(8,128)(2,1)}, bf16[16,2,128,128]{3,2,1,0:T(8,128)(2,1)}, u32[]{:S(2)}, u32[]{:S(2)}) collective-permute-start(bf16[16,2,128,128]{3,2,1,0:T(8,128)(2,1)} %get-tuple-element.20), channel_id=1, source_target_pairs={{0,2},{1,3},{2,0},{3,1},{4,6},{5,7},{6,4},{7,5},{8,10},{9,11},{10,... | collective-permute-start | bytes 3145736 | tf_op jit(solution)/shard_map/ppermute | solution.py:28
  39.5 71.8 %collective-permute-start.7 = (bf16[1,2,128,512]{3,2,1,0:T(8,128)(2,1)S(1)}, bf16[1,2,128,512]{3,2,1,0:T(8,128)(2,1)S(1)}, u32[]{:S(2)}, u32[]{:S(2)}) collective-permute-start(bf16[1,2,128,512]{3,2,1,0:T(8,128)(2,1)S(1)} %bitcast.11), channel_id=1, source_target_pairs={{0,1},{1,2},{2,3},{3,4},{4,5},{5,6},{6,7},{7,8},{8,9},{9,10},{10,1... | collective-permute-start | bytes 786440 | tf_op jit(solution)/shard_map/ppermute | solution.py:33
  39.5 94.2 %collective-permute-start.8 = (bf16[16,2,128,128]{3,2,1,0:T(8,128)(2,1)}, bf16[16,2,128,128]{3,2,1,0:T(8,128)(2,1)}, u32[]{:S(2)}, u32[]{:S(2)}) collective-permute-start(bf16[16,2,128,128]{3,2,1,0:T(8,128)(2,1)} %slice.32), channel_id=1, source_target_pairs={{0,2},{1,3},{2,0},{3,1},{4,6},{5,7},{6,4},{7,5},{8,10},{9,11},{10,... | collective-permute-start | bytes 3145736 | tf_op jit(solution)/shard_map/ppermute | solution.py:28
  40.1 70.5 %collective-permute-start.3 = (bf16[16,2,128,128]{3,2,1,0:T(8,128)(2,1)}, bf16[16,2,128,128]{3,2,1,0:T(8,128)(2,1)}, u32[]{:S(2)}, u32[]{:S(2)}) collective-permute-start(bf16[16,2,128,128]{3,2,1,0:T(8,128)(2,1)} %get-tuple-element.21), channel_id=1, source_target_pairs={{0,2},{1,3},{2,0},{3,1},{4,6},{5,7},{6,4},{7,5},{8,10},{9,11},{10,... | collective-permute-start | bytes 3145736 | tf_op jit(solution)/shard_map/ppermute | solution.py:28
  77.5 33.8 %collective-permute-start.6 = (bf16[16,2,128,128]{3,2,1,0:T(8,128)(2,1)}, bf16[16,2,128,128]{3,2,1,0:T(8,128)(2,1)}, u32[]{:S(2)}, u32[]{:S(2)}) collective-permute-start(bf16[16,2,128,128]{3,2,1,0:T(8,128)(2,1)} %collective-permute-done.5.refs_3_), channel_id=1, source_target_pairs={{0,1},{1,0},{2,3},{3,2},{4,5},{5,4},{6,7},{7,6},{8,9},{9,8},{10,11... | collective-permute-start | bytes 3145736 | tf_op jit(solution)/shard_map/ppermute | solution.py:28
  110.5 23.2 %collective-permute-start.4 = (bf16[16,2,128,128]{3,2,1,0:T(8,128)(2,1)}, bf16[16,2,128,128]{3,2,1,0:T(8,128)(2,1)}, u32[]{:S(2)}, u32[]{:S(2)}) collective-permute-start(bf16[16,2,128,128]{3,2,1,0:T(8,128)(2,1)} %collective-permute-done.3.refs_3_), channel_id=1, source_target_pairs={{0,1},{1,0},{2,3},{3,2},{4,5},{5,4},{6,7},{7,6},{8,9},{9,8},{10,11... | collective-permute-start | bytes 3145736 | tf_op jit(solution)/shard_map/ppermute | solution.py:28
  111.4 2.2 copy-start
  127.0 22.6 %all-to-all-start.4 = ((bf16[4,656,128]{2,1,0:T(8,128)(2,1)}), bf16[4,656,128]{2,1,0:T(8,128)(2,1)}, u32[]{:S(2)}, u32[]{:S(2)}) async-start(bf16[4,656,128]{2,1,0:T(8,128)(2,1)} %get-tuple-element.10), calls=%async_computation.4 | async-start | bytes 1343488 | tf_op jit(solution)/shard_map/all_to_all | solution.py:322
  131.8 25.0 %collective-permute-start.1 = (bf16[16,2,128,128]{3,2,1,0:T(8,128)(2,1)}, bf16[16,2,128,128]{3,2,1,0:T(8,128)(2,1)}, u32[]{:S(2)}, u32[]{:S(2)}) collective-permute-start(bf16[16,2,128,128]{3,2,1,0:T(8,128)(2,1)} %get-tuple-element.22), channel_id=1, source_target_pairs={{0,2},{1,3},{2,0},{3,1},{4,6},{5,7},{6,4},{7,5},{8,10},{9,11},{10,... | collective-permute-start | bytes 3145736 | tf_op jit(solution)/shard_map/ppermute | solution.py:28
  133.7 23.1 %collective-permute-start.9 = (bf16[16,2,128,128]{3,2,1,0:T(8,128)(2,1)}, bf16[16,2,128,128]{3,2,1,0:T(8,128)(2,1)}, u32[]{:S(2)}, u32[]{:S(2)}) collective-permute-start(bf16[16,2,128,128]{3,2,1,0:T(8,128)(2,1)} %collective-permute-done.8.refs_3_), channel_id=1, source_target_pairs={{0,1},{1,0},{2,3},{3,2},{4,5},{5,4},{6,7},{7,6},{8,9},{9,8},{10,11... | collective-permute-start | bytes 3145736 | tf_op jit(solution)/shard_map/ppermute | solution.py:28
  133.7 2.2 copy-start.1
  149.6 23.3 %all-to-all-start.3 = ((bf16[4,656,128]{2,1,0:T(8,128)(2,1)}), bf16[4,656,128]{2,1,0:T(8,128)(2,1)}, u32[]{:S(2)}, u32[]{:S(2)}) async-start(bf16[4,656,128]{2,1,0:T(8,128)(2,1)} %shard_map.87), calls=%async_computation.3 | async-start | bytes 1343488 | tf_op jit(solution)/shard_map/all_to_all | solution.py:322
  156.8 20.9 %collective-permute-start.2 = (bf16[16,2,128,128]{3,2,1,0:T(8,128)(2,1)}, bf16[16,2,128,128]{3,2,1,0:T(8,128)(2,1)}, u32[]{:S(2)}, u32[]{:S(2)}) collective-permute-start(bf16[16,2,128,128]{3,2,1,0:T(8,128)(2,1)} %collective-permute-done.1.refs_3_), channel_id=1, source_target_pairs={{0,1},{1,0},{2,3},{3,2},{4,5},{5,4},{6,7},{7,6},{8,9},{9,8},{10,11... | collective-permute-start | bytes 3145736 | tf_op jit(solution)/shard_map/ppermute | solution.py:28
  156.8 2.2 copy-start.2
  172.9 22.6 %all-to-all-start.5 = ((bf16[4,656,128]{2,1,0:T(8,128)(2,1)}), bf16[4,656,128]{2,1,0:T(8,128)(2,1)}, u32[]{:S(2)}, u32[]{:S(2)}) async-start(bf16[4,656,128]{2,1,0:T(8,128)(2,1)} %shard_map.89), calls=%async_computation.5 | async-start | bytes 1343488 | tf_op jit(solution)/shard_map/all_to_all | solution.py:322
  177.7 2.2 copy-start.3
  195.5 20.6 %all-to-all-start.2 = ((bf16[4,656,128]{2,1,0:T(8,128)(2,1)}), bf16[4,656,128]{2,1,0:T(8,128)(2,1)S(1)}, u32[]{:S(2)}, u32[]{:S(2)}) async-start(bf16[4,656,128]{2,1,0:T(8,128)(2,1)} %shard_map.86), calls=%async_computation.2 | async-start | bytes 1343488 | tf_op jit(solution)/shard_map/all_to_all | solution.py:322
  216.1 0.8 copy-start.5

commit v3 on v2

--- a/solution.py
+++ b/solution.py
@@ -18,6 +18,7 @@
 CLUSTER = 4
 BLOCK = 4
 STAT = 16
+HEADS = ((0, 1, 2), (3, 4))
 ROWS = GQ * PAGE + STAT
 CHUNK = GQ * HD
 CONTRACT_LAST = (((1,), (1,)), ((), ()))
@@ -51,9 +52,9 @@
     def request_of(t):
         return lax.rem(mine[0] - t + lines, lines)
 
-    def q_copy(t):
-        origin = q_all.at[request_of(t), :, pl.ds(q_head * CHUNK, CHUNK)]
-        return pltpu.make_async_copy(origin, queries.at[t], q_sems.at[t])
+    def q_copy(t, h):
+        origin = q_all.at[request_of(t), :, pl.ds((q_head * GQ + h) * HD, HD)]
+        return pltpu.make_async_copy(origin, queries.at[t, h], q_sems.at[t, h])
 
     def out_copy(t):
         return pltpu.make_async_copy(results.at[t], out.at[request_of(t)], out_sems.at[t])
@@ -91,7 +92,8 @@
 
     fresh_copy = pltpu.make_async_copy(fresh.at[:, :, columns], pages.at[0, extra], page_sems.at[0, extra])
     for t in range(lines):
-        q_copy(t).start()
+        for h in range(GQ):
+            q_copy(t, h).start()
     for buffer in range(2):
         pages[buffer, :extra] = jnp.zeros((extra,) + pages.shape[2:], pages.dtype)
     fresh_copy.start()
@@ -107,23 +109,30 @@
 
         pltpu.make_async_copy(incoming.at[0], pool_out.at[store[0]], store_sems.at[store[0]]).start()
 
-    def soften(h, s, values):
-        old = tops[h]
-        new = jnp.maximum(old, jnp.max(s, axis=1, keepdims=True))
-        tops[h] = new
+    def soften(heads, scored, values):
         factor = SCALE * LOG2E
-        fade = jnp.exp2((old - new) * factor)
-        wide = jnp.concatenate([new] * (s.shape[1] // PAGE), axis=1)
-        expo = jnp.exp2((s - wide) * factor).astype(jnp.bfloat16)
-        added = jnp.dot(expo, values, preferred_element_type=jnp.float32)
-        acc[h] = acc[h] * jnp.concatenate([fade, fade], axis=1) + added
+        expos = []
+        fades = []
+        for h in heads:
+            s = scored(h)
+            old = tops[h]
+            new = jnp.maximum(old, jnp.max(s, axis=1, keepdims=True))
+            tops[h] = new
+            fades.append(jnp.exp2((old - new) * factor))
+            wide = jnp.concatenate([new] * (s.shape[1] // PAGE), axis=1)
+            expos.append(jnp.exp2((s - wide) * factor).astype(jnp.bfloat16))
+        added = jnp.dot(jnp.concatenate(expos, axis=0), values, preferred_element_type=jnp.float32)
+        for i, h in enumerate(heads):
+            fade = fades[i]
+            acc[h] = acc[h] * jnp.concatenate([fade, fade], axis=1) + added[i * PAGE:(i + 1) * PAGE]
 
     def with_ones(values):
         return jnp.concatenate([values, jnp.ones_like(values)], axis=1)
 
-    def score(t, h, keys):
-        query = queries[t, :, h * HD:(h + 1) * HD]
-        return lax.dot_general(query, keys, CONTRACT_LAST, preferred_element_type=jnp.float32)
+    def score(t, heads, keys):
+        query = queries[t, heads[0]:heads[-1] + 1].reshape(len(heads) * PAGE, HD)
+        s = lax.dot_general(query, keys, CONTRACT_LAST, preferred_element_type=jnp.float32)
+        return s.reshape(len(heads), PAGE, keys.shape[0])
 
     def keys_of(t, index):
         return pages[lax.rem(t, 2), pl.ds(index * BLOCK, BLOCK), 0].reshape(BLOCK * PAGE, HD)
@@ -156,18 +165,19 @@
         out_copy(t).start()
 
     for t in range(lines):
-        q_copy(t).wait()
+        for h in range(GQ):
+            q_copy(t, h).wait()
     fresh_copy.wait()
     reset()
     span_values = with_ones(pages[0, extra, 1])
-    for h in range(GQ):
-        s = score(0, h, pages[0, extra, 0])
-        seen = lax.broadcasted_iota(jnp.int32, s.shape, 1) <= lax.broadcasted_iota(jnp.int32, s.shape, 0)
-        soften(h, jnp.where(seen, s, LOW), span_values)
+    seen = lax.broadcasted_iota(jnp.int32, (PAGE, PAGE), 1) <= lax.broadcasted_iota(jnp.int32, (PAGE, PAGE), 0)
+    for heads in HEADS:
+        s = score(0, heads, pages[0, extra, 0])
+        soften(heads, lambda h: jnp.where(seen, s[h - heads[0]], LOW), span_values)
     arrive(0)
     first = keys_of(0, 0)
-    for h in range(GQ):
-        scores[h] = score(0, h, first)
+    for heads in HEADS:
+        scores[heads[0]:heads[-1] + 1] = score(0, heads, first)
 
     def step(_, carry):
         t, index = carry
@@ -185,9 +195,9 @@
         column = lax.broadcasted_iota(jnp.int32, (PAGE, BLOCK * PAGE), 1)
         values = values_of(t, index)
         keys = keys_of(ahead_t, later_index)
-        for h in range(GQ):
-            soften(h, jnp.where(column < limit, scores[h], LOW), values)
-            scores[h] = score(ahead_t, h, keys)
+        for heads in HEADS:
+            soften(heads, lambda h: jnp.where(column < limit, scores[h], LOW), values)
+            scores[heads[0]:heads[-1] + 1] = score(ahead_t, heads, keys)
 
         @pl.when(ends)
         def _():
@@ -221,12 +231,12 @@
     out_shape = [jax.ShapeDtypeStruct((lines, ROWS, HD), jnp.bfloat16)]
     scratch = [
         pltpu.VMEM((2, places + 1, 2, PAGE, HD), jnp.bfloat16),
-        pltpu.VMEM((lines, PAGE, CHUNK), jnp.bfloat16),
+        pltpu.VMEM((lines, GQ, PAGE, HD), jnp.bfloat16),
         pltpu.VMEM((lines, ROWS, HD), jnp.bfloat16),
         pltpu.VMEM((GQ, PAGE, BLOCK * PAGE), jnp.float32),
         pltpu.VMEM((GQ, PAGE, PAGE), jnp.float32),
         pltpu.VMEM((GQ, PAGE, 2 * HD), jnp.float32),
-        pltpu.SemaphoreType.DMA((lines,)),
+        pltpu.SemaphoreType.DMA((lines, GQ)),
         pltpu.SemaphoreType.DMA((2, places + 1)),
         pltpu.SemaphoreType.DMA((lines,)),
     ]
@@ -238,8 +248,8 @@
     grid_spec = pltpu.PrefetchScalarGridSpec(
         num_scalar_prefetch=5,
         grid=(),
-        in_specs=[pl.BlockSpec(memory_space=pl.ANY)] * len(operands),
-        out_specs=[pl.BlockSpec(memory_space=pl.ANY)] * len(out_shape),
+        in_specs=[pl.BlockSpec(memory_space=pltpu.HBM)] * 3 + [pl.BlockSpec(memory_space=pl.ANY)] * (len(operands) - 3),
+        out_specs=[pl.BlockSpec(memory_space=pl.ANY), pl.BlockSpec(memory_space=pltpu.HBM)][:len(out_shape)],
         scratch_shapes=scratch,
     )
     return pl.pallas_call(
@@ -322,6 +332,10 @@
     return lax.all_to_all(array, "serve", 0, 0, axis_index_groups=groups, tiled=True)
 
 
+def after(array, *others):
+    return lax.optimization_barrier((array, *others))[0]
+
+
 def per_device(queries, new_kv, pool, page_owner, page_slot, prefix_len, store_slot):
     width = lax.axis_size("serve")
     lines = width // CLUSTER
@@ -329,25 +343,25 @@
     me = lax.axis_index("serve")
     slots = pool.shape[0]
     first = pool[:, :, :, :HD]
-    rest, first = lax.optimization_barrier((pool, first))
+    rest = after(pool, first)
     sides = [swapped(first, "serve", 2)]
     sides += [swapped(rest[:, :, :, g * HD:(g + 1) * HD], "serve", 2) for g in range(1, KVH)]
-    twin = swapped(pool, "serve", 1)
-    early = exchanged(jnp.broadcast_to(queries[None, :, :CHUNK], (lines, PAGE, CHUNK)), groups)
-    rest_q, early = lax.optimization_barrier((queries, early))
-    later = exchanged(jnp.broadcast_to(rest_q[None, :, CHUNK:], (lines, PAGE, 3 * CHUNK)), groups)
     tables = page_tables(me, width, slots, page_owner, page_slot, prefix_len) + (store_slot[0],)
+    twin = swapped(rest, "serve", 1)
+    q_all = jnp.broadcast_to(after(queries, tables[0])[None], (lines, PAGE, KVH * CHUNK))
+    q_all = exchanged(q_all, groups)
     fresh = new_kv[0, 0]
-    incoming = shifted(new_kv[0], "serve", 1)
+    incoming = shifted(after(new_kv[0], tables[0]), "serve", 1)
     attended = None
+    parts = None
     for g in range(KVH):
-        both = swapped(sides[g], "serve", 1)
-        pools = (pool, twin, sides[g], both)
-        q_all = early if g == 0 else later
-        if g == 1:
-            parts, pool_out = attend(g, max(g - 1, 0), tables, q_all, pools, fresh, incoming)
+        side = sides[g] if g == 0 else after(sides[g], parts)
+        both = swapped(side, "serve", 1)
+        pools = (pool, twin, side, both)
+        if g == KVH - 2:
+            parts, pool_out = attend(g, g, tables, q_all, pools, fresh, incoming)
         else:
-            parts = attend(g, max(g - 1, 0), tables, q_all, pools, fresh)[0]
+            parts = attend(g, g, tables, q_all, pools, fresh)[0]
         attended = merge(g, exchanged(parts, groups), attended)
     return (attended, pool_out)
 

time: 222 us -> 220 us (level)
  blocking collectives: 57.2 us -> 9.44 us
  waiting for transfers between devices: 48.1 us -> 86.5 us
  local copies, waits for them, and re-layouts: 19.9 us -> 23.5 us
  starting transfers between devices: 27.2 us -> 30.1 us
    all_to_all x5, waiting for transfers between devices: 13.1 us -> 40.4 us  [exchanged(): lax.all_to_all(array, 'serve', 0, 0, axis_index_groups=groups, tiled=True)]
    unnamed x1, blocking collectives: 33.6 us -> 9.44 us
    all_to_all x1 -> x0, blocking collectives: 23.6 us -> none  [exchanged(): lax.all_to_all(array, 'serve', 0, 0, axis_index_groups=groups, tiled=True)]
    ppermute x1, waiting for transfers between devices: 0.01 us -> 18.5 us  [shifted(): lax.ppermute(array, axis, [(i, (i + by) % size) for i in range(size)])]
    ppermute x9, waiting for transfers between devices: 35 us -> 27.6 us  [swapped(): return lax.ppermute(array, axis, [(i, i ^ bit) for i in range(size)])]
    unnamed x20 -> x22, local copies, waits for them, and re-layouts: 10.2 us -> 14.2 us
    ppermute x9, starting transfers between devices: 6.13 us -> 10.2 us  [swapped(): return lax.ppermute(array, axis, [(i, i ^ bit) for i in range(size)])]
  transfers between devices with their start and end apart: 15 -> 15, of which waited for: 5 -> 6; matrix products, arithmetic and copies ran while one was open for 5% -> 5% of each run, Pallas kernels for 28% -> 28%
where the time goes in v3:
time: 220 us; the launch traced here: 217 us
  waiting for transfers between devices  86.5 us (39%)
  Pallas kernels  62.9 us (29%)
  starting transfers between devices  30.1 us (14%)
  local copies, waits for them, and re-layouts  23.5 us (11%)
  blocking collectives  9.44 us (4%)
  between operations  2.99 us (1%)
    pallas_call x4, Pallas kernels, attend(): pl.pallas_call(functools.partial(attend_kernel, lines, head, q_head), gri...  53.5 us
    all_to_all x5, waiting for transfers between devices, exchanged(): lax.all_to_all(array, 'serve', 0, 0, axis_index_groups=groups, tiled=True)  40.4 us
    ppermute x9, waiting for transfers between devices, swapped(): return lax.ppermute(array, axis, [(i, i ^ bit) for i in range(size)])  27.6 us
    all_to_all x5, starting transfers between devices, exchanged(): lax.all_to_all(array, 'serve', 0, 0, axis_index_groups=groups, tiled=True)  19.7 us
    ppermute x1, waiting for transfers between devices, shifted(): lax.ppermute(array, axis, [(i, (i + by) % size) for i in range(size)])  18.5 us
    unnamed x22, local copies, waits for them, and re-layouts  14.2 us
    ppermute x9, starting transfers between devices, swapped(): return lax.ppermute(array, axis, [(i, i ^ bit) for i in range(size)])  10.2 us
    unnamed x1, blocking collectives  9.44 us
  transfers between devices with their start and end apart: 15, of which 6 were waited for; matrix products, arithmetic and copies ran while one was open for 5% of the time, Pallas kernels for 28%

profile of v3, /device:TPU:0, one launch (start us, length us, event | category | flops | bytes accessed | tf_op | source)
XLA Modules:
  0.0 217.3 jit_solution(1496648795063396840)
XLA Ops:
  0.6 2.3 %slice.24 = bf16[16,2,128,128]{3,2,1,0:T(8,128)(2,1)} slice(bf16[16,2,128,512]{3,2,1,0:T(8,128)(2,1)} %refs_1_.7), slice={[0:16], [0:2], [0:128], [0:128]} | slice | bytes 2097152 | tf_op jit(solution)/shard_map/slice | solution.py:345
  2.9 0.5 collective-permute-start
  4.0 1.2 dynamic-slice
  5.9 0.8 add_dynamic-update-slice_fusion
  6.8 9.4 %all-reduce = s32[388]{0:T(512)S(1)} all-reduce(s32[388]{0:T(512)S(1)} %add_dynamic-update-slice_fusion), channel_id=2, replica_groups={{0,4,8,12},{1,5,9,13},{2,6,10,14},{3,7,11,15},{16,20,24,28},{17,21,25,2..., use_global_device_ids=true, to_apply=%add | all-reduce | flops 388 | bytes 3104
  16.2 0.1 reshape.27
  16.3 0.2 slice_reduce_fusion
  16.5 0.1 add_reduce_fusion
  16.7 0.2 select_reduce_fusion.1
  16.9 0.1 fusion.6
  17.0 0.1 multiply_reduce_fusion
  17.1 0.2 select_reduce_fusion.picks
  17.3 2.8 %broadcast_in_dim.28 = bf16[4,128,2560]{2,1,0:T(8,128)(2,1)} broadcast(bf16[128,2560]{1,0:T(8,128)(2,1)} %param.7), dimensions={1,2} | broadcast | bytes 3276800 | tf_op jit(solution)/shard_map/broadcast_in_dim | solution.py:351
  20.1 3.7 %all-to-all-start = ((bf16[4,128,2560]{2,1,0:T(8,128)(2,1)}), bf16[4,128,2560]{2,1,0:T(8,128)(2,1)S(1)}, u32[]{:S(2)}, u32[]{:S(2)}) async-start(bf16[4,128,2560]{2,1,0:T(8,128)(2,1)} %broadcast_in_dim.28), calls=%async_computation | async-start | bytes 5242880 | tf_op jit(solution)/shard_map/all_to_all | solution.py:332
  23.7 1.6 collective-permute-start.4
  25.3 22.2 %collective-permute-done.4.refs_3_ = bf16[16,2,128,128]{3,2,1,0:T(8,128)(2,1)S(1)} collective-permute-done((bf16[16,2,128,128]{3,2,1,0:T(8,128)(2,1)}, bf16[16,2,128,128]{3,2,1,0:T(8,128)(2,1)S(1)}, u32[]{:S(2)}, u32[]{:S(2)}) %collective-permute-start.4) | collective-permute-done | bytes 1048608 | tf_op jit(solution)/shard_map/ppermute | solution.py:29
  47.6 4.1 %fusion.12 = (bf16[16,2,128,128]{3,2,1,0:T(8,128)(2,1)}, bf16[16,2,128,128]{3,2,1,0:T(8,128)(2,1)}, bf16[16,2,128,128]{3,2,1,0:T(8,128)(2,1)}) fusion(bf16[16,2,128,512]{3,2,1,0:T(8,128)(2,1)} %refs_1_.7), kind=kLoop, calls=%fused_computation.40 | loop fusion | bytes 6291456 | tf_op jit(solution)/shard_map/slice | solution.py:348
  51.7 1.5 collective-permute-start.3
  53.9 1.0 copy-done.7
  54.9 27.2 %all-to-all-done.refs_0_ = bf16[4,128,2560]{2,1,0:T(8,128)(2,1)S(1)} async-done(((bf16[4,128,2560]{2,1,0:T(8,128)(2,1)}), bf16[4,128,2560]{2,1,0:T(8,128)(2,1)S(1)}, u32[]{:S(2)}, u32[]{:S(2)}) %all-to-all-start) | async-done | bytes 2621472 | tf_op jit(solution)/shard_map/all_to_all | solution.py:332
  82.1 2.2 %copy-done = bf16[16,2,128,512]{3,2,1,0:T(8,128)(2,1)S(1)} copy-done((bf16[16,2,128,512]{3,2,1,0:T(8,128)(2,1)S(1)}, bf16[16,2,128,512]{3,2,1,0:T(8,128)(2,1)}, u32[]{:S(2)}) %copy-start) | copy-done | bytes 4194328
  84.3 1.2 copy-done.6
  85.5 1.2 copy-done.8
  86.7 14.7 %shard_map.86 = bf16[4,656,128]{2,1,0:T(8,128)(2,1)} custom-call(s32[4,16]{1,0:T(4,128)S(1)} %select_reduce_fusion.picks, s32[4]{0:T(128)S(1)} %get-tuple-element.21.counts, s32[4]{0:T(128)S(1)} %compare_select_fusion.lasts, s32[1]{0:T(128)} %bitcast.3.mine, s32[1]{0:T(128)} %bitcast.7.store, bf16[4,128,2560]{2,1,0:T(8,128)(2,1)S(1)} %all-to-all-done.refs_0_, ...), custom_call_target="tpu_custom_call" | custom-call | flops 1677721600 | bytes 3948544 | tf_op jit(solution)/shard_map/pallas_call | solution.py:255
  101.4 0.1 collective-permute-start.6
  101.5 1.4 collective-permute-start.2
  102.9 4.2 %all-to-all-start.4 = ((bf16[4,656,128]{2,1,0:T(8,128)(2,1)}), bf16[4,656,128]{2,1,0:T(8,128)(2,1)}, u32[]{:S(2)}, u32[]{:S(2)}) async-start(bf16[4,656,128]{2,1,0:T(8,128)(2,1)} %shard_map.86), calls=%async_computation.4 | async-start | bytes 1343488 | tf_op jit(solution)/shard_map/all_to_all | solution.py:332
  107.1 2.2 %copy-done.1 = bf16[16,2,128,512]{3,2,1,0:T(8,128)(2,1)S(1)} copy-done((bf16[16,2,128,512]{3,2,1,0:T(8,128)(2,1)S(1)}, bf16[16,2,128,512]{3,2,1,0:T(8,128)(2,1)}, u32[]{:S(2)}) %copy-start.1) | copy-done | bytes 4194328
  109.2 12.8 %shard_map.87 = bf16[4,656,128]{2,1,0:T(8,128)(2,1)} custom-call(s32[4,16]{1,0:T(4,128)S(1)} %select_reduce_fusion.picks, s32[4]{0:T(128)S(1)} %get-tuple-element.21.counts, s32[4]{0:T(128)S(1)} %compare_select_fusion.lasts, s32[1]{0:T(128)} %bitcast.3.mine, s32[1]{0:T(128)} %bitcast.8.store, bf16[4,128,2560]{2,1,0:T(8,128)(2,1)S(1)} %all-to-all-done.refs_0_, ...), custom_call_target="tpu_custom_call" | custom-call | flops 1677721600 | bytes 3948544 | tf_op jit(solution)/shard_map/pallas_call | solution.py:255
  122.1 5.3 %collective-permute-done.2.refs_3_ = bf16[16,2,128,128]{3,2,1,0:T(8,128)(2,1)} collective-permute-done((bf16[16,2,128,128]{3,2,1,0:T(8,128)(2,1)}, bf16[16,2,128,128]{3,2,1,0:T(8,128)(2,1)}, u32[]{:S(2)}, u32[]{:S(2)}) %collective-permute-start.2) | collective-permute-done | bytes 1048608 | tf_op jit(solution)/shard_map/ppermute | solution.py:29
  127.4 1.3 collective-permute-start.1
  128.7 4.2 %all-to-all-start.3 = ((bf16[4,656,128]{2,1,0:T(8,128)(2,1)}), bf16[4,656,128]{2,1,0:T(8,128)(2,1)}, u32[]{:S(2)}, u32[]{:S(2)}) async-start(bf16[4,656,128]{2,1,0:T(8,128)(2,1)} %shard_map.87), calls=%async_computation.3 | async-start | bytes 1343488 | tf_op jit(solution)/shard_map/all_to_all | solution.py:332
  132.9 0.3 collective-permute-start.8
  133.2 18.5 %collective-permute-done.8.refs_6_ = bf16[1,2,128,512]{3,2,1,0:T(8,128)(2,1)S(1)} collective-permute-done((bf16[1,2,128,512]{3,2,1,0:T(8,128)(2,1)S(1)}, bf16[1,2,128,512]{3,2,1,0:T(8,128)(2,1)S(1)}, u32[]{:S(2)}, u32[]{:S(2)}) %collective-permute-start.8) | collective-permute-done | bytes 262176 | tf_op jit(solution)/shard_map/ppermute | solution.py:34
  151.7 2.2 %copy-done.2 = bf16[16,2,128,512]{3,2,1,0:T(8,128)(2,1)S(1)} copy-done((bf16[16,2,128,512]{3,2,1,0:T(8,128)(2,1)S(1)}, bf16[16,2,128,512]{3,2,1,0:T(8,128)(2,1)}, u32[]{:S(2)}) %copy-start.2) | copy-done | bytes 4194328
  153.9 13.1 %shard_map.88 = (bf16[4,656,128]{2,1,0:T(8,128)(2,1)}, bf16[16,2,128,512]{3,2,1,0:T(8,128)(2,1)}) custom-call(s32[4,16]{1,0:T(4,128)S(1)} %select_reduce_fusion.picks, s32[4]{0:T(128)S(1)} %get-tuple-element.21.counts, s32[4]{0:T(128)S(1)} %compare_select_fusion.lasts, s32[1]{0:T(128)} %bitcast.3.mine, s32[1]{0:T(128)} %bitcast.9.store, ...), custom_call_target="tpu_custom_call" | custom-call | flops 1677721600 | bytes 3948544 | tf_op jit(solution)/shard_map/pallas_call | solution.py:255
  167.0 3.8 %collective-permute-start.9 = (bf16[16,2,128,128]{3,2,1,0:T(8,128)(2,1)}, bf16[16,2,128,128]{3,2,1,0:T(8,128)(2,1)}, u32[]{:S(2)}, u32[]{:S(2)}) collective-permute-start(bf16[16,2,128,128]{3,2,1,0:T(8,128)(2,1)} %collective-permute-done.1.refs_3_), channel_id=1, source_target_pairs={{0,1},{1,0},{2,3},{3,2},{4,5},{5,4},{6,7},{7,6},{8,9},{9,8},{10,11... | collective-permute-start | bytes 3145736 | tf_op jit(solution)/shard_map/ppermute | solution.py:29
  170.8 4.2 %all-to-all-start.2 = ((bf16[4,656,128]{2,1,0:T(8,128)(2,1)}), bf16[4,656,128]{2,1,0:T(8,128)(2,1)}, u32[]{:S(2)}, u32[]{:S(2)}) async-start(bf16[4,656,128]{2,1,0:T(8,128)(2,1)} %get-tuple-element.15), calls=%async_computation.2 | async-start | bytes 1343488 | tf_op jit(solution)/shard_map/all_to_all | solution.py:332
  175.0 2.2 %copy-done.3 = bf16[16,2,128,512]{3,2,1,0:T(8,128)(2,1)S(1)} copy-done((bf16[16,2,128,512]{3,2,1,0:T(8,128)(2,1)S(1)}, bf16[16,2,128,512]{3,2,1,0:T(8,128)(2,1)}, u32[]{:S(2)}) %copy-start.3) | copy-done | bytes 4194328
  177.2 13.0 %shard_map.89 = bf16[4,656,128]{2,1,0:T(8,128)(2,1)} custom-call(s32[4,16]{1,0:T(4,128)S(1)} %select_reduce_fusion.picks, s32[4]{0:T(128)S(1)} %get-tuple-element.21.counts, s32[4]{0:T(128)S(1)} %compare_select_fusion.lasts, s32[1]{0:T(128)} %bitcast.3.mine, s32[1]{0:T(128)} %bitcast.10.store, bf16[4,128,2560]{2,1,0:T(8,128)(2,1)S(1)} %all-to-all-done.refs_0_, ...), custom_call_target="tpu_custom_call" | custom-call | flops 1677721600 | bytes 3948544 | tf_op jit(solution)/shard_map/pallas_call | solution.py:255
  190.2 3.0 %all-to-all-done.2.parts = bf16[4,656,128]{2,1,0:T(8,128)(2,1)} async-done(((bf16[4,656,128]{2,1,0:T(8,128)(2,1)}), bf16[4,656,128]{2,1,0:T(8,128)(2,1)}, u32[]{:S(2)}, u32[]{:S(2)}) %all-to-all-start.2) | async-done | bytes 671776 | tf_op jit(solution)/shard_map/all_to_all | solution.py:332
  193.2 3.5 %all-to-all-start.1 = ((bf16[4,656,128]{2,1,0:T(8,128)(2,1)}), bf16[4,656,128]{2,1,0:T(8,128)(2,1)S(1)}, u32[]{:S(2)}, u32[]{:S(2)}) async-start(bf16[4,656,128]{2,1,0:T(8,128)(2,1)} %shard_map.89), calls=%async_computation.1 | async-start | bytes 1343488 | tf_op jit(solution)/shard_map/all_to_all | solution.py:332
  196.7 2.3 %shard_map.90.refs_0_ = bf16[128,2560]{1,0:T(8,128)(2,1)} custom-call(bf16[4,656,128]{2,1,0:T(8,128)(2,1)} %all-to-all-done.4.parts), custom_call_target="tpu_custom_call" | custom-call | flops 671744 | bytes 835584 | tf_op jit(solution)/shard_map/pallas_call | solution.py:294
  199.1 2.4 %shard_map.91.refs_0_ = bf16[128,2560]{1,0:T(8,128)(2,1)} custom-call(bf16[4,656,128]{2,1,0:T(8,128)(2,1)} %all-to-all-done.3.parts, bf16[128,2560]{1,0:T(8,128)(2,1)} %shard_map.90.refs_0_), custom_call_target="tpu_custom_call", output_to_operand_aliasing={{}: (1, {})} | custom-call | flops 671744 | bytes 835584 | tf_op jit(solution)/shard_map/pallas_call | solution.py:294
  201.4 2.4 %shard_map.92.refs_0_ = bf16[128,2560]{1,0:T(8,128)(2,1)} custom-call(bf16[4,656,128]{2,1,0:T(8,128)(2,1)} %all-to-all-done.2.parts, bf16[128,2560]{1,0:T(8,128)(2,1)} %shard_map.91.refs_0_), custom_call_target="tpu_custom_call", output_to_operand_aliasing={{}: (1, {})} | custom-call | flops 671744 | bytes 835584 | tf_op jit(solution)/shard_map/pallas_call | solution.py:294
  203.8 10.2 %all-to-all-done.1.parts = bf16[4,656,128]{2,1,0:T(8,128)(2,1)S(1)} async-done(((bf16[4,656,128]{2,1,0:T(8,128)(2,1)}), bf16[4,656,128]{2,1,0:T(8,128)(2,1)S(1)}, u32[]{:S(2)}, u32[]{:S(2)}) %all-to-all-start.1) | async-done | bytes 671776 | tf_op jit(solution)/shard_map/all_to_all | solution.py:332
  214.0 0.8 copy-done.9
  214.8 2.3 %shard_map.93 = bf16[128,2560]{1,0:T(8,128)(2,1)} custom-call(bf16[4,656,128]{2,1,0:T(8,128)(2,1)} %copy-done.9, bf16[128,2560]{1,0:T(8,128)(2,1)} %shard_map.92.refs_0_), custom_call_target="tpu_custom_call", output_to_operand_aliasing={{}: (1, {})} | custom-call | flops 671744 | bytes 835584 | tf_op jit(solution)/shard_map/pallas_call | solution.py:294
  (27 shorter events, 0.1 us)
Async XLA Ops:
  2.9 79.1 %collective-permute-start = (bf16[16,2,128,512]{3,2,1,0:T(8,128)(2,1)}, bf16[16,2,128,512]{3,2,1,0:T(8,128)(2,1)}, u32[]{:S(2)}, u32[]{:S(2)}) collective-permute-start(bf16[16,2,128,512]{3,2,1,0:T(8,128)(2,1)} %refs_1_.7), channel_id=1, source_target_pairs={{0,1},{1,0},{2,3},{3,2},{4,5},{5,4},{6,7},{7,6},{8,9},{9,8},{10,11... | collective-permute-start | bytes 12582920 | tf_op jit(solution)/shard_map/ppermute | solution.py:29
  20.1 62.0 %all-to-all-start = ((bf16[4,128,2560]{2,1,0:T(8,128)(2,1)}), bf16[4,128,2560]{2,1,0:T(8,128)(2,1)S(1)}, u32[]{:S(2)}, u32[]{:S(2)}) async-start(bf16[4,128,2560]{2,1,0:T(8,128)(2,1)} %broadcast_in_dim.28), calls=%async_computation | async-start | bytes 5242880 | tf_op jit(solution)/shard_map/all_to_all | solution.py:332
  23.7 58.3 %copy-start.4 = (bf16[1,1,2,128,512]{4,3,2,1,0:T(8,128)(2,1)S(1)}, bf16[1,1,2,128,512]{4,3,2,1,0:T(8,128)(2,1)}, u32[]{:S(2)}) copy-start(bf16[1,1,2,128,512]{4,3,2,1,0:T(8,128)(2,1)} %param.8) | copy-start | bytes 786436
  23.7 23.8 %collective-permute-start.4 = (bf16[16,2,128,128]{3,2,1,0:T(8,128)(2,1)}, bf16[16,2,128,128]{3,2,1,0:T(8,128)(2,1)S(1)}, u32[]{:S(2)}, u32[]{:S(2)}) collective-permute-start(bf16[16,2,128,128]{3,2,1,0:T(8,128)(2,1)} %slice.24), channel_id=1, source_target_pairs={{0,2},{1,3},{2,0},{3,1},{4,6},{5,7},{6,4},{7,5},{8,10},{9,11},{10,... | collective-permute-start | bytes 3145736 | tf_op jit(solution)/shard_map/ppermute | solution.py:29
  47.6 6.3 %copy-start.5 = (bf16[16,2,128,128]{3,2,1,0:T(8,128)(2,1)}, bf16[16,2,128,128]{3,2,1,0:T(8,128)(2,1)S(1)}, u32[]{:S(2)}) copy-start(bf16[16,2,128,128]{3,2,1,0:T(8,128)(2,1)S(1)} %collective-permute-done.4.refs_3_) | copy-start | bytes 3145732
  47.6 6.3 %collective-permute-start.5 = (bf16[16,2,128,128]{3,2,1,0:T(8,128)(2,1)S(1)}, bf16[16,2,128,128]{3,2,1,0:T(8,128)(2,1)S(1)}, u32[]{:S(2)}, u32[]{:S(2)}) collective-permute-start(bf16[16,2,128,128]{3,2,1,0:T(8,128)(2,1)S(1)} %collective-permute-done.4.refs_3_), channel_id=1, source_target_pairs={{0,1},{1,0},{2,3},{3,2},{4,5},{5,4},{6,7},{7,6},{8,9},{9,8},{10,11... | collective-permute-start | bytes 3145736 | tf_op jit(solution)/shard_map/ppermute | solution.py:29
  51.7 49.7 %collective-permute-start.3 = (bf16[16,2,128,128]{3,2,1,0:T(8,128)(2,1)}, bf16[16,2,128,128]{3,2,1,0:T(8,128)(2,1)}, u32[]{:S(2)}, u32[]{:S(2)}) collective-permute-start(bf16[16,2,128,128]{3,2,1,0:T(8,128)(2,1)} %get-tuple-element.24), channel_id=1, source_target_pairs={{0,2},{1,3},{2,0},{3,1},{4,6},{5,7},{6,4},{7,5},{8,10},{9,11},{10,... | collective-permute-start | bytes 3145736 | tf_op jit(solution)/shard_map/ppermute | solution.py:29
  53.9 1.0 copy-start.7
  82.1 2.2 %copy-start = (bf16[16,2,128,512]{3,2,1,0:T(8,128)(2,1)S(1)}, bf16[16,2,128,512]{3,2,1,0:T(8,128)(2,1)}, u32[]{:S(2)}) copy-start(bf16[16,2,128,512]{3,2,1,0:T(8,128)(2,1)} %refs_1_.7) | copy-start | bytes 12582916
  84.3 1.2 copy-start.6
  85.5 1.2 copy-start.8
  101.4 5.6 %collective-permute-start.6 = (bf16[16,2,128,128]{3,2,1,0:T(8,128)(2,1)}, bf16[16,2,128,128]{3,2,1,0:T(8,128)(2,1)}, u32[]{:S(2)}, u32[]{:S(2)}) collective-permute-start(bf16[16,2,128,128]{3,2,1,0:T(8,128)(2,1)} %collective-permute-done.3.refs_3_), channel_id=1, source_target_pairs={{0,1},{1,0},{2,3},{3,2},{4,5},{5,4},{6,7},{7,6},{8,9},{9,8},{10,11... | collective-permute-start | bytes 3145736 | tf_op jit(solution)/shard_map/ppermute | solution.py:29
  101.5 25.9 %collective-permute-start.2 = (bf16[16,2,128,128]{3,2,1,0:T(8,128)(2,1)}, bf16[16,2,128,128]{3,2,1,0:T(8,128)(2,1)}, u32[]{:S(2)}, u32[]{:S(2)}) collective-permute-start(bf16[16,2,128,128]{3,2,1,0:T(8,128)(2,1)} %get-tuple-element.25), channel_id=1, source_target_pairs={{0,2},{1,3},{2,0},{3,1},{4,6},{5,7},{6,4},{7,5},{8,10},{9,11},{10,... | collective-permute-start | bytes 3145736 | tf_op jit(solution)/shard_map/ppermute | solution.py:29
  102.9 25.8 %all-to-all-start.4 = ((bf16[4,656,128]{2,1,0:T(8,128)(2,1)}), bf16[4,656,128]{2,1,0:T(8,128)(2,1)}, u32[]{:S(2)}, u32[]{:S(2)}) async-start(bf16[4,656,128]{2,1,0:T(8,128)(2,1)} %shard_map.86), calls=%async_computation.4 | async-start | bytes 1343488 | tf_op jit(solution)/shard_map/all_to_all | solution.py:332
  107.1 2.2 %copy-start.1 = (bf16[16,2,128,512]{3,2,1,0:T(8,128)(2,1)S(1)}, bf16[16,2,128,512]{3,2,1,0:T(8,128)(2,1)}, u32[]{:S(2)}) copy-start(bf16[16,2,128,512]{3,2,1,0:T(8,128)(2,1)} %refs_1_.7) | copy-start | bytes 12582916
  127.4 24.3 %collective-permute-start.7 = (bf16[16,2,128,128]{3,2,1,0:T(8,128)(2,1)}, bf16[16,2,128,128]{3,2,1,0:T(8,128)(2,1)}, u32[]{:S(2)}, u32[]{:S(2)}) collective-permute-start(bf16[16,2,128,128]{3,2,1,0:T(8,128)(2,1)} %collective-permute-done.2.refs_3_), channel_id=1, source_target_pairs={{0,1},{1,0},{2,3},{3,2},{4,5},{5,4},{6,7},{7,6},{8,9},{9,8},{10,11... | collective-permute-start | bytes 3145736 | tf_op jit(solution)/shard_map/ppermute | solution.py:29
  127.4 39.6 %collective-permute-start.1 = (bf16[16,2,128,128]{3,2,1,0:T(8,128)(2,1)}, bf16[16,2,128,128]{3,2,1,0:T(8,128)(2,1)}, u32[]{:S(2)}, u32[]{:S(2)}) collective-permute-start(bf16[16,2,128,128]{3,2,1,0:T(8,128)(2,1)} %get-tuple-element.26), channel_id=1, source_target_pairs={{0,2},{1,3},{2,0},{3,1},{4,6},{5,7},{6,4},{7,5},{8,10},{9,11},{10,... | collective-permute-start | bytes 3145736 | tf_op jit(solution)/shard_map/ppermute | solution.py:29
  128.7 42.1 %all-to-all-start.3 = ((bf16[4,656,128]{2,1,0:T(8,128)(2,1)}), bf16[4,656,128]{2,1,0:T(8,128)(2,1)}, u32[]{:S(2)}, u32[]{:S(2)}) async-start(bf16[4,656,128]{2,1,0:T(8,128)(2,1)} %shard_map.87), calls=%async_computation.3 | async-start | bytes 1343488 | tf_op jit(solution)/shard_map/all_to_all | solution.py:332
  132.9 18.8 %collective-permute-start.8 = (bf16[1,2,128,512]{3,2,1,0:T(8,128)(2,1)S(1)}, bf16[1,2,128,512]{3,2,1,0:T(8,128)(2,1)S(1)}, u32[]{:S(2)}, u32[]{:S(2)}) collective-permute-start(bf16[1,2,128,512]{3,2,1,0:T(8,128)(2,1)S(1)} %bitcast.13), channel_id=1, source_target_pairs={{0,1},{1,2},{2,3},{3,4},{4,5},{5,6},{6,7},{7,8},{8,9},{9,10},{10,1... | collective-permute-start | bytes 786440 | tf_op jit(solution)/shard_map/ppermute | solution.py:34
  151.7 2.2 %copy-start.2 = (bf16[16,2,128,512]{3,2,1,0:T(8,128)(2,1)S(1)}, bf16[16,2,128,512]{3,2,1,0:T(8,128)(2,1)}, u32[]{:S(2)}) copy-start(bf16[16,2,128,512]{3,2,1,0:T(8,128)(2,1)} %refs_1_.7) | copy-start | bytes 12582916
  167.0 8.0 %collective-permute-start.9 = (bf16[16,2,128,128]{3,2,1,0:T(8,128)(2,1)}, bf16[16,2,128,128]{3,2,1,0:T(8,128)(2,1)}, u32[]{:S(2)}, u32[]{:S(2)}) collective-permute-start(bf16[16,2,128,128]{3,2,1,0:T(8,128)(2,1)} %collective-permute-done.1.refs_3_), channel_id=1, source_target_pairs={{0,1},{1,0},{2,3},{3,2},{4,5},{5,4},{6,7},{7,6},{8,9},{9,8},{10,11... | collective-permute-start | bytes 3145736 | tf_op jit(solution)/shard_map/ppermute | solution.py:29
  170.8 22.4 %all-to-all-start.2 = ((bf16[4,656,128]{2,1,0:T(8,128)(2,1)}), bf16[4,656,128]{2,1,0:T(8,128)(2,1)}, u32[]{:S(2)}, u32[]{:S(2)}) async-start(bf16[4,656,128]{2,1,0:T(8,128)(2,1)} %get-tuple-element.15), calls=%async_computation.2 | async-start | bytes 1343488 | tf_op jit(solution)/shard_map/all_to_all | solution.py:332
  175.0 2.2 %copy-start.3 = (bf16[16,2,128,512]{3,2,1,0:T(8,128)(2,1)S(1)}, bf16[16,2,128,512]{3,2,1,0:T(8,128)(2,1)}, u32[]{:S(2)}) copy-start(bf16[16,2,128,512]{3,2,1,0:T(8,128)(2,1)} %refs_1_.7) | copy-start | bytes 12582916
  193.2 20.7 %all-to-all-start.1 = ((bf16[4,656,128]{2,1,0:T(8,128)(2,1)}), bf16[4,656,128]{2,1,0:T(8,128)(2,1)S(1)}, u32[]{:S(2)}, u32[]{:S(2)}) async-start(bf16[4,656,128]{2,1,0:T(8,128)(2,1)} %shard_map.89), calls=%async_computation.1 | async-start | bytes 1343488 | tf_op jit(solution)/shard_map/all_to_all | solution.py:332
  214.0 0.8 copy-start.9

commit v4 on v3

--- a/solution.py
+++ b/solution.py
@@ -226,7 +226,6 @@
     picks, counts, lasts, mine, store = tables
     lines = q_all.shape[0]
     places = picks.shape[1]
-    keys = places * PAGE * 5 // 8
     pool = pools[0]
     out_shape = [jax.ShapeDtypeStruct((lines, ROWS, HD), jnp.bfloat16)]
     scratch = [
@@ -257,11 +256,7 @@
         grid_spec=grid_spec,
         out_shape=out_shape,
         compiler_params=pltpu.CompilerParams(vmem_limit_bytes=24 * 2**20),
-        cost_estimate=pl.CostEstimate(
-            flops=lines * 4 * GQ * PAGE * keys * HD,
-            bytes_accessed=lines * keys * 4 * HD + lines * 2 * (CHUNK * PAGE + ROWS * HD),
-            transcendentals=lines * GQ * PAGE * keys,
-        ),
+        cost_estimate=pl.CostEstimate(flops=1, bytes_accessed=1, transcendentals=0),
     )(picks, counts, lasts, mine, store, *operands)
 
 
@@ -298,9 +293,7 @@
         out_shape=jax.ShapeDtypeStruct((PAGE, KVH * CHUNK), jnp.bfloat16),
         scratch_shapes=[pltpu.VMEM((PAGE, CHUNK), jnp.bfloat16), pltpu.SemaphoreType.DMA],
         input_output_aliases={1: 0} if before else {},
-        cost_estimate=pl.CostEstimate(
-            flops=2 * parts.size, bytes_accessed=2 * parts.size + 2 * PAGE * CHUNK, transcendentals=0
-        ),
+        cost_estimate=pl.CostEstimate(flops=1, bytes_accessed=1, transcendentals=0),
     )(parts, *before)
 
 
@@ -348,20 +341,27 @@
     sides += [swapped(rest[:, :, :, g * HD:(g + 1) * HD], "serve", 2) for g in range(1, KVH)]
     tables = page_tables(me, width, slots, page_owner, page_slot, prefix_len) + (store_slot[0],)
     twin = swapped(rest, "serve", 1)
-    q_all = jnp.broadcast_to(after(queries, tables[0])[None], (lines, PAGE, KVH * CHUNK))
-    q_all = exchanged(q_all, groups)
+    q_parts = []
+    last = tables[0]
+    for begin, end in ((0, 1), (1, KVH)):
+        part = after(queries, last)[None, :, begin * CHUNK:end * CHUNK]
+        part = jnp.broadcast_to(part, (lines, PAGE, (end - begin) * CHUNK))
+        last = part
+        part = exchanged(part, groups)
+        q_parts += [(part, i) for i in range(end - begin)]
     fresh = new_kv[0, 0]
     incoming = shifted(after(new_kv[0], tables[0]), "serve", 1)
     attended = None
     parts = None
     for g in range(KVH):
         side = sides[g] if g == 0 else after(sides[g], parts)
+        q_all, q_head = q_parts[g]
         both = swapped(side, "serve", 1)
         pools = (pool, twin, side, both)
         if g == KVH - 2:
-            parts, pool_out = attend(g, g, tables, q_all, pools, fresh, incoming)
+            parts, pool_out = attend(g, q_head, tables, q_all, pools, fresh, incoming)
         else:
-            parts = attend(g, g, tables, q_all, pools, fresh)[0]
+            parts = attend(g, q_head, tables, q_all, pools, fresh)[0]
         attended = merge(g, exchanged(parts, groups), attended)
     return (attended, pool_out)
 

time: 220 us -> 218 us (level)
  waiting for transfers between devices: 86.5 us -> 77.5 us
  Pallas kernels: 62.9 us -> 71.5 us
  local copies, waits for them, and re-layouts: 23.5 us -> 18.8 us
  starting transfers between devices: 30.1 us -> 33.8 us
    all_to_all x5 -> x6, waiting for transfers between devices: 40.4 us -> 27.2 us  [exchanged(): lax.all_to_all(array, 'serve', 0, 0, axis_index_groups=groups, tiled=True)]
    pallas_call x4, Pallas kernels: 53.5 us -> 62.1 us  [attend(): pl.pallas_call(functools.partial(attend_kernel, lines, head, q_head), gri...]
    all_to_all x5 -> x6, starting transfers between devices: 19.7 us -> 25.5 us  [exchanged(): lax.all_to_all(array, 'serve', 0, 0, axis_index_groups=groups, tiled=True)]
    unnamed x22 -> x16, local copies, waits for them, and re-layouts: 14.2 us -> 9.55 us
    ppermute x9, waiting for transfers between devices: 27.6 us -> 31.9 us  [swapped(): return lax.ppermute(array, axis, [(i, i ^ bit) for i in range(size)])]
  transfers between devices with their start and end apart: 15 -> 16, of which waited for: 6 -> 7; matrix products, arithmetic and copies ran while one was open for 5% -> 5% of each run, Pallas kernels for 28% -> 32%
where the time goes in v4:
time: 218 us; the launch traced here: 216 us
  waiting for transfers between devices  77.5 us (36%)
  Pallas kernels  71.5 us (33%)
  starting transfers between devices  33.8 us (16%)
  local copies, waits for them, and re-layouts  18.8 us (9%)
  blocking collectives  9.45 us (4%)
  between operations  2.96 us (1%)
    pallas_call x4, Pallas kernels, attend(): pl.pallas_call(functools.partial(attend_kernel, lines, head, q_head), gri...  62.1 us
    ppermute x9, waiting for transfers between devices, swapped(): return lax.ppermute(array, axis, [(i, i ^ bit) for i in range(size)])  31.9 us
    all_to_all x6, waiting for transfers between devices, exchanged(): lax.all_to_all(array, 'serve', 0, 0, axis_index_groups=groups, tiled=True)  27.2 us
    all_to_all x6, starting transfers between devices, exchanged(): lax.all_to_all(array, 'serve', 0, 0, axis_index_groups=groups, tiled=True)  25.5 us
    ppermute x1, waiting for transfers between devices, shifted(): lax.ppermute(array, axis, [(i, (i + by) % size) for i in range(size)])  18.3 us
    unnamed x16, local copies, waits for them, and re-layouts  9.55 us
    unnamed x1, blocking collectives  9.45 us
    pallas_call x4, Pallas kernels, merge(): pl.pallas_call(functools.partial(merge_kernel, head), in_specs=[pl.BlockS...  9.4 us
  transfers between devices with their start and end apart: 16, of which 7 were waited for; matrix products, arithmetic and copies ran while one was open for 5% of the time, Pallas kernels for 32%

profile of v4, /device:TPU:0, one launch (start us, length us, event | category | flops | bytes accessed | tf_op | source)
XLA Modules:
  0.0 215.8 jit_solution(1391802761276037495)
XLA Ops:
  0.6 0.0 slice-start
  0.6 2.4 %slice.32 = bf16[16,2,128,128]{3,2,1,0:T(8,128)(2,1)} slice(bf16[16,2,128,512]{3,2,1,0:T(8,128)(2,1)} %refs_1_.7), slice={[0:16], [0:2], [0:128], [0:128]} | slice | bytes 2097152 | tf_op jit(solution)/shard_map/slice | solution.py:338
  3.0 0.5 collective-permute-start
  4.1 1.2 dynamic-slice
  6.0 0.8 add_dynamic-update-slice_fusion
  6.9 9.5 %all-reduce = s32[388]{0:T(512)S(1)} all-reduce(s32[388]{0:T(512)S(1)} %add_dynamic-update-slice_fusion), channel_id=2, replica_groups={{0,4,8,12},{1,5,9,13},{2,6,10,14},{3,7,11,15},{16,20,24,28},{17,21,25,2..., use_global_device_ids=true, to_apply=%add | all-reduce | flops 388 | bytes 3104
  16.3 0.1 reshape.28
  16.4 0.2 slice_reduce_fusion
  16.6 0.1 add_reduce_fusion
  16.7 0.2 select_reduce_fusion.1
  17.0 0.1 multiply_reduce_fusion
  17.1 0.1 fusion.6
  17.2 0.1 select_reduce_fusion.picks
  17.4 0.9 slice.30
  18.3 0.9 broadcast_in_dim.30
  19.2 3.5 %all-to-all-start.1 = ((bf16[4,128,640]{2,1,0:T(8,128)(2,1)}), bf16[4,128,640]{2,1,0:T(8,128)(2,1)S(1)}, u32[]{:S(2)}, u32[]{:S(2)}) async-start(bf16[4,128,640]{2,1,0:T(8,128)(2,1)} %broadcast_in_dim.30), calls=%async_computation.1 | async-start | bytes 1310720 | tf_op jit(solution)/shard_map/all_to_all | solution.py:325
  22.7 16.2 %all-to-all-done.1.refs_0_ = bf16[4,128,640]{2,1,0:T(8,128)(2,1)S(1)} async-done(((bf16[4,128,640]{2,1,0:T(8,128)(2,1)}), bf16[4,128,640]{2,1,0:T(8,128)(2,1)S(1)}, u32[]{:S(2)}, u32[]{:S(2)}) %all-to-all-start.1) | async-done | bytes 655392 | tf_op jit(solution)/shard_map/all_to_all | solution.py:325
  38.9 1.4 broadcast_in_dim.31
  40.3 3.7 %all-to-all-start = ((bf16[4,128,1920]{2,1,0:T(8,128)(2,1)}), bf16[4,128,1920]{2,1,0:T(8,128)(2,1)S(1)}, u32[]{:S(2)}, u32[]{:S(2)}) async-start(bf16[4,128,1920]{2,1,0:T(8,128)(2,1)} %broadcast_in_dim.31), calls=%async_computation | async-start | bytes 3932160 | tf_op jit(solution)/shard_map/all_to_all | solution.py:325
  44.0 1.6 collective-permute-start.4
  45.6 22.8 %collective-permute-done.4.refs_3_ = bf16[16,2,128,128]{3,2,1,0:T(8,128)(2,1)S(1)} collective-permute-done((bf16[16,2,128,128]{3,2,1,0:T(8,128)(2,1)}, bf16[16,2,128,128]{3,2,1,0:T(8,128)(2,1)S(1)}, u32[]{:S(2)}, u32[]{:S(2)}) %collective-permute-start.4) | collective-permute-done | bytes 1048608 | tf_op jit(solution)/shard_map/ppermute | solution.py:29
  68.4 3.5 %fusion.12 = (bf16[16,2,128,128]{3,2,1,0:T(8,128)(2,1)S(1)}, bf16[16,2,128,128]{3,2,1,0:T(8,128)(2,1)}, bf16[16,2,128,128]{3,2,1,0:T(8,128)(2,1)}) fusion(bf16[16,2,128,512]{3,2,1,0:T(8,128)(2,1)} %refs_1_.7), kind=kLoop, calls=%fused_computation.40 | loop fusion | bytes 6291456 | tf_op jit(solution)/shard_map/slice | solution.py:341
  72.0 1.5 collective-permute-start.3
  74.2 16.4 %shard_map.86 = bf16[4,656,128]{2,1,0:T(8,128)(2,1)} custom-call(s32[4,16]{1,0:T(4,128)S(1)} %select_reduce_fusion.picks, s32[4]{0:T(128)S(1)} %get-tuple-element.23.counts, s32[4]{0:T(128)S(1)} %compare_select_fusion.lasts, s32[1]{0:T(128)} %bitcast.3.mine, s32[1]{0:T(128)} %bitcast.7.store, bf16[4,128,640]{2,1,0:T(8,128)(2,1)S(1)} %all-to-all-done.1.refs_0_, ...), custom_call_target="tpu_custom_call" | custom-call | flops 1 | bytes 1 | tf_op jit(solution)/shard_map/pallas_call | solution.py:254
  90.6 7.1 %collective-permute-done.3.refs_3_ = bf16[16,2,128,128]{3,2,1,0:T(8,128)(2,1)} collective-permute-done((bf16[16,2,128,128]{3,2,1,0:T(8,128)(2,1)S(1)}, bf16[16,2,128,128]{3,2,1,0:T(8,128)(2,1)}, u32[]{:S(2)}, u32[]{:S(2)}) %collective-permute-start.3) | collective-permute-done | bytes 1048608 | tf_op jit(solution)/shard_map/ppermute | solution.py:29
  97.6 1.5 collective-permute-start.2
  99.2 4.7 %all-to-all-start.5 = ((bf16[4,656,128]{2,1,0:T(8,128)(2,1)}), bf16[4,656,128]{2,1,0:T(8,128)(2,1)}, u32[]{:S(2)}, u32[]{:S(2)}) async-start(bf16[4,656,128]{2,1,0:T(8,128)(2,1)} %shard_map.86), calls=%async_computation.5 | async-start | bytes 1343488 | tf_op jit(solution)/shard_map/all_to_all | solution.py:325
  103.9 2.2 %copy-done.1 = bf16[16,2,128,512]{3,2,1,0:T(8,128)(2,1)S(1)} copy-done((bf16[16,2,128,512]{3,2,1,0:T(8,128)(2,1)S(1)}, bf16[16,2,128,512]{3,2,1,0:T(8,128)(2,1)}, u32[]{:S(2)}) %copy-start.1) | copy-done | bytes 4194328
  106.1 15.4 %shard_map.87 = bf16[4,656,128]{2,1,0:T(8,128)(2,1)} custom-call(s32[4,16]{1,0:T(4,128)S(1)} %select_reduce_fusion.picks, s32[4]{0:T(128)S(1)} %get-tuple-element.23.counts, s32[4]{0:T(128)S(1)} %compare_select_fusion.lasts, s32[1]{0:T(128)} %bitcast.3.mine, s32[1]{0:T(128)} %bitcast.8.store, bf16[4,128,1920]{2,1,0:T(8,128)(2,1)S(1)} %all-to-all-done.refs_0_, ...), custom_call_target="tpu_custom_call" | custom-call | flops 1 | bytes 1 | tf_op jit(solution)/shard_map/pallas_call | solution.py:254
  121.5 2.0 collective-permute-done.2.refs_3_
  123.5 1.5 collective-permute-start.1
  125.1 4.7 %all-to-all-start.4 = ((bf16[4,656,128]{2,1,0:T(8,128)(2,1)}), bf16[4,656,128]{2,1,0:T(8,128)(2,1)}, u32[]{:S(2)}, u32[]{:S(2)}) async-start(bf16[4,656,128]{2,1,0:T(8,128)(2,1)} %shard_map.87), calls=%async_computation.4 | async-start | bytes 1343488 | tf_op jit(solution)/shard_map/all_to_all | solution.py:325
  129.8 18.3 %collective-permute-done.8.refs_6_ = bf16[1,2,128,512]{3,2,1,0:T(8,128)(2,1)S(1)} collective-permute-done((bf16[1,2,128,512]{3,2,1,0:T(8,128)(2,1)S(1)}, bf16[1,2,128,512]{3,2,1,0:T(8,128)(2,1)S(1)}, u32[]{:S(2)}, u32[]{:S(2)}) %collective-permute-start.8) | collective-permute-done | bytes 262176 | tf_op jit(solution)/shard_map/ppermute | solution.py:34
  148.1 2.2 %copy-done.2 = bf16[16,2,128,512]{3,2,1,0:T(8,128)(2,1)S(1)} copy-done((bf16[16,2,128,512]{3,2,1,0:T(8,128)(2,1)S(1)}, bf16[16,2,128,512]{3,2,1,0:T(8,128)(2,1)}, u32[]{:S(2)}) %copy-start.2) | copy-done | bytes 4194328
  150.3 14.9 %shard_map.88 = (bf16[4,656,128]{2,1,0:T(8,128)(2,1)S(1)}, bf16[16,2,128,512]{3,2,1,0:T(8,128)(2,1)}) custom-call(s32[4,16]{1,0:T(4,128)S(1)} %select_reduce_fusion.picks, s32[4]{0:T(128)S(1)} %get-tuple-element.23.counts, s32[4]{0:T(128)S(1)} %compare_select_fusion.lasts, s32[1]{0:T(128)} %bitcast.3.mine, s32[1]{0:T(128)} %bitcast.9.store, ...), custom_call_target="tpu_custom_call" | custom-call | flops 1 | bytes 1 | tf_op jit(solution)/shard_map/pallas_call | solution.py:254
  165.3 0.9 copy-done.5
  166.1 1.7 collective-permute-start.9
  167.8 5.4 %all-to-all-start.3 = ((bf16[4,656,128]{2,1,0:T(8,128)(2,1)}), bf16[4,656,128]{2,1,0:T(8,128)(2,1)}, u32[]{:S(2)}, u32[]{:S(2)}) async-start(bf16[4,656,128]{2,1,0:T(8,128)(2,1)} %copy-done.5), calls=%async_computation.3 | async-start | bytes 1343488 | tf_op jit(solution)/shard_map/all_to_all | solution.py:325
  173.2 2.2 %copy-done.3 = bf16[16,2,128,512]{3,2,1,0:T(8,128)(2,1)S(1)} copy-done((bf16[16,2,128,512]{3,2,1,0:T(8,128)(2,1)S(1)}, bf16[16,2,128,512]{3,2,1,0:T(8,128)(2,1)}, u32[]{:S(2)}) %copy-start.3) | copy-done | bytes 4194328
  175.4 15.4 %shard_map.89 = bf16[4,656,128]{2,1,0:T(8,128)(2,1)} custom-call(s32[4,16]{1,0:T(4,128)S(1)} %select_reduce_fusion.picks, s32[4]{0:T(128)S(1)} %get-tuple-element.23.counts, s32[4]{0:T(128)S(1)} %compare_select_fusion.lasts, s32[1]{0:T(128)} %bitcast.3.mine, s32[1]{0:T(128)} %bitcast.10.store, bf16[4,128,1920]{2,1,0:T(8,128)(2,1)S(1)} %all-to-all-done.refs_0_, ...), custom_call_target="tpu_custom_call" | custom-call | flops 1 | bytes 1 | tf_op jit(solution)/shard_map/pallas_call | solution.py:254
  190.8 0.3 all-to-all-done.3.parts
  191.1 3.5 %all-to-all-start.2 = ((bf16[4,656,128]{2,1,0:T(8,128)(2,1)}), bf16[4,656,128]{2,1,0:T(8,128)(2,1)S(1)}, u32[]{:S(2)}, u32[]{:S(2)}) async-start(bf16[4,656,128]{2,1,0:T(8,128)(2,1)} %shard_map.89), calls=%async_computation.2 | async-start | bytes 1343488 | tf_op jit(solution)/shard_map/all_to_all | solution.py:325
  194.6 2.3 %shard_map.90.refs_0_ = bf16[128,2560]{1,0:T(8,128)(2,1)} custom-call(bf16[4,656,128]{2,1,0:T(8,128)(2,1)} %all-to-all-done.5.parts), custom_call_target="tpu_custom_call" | custom-call | flops 1 | bytes 1 | tf_op jit(solution)/shard_map/pallas_call | solution.py:289
  197.0 2.4 %shard_map.91.refs_0_ = bf16[128,2560]{1,0:T(8,128)(2,1)} custom-call(bf16[4,656,128]{2,1,0:T(8,128)(2,1)} %all-to-all-done.4.parts, bf16[128,2560]{1,0:T(8,128)(2,1)} %shard_map.90.refs_0_), custom_call_target="tpu_custom_call", output_to_operand_aliasing={{}: (1, {})} | custom-call | flops 1 | bytes 1 | tf_op jit(solution)/shard_map/pallas_call | solution.py:289
  199.3 2.4 %shard_map.92.refs_0_ = bf16[128,2560]{1,0:T(8,128)(2,1)} custom-call(bf16[4,656,128]{2,1,0:T(8,128)(2,1)} %all-to-all-done.3.parts, bf16[128,2560]{1,0:T(8,128)(2,1)} %shard_map.91.refs_0_), custom_call_target="tpu_custom_call", output_to_operand_aliasing={{}: (1, {})} | custom-call | flops 1 | bytes 1 | tf_op jit(solution)/shard_map/pallas_call | solution.py:289
  201.7 10.7 %all-to-all-done.2.parts = bf16[4,656,128]{2,1,0:T(8,128)(2,1)S(1)} async-done(((bf16[4,656,128]{2,1,0:T(8,128)(2,1)}), bf16[4,656,128]{2,1,0:T(8,128)(2,1)S(1)}, u32[]{:S(2)}, u32[]{:S(2)}) %all-to-all-start.2) | async-done | bytes 671776 | tf_op jit(solution)/shard_map/all_to_all | solution.py:325
  212.4 0.9 copy-done.6
  213.2 2.3 %shard_map.93 = bf16[128,2560]{1,0:T(8,128)(2,1)} custom-call(bf16[4,656,128]{2,1,0:T(8,128)(2,1)} %copy-done.6, bf16[128,2560]{1,0:T(8,128)(2,1)} %shard_map.92.refs_0_), custom_call_target="tpu_custom_call", output_to_operand_aliasing={{}: (1, {})} | custom-call | flops 1 | bytes 1 | tf_op jit(solution)/shard_map/pallas_call | solution.py:289
  (27 shorter events, 0.1 us)
Async XLA Ops:
  0.6 38.2 %slice-start = ((bf16[128,2560]{1,0:T(8,128)(2,1)}), bf16[128,1920]{1,0:T(8,128)(2,1)S(1)}, s32[]{:S(2)}) async-start(bf16[128,2560]{1,0:T(8,128)(2,1)} %param.7), calls=%async_computation.6 | async-start | bytes 983040 | tf_op jit(solution)/shard_map/slice | solution.py:347
  3.0 71.2 %collective-permute-start = (bf16[16,2,128,512]{3,2,1,0:T(8,128)(2,1)}, bf16[16,2,128,512]{3,2,1,0:T(8,128)(2,1)}, u32[]{:S(2)}, u32[]{:S(2)}) collective-permute-start(bf16[16,2,128,512]{3,2,1,0:T(8,128)(2,1)} %refs_1_.7), channel_id=1, source_target_pairs={{0,1},{1,0},{2,3},{3,2},{4,5},{5,4},{6,7},{7,6},{8,9},{9,8},{10,11... | collective-permute-start | bytes 12582920 | tf_op jit(solution)/shard_map/ppermute | solution.py:29
  19.2 19.7 %all-to-all-start.1 = ((bf16[4,128,640]{2,1,0:T(8,128)(2,1)}), bf16[4,128,640]{2,1,0:T(8,128)(2,1)S(1)}, u32[]{:S(2)}, u32[]{:S(2)}) async-start(bf16[4,128,640]{2,1,0:T(8,128)(2,1)} %broadcast_in_dim.30), calls=%async_computation.1 | async-start | bytes 1310720 | tf_op jit(solution)/shard_map/all_to_all | solution.py:325
  40.3 33.9 %copy-start.4 = (bf16[1,1,2,128,512]{4,3,2,1,0:T(8,128)(2,1)S(1)}, bf16[1,1,2,128,512]{4,3,2,1,0:T(8,128)(2,1)}, u32[]{:S(2)}) copy-start(bf16[1,1,2,128,512]{4,3,2,1,0:T(8,128)(2,1)} %param.8) | copy-start | bytes 786436
  40.3 58.9 %all-to-all-start = ((bf16[4,128,1920]{2,1,0:T(8,128)(2,1)}), bf16[4,128,1920]{2,1,0:T(8,128)(2,1)S(1)}, u32[]{:S(2)}, u32[]{:S(2)}) async-start(bf16[4,128,1920]{2,1,0:T(8,128)(2,1)} %broadcast_in_dim.31), calls=%async_computation | async-start | bytes 3932160 | tf_op jit(solution)/shard_map/all_to_all | solution.py:325
  44.0 30.2 %copy-start = (bf16[16,2,128,512]{3,2,1,0:T(8,128)(2,1)S(1)}, bf16[16,2,128,512]{3,2,1,0:T(8,128)(2,1)}, u32[]{:S(2)}) copy-start(bf16[16,2,128,512]{3,2,1,0:T(8,128)(2,1)} %refs_1_.7) | copy-start | bytes 12582916
  44.0 24.4 %collective-permute-start.4 = (bf16[16,2,128,128]{3,2,1,0:T(8,128)(2,1)}, bf16[16,2,128,128]{3,2,1,0:T(8,128)(2,1)S(1)}, u32[]{:S(2)}, u32[]{:S(2)}) collective-permute-start(bf16[16,2,128,128]{3,2,1,0:T(8,128)(2,1)} %slice.32), channel_id=1, source_target_pairs={{0,2},{1,3},{2,0},{3,1},{4,6},{5,7},{6,4},{7,5},{8,10},{9,11},{10,... | collective-permute-start | bytes 3145736 | tf_op jit(solution)/shard_map/ppermute | solution.py:29
  68.4 5.7 %collective-permute-start.5 = (bf16[16,2,128,128]{3,2,1,0:T(8,128)(2,1)S(1)}, bf16[16,2,128,128]{3,2,1,0:T(8,128)(2,1)S(1)}, u32[]{:S(2)}, u32[]{:S(2)}) collective-permute-start(bf16[16,2,128,128]{3,2,1,0:T(8,128)(2,1)S(1)} %collective-permute-done.4.refs_3_), channel_id=1, source_target_pairs={{0,1},{1,0},{2,3},{3,2},{4,5},{5,4},{6,7},{7,6},{8,9},{9,8},{10,11... | collective-permute-start | bytes 3145736 | tf_op jit(solution)/shard_map/ppermute | solution.py:29
  72.0 25.7 %collective-permute-start.3 = (bf16[16,2,128,128]{3,2,1,0:T(8,128)(2,1)S(1)}, bf16[16,2,128,128]{3,2,1,0:T(8,128)(2,1)}, u32[]{:S(2)}, u32[]{:S(2)}) collective-permute-start(bf16[16,2,128,128]{3,2,1,0:T(8,128)(2,1)S(1)} %get-tuple-element.26), channel_id=1, source_target_pairs={{0,2},{1,3},{2,0},{3,1},{4,6},{5,7},{6,4},{7,5},{8,10},{9,11},{10,... | collective-permute-start | bytes 3145736 | tf_op jit(solution)/shard_map/ppermute | solution.py:29
  97.6 6.2 %collective-permute-start.6 = (bf16[16,2,128,128]{3,2,1,0:T(8,128)(2,1)}, bf16[16,2,128,128]{3,2,1,0:T(8,128)(2,1)S(1)}, u32[]{:S(2)}, u32[]{:S(2)}) collective-permute-start(bf16[16,2,128,128]{3,2,1,0:T(8,128)(2,1)} %collective-permute-done.3.refs_3_), channel_id=1, source_target_pairs={{0,1},{1,0},{2,3},{3,2},{4,5},{5,4},{6,7},{7,6},{8,9},{9,8},{10,11... | collective-permute-start | bytes 3145736 | tf_op jit(solution)/shard_map/ppermute | solution.py:29
  97.6 25.9 %collective-permute-start.2 = (bf16[16,2,128,128]{3,2,1,0:T(8,128)(2,1)}, bf16[16,2,128,128]{3,2,1,0:T(8,128)(2,1)}, u32[]{:S(2)}, u32[]{:S(2)}) collective-permute-start(bf16[16,2,128,128]{3,2,1,0:T(8,128)(2,1)} %get-tuple-element.27), channel_id=1, source_target_pairs={{0,2},{1,3},{2,0},{3,1},{4,6},{5,7},{6,4},{7,5},{8,10},{9,11},{10,... | collective-permute-start | bytes 3145736 | tf_op jit(solution)/shard_map/ppermute | solution.py:29
  99.2 25.9 %all-to-all-start.5 = ((bf16[4,656,128]{2,1,0:T(8,128)(2,1)}), bf16[4,656,128]{2,1,0:T(8,128)(2,1)}, u32[]{:S(2)}, u32[]{:S(2)}) async-start(bf16[4,656,128]{2,1,0:T(8,128)(2,1)} %shard_map.86), calls=%async_computation.5 | async-start | bytes 1343488 | tf_op jit(solution)/shard_map/all_to_all | solution.py:325
  103.9 2.2 %copy-start.1 = (bf16[16,2,128,512]{3,2,1,0:T(8,128)(2,1)S(1)}, bf16[16,2,128,512]{3,2,1,0:T(8,128)(2,1)}, u32[]{:S(2)}) copy-start(bf16[16,2,128,512]{3,2,1,0:T(8,128)(2,1)} %refs_1_.7) | copy-start | bytes 12582916
  123.5 24.6 %collective-permute-start.7 = (bf16[16,2,128,128]{3,2,1,0:T(8,128)(2,1)}, bf16[16,2,128,128]{3,2,1,0:T(8,128)(2,1)}, u32[]{:S(2)}, u32[]{:S(2)}) collective-permute-start(bf16[16,2,128,128]{3,2,1,0:T(8,128)(2,1)} %collective-permute-done.2.refs_3_), channel_id=1, source_target_pairs={{0,1},{1,0},{2,3},{3,2},{4,5},{5,4},{6,7},{7,6},{8,9},{9,8},{10,11... | collective-permute-start | bytes 3145736 | tf_op jit(solution)/shard_map/ppermute | solution.py:29
  123.5 42.6 %collective-permute-start.1 = (bf16[16,2,128,128]{3,2,1,0:T(8,128)(2,1)}, bf16[16,2,128,128]{3,2,1,0:T(8,128)(2,1)S(1)}, u32[]{:S(2)}, u32[]{:S(2)}) collective-permute-start(bf16[16,2,128,128]{3,2,1,0:T(8,128)(2,1)} %get-tuple-element.28), channel_id=1, source_target_pairs={{0,2},{1,3},{2,0},{3,1},{4,6},{5,7},{6,4},{7,5},{8,10},{9,11},{10,... | collective-permute-start | bytes 3145736 | tf_op jit(solution)/shard_map/ppermute | solution.py:29
  125.1 42.8 %all-to-all-start.4 = ((bf16[4,656,128]{2,1,0:T(8,128)(2,1)}), bf16[4,656,128]{2,1,0:T(8,128)(2,1)}, u32[]{:S(2)}, u32[]{:S(2)}) async-start(bf16[4,656,128]{2,1,0:T(8,128)(2,1)} %shard_map.87), calls=%async_computation.4 | async-start | bytes 1343488 | tf_op jit(solution)/shard_map/all_to_all | solution.py:325
  129.8 18.3 %collective-permute-start.8 = (bf16[1,2,128,512]{3,2,1,0:T(8,128)(2,1)S(1)}, bf16[1,2,128,512]{3,2,1,0:T(8,128)(2,1)S(1)}, u32[]{:S(2)}, u32[]{:S(2)}) collective-permute-start(bf16[1,2,128,512]{3,2,1,0:T(8,128)(2,1)S(1)} %bitcast.13), channel_id=1, source_target_pairs={{0,1},{1,2},{2,3},{3,4},{4,5},{5,6},{6,7},{7,8},{8,9},{9,10},{10,1... | collective-permute-start | bytes 786440 | tf_op jit(solution)/shard_map/ppermute | solution.py:34
  148.1 2.2 %copy-start.2 = (bf16[16,2,128,512]{3,2,1,0:T(8,128)(2,1)S(1)}, bf16[16,2,128,512]{3,2,1,0:T(8,128)(2,1)}, u32[]{:S(2)}) copy-start(bf16[16,2,128,512]{3,2,1,0:T(8,128)(2,1)} %refs_1_.7) | copy-start | bytes 12582916
  165.2 0.9 copy-start.5
  166.1 7.1 %collective-permute-start.9 = (bf16[16,2,128,128]{3,2,1,0:T(8,128)(2,1)S(1)}, bf16[16,2,128,128]{3,2,1,0:T(8,128)(2,1)}, u32[]{:S(2)}, u32[]{:S(2)}) collective-permute-start(bf16[16,2,128,128]{3,2,1,0:T(8,128)(2,1)S(1)} %collective-permute-done.1.refs_3_), channel_id=1, source_target_pairs={{0,1},{1,0},{2,3},{3,2},{4,5},{5,4},{6,7},{7,6},{8,9},{9,8},{10,11... | collective-permute-start | bytes 3145736 | tf_op jit(solution)/shard_map/ppermute | solution.py:29
  167.8 23.3 %all-to-all-start.3 = ((bf16[4,656,128]{2,1,0:T(8,128)(2,1)}), bf16[4,656,128]{2,1,0:T(8,128)(2,1)}, u32[]{:S(2)}, u32[]{:S(2)}) async-start(bf16[4,656,128]{2,1,0:T(8,128)(2,1)} %copy-done.5), calls=%async_computation.3 | async-start | bytes 1343488 | tf_op jit(solution)/shard_map/all_to_all | solution.py:325
  173.2 2.2 %copy-start.3 = (bf16[16,2,128,512]{3,2,1,0:T(8,128)(2,1)S(1)}, bf16[16,2,128,512]{3,2,1,0:T(8,128)(2,1)}, u32[]{:S(2)}) copy-start(bf16[16,2,128,512]{3,2,1,0:T(8,128)(2,1)} %refs_1_.7) | copy-start | bytes 12582916
  191.1 21.3 %all-to-all-start.2 = ((bf16[4,656,128]{2,1,0:T(8,128)(2,1)}), bf16[4,656,128]{2,1,0:T(8,128)(2,1)S(1)}, u32[]{:S(2)}, u32[]{:S(2)}) async-start(bf16[4,656,128]{2,1,0:T(8,128)(2,1)} %shard_map.89), calls=%async_computation.2 | async-start | bytes 1343488 | tf_op jit(solution)/shard_map/all_to_all | solution.py:325
  212.4 0.9 copy-start.6

commit v5 on v4

--- a/solution.py
+++ b/solution.py
@@ -17,7 +17,7 @@
 LOW = -1e30
 CLUSTER = 4
 BLOCK = 4
-STAT = 16
+STAT = 32
 HEADS = ((0, 1, 2), (3, 4))
 ROWS = GQ * PAGE + STAT
 CHUNK = GQ * HD
@@ -36,11 +36,11 @@
 
 def attend_kernel(lines, head, q_head, picks, counts, lasts, mine, store, *refs):
     q_all, own, twin, side, both, fresh = refs[:6]
-    stores = len(refs) == 19
+    stores = len(refs) == 20
     if stores:
-        incoming, out, pool_out = refs[6:9]
+        pool, incoming, out, pool_out = refs[6:10]
         store_sems = refs[-1]
-        scratch = refs[9:-1]
+        scratch = refs[10:-1]
     else:
         out = refs[6]
         scratch = refs[7:]
@@ -53,7 +53,7 @@
         return lax.rem(mine[0] - t + lines, lines)
 
     def q_copy(t, h):
-        origin = q_all.at[request_of(t), :, pl.ds((q_head * GQ + h) * HD, HD)]
+        origin = q_all.at[request_of(t), pl.ds(0, PAGE), pl.ds((q_head * GQ + h) * HD, HD)]
         return pltpu.make_async_copy(origin, queries.at[t, h], q_sems.at[t, h])
 
     def out_copy(t):
@@ -88,7 +88,7 @@
             page_copy(own, 0, buffer, place).wait()
 
     def store_copy(slot):
-        return pltpu.make_async_copy(own.at[slot], pool_out.at[slot], store_sems.at[slot])
+        return pltpu.make_async_copy(pool.at[slot], pool_out.at[slot], store_sems.at[slot])
 
     fresh_copy = pltpu.make_async_copy(fresh.at[:, :, columns], pages.at[0, extra], page_sems.at[0, extra])
     for t in range(lines):
@@ -101,7 +101,7 @@
     if lines > 1:
         fetch(1)
     if stores:
-        @pl.loop(0, slots)
+        @pl.loop(0, pool.shape[0])
         def _(slot):
             @pl.when(slot != store[0])
             def _():
@@ -150,18 +150,20 @@
     def finish(t):
         some = (counts[request_of(t)] > 0) | (t == 0)
         lane = lax.broadcasted_iota(jnp.int32, (PAGE, PAGE), 1)
-        stat = jnp.zeros((PAGE, PAGE), jnp.float32)
+        sums = jnp.ones((PAGE, PAGE), jnp.float32)
+        heights = jnp.zeros((PAGE, PAGE), jnp.float32)
         for h in range(GQ):
             total = acc[h, :, HD:]
             results[t, h * PAGE:(h + 1) * PAGE, :] = (acc[h, :, :HD] * (1.0 / total)).astype(jnp.bfloat16)
-            level = jnp.where(some, tops[h] * SCALE + jnp.log(total), LOW)
-            high = level.astype(jnp.bfloat16).astype(jnp.float32)
-            middle = (level - high).astype(jnp.bfloat16).astype(jnp.float32)
-            low = level - high - middle
-            stat = jnp.where(lane == h, high, stat)
-            stat = jnp.where(lane == GQ + h, middle, stat)
-            stat = jnp.where(lane == 2 * GQ + h, low, stat)
-        results[t, GQ * PAGE:, :] = stat.T[:STAT].astype(jnp.bfloat16)
+            sums = jnp.where(lane == h, total, sums)
+            heights = jnp.where(lane == h, tops[h], heights)
+        level = heights.T[:8] * SCALE + jnp.log(sums.T[:8])
+        level = jnp.where(some, level, LOW)
+        high = level.astype(jnp.bfloat16).astype(jnp.float32)
+        middle = (level - high).astype(jnp.bfloat16).astype(jnp.float32)
+        low = level - high - middle
+        stat = jnp.concatenate([high, middle, low, jnp.zeros_like(low)], axis=0)
+        results[t, GQ * PAGE:, :] = stat.astype(jnp.bfloat16)
         out_copy(t).start()
 
     for t in range(lines):
@@ -217,16 +219,15 @@
     for t in range(lines):
         out_copy(t).wait()
     if stores:
-        @pl.loop(0, slots)
+        @pl.loop(0, pool.shape[0])
         def _(slot):
             store_copy(slot).wait()
 
 
-def attend(head, q_head, tables, q_all, pools, fresh, incoming=None):
+def attend(head, q_head, tables, q_all, pools, fresh, pool=None, incoming=None):
     picks, counts, lasts, mine, store = tables
     lines = q_all.shape[0]
     places = picks.shape[1]
-    pool = pools[0]
     out_shape = [jax.ShapeDtypeStruct((lines, ROWS, HD), jnp.bfloat16)]
     scratch = [
         pltpu.VMEM((2, places + 1, 2, PAGE, HD), jnp.bfloat16),
@@ -241,13 +242,13 @@
     ]
     operands = [q_all, *pools, fresh]
     if incoming is not None:
-        operands.append(incoming)
+        operands += [pool, incoming]
         out_shape.append(jax.ShapeDtypeStruct(pool.shape, pool.dtype))
         scratch.append(pltpu.SemaphoreType.DMA((pool.shape[0],)))
     grid_spec = pltpu.PrefetchScalarGridSpec(
         num_scalar_prefetch=5,
         grid=(),
-        in_specs=[pl.BlockSpec(memory_space=pltpu.HBM)] * 3 + [pl.BlockSpec(memory_space=pl.ANY)] * (len(operands) - 3),
+        in_specs=[pl.BlockSpec(memory_space=pl.ANY)] * len(operands),
         out_specs=[pl.BlockSpec(memory_space=pl.ANY), pl.BlockSpec(memory_space=pltpu.HBM)][:len(out_shape)],
         scratch_shapes=scratch,
     )
@@ -266,17 +267,19 @@
     levels = []
     for i in range(lines):
         block = parts[i, GQ * PAGE:, :].astype(jnp.float32)
-        levels.append(block[:GQ] + block[GQ:2 * GQ] + block[2 * GQ:3 * GQ])
+        levels.append(block[:8] + block[8:16] + block[16:24])
     top = functools.reduce(jnp.maximum, levels)
     weights = [jnp.exp(level - top) for level in levels]
     total = functools.reduce(jnp.add, weights)
     weights = [weight / total for weight in weights]
-    filler = PAGE - lines * GQ
-    table = jnp.concatenate(weights + [jnp.zeros((filler, PAGE), jnp.float32)], axis=0).T
+    filler = PAGE - lines * 8
+    if filler:
+        weights.append(jnp.zeros((filler, PAGE), jnp.float32))
+    table = jnp.concatenate(weights, axis=0).T
     for h in range(GQ):
         merged = jnp.zeros((PAGE, HD), jnp.float32)
         for i in range(lines):
-            column = i * GQ + h
+            column = i * 8 + h
             merged += table[:, column:column + 1] * parts[i, h * PAGE:(h + 1) * PAGE, :].astype(jnp.float32)
         result[:, h * HD:(h + 1) * HD] = merged.astype(jnp.bfloat16)
     copy = pltpu.make_async_copy(result, out.at[:, pl.ds(head * CHUNK, CHUNK)], sem)
@@ -297,28 +300,20 @@
     )(parts, *before)
 
 
-def page_tables(me, width, slots, page_owner, page_slot, prefix_len):
-    lines = width // CLUSTER
-    capacity = (MAXP + width - 2) // (width - 1)
-    limit = min(MAXP, CLUSTER * capacity)
-    groups = [[c * CLUSTER + i for c in range(lines)] for i in range(CLUSTER)]
-    table = jnp.concatenate([page_owner[0], page_slot[0], prefix_len])[None]
-    tables = lax.all_gather(table, "serve", axis_index_groups=groups, tiled=True)
-    owners = tables[:, :MAXP]
-    places = tables[:, MAXP:2 * MAXP]
-    length = tables[:, 2 * MAXP]
+def page_rows(me, lines, limit, slots, page_owner, page_slot, prefix_len):
+    owners = page_owner[0]
+    length = prefix_len[0]
     used = (length + PAGE - 1) // PAGE
     spot = jnp.arange(MAXP)
-    here = (spot[None] < used[:, None]) & (owners // CLUSTER == me // CLUSTER)
-    hits = here.astype(jnp.int32)
-    before = jnp.sum(hits[:, None, :] * (spot[None, None, :] < spot[None, :, None]), axis=2)
-    local = ((owners % CLUSTER) ^ (me % CLUSTER)) * slots + places
+    here = (spot < used)[None] & (owners[None] // CLUSTER == jnp.arange(lines)[:, None])
+    before = jnp.sum(here[:, None, :] & (spot[None, None, :] < spot[None, :, None]), axis=2)
+    local = ((owners % CLUSTER) ^ (me % CLUSTER)) * slots + page_slot[0]
     chosen = here[:, :, None] & (before[:, :, None] == jnp.arange(limit)[None, None, :])
-    picks = jnp.sum(jnp.where(chosen, local[:, :, None], 0), axis=1)
-    counts = jnp.sum(hits, axis=1)
-    tail = jnp.sum(jnp.where(here & (spot[None] == used[:, None] - 1), 1, 0), axis=1)
-    lasts = jnp.where(tail > 0, length - (used - 1) * PAGE, PAGE)
-    return picks, counts, lasts, (me // CLUSTER)[None]
+    picks = jnp.sum(jnp.where(chosen, local[None, :, None], 0), axis=1)
+    counts = jnp.sum(here, axis=1)
+    tail = jnp.any(here & (spot == used - 1)[None], axis=1)
+    lasts = jnp.where(tail, length - (used - 1) * PAGE, PAGE)
+    return jnp.concatenate([picks, counts[:, None], lasts[:, None]], axis=1)
 
 
 def exchanged(array, groups):
@@ -335,33 +330,34 @@
     groups = [[c * CLUSTER + i for c in range(lines)] for i in range(CLUSTER)]
     me = lax.axis_index("serve")
     slots = pool.shape[0]
-    first = pool[:, :, :, :HD]
-    rest = after(pool, first)
-    sides = [swapped(first, "serve", 2)]
-    sides += [swapped(rest[:, :, :, g * HD:(g + 1) * HD], "serve", 2) for g in range(1, KVH)]
-    tables = page_tables(me, width, slots, page_owner, page_slot, prefix_len) + (store_slot[0],)
+    capacity = (MAXP + width - 2) // (width - 1)
+    limit = min(MAXP, CLUSTER * capacity)
+    owns = [pool[:, :, :, :HD]]
+    rest = after(pool, owns[0])
+    owns += [rest[:, :, :, g * HD:(g + 1) * HD] for g in range(1, KVH)]
+    sides = [swapped(own, "serve", 2) for own in owns]
     twin = swapped(rest, "serve", 1)
-    q_parts = []
-    last = tables[0]
-    for begin, end in ((0, 1), (1, KVH)):
-        part = after(queries, last)[None, :, begin * CHUNK:end * CHUNK]
-        part = jnp.broadcast_to(part, (lines, PAGE, (end - begin) * CHUNK))
-        last = part
-        part = exchanged(part, groups)
-        q_parts += [(part, i) for i in range(end - begin)]
+    incoming = shifted(new_kv[0], "serve", 1)
+    rows = page_rows(me, lines, limit, slots, page_owner, page_slot, prefix_len).astype(queries.dtype)
+    rows = jnp.pad(rows[:, None], ((0, 0), (0, 15), (0, CHUNK - limit - 2)))
+    early = after(queries, owns[1])[:, :CHUNK]
+    early = jnp.concatenate([jnp.broadcast_to(early[None], (lines, PAGE, CHUNK)), rows], axis=1)
+    early = exchanged(early, groups)
+    later = after(queries, sides[0], incoming)[None, :, CHUNK:]
+    later = exchanged(jnp.broadcast_to(later, (lines, PAGE, (KVH - 1) * CHUNK)), groups)
+    numbers = early[:, PAGE, :limit + 2].astype(jnp.int32)
+    tables = (numbers[:, :limit], numbers[:, limit], numbers[:, limit + 1], (me // CLUSTER)[None], store_slot[0])
     fresh = new_kv[0, 0]
-    incoming = shifted(after(new_kv[0], tables[0]), "serve", 1)
     attended = None
     parts = None
     for g in range(KVH):
         side = sides[g] if g == 0 else after(sides[g], parts)
-        q_all, q_head = q_parts[g]
         both = swapped(side, "serve", 1)
-        pools = (pool, twin, side, both)
-        if g == KVH - 2:
-            parts, pool_out = attend(g, q_head, tables, q_all, pools, fresh, incoming)
+        pools = (owns[g], twin, side, both)
+        if g == 0:
+            parts, pool_out = attend(g, 0, tables, early, pools, fresh, pool, incoming)
         else:
-            parts = attend(g, q_head, tables, q_all, pools, fresh)[0]
+            parts = attend(g, g - 1, tables, later, pools, fresh)[0]
         attended = merge(g, exchanged(parts, groups), attended)
     return (attended, pool_out)
 

time: 218 us -> 192 us (0.88)
  blocking collectives: 9.45 us -> 0 us
  waiting for transfers between devices: 77.5 us -> 69.7 us
  Pallas kernels: 71.5 us -> 67.6 us
    ppermute x9, waiting for transfers between devices: 31.9 us -> 18.4 us  [swapped(): return lax.ppermute(array, axis, [(i, i ^ bit) for i in range(size)])]
    unnamed x1 -> x0, blocking collectives: 9.45 us -> none
    all_to_all x6, waiting for transfers between devices: 27.2 us -> 32.1 us  [exchanged(): lax.all_to_all(array, 'serve', 0, 0, axis_index_groups=groups, tiled=True)]
    pallas_call x4, Pallas kernels: 62.1 us -> 58.2 us  [attend(): pl.pallas_call(functools.partial(attend_kernel, lines, head, q_head), gri...]
    ppermute x9, starting transfers between devices: 8.29 us -> 4.96 us  [swapped(): return lax.ppermute(array, axis, [(i, i ^ bit) for i in range(size)])]
    unnamed x16 -> x30, local copies, waits for them, and re-layouts: 9.55 us -> 11.1 us
    slice x5 -> x7, local copies, waits for them, and re-layouts: 6.85 us -> 5.32 us  [the longest x1 3.77 us: per_device(): owns += [rest[:, :, :, g * HD:(g + 1) * HD] for g in range(1, KVH)]]
  transfers between devices with their start and end apart: 16 -> 16, of which waited for: 7 -> 7; matrix products, arithmetic and copies ran while one was open for 5% -> 4% of each run, Pallas kernels for 32% -> 34%
where the time goes in v5:
time: 192 us
  waiting for transfers between devices  69.7 us (36%)
  Pallas kernels  67.6 us (35%)
  starting transfers between devices  31.7 us (17%)
  local copies, waits for them, and re-layouts  18.3 us (10%)
  other arithmetic  2.32 us (1%)
  between operations  2.3 us (1%)
    pallas_call x4, Pallas kernels, attend(): pl.pallas_call(functools.partial(attend_kernel, lines, head, q_head), gri...  58.2 us
    all_to_all x6, waiting for transfers between devices, exchanged(): lax.all_to_all(array, 'serve', 0, 0, axis_index_groups=groups, tiled=True)  32.1 us
    all_to_all x6, starting transfers between devices, exchanged(): lax.all_to_all(array, 'serve', 0, 0, axis_index_groups=groups, tiled=True)  26.7 us
    ppermute x1, waiting for transfers between devices, shifted(): lax.ppermute(array, axis, [(i, (i + by) % size) for i in range(size)])  19.1 us
    ppermute x9, waiting for transfers between devices, swapped(): return lax.ppermute(array, axis, [(i, i ^ bit) for i in range(size)])  18.4 us
    unnamed x30, local copies, waits for them, and re-layouts  11.1 us
    pallas_call x4, Pallas kernels, merge(): pl.pallas_call(functools.partial(merge_kernel, head), in_specs=[pl.BlockS...  9.41 us
    ppermute x9, starting transfers between devices, swapped(): return lax.ppermute(array, axis, [(i, i ^ bit) for i in range(size)])  4.96 us
  transfers between devices with their start and end apart: 16, of which 7 were waited for; matrix products, arithmetic and copies ran while one was open for 4% of the time, Pallas kernels for 34%

profile of v5, /device:TPU:0, one launch (start us, length us, event | category | flops | bytes accessed | tf_op | source)
XLA Modules:
  0.0 191.9 jit_solution(18422835225139736037)
XLA Ops:
  0.6 1.3 slice.30.refs_1_
  2.0 0.5 collective-permute-start.2
  3.2 3.8 %fusion.17 = (bf16[16,2,128,128]{3,2,1,0:T(8,128)(2,1)}, bf16[16,2,128,128]{3,2,1,0:T(8,128)(2,1)}, bf16[16,2,128,128]{3,2,1,0:T(8,128)(2,1)}) fusion(bf16[16,2,128,512]{3,2,1,0:T(8,128)(2,1)} %refs_6_.1), kind=kLoop, calls=%fused_computation.41 | loop fusion | bytes 6291456 | tf_op jit(solution)/shard_map/slice | solution.py:337
  7.0 0.1 convert_reduce_fusion.1
  7.2 0.1 convert_reduce_fusion
  7.3 0.1 select_reduce_fusion
  7.5 0.1 and_reduce_fusion
  7.6 0.1 copy.20
  7.8 0.1 copy.19
  7.9 0.1 fusion.8
  8.0 0.9 pad_maximum_fusion
  9.0 5.9 %all-to-all-start = ((bf16[4,144,640]{2,1,0:T(8,128)(2,1)}), bf16[4,144,640]{2,1,0:T(8,128)(2,1)S(1)}, u32[]{:S(2)}, u32[]{:S(2)}) async-start(bf16[4,144,640]{2,1,0:T(8,128)(2,1)} %pad_maximum_fusion), calls=%async_computation | async-start | bytes 1474560 | tf_op jit(solution)/shard_map/all_to_all | solution.py:320
  14.9 1.5 collective-permute-start
  16.4 19.1 %collective-permute-done.1.refs_7_ = bf16[1,2,128,512]{3,2,1,0:T(8,128)(2,1)S(1)} collective-permute-done((bf16[1,2,128,512]{3,2,1,0:T(8,128)(2,1)S(1)}, bf16[1,2,128,512]{3,2,1,0:T(8,128)(2,1)S(1)}, u32[]{:S(2)}, u32[]{:S(2)}) %collective-permute-start.1) | collective-permute-done | bytes 262176 | tf_op jit(solution)/shard_map/ppermute | solution.py:34
  35.5 7.5 %collective-permute-done.refs_3_ = bf16[16,2,128,128]{3,2,1,0:T(8,128)(2,1)} collective-permute-done((bf16[16,2,128,128]{3,2,1,0:T(8,128)(2,1)S(1)}, bf16[16,2,128,128]{3,2,1,0:T(8,128)(2,1)}, u32[]{:S(2)}, u32[]{:S(2)}) %collective-permute-start) | collective-permute-done | bytes 1048608 | tf_op jit(solution)/shard_map/ppermute | solution.py:29
  43.1 1.6 broadcast_in_dim.32
  44.6 4.8 %all-to-all-start.1 = ((bf16[4,128,1920]{2,1,0:T(8,128)(2,1)}), bf16[4,128,1920]{2,1,0:T(8,128)(2,1)S(1)}, u32[]{:S(2)}, u32[]{:S(2)}) async-start(bf16[4,128,1920]{2,1,0:T(8,128)(2,1)} %broadcast_in_dim.32), calls=%async_computation.1 | async-start | bytes 3932160 | tf_op jit(solution)/shard_map/all_to_all | solution.py:320
  49.4 1.4 collective-permute-start.5
  51.5 0.7 slice_convert_fusion
  52.2 0.2 slice_reduce_fusion
  52.5 2.2 %copy-done = bf16[16,2,128,512]{3,2,1,0:T(8,128)(2,1)S(1)} copy-done((bf16[16,2,128,512]{3,2,1,0:T(8,128)(2,1)S(1)}, bf16[16,2,128,512]{3,2,1,0:T(8,128)(2,1)}, u32[]{:S(2)}) %copy-start) | copy-done | bytes 4194328
  54.6 1.1 copy-done.5
  55.8 14.8 %shard_map.86 = (bf16[4,672,128]{2,1,0:T(8,128)(2,1)S(1)}, bf16[16,2,128,512]{3,2,1,0:T(8,128)(2,1)}) custom-call(s32[4,16]{1,0:T(4,128)S(1)} %bitcast.31, s32[4]{0:T(128)S(1)} %get-tuple-element.19.counts, s32[4]{0:T(128)S(1)} %get-tuple-element.18.lasts, s32[1]{0:T(128)} %bitcast.8.mine, s32[1]{0:T(128)} %bitcast.21.store, ...), custom_call_target="tpu_custom_call" | custom-call | flops 1 | bytes 1 | tf_op jit(solution)/shard_map/pallas_call | solution.py:255
  70.6 0.9 copy-done.11
  71.5 3.8 %collective-permute-done.5.refs_3_ = bf16[16,2,128,128]{3,2,1,0:T(8,128)(2,1)} collective-permute-done((bf16[16,2,128,128]{3,2,1,0:T(8,128)(2,1)}, bf16[16,2,128,128]{3,2,1,0:T(8,128)(2,1)}, u32[]{:S(2)}, u32[]{:S(2)}) %collective-permute-start.5) | collective-permute-done | bytes 1048608 | tf_op jit(solution)/shard_map/ppermute | solution.py:29
  75.3 1.4 collective-permute-start.4
  76.7 17.3 %all-to-all-done.1.refs_0_ = bf16[4,128,1920]{2,1,0:T(8,128)(2,1)S(1)} async-done(((bf16[4,128,1920]{2,1,0:T(8,128)(2,1)}), bf16[4,128,1920]{2,1,0:T(8,128)(2,1)S(1)}, u32[]{:S(2)}, u32[]{:S(2)}) %all-to-all-start.1) | async-done | bytes 1966112 | tf_op jit(solution)/shard_map/all_to_all | solution.py:320
  94.0 4.2 %all-to-all-start.5 = ((bf16[4,672,128]{2,1,0:T(8,128)(2,1)}), bf16[4,672,128]{2,1,0:T(8,128)(2,1)}, u32[]{:S(2)}, u32[]{:S(2)}) async-start(bf16[4,672,128]{2,1,0:T(8,128)(2,1)} %copy-done.11), calls=%async_computation.5 | async-start | bytes 1376256 | tf_op jit(solution)/shard_map/all_to_all | solution.py:320
  98.2 1.0 copy-done.9
  99.2 1.2 copy-done.3
  100.5 1.2 copy-done.10
  101.7 15.5 %shard_map.87 = bf16[4,672,128]{2,1,0:T(8,128)(2,1)S(1)} custom-call(s32[4,16]{1,0:T(4,128)S(1)} %bitcast.32, s32[4]{0:T(128)S(1)} %get-tuple-element.19.counts, s32[4]{0:T(128)S(1)} %get-tuple-element.18.lasts, s32[1]{0:T(128)} %bitcast.8.mine, s32[1]{0:T(128)} %bitcast.22.store, bf16[4,128,1920]{2,1,0:T(8,128)(2,1)S(1)} %all-to-all-done.1.refs_0_, ...), custom_call_target="tpu_custom_call" | custom-call | flops 1 | bytes 1 | tf_op jit(solution)/shard_map/pallas_call | solution.py:255
  117.2 0.9 copy-done.6
  118.2 4.2 %all-to-all-start.4 = ((bf16[4,672,128]{2,1,0:T(8,128)(2,1)}), bf16[4,672,128]{2,1,0:T(8,128)(2,1)}, u32[]{:S(2)}, u32[]{:S(2)}) async-start(bf16[4,672,128]{2,1,0:T(8,128)(2,1)} %copy-done.6), calls=%async_computation.4 | async-start | bytes 1376256 | tf_op jit(solution)/shard_map/all_to_all | solution.py:320
  122.4 13.4 %shard_map.88 = bf16[4,672,128]{2,1,0:T(8,128)(2,1)S(1)} custom-call(s32[4,16]{1,0:T(4,128)S(1)} %bitcast.33, s32[4]{0:T(128)S(1)} %get-tuple-element.19.counts, s32[4]{0:T(128)S(1)} %get-tuple-element.18.lasts, s32[1]{0:T(128)} %bitcast.8.mine, s32[1]{0:T(128)} %bitcast.23.store, bf16[4,128,1920]{2,1,0:T(8,128)(2,1)S(1)} %all-to-all-done.1.refs_0_, ...), custom_call_target="tpu_custom_call" | custom-call | flops 1 | bytes 1 | tf_op jit(solution)/shard_map/pallas_call | solution.py:255
  135.8 0.9 copy-done.7
  136.7 7.0 %collective-permute-done.3.refs_3_ = bf16[16,2,128,128]{3,2,1,0:T(8,128)(2,1)} collective-permute-done((bf16[16,2,128,128]{3,2,1,0:T(8,128)(2,1)S(1)}, bf16[16,2,128,128]{3,2,1,0:T(8,128)(2,1)}, u32[]{:S(2)}, u32[]{:S(2)}) %collective-permute-start.3) | collective-permute-done | bytes 1048608 | tf_op jit(solution)/shard_map/ppermute | solution.py:29
  143.7 4.2 %all-to-all-start.3 = ((bf16[4,672,128]{2,1,0:T(8,128)(2,1)}), bf16[4,672,128]{2,1,0:T(8,128)(2,1)}, u32[]{:S(2)}, u32[]{:S(2)}) async-start(bf16[4,672,128]{2,1,0:T(8,128)(2,1)} %copy-done.7), calls=%async_computation.3 | async-start | bytes 1376256 | tf_op jit(solution)/shard_map/all_to_all | solution.py:320
  147.9 14.5 %shard_map.89 = bf16[4,672,128]{2,1,0:T(8,128)(2,1)S(1)} custom-call(s32[4,16]{1,0:T(4,128)S(1)} %bitcast.34, s32[4]{0:T(128)S(1)} %get-tuple-element.19.counts, s32[4]{0:T(128)S(1)} %get-tuple-element.18.lasts, s32[1]{0:T(128)} %bitcast.8.mine, s32[1]{0:T(128)} %bitcast.24.store, bf16[4,128,1920]{2,1,0:T(8,128)(2,1)S(1)} %all-to-all-done.1.refs_0_, ...), custom_call_target="tpu_custom_call" | custom-call | flops 1 | bytes 1 | tf_op jit(solution)/shard_map/pallas_call | solution.py:255
  162.4 0.9 copy-done.8
  163.3 3.7 %all-to-all-done.3.parts = bf16[4,672,128]{2,1,0:T(8,128)(2,1)} async-done(((bf16[4,672,128]{2,1,0:T(8,128)(2,1)}), bf16[4,672,128]{2,1,0:T(8,128)(2,1)}, u32[]{:S(2)}, u32[]{:S(2)}) %all-to-all-start.3) | async-done | bytes 688160 | tf_op jit(solution)/shard_map/all_to_all | solution.py:320
  167.0 3.5 %all-to-all-start.2 = ((bf16[4,672,128]{2,1,0:T(8,128)(2,1)}), bf16[4,672,128]{2,1,0:T(8,128)(2,1)S(1)}, u32[]{:S(2)}, u32[]{:S(2)}) async-start(bf16[4,672,128]{2,1,0:T(8,128)(2,1)} %copy-done.8), calls=%async_computation.2 | async-start | bytes 1376256 | tf_op jit(solution)/shard_map/all_to_all | solution.py:320
  170.5 2.4 %shard_map.90.refs_0_ = bf16[128,2560]{1,0:T(8,128)(2,1)} custom-call(bf16[4,672,128]{2,1,0:T(8,128)(2,1)} %all-to-all-done.5.parts), custom_call_target="tpu_custom_call" | custom-call | flops 1 | bytes 1 | tf_op jit(solution)/shard_map/pallas_call | solution.py:292
  172.8 2.4 %shard_map.91.refs_0_ = bf16[128,2560]{1,0:T(8,128)(2,1)} custom-call(bf16[4,672,128]{2,1,0:T(8,128)(2,1)} %all-to-all-done.4.parts, bf16[128,2560]{1,0:T(8,128)(2,1)} %shard_map.90.refs_0_), custom_call_target="tpu_custom_call", output_to_operand_aliasing={{}: (1, {})} | custom-call | flops 1 | bytes 1 | tf_op jit(solution)/shard_map/pallas_call | solution.py:292
  175.2 2.4 %shard_map.92.refs_0_ = bf16[128,2560]{1,0:T(8,128)(2,1)} custom-call(bf16[4,672,128]{2,1,0:T(8,128)(2,1)} %all-to-all-done.3.parts, bf16[128,2560]{1,0:T(8,128)(2,1)} %shard_map.91.refs_0_), custom_call_target="tpu_custom_call", output_to_operand_aliasing={{}: (1, {})} | custom-call | flops 1 | bytes 1 | tf_op jit(solution)/shard_map/pallas_call | solution.py:292
  177.6 11.1 %all-to-all-done.2.parts = bf16[4,672,128]{2,1,0:T(8,128)(2,1)S(1)} async-done(((bf16[4,672,128]{2,1,0:T(8,128)(2,1)}), bf16[4,672,128]{2,1,0:T(8,128)(2,1)S(1)}, u32[]{:S(2)}, u32[]{:S(2)}) %all-to-all-start.2) | async-done | bytes 688160 | tf_op jit(solution)/shard_map/all_to_all | solution.py:320
  188.7 0.8 copy-done.12
  189.5 2.4 %shard_map.93 = bf16[128,2560]{1,0:T(8,128)(2,1)} custom-call(bf16[4,672,128]{2,1,0:T(8,128)(2,1)} %copy-done.12, bf16[128,2560]{1,0:T(8,128)(2,1)} %shard_map.92.refs_0_), custom_call_target="tpu_custom_call", output_to_operand_aliasing={{}: (1, {})} | custom-call | flops 1 | bytes 1 | tf_op jit(solution)/shard_map/pallas_call | solution.py:292
  (49 shorter events, 0.3 us)
Async XLA Ops:
  2.0 50.5 %collective-permute-start.2 = (bf16[16,2,128,512]{3,2,1,0:T(8,128)(2,1)}, bf16[16,2,128,512]{3,2,1,0:T(8,128)(2,1)}, u32[]{:S(2)}, u32[]{:S(2)}) collective-permute-start(bf16[16,2,128,512]{3,2,1,0:T(8,128)(2,1)} %refs_6_.1), channel_id=1, source_target_pairs={{0,1},{1,0},{2,3},{3,2},{4,5},{5,4},{6,7},{7,6},{8,9},{9,8},{10,11... | collective-permute-start | bytes 12582920 | tf_op jit(solution)/shard_map/ppermute | solution.py:29
  3.2 3.8 %copy-start.13 = (s32[1,48]{1,0:T(1,128)S(1)}, s32[1,48]{1,0:T(1,128)}, u32[]{:S(2)}) copy-start(s32[1,48]{1,0:T(1,128)} %param.10) | copy-start | bytes 580
  3.2 3.8 %copy-start.14 = (s32[1,48]{1,0:T(1,128)S(1)}, s32[1,48]{1,0:T(1,128)}, u32[]{:S(2)}) copy-start(s32[1,48]{1,0:T(1,128)} %param.11) | copy-start | bytes 580
  3.2 4.7 %slice-start = ((bf16[128,2560]{1,0:T(8,128)(2,1)}), bf16[128,640]{1,0:T(8,128)(2,1)S(1)}, s32[]{:S(2)}) async-start(bf16[128,2560]{1,0:T(8,128)(2,1)} %param.7), calls=%async_computation.6 | async-start | bytes 327680 | tf_op jit(solution)/shard_map/slice | solution.py:343
  7.9 8.5 %copy-start.1 = (bf16[1,1,2,128,512]{4,3,2,1,0:T(8,128)(2,1)S(1)}, bf16[1,1,2,128,512]{4,3,2,1,0:T(8,128)(2,1)}, u32[]{:S(2)}) copy-start(bf16[1,1,2,128,512]{4,3,2,1,0:T(8,128)(2,1)} %param.8) | copy-start | bytes 786436
  8.0 35.0 %slice-start.1 = ((bf16[128,2560]{1,0:T(8,128)(2,1)}), bf16[128,1920]{1,0:T(8,128)(2,1)S(1)}, s32[]{:S(2)}) async-start(bf16[128,2560]{1,0:T(8,128)(2,1)} %param.7), calls=%async_computation.7 | async-start | bytes 983040 | tf_op jit(solution)/shard_map/slice | solution.py:346
  9.0 34.1 %all-to-all-start = ((bf16[4,144,640]{2,1,0:T(8,128)(2,1)}), bf16[4,144,640]{2,1,0:T(8,128)(2,1)S(1)}, u32[]{:S(2)}, u32[]{:S(2)}) async-start(bf16[4,144,640]{2,1,0:T(8,128)(2,1)} %pad_maximum_fusion), calls=%async_computation | async-start | bytes 1474560 | tf_op jit(solution)/shard_map/all_to_all | solution.py:320
  14.9 28.2 %collective-permute-start = (bf16[16,2,128,128]{3,2,1,0:T(8,128)(2,1)S(1)}, bf16[16,2,128,128]{3,2,1,0:T(8,128)(2,1)}, u32[]{:S(2)}, u32[]{:S(2)}) collective-permute-start(bf16[16,2,128,128]{3,2,1,0:T(8,128)(2,1)S(1)} %slice.30.refs_1_), channel_id=1, source_target_pairs={{0,2},{1,3},{2,0},{3,1},{4,6},{5,7},{6,4},{7,5},{8,10},{9,11},{10,... | collective-permute-start | bytes 3145736 | tf_op jit(solution)/shard_map/ppermute | solution.py:29
  16.4 19.1 %collective-permute-start.1 = (bf16[1,2,128,512]{3,2,1,0:T(8,128)(2,1)S(1)}, bf16[1,2,128,512]{3,2,1,0:T(8,128)(2,1)S(1)}, u32[]{:S(2)}, u32[]{:S(2)}) collective-permute-start(bf16[1,2,128,512]{3,2,1,0:T(8,128)(2,1)S(1)} %bitcast.25), channel_id=1, source_target_pairs={{0,1},{1,2},{2,3},{3,4},{4,5},{5,6},{6,7},{7,8},{8,9},{9,10},{10,1... | collective-permute-start | bytes 786440 | tf_op jit(solution)/shard_map/ppermute | solution.py:34
  43.0 1.6 copy-start.4
  44.6 49.4 %all-to-all-start.1 = ((bf16[4,128,1920]{2,1,0:T(8,128)(2,1)}), bf16[4,128,1920]{2,1,0:T(8,128)(2,1)S(1)}, u32[]{:S(2)}, u32[]{:S(2)}) async-start(bf16[4,128,1920]{2,1,0:T(8,128)(2,1)} %broadcast_in_dim.32), calls=%async_computation.1 | async-start | bytes 3932160 | tf_op jit(solution)/shard_map/all_to_all | solution.py:320
  49.4 3.0 %collective-permute-start.6 = (bf16[16,2,128,128]{3,2,1,0:T(8,128)(2,1)}, bf16[16,2,128,128]{3,2,1,0:T(8,128)(2,1)}, u32[]{:S(2)}, u32[]{:S(2)}) collective-permute-start(bf16[16,2,128,128]{3,2,1,0:T(8,128)(2,1)} %collective-permute-done.refs_3_), channel_id=1, source_target_pairs={{0,1},{1,0},{2,3},{3,2},{4,5},{5,4},{6,7},{7,6},{8,9},{9,8},{10,11... | collective-permute-start | bytes 3145736 | tf_op jit(solution)/shard_map/ppermute | solution.py:29
  49.4 25.9 %collective-permute-start.5 = (bf16[16,2,128,128]{3,2,1,0:T(8,128)(2,1)}, bf16[16,2,128,128]{3,2,1,0:T(8,128)(2,1)}, u32[]{:S(2)}, u32[]{:S(2)}) collective-permute-start(bf16[16,2,128,128]{3,2,1,0:T(8,128)(2,1)} %get-tuple-element.24.refs_1_), channel_id=1, source_target_pairs={{0,2},{1,3},{2,0},{3,1},{4,6},{5,7},{6,4},{7,5},{8,10},{9,11},{10,... | collective-permute-start | bytes 3145736 | tf_op jit(solution)/shard_map/ppermute | solution.py:29
  52.4 2.2 %copy-start = (bf16[16,2,128,512]{3,2,1,0:T(8,128)(2,1)S(1)}, bf16[16,2,128,512]{3,2,1,0:T(8,128)(2,1)}, u32[]{:S(2)}) copy-start(bf16[16,2,128,512]{3,2,1,0:T(8,128)(2,1)} %refs_6_.1) | copy-start | bytes 12582916
  54.6 1.1 copy-start.5
  70.6 0.9 copy-start.11
  75.3 22.9 %collective-permute-start.7 = (bf16[16,2,128,128]{3,2,1,0:T(8,128)(2,1)}, bf16[16,2,128,128]{3,2,1,0:T(8,128)(2,1)S(1)}, u32[]{:S(2)}, u32[]{:S(2)}) collective-permute-start(bf16[16,2,128,128]{3,2,1,0:T(8,128)(2,1)} %collective-permute-done.5.refs_3_), channel_id=1, source_target_pairs={{0,1},{1,0},{2,3},{3,2},{4,5},{5,4},{6,7},{7,6},{8,9},{9,8},{10,11... | collective-permute-start | bytes 3145736 | tf_op jit(solution)/shard_map/ppermute | solution.py:29
  75.3 42.7 %collective-permute-start.4 = (bf16[16,2,128,128]{3,2,1,0:T(8,128)(2,1)}, bf16[16,2,128,128]{3,2,1,0:T(8,128)(2,1)}, u32[]{:S(2)}, u32[]{:S(2)}) collective-permute-start(bf16[16,2,128,128]{3,2,1,0:T(8,128)(2,1)} %get-tuple-element.22.refs_1_), channel_id=1, source_target_pairs={{0,2},{1,3},{2,0},{3,1},{4,6},{5,7},{6,4},{7,5},{8,10},{9,11},{10,... | collective-permute-start | bytes 3145736 | tf_op jit(solution)/shard_map/ppermute | solution.py:29
  94.0 24.1 %all-to-all-start.5 = ((bf16[4,672,128]{2,1,0:T(8,128)(2,1)}), bf16[4,672,128]{2,1,0:T(8,128)(2,1)}, u32[]{:S(2)}, u32[]{:S(2)}) async-start(bf16[4,672,128]{2,1,0:T(8,128)(2,1)} %copy-done.11), calls=%async_computation.5 | async-start | bytes 1376256 | tf_op jit(solution)/shard_map/all_to_all | solution.py:320
  98.2 1.0 copy-start.9
  99.2 1.2 copy-start.3
  100.5 1.2 copy-start.10
  101.7 16.4 %copy-start.2 = (bf16[16,2,128,128]{3,2,1,0:T(8,128)(2,1)S(1)}, bf16[16,2,128,128]{3,2,1,0:T(8,128)(2,1)}, u32[]{:S(2)}) copy-start(bf16[16,2,128,128]{3,2,1,0:T(8,128)(2,1)} %get-tuple-element.23.refs_1_) | copy-start | bytes 3145732
  117.2 0.9 copy-start.6
  118.1 4.3 %collective-permute-start.8 = (bf16[16,2,128,128]{3,2,1,0:T(8,128)(2,1)}, bf16[16,2,128,128]{3,2,1,0:T(8,128)(2,1)}, u32[]{:S(2)}, u32[]{:S(2)}) collective-permute-start(bf16[16,2,128,128]{3,2,1,0:T(8,128)(2,1)} %collective-permute-done.4.refs_3_), channel_id=1, source_target_pairs={{0,1},{1,0},{2,3},{3,2},{4,5},{5,4},{6,7},{7,6},{8,9},{9,8},{10,11... | collective-permute-start | bytes 3145736 | tf_op jit(solution)/shard_map/ppermute | solution.py:29
  118.1 25.7 %collective-permute-start.3 = (bf16[16,2,128,128]{3,2,1,0:T(8,128)(2,1)S(1)}, bf16[16,2,128,128]{3,2,1,0:T(8,128)(2,1)}, u32[]{:S(2)}, u32[]{:S(2)}) collective-permute-start(bf16[16,2,128,128]{3,2,1,0:T(8,128)(2,1)S(1)} %copy-done.2), channel_id=1, source_target_pairs={{0,2},{1,3},{2,0},{3,1},{4,6},{5,7},{6,4},{7,5},{8,10},{9,11},{10,... | collective-permute-start | bytes 3145736 | tf_op jit(solution)/shard_map/ppermute | solution.py:29
  118.2 25.6 %all-to-all-start.4 = ((bf16[4,672,128]{2,1,0:T(8,128)(2,1)}), bf16[4,672,128]{2,1,0:T(8,128)(2,1)}, u32[]{:S(2)}, u32[]{:S(2)}) async-start(bf16[4,672,128]{2,1,0:T(8,128)(2,1)} %copy-done.6), calls=%async_computation.4 | async-start | bytes 1376256 | tf_op jit(solution)/shard_map/all_to_all | solution.py:320
  135.8 0.9 copy-start.7
  143.7 4.2 %collective-permute-start.9 = (bf16[16,2,128,128]{3,2,1,0:T(8,128)(2,1)}, bf16[16,2,128,128]{3,2,1,0:T(8,128)(2,1)}, u32[]{:S(2)}, u32[]{:S(2)}) collective-permute-start(bf16[16,2,128,128]{3,2,1,0:T(8,128)(2,1)} %collective-permute-done.3.refs_3_), channel_id=1, source_target_pairs={{0,1},{1,0},{2,3},{3,2},{4,5},{5,4},{6,7},{7,6},{8,9},{9,8},{10,11... | collective-permute-start | bytes 3145736 | tf_op jit(solution)/shard_map/ppermute | solution.py:29
  143.7 23.2 %all-to-all-start.3 = ((bf16[4,672,128]{2,1,0:T(8,128)(2,1)}), bf16[4,672,128]{2,1,0:T(8,128)(2,1)}, u32[]{:S(2)}, u32[]{:S(2)}) async-start(bf16[4,672,128]{2,1,0:T(8,128)(2,1)} %copy-done.7), calls=%async_computation.3 | async-start | bytes 1376256 | tf_op jit(solution)/shard_map/all_to_all | solution.py:320
  162.4 0.9 copy-start.8
  167.0 21.7 %all-to-all-start.2 = ((bf16[4,672,128]{2,1,0:T(8,128)(2,1)}), bf16[4,672,128]{2,1,0:T(8,128)(2,1)S(1)}, u32[]{:S(2)}, u32[]{:S(2)}) async-start(bf16[4,672,128]{2,1,0:T(8,128)(2,1)} %copy-done.8), calls=%async_computation.2 | async-start | bytes 1376256 | tf_op jit(solution)/shard_map/all_to_all | solution.py:320
  188.7 0.8 copy-start.12

commit v6 on v5

--- a/solution.py
+++ b/solution.py
@@ -34,26 +34,24 @@
     return lax.ppermute(array, axis, [(i, (i + by) % size) for i in range(size)])
 
 
-def attend_kernel(lines, head, q_head, picks, counts, lasts, mine, store, *refs):
-    q_all, own, twin, side, both, fresh = refs[:6]
-    stores = len(refs) == 20
-    if stores:
-        pool, incoming, out, pool_out = refs[6:10]
-        store_sems = refs[-1]
-        scratch = refs[10:-1]
-    else:
-        out = refs[6]
-        scratch = refs[7:]
-    pages, queries, results, scores, tops, acc, q_sems, page_sems, out_sems = scratch
+def attend_kernel(lines, head, limit, numbers, mine, *refs):
+    q_all, own, twin, side, both, fresh, out = refs[:7]
+    pages, queries, results, scores, tops, acc, q_sems, page_sems, out_sems = refs[7:]
     slots = own.shape[0]
     columns = pl.ds(head * HD, HD)
     extra = pages.shape[1] - 1
 
+    def number(request, place):
+        return numbers[request, mine[0] * (limit + 2) + place]
+
+    def count_of(t):
+        return number(request_of(t), limit)
+
     def request_of(t):
         return lax.rem(mine[0] - t + lines, lines)
 
     def q_copy(t, h):
-        origin = q_all.at[request_of(t), pl.ds(0, PAGE), pl.ds((q_head * GQ + h) * HD, HD)]
+        origin = q_all.at[request_of(t), pl.ds(0, PAGE), pl.ds((head * GQ + h) * HD, HD)]
         return pltpu.make_async_copy(origin, queries.at[t, h], q_sems.at[t, h])
 
     def out_copy(t):
@@ -70,9 +68,9 @@
         request = request_of(t)
         buffer = lax.rem(t, 2)
 
-        @pl.loop(0, counts[request])
+        @pl.loop(0, count_of(t))
         def _(place):
-            code = picks[request, place]
+            code = number(request, place)
             rank = lax.div(code, slots)
             slot = lax.rem(code, slots)
             for index, source in enumerate((own, twin, side, both)):
@@ -83,12 +81,9 @@
     def arrive(t):
         buffer = lax.rem(t, 2)
 
-        @pl.loop(0, counts[request_of(t)])
+        @pl.loop(0, count_of(t))
         def _(place):
             page_copy(own, 0, buffer, place).wait()
-
-    def store_copy(slot):
-        return pltpu.make_async_copy(pool.at[slot], pool_out.at[slot], store_sems.at[slot])
 
     fresh_copy = pltpu.make_async_copy(fresh.at[:, :, columns], pages.at[0, extra], page_sems.at[0, extra])
     for t in range(lines):
@@ -100,15 +95,6 @@
     fetch(0)
     if lines > 1:
         fetch(1)
-    if stores:
-        @pl.loop(0, pool.shape[0])
-        def _(slot):
-            @pl.when(slot != store[0])
-            def _():
-                store_copy(slot).start()
-
-        pltpu.make_async_copy(incoming.at[0], pool_out.at[store[0]], store_sems.at[store[0]]).start()
-
     def soften(heads, scored, values):
         factor = SCALE * LOG2E
         expos = []
@@ -141,14 +127,14 @@
         return with_ones(pages[lax.rem(t, 2), pl.ds(index * BLOCK, BLOCK), 1].reshape(BLOCK * PAGE, HD))
 
     def blocks_of(t):
-        return jnp.maximum(lax.div(counts[request_of(t)] + BLOCK - 1, BLOCK), 1)
+        return jnp.maximum(lax.div(count_of(t) + BLOCK - 1, BLOCK), 1)
 
     def reset():
         tops[...] = jnp.full(tops.shape, LOW, jnp.float32)
         acc[...] = jnp.zeros(acc.shape, jnp.float32)
 
     def finish(t):
-        some = (counts[request_of(t)] > 0) | (t == 0)
+        some = (count_of(t) > 0) | (t == 0)
         lane = lax.broadcasted_iota(jnp.int32, (PAGE, PAGE), 1)
         sums = jnp.ones((PAGE, PAGE), jnp.float32)
         heights = jnp.zeros((PAGE, PAGE), jnp.float32)
@@ -193,12 +179,12 @@
         def _():
             arrive(t + 1)
 
-        limit = (counts[request] - 1 - index * BLOCK) * PAGE + lasts[request]
+        seen_here = (count_of(t) - 1 - index * BLOCK) * PAGE + number(request, limit + 1)
         column = lax.broadcasted_iota(jnp.int32, (PAGE, BLOCK * PAGE), 1)
         values = values_of(t, index)
         keys = keys_of(ahead_t, later_index)
         for heads in HEADS:
-            soften(heads, lambda h: jnp.where(column < limit, scores[h], LOW), values)
+            soften(heads, lambda h: jnp.where(column < seen_here, scores[h], LOW), values)
             scores[heads[0]:heads[-1] + 1] = score(ahead_t, heads, keys)
 
         @pl.when(ends)
@@ -218,47 +204,71 @@
     lax.fori_loop(0, steps, step, (jnp.int32(0), jnp.int32(0)))
     for t in range(lines):
         out_copy(t).wait()
-    if stores:
-        @pl.loop(0, pool.shape[0])
-        def _(slot):
-            store_copy(slot).wait()
-
-
-def attend(head, q_head, tables, q_all, pools, fresh, pool=None, incoming=None):
-    picks, counts, lasts, mine, store = tables
+
+
+def attend(head, limit, numbers, mine, q_all, pools, fresh):
     lines = q_all.shape[0]
-    places = picks.shape[1]
-    out_shape = [jax.ShapeDtypeStruct((lines, ROWS, HD), jnp.bfloat16)]
-    scratch = [
-        pltpu.VMEM((2, places + 1, 2, PAGE, HD), jnp.bfloat16),
-        pltpu.VMEM((lines, GQ, PAGE, HD), jnp.bfloat16),
-        pltpu.VMEM((lines, ROWS, HD), jnp.bfloat16),
-        pltpu.VMEM((GQ, PAGE, BLOCK * PAGE), jnp.float32),
-        pltpu.VMEM((GQ, PAGE, PAGE), jnp.float32),
-        pltpu.VMEM((GQ, PAGE, 2 * HD), jnp.float32),
-        pltpu.SemaphoreType.DMA((lines, GQ)),
-        pltpu.SemaphoreType.DMA((2, places + 1)),
-        pltpu.SemaphoreType.DMA((lines,)),
-    ]
     operands = [q_all, *pools, fresh]
-    if incoming is not None:
-        operands += [pool, incoming]
-        out_shape.append(jax.ShapeDtypeStruct(pool.shape, pool.dtype))
-        scratch.append(pltpu.SemaphoreType.DMA((pool.shape[0],)))
     grid_spec = pltpu.PrefetchScalarGridSpec(
-        num_scalar_prefetch=5,
+        num_scalar_prefetch=2,
         grid=(),
         in_specs=[pl.BlockSpec(memory_space=pl.ANY)] * len(operands),
-        out_specs=[pl.BlockSpec(memory_space=pl.ANY), pl.BlockSpec(memory_space=pltpu.HBM)][:len(out_shape)],
-        scratch_shapes=scratch,
+        out_specs=pl.BlockSpec(memory_space=pltpu.HBM),
+        scratch_shapes=[
+            pltpu.VMEM((2, limit + 1, 2, PAGE, HD), jnp.bfloat16),
+            pltpu.VMEM((lines, GQ, PAGE, HD), jnp.bfloat16),
+            pltpu.VMEM((lines, ROWS, HD), jnp.bfloat16),
+            pltpu.VMEM((GQ, PAGE, BLOCK * PAGE), jnp.float32),
+            pltpu.VMEM((GQ, PAGE, PAGE), jnp.float32),
+            pltpu.VMEM((GQ, PAGE, 2 * HD), jnp.float32),
+            pltpu.SemaphoreType.DMA((lines, GQ)),
+            pltpu.SemaphoreType.DMA((2, limit + 1)),
+            pltpu.SemaphoreType.DMA((lines,)),
+        ],
     )
     return pl.pallas_call(
-        functools.partial(attend_kernel, lines, head, q_head),
+        functools.partial(attend_kernel, lines, head, limit),
         grid_spec=grid_spec,
-        out_shape=out_shape,
-        compiler_params=pltpu.CompilerParams(vmem_limit_bytes=24 * 2**20),
+        out_shape=jax.ShapeDtypeStruct((lines, ROWS, HD), jnp.bfloat16),
+        compiler_params=pltpu.CompilerParams(vmem_limit_bytes=16 * 2**20),
         cost_estimate=pl.CostEstimate(flops=1, bytes_accessed=1, transcendentals=0),
-    )(picks, counts, lasts, mine, store, *operands)
+    )(numbers, mine, *operands)
+
+
+def store_kernel(slot, pool, incoming, out, sems):
+    pages = pool.shape[0]
+
+    def copy(page):
+        return pltpu.make_async_copy(pool.at[page], out.at[page], sems.at[page])
+
+    for page in range(pages):
+        @pl.when(slot[0] != page)
+        def _():
+            copy(page).start()
+
+        @pl.when(slot[0] == page)
+        def _():
+            pltpu.make_async_copy(incoming.at[0], out.at[page], sems.at[page]).start()
+
+    for page in range(pages):
+        copy(page).wait()
+
+
+def store(slot, pool, incoming):
+    grid_spec = pltpu.PrefetchScalarGridSpec(
+        num_scalar_prefetch=1,
+        grid=(),
+        in_specs=[pl.BlockSpec(memory_space=pl.ANY)] * 2,
+        out_specs=pl.BlockSpec(memory_space=pltpu.HBM),
+        scratch_shapes=[pltpu.SemaphoreType.DMA((pool.shape[0],))],
+    )
+    return pl.pallas_call(
+        store_kernel,
+        grid_spec=grid_spec,
+        out_shape=jax.ShapeDtypeStruct(pool.shape, pool.dtype),
+        compiler_params=pltpu.CompilerParams(vmem_limit_bytes=16 * 2**20),
+        cost_estimate=pl.CostEstimate(flops=1, bytes_accessed=1, transcendentals=0),
+    )(slot, pool, incoming)
 
 
 def merge_kernel(head, parts, *refs):
@@ -338,27 +348,21 @@
     sides = [swapped(own, "serve", 2) for own in owns]
     twin = swapped(rest, "serve", 1)
     incoming = shifted(new_kv[0], "serve", 1)
-    rows = page_rows(me, lines, limit, slots, page_owner, page_slot, prefix_len).astype(queries.dtype)
-    rows = jnp.pad(rows[:, None], ((0, 0), (0, 15), (0, CHUNK - limit - 2)))
-    early = after(queries, owns[1])[:, :CHUNK]
-    early = jnp.concatenate([jnp.broadcast_to(early[None], (lines, PAGE, CHUNK)), rows], axis=1)
-    early = exchanged(early, groups)
-    later = after(queries, sides[0], incoming)[None, :, CHUNK:]
-    later = exchanged(jnp.broadcast_to(later, (lines, PAGE, (KVH - 1) * CHUNK)), groups)
-    numbers = early[:, PAGE, :limit + 2].astype(jnp.int32)
-    tables = (numbers[:, :limit], numbers[:, limit], numbers[:, limit + 1], (me // CLUSTER)[None], store_slot[0])
+    numbers = page_rows(me, lines, limit, slots, page_owner, page_slot, prefix_len).astype(queries.dtype)
+    numbers = jnp.pad(numbers.reshape(1, -1), ((0, PAGE - 1), (0, PAGE - lines * (limit + 2))))
+    sent = jnp.concatenate([after(queries, owns[1]), numbers], axis=1)
+    q_all = lax.all_gather(sent, "serve", axis_index_groups=groups)
+    numbers = q_all[:, 0, KVH * CHUNK:].astype(jnp.int32)
+    mine = (me // CLUSTER)[None]
     fresh = new_kv[0, 0]
     attended = None
     parts = None
     for g in range(KVH):
         side = sides[g] if g == 0 else after(sides[g], parts)
         both = swapped(side, "serve", 1)
-        pools = (owns[g], twin, side, both)
-        if g == 0:
-            parts, pool_out = attend(g, 0, tables, early, pools, fresh, pool, incoming)
-        else:
-            parts = attend(g, g - 1, tables, later, pools, fresh)[0]
+        parts = attend(g, limit, numbers, mine, q_all, (owns[g], twin, side, both), fresh)
         attended = merge(g, exchanged(parts, groups), attended)
+    pool_out = store(store_slot[0], pool, after(incoming, parts))
     return (attended, pool_out)
 
 

time: 192 us -> 213 us (1.11)
  waiting for transfers between devices: 69.7 us -> 87.9 us
  between operations: 2.3 us -> 15.6 us
  Pallas kernels: 67.6 us -> 59.9 us
  starting transfers between devices: 31.7 us -> 25.7 us
    all_gather x0 -> x1, waiting for transfers between devices: none -> 30.2 us  [per_device(): q_all = lax.all_gather(sent, 'serve', axis_index_groups=groups)]
    all_to_all x6 -> x4, waiting for transfers between devices: 32.1 us -> 6.78 us  [exchanged(): lax.all_to_all(array, 'serve', 0, 0, axis_index_groups=groups, tiled=True)]
    ppermute x9, waiting for transfers between devices: 18.4 us -> 39.2 us  [swapped(): return lax.ppermute(array, axis, [(i, i ^ bit) for i in range(size)])]
    all_to_all x6 -> x4, starting transfers between devices: 26.7 us -> 16 us  [exchanged(): lax.all_to_all(array, 'serve', 0, 0, axis_index_groups=groups, tiled=True)]
    pallas_call x4 -> x5, Pallas kernels: 58.2 us -> 50.5 us  [the longest x4 48.4 us: attend(): pl.pallas_call(functools.partial(attend_kernel, lines, head, limit), grid...]
    ppermute x1, waiting for transfers between devices: 19.1 us -> 11.7 us  [shifted(): lax.ppermute(array, axis, [(i, (i + by) % size) for i in range(size)])]
    ppermute x9, starting transfers between devices: 4.96 us -> 9.6 us  [swapped(): return lax.ppermute(array, axis, [(i, i ^ bit) for i in range(size)])]
    unnamed x30 -> x32, local copies, waits for them, and re-layouts: 11.1 us -> 13.9 us
  transfers between devices with their start and end apart: 16 -> 15, of which waited for: 7 -> 6; matrix products, arithmetic and copies ran while one was open for 4% -> 0% of each run, Pallas kernels for 34% -> 27%
where the time goes in v6:
time: 213 us; the launch traced here: 212 us
  waiting for transfers between devices  87.9 us (41%)
  Pallas kernels  59.9 us (28%)
  starting transfers between devices  25.7 us (12%)
  local copies, waits for them, and re-layouts  19.7 us (9%)
  between operations  15.6 us (7%)
  other arithmetic  3.63 us (2%)
    pallas_call x4, Pallas kernels, attend(): pl.pallas_call(functools.partial(attend_kernel, lines, head, limit), grid...  48.4 us
    ppermute x9, waiting for transfers between devices, swapped(): return lax.ppermute(array, axis, [(i, i ^ bit) for i in range(size)])  39.2 us
    all_gather x1, waiting for transfers between devices, per_device(): q_all = lax.all_gather(sent, 'serve', axis_index_groups=groups)  30.2 us
    all_to_all x4, starting transfers between devices, exchanged(): lax.all_to_all(array, 'serve', 0, 0, axis_index_groups=groups, tiled=True)  16 us
    unnamed x32, local copies, waits for them, and re-layouts  13.9 us
    ppermute x1, waiting for transfers between devices, shifted(): lax.ppermute(array, axis, [(i, (i + by) % size) for i in range(size)])  11.7 us
    ppermute x9, starting transfers between devices, swapped(): return lax.ppermute(array, axis, [(i, i ^ bit) for i in range(size)])  9.6 us
    pallas_call x4, Pallas kernels, merge(): pl.pallas_call(functools.partial(merge_kernel, head), in_specs=[pl.BlockS...  9.41 us
  transfers between devices with their start and end apart: 15, of which 6 were waited for; matrix products, arithmetic and copies ran while one was open for 0% of the time, Pallas kernels for 27%

profile of v6, /device:TPU:0, one launch (start us, length us, event | category | flops | bytes accessed | tf_op | source)
XLA Modules:
  0.0 212.4 jit_solution(11844938456438248974)
XLA Ops:
  7.9 0.7 fusion.8
  8.6 0.7 fusion.6
  9.3 0.1 convert_reduce_fusion.1
  9.4 0.1 convert_reduce_fusion
  9.5 0.1 select_reduce_fusion
  9.7 0.1 and_reduce_fusion
  10.0 0.1 copy.14
  10.2 1.3 slice.15.refs_1_
  11.6 4.1 %fusion.10 = (bf16[16,2,128,128]{3,2,1,0:T(8,128)(2,1)}, bf16[16,2,128,128]{3,2,1,0:T(8,128)(2,1)}, bf16[16,2,128,128]{3,2,1,0:T(8,128)(2,1)}) fusion(bf16[16,2,128,512]{3,2,1,0:T(8,128)(2,1)} %pool.1), kind=kLoop, calls=%fused_computation.30 | loop fusion | bytes 6291456 | tf_op jit(solution)/shard_map/slice | solution.py:347
  15.7 0.9 fusion.1
  16.7 0.5 collective-permute-start
  17.2 2.6 %collective-permute-start.4 = (bf16[16,2,128,128]{3,2,1,0:T(8,128)(2,1)S(1)}, bf16[16,2,128,128]{3,2,1,0:T(8,128)(2,1)S(1)}, u32[]{:S(2)}, u32[]{:S(2)}) collective-permute-start(bf16[16,2,128,128]{3,2,1,0:T(8,128)(2,1)S(1)} %slice.15.refs_1_), channel_id=1, source_target_pairs={{0,2},{1,3},{2,0},{3,1},{4,6},{5,7},{6,4},{7,5},{8,10},{9,11},{10,... | collective-permute-start | bytes 3145736 | tf_op jit(solution)/shard_map/ppermute | solution.py:29
  19.8 23.7 %collective-permute-done.4.refs_3_ = bf16[16,2,128,128]{3,2,1,0:T(8,128)(2,1)S(1)} collective-permute-done((bf16[16,2,128,128]{3,2,1,0:T(8,128)(2,1)S(1)}, bf16[16,2,128,128]{3,2,1,0:T(8,128)(2,1)S(1)}, u32[]{:S(2)}, u32[]{:S(2)}) %collective-permute-start.4) | collective-permute-done | bytes 1048608 | tf_op jit(solution)/shard_map/ppermute | solution.py:29
  43.5 1.0 copy-done.10
  44.5 1.8 collective-permute-start.3
  46.3 30.2 %all-gather.3.cloned.1.call-done = bf16[512,2688]{1,0:T(8,128)(2,1)} async-done(((bf16[128,2688]{1,0:T(8,128)(2,1)}), bf16[512,2688]{1,0:T(8,128)(2,1)}) %all-gather.3.cloned.1.call-update) | async-done | bytes 2752528 | tf_op jit(solution)/shard_map/all_gather | solution.py:354
  76.5 0.7 slice_convert_fusion
  77.2 1.0 copy-done.12
  78.3 1.8 copy-done
  80.0 1.2 copy-done.5
  81.3 1.2 copy-done.11
  82.5 1.2 copy-done.13
  83.7 14.3 %shard_map.86 = bf16[4,672,128]{2,1,0:T(8,128)(2,1)S(1)} custom-call(s32[4,128]{1,0:T(4,128)S(1)} %bitcast.30, s32[1]{0:T(128)} %bitcast.8.mine, bf16[4,128,2688]{2,1,0:T(8,128)(2,1)S(1)} %bitcast.21, bf16[16,2,128,128]{3,2,1,0:T(8,128)(2,1)S(1)} %copy-done.5, bf16[16,2,128,512]{3,2,1,0:T(8,128)(2,1)} %collective-permute-done.refs_2_, ...), custom_call_target="tpu_custom_call" | custom-call | flops 1 | bytes 1 | tf_op jit(solution)/shard_map/pallas_call | solution.py:229
  98.0 0.8 copy-done.7
  98.9 0.1 collective-permute-start.6
  99.0 2.8 %collective-permute-start.2 = (bf16[16,2,128,128]{3,2,1,0:T(8,128)(2,1)}, bf16[16,2,128,128]{3,2,1,0:T(8,128)(2,1)}, u32[]{:S(2)}, u32[]{:S(2)}) collective-permute-start(bf16[16,2,128,128]{3,2,1,0:T(8,128)(2,1)} %get-tuple-element.16.refs_1_), channel_id=1, source_target_pairs={{0,2},{1,3},{2,0},{3,1},{4,6},{5,7},{6,4},{7,5},{8,10},{9,11},{10,... | collective-permute-start | bytes 3145736 | tf_op jit(solution)/shard_map/ppermute | solution.py:29
  101.8 4.2 %all-to-all-start.3 = ((bf16[4,672,128]{2,1,0:T(8,128)(2,1)}), bf16[4,672,128]{2,1,0:T(8,128)(2,1)}, u32[]{:S(2)}, u32[]{:S(2)}) async-start(bf16[4,672,128]{2,1,0:T(8,128)(2,1)} %copy-done.7), calls=%async_computation.3 | async-start | bytes 1376256 | tf_op jit(solution)/shard_map/all_to_all | solution.py:330
  106.0 11.4 %shard_map.87 = bf16[4,672,128]{2,1,0:T(8,128)(2,1)S(1)} custom-call(s32[4,128]{1,0:T(4,128)S(1)} %bitcast.31, s32[1]{0:T(128)} %bitcast.8.mine, bf16[4,128,2688]{2,1,0:T(8,128)(2,1)S(1)} %bitcast.22, bf16[16,2,128,128]{3,2,1,0:T(8,128)(2,1)} %get-tuple-element.18.refs_1_, bf16[16,2,128,512]{3,2,1,0:T(8,128)(2,1)} %collective-permute-done.refs_2_, ...), custom_call_target="tpu_custom_call" | custom-call | flops 1 | bytes 1 | tf_op jit(solution)/shard_map/pallas_call | solution.py:229
  117.4 0.8 copy-done.6
  118.2 7.7 %collective-permute-done.2.refs_3_ = bf16[16,2,128,128]{3,2,1,0:T(8,128)(2,1)} collective-permute-done((bf16[16,2,128,128]{3,2,1,0:T(8,128)(2,1)}, bf16[16,2,128,128]{3,2,1,0:T(8,128)(2,1)}, u32[]{:S(2)}, u32[]{:S(2)}) %collective-permute-start.2) | collective-permute-done | bytes 1048608 | tf_op jit(solution)/shard_map/ppermute | solution.py:29
  126.0 1.7 collective-permute-start.1
  127.7 4.2 %all-to-all-start.2 = ((bf16[4,672,128]{2,1,0:T(8,128)(2,1)}), bf16[4,672,128]{2,1,0:T(8,128)(2,1)}, u32[]{:S(2)}, u32[]{:S(2)}) async-start(bf16[4,672,128]{2,1,0:T(8,128)(2,1)} %copy-done.6), calls=%async_computation.2 | async-start | bytes 1376256 | tf_op jit(solution)/shard_map/all_to_all | solution.py:330
  131.9 11.4 %shard_map.88 = bf16[4,672,128]{2,1,0:T(8,128)(2,1)S(1)} custom-call(s32[4,128]{1,0:T(4,128)S(1)} %bitcast.32, s32[1]{0:T(128)} %bitcast.8.mine, bf16[4,128,2688]{2,1,0:T(8,128)(2,1)S(1)} %bitcast.23, bf16[16,2,128,128]{3,2,1,0:T(8,128)(2,1)} %get-tuple-element.16.refs_1_, bf16[16,2,128,512]{3,2,1,0:T(8,128)(2,1)} %collective-permute-done.refs_2_, ...), custom_call_target="tpu_custom_call" | custom-call | flops 1 | bytes 1 | tf_op jit(solution)/shard_map/pallas_call | solution.py:229
  143.3 0.8 copy-done.9
  144.1 7.7 %collective-permute-done.1.refs_3_ = bf16[16,2,128,128]{3,2,1,0:T(8,128)(2,1)} collective-permute-done((bf16[16,2,128,128]{3,2,1,0:T(8,128)(2,1)}, bf16[16,2,128,128]{3,2,1,0:T(8,128)(2,1)}, u32[]{:S(2)}, u32[]{:S(2)}) %collective-permute-start.1) | collective-permute-done | bytes 1048608 | tf_op jit(solution)/shard_map/ppermute | solution.py:29
  151.9 4.2 %all-to-all-start.1 = ((bf16[4,672,128]{2,1,0:T(8,128)(2,1)}), bf16[4,672,128]{2,1,0:T(8,128)(2,1)}, u32[]{:S(2)}, u32[]{:S(2)}) async-start(bf16[4,672,128]{2,1,0:T(8,128)(2,1)} %copy-done.9), calls=%async_computation.1 | async-start | bytes 1376256 | tf_op jit(solution)/shard_map/all_to_all | solution.py:330
  156.1 11.4 %shard_map.89 = bf16[4,672,128]{2,1,0:T(8,128)(2,1)S(1)} custom-call(s32[4,128]{1,0:T(4,128)S(1)} %bitcast.33, s32[1]{0:T(128)} %bitcast.8.mine, bf16[4,128,2688]{2,1,0:T(8,128)(2,1)S(1)} %bitcast.24, bf16[16,2,128,128]{3,2,1,0:T(8,128)(2,1)} %get-tuple-element.17.refs_1_, bf16[16,2,128,512]{3,2,1,0:T(8,128)(2,1)} %collective-permute-done.refs_2_, ...), custom_call_target="tpu_custom_call" | custom-call | flops 1 | bytes 1 | tf_op jit(solution)/shard_map/pallas_call | solution.py:229
  167.4 0.9 copy-done.8
  168.3 6.8 %all-to-all-done.1.parts = bf16[4,672,128]{2,1,0:T(8,128)(2,1)} async-done(((bf16[4,672,128]{2,1,0:T(8,128)(2,1)}), bf16[4,672,128]{2,1,0:T(8,128)(2,1)}, u32[]{:S(2)}, u32[]{:S(2)}) %all-to-all-start.1) | async-done | bytes 688160 | tf_op jit(solution)/shard_map/all_to_all | solution.py:330
  175.1 3.5 %all-to-all-start = ((bf16[4,672,128]{2,1,0:T(8,128)(2,1)}), bf16[4,672,128]{2,1,0:T(8,128)(2,1)S(1)}, u32[]{:S(2)}, u32[]{:S(2)}) async-start(bf16[4,672,128]{2,1,0:T(8,128)(2,1)} %copy-done.8), calls=%async_computation | async-start | bytes 1376256 | tf_op jit(solution)/shard_map/all_to_all | solution.py:330
  178.6 2.4 %shard_map.90.refs_0_ = bf16[128,2560]{1,0:T(8,128)(2,1)} custom-call(bf16[4,672,128]{2,1,0:T(8,128)(2,1)} %all-to-all-done.3.parts), custom_call_target="tpu_custom_call" | custom-call | flops 1 | bytes 1 | tf_op jit(solution)/shard_map/pallas_call | solution.py:302
  181.0 2.4 %shard_map.91.refs_0_ = bf16[128,2560]{1,0:T(8,128)(2,1)} custom-call(bf16[4,672,128]{2,1,0:T(8,128)(2,1)} %all-to-all-done.2.parts, bf16[128,2560]{1,0:T(8,128)(2,1)} %shard_map.90.refs_0_), custom_call_target="tpu_custom_call", output_to_operand_aliasing={{}: (1, {})} | custom-call | flops 1 | bytes 1 | tf_op jit(solution)/shard_map/pallas_call | solution.py:302
  184.0 2.4 %shard_map.92.refs_0_ = bf16[128,2560]{1,0:T(8,128)(2,1)} custom-call(bf16[4,672,128]{2,1,0:T(8,128)(2,1)} %all-to-all-done.1.parts, bf16[128,2560]{1,0:T(8,128)(2,1)} %shard_map.91.refs_0_), custom_call_target="tpu_custom_call", output_to_operand_aliasing={{}: (1, {})} | custom-call | flops 1 | bytes 1 | tf_op jit(solution)/shard_map/pallas_call | solution.py:302
  186.4 11.7 %collective-permute-done.9.incoming = bf16[1,2,128,512]{3,2,1,0:T(8,128)(2,1)S(1)} collective-permute-done((bf16[1,2,128,512]{3,2,1,0:T(8,128)(2,1)S(1)}, bf16[1,2,128,512]{3,2,1,0:T(8,128)(2,1)S(1)}, u32[]{:S(2)}, u32[]{:S(2)}) %collective-permute-start.9) | collective-permute-done | bytes 262176 | tf_op jit(solution)/shard_map/ppermute | solution.py:34
  198.0 2.2 %copy-done.2 = bf16[16,2,128,512]{3,2,1,0:T(8,128)(2,1)S(1)} copy-done((bf16[16,2,128,512]{3,2,1,0:T(8,128)(2,1)S(1)}, bf16[16,2,128,512]{3,2,1,0:T(8,128)(2,1)}, u32[]{:S(2)}) %copy-start.2) | copy-done | bytes 4194328
  200.2 2.1 %shard_map.94 = bf16[16,2,128,512]{3,2,1,0:T(8,128)(2,1)} custom-call(s32[1]{0:T(128)} %bitcast.19.slot, bf16[16,2,128,512]{3,2,1,0:T(8,128)(2,1)S(1)} %copy-done.2, bf16[1,2,128,512]{3,2,1,0:T(8,128)(2,1)S(1)} %collective-permute-done.9.incoming), custom_call_target="tpu_custom_call" | custom-call | flops 1 | bytes 1 | tf_op jit(solution)/shard_map/pallas_call | solution.py:265
  202.4 0.8 copy-done.14
  203.2 2.4 %shard_map.93 = bf16[128,2560]{1,0:T(8,128)(2,1)} custom-call(bf16[4,672,128]{2,1,0:T(8,128)(2,1)} %copy-done.14, bf16[128,2560]{1,0:T(8,128)(2,1)} %shard_map.92.refs_0_), custom_call_target="tpu_custom_call", output_to_operand_aliasing={{}: (1, {})} | custom-call | flops 1 | bytes 1 | tf_op jit(solution)/shard_map/pallas_call | solution.py:302
  (44 shorter events, 0.5 us)
Async XLA Ops:
  7.2 69.3 %all-gather.3.cloned.1.call-start = ((), (), s32[]{:S(2)}) async-start(), calls=%async_computation.4 | async-start | bytes 3440640 | tf_op jit(solution)/shard_map/all_gather | solution.py:354
  11.5 5.6 %copy-start.4 = (bf16[16,2,128,128]{3,2,1,0:T(8,128)(2,1)}, bf16[16,2,128,128]{3,2,1,0:T(8,128)(2,1)S(1)}, u32[]{:S(2)}) copy-start(bf16[16,2,128,128]{3,2,1,0:T(8,128)(2,1)S(1)} %slice.15.refs_1_) | copy-start | bytes 3145732
  11.6 4.2 %copy-start.15 = (bf16[128,2560]{1,0:T(8,128)(2,1)S(1)}, bf16[128,2560]{1,0:T(8,128)(2,1)}, u32[]{:S(2)}) copy-start(bf16[128,2560]{1,0:T(8,128)(2,1)} %param.7) | copy-start | bytes 1966084
  11.6 66.7 %copy-start.3 = (bf16[1,1,2,128,512]{4,3,2,1,0:T(8,128)(2,1)S(1)}, bf16[1,1,2,128,512]{4,3,2,1,0:T(8,128)(2,1)}, u32[]{:S(2)}) copy-start(bf16[1,1,2,128,512]{4,3,2,1,0:T(8,128)(2,1)} %param.8) | copy-start | bytes 786436
  16.7 61.6 %collective-permute-start = (bf16[16,2,128,512]{3,2,1,0:T(8,128)(2,1)}, bf16[16,2,128,512]{3,2,1,0:T(8,128)(2,1)}, u32[]{:S(2)}, u32[]{:S(2)}) collective-permute-start(bf16[16,2,128,512]{3,2,1,0:T(8,128)(2,1)} %pool.1), channel_id=1, source_target_pairs={{0,1},{1,0},{2,3},{3,2},{4,5},{5,4},{6,7},{7,6},{8,9},{9,8},{10,11... | collective-permute-start | bytes 12582920 | tf_op jit(solution)/shard_map/ppermute | solution.py:29
  17.2 26.3 %collective-permute-start.4 = (bf16[16,2,128,128]{3,2,1,0:T(8,128)(2,1)S(1)}, bf16[16,2,128,128]{3,2,1,0:T(8,128)(2,1)S(1)}, u32[]{:S(2)}, u32[]{:S(2)}) collective-permute-start(bf16[16,2,128,128]{3,2,1,0:T(8,128)(2,1)S(1)} %slice.15.refs_1_), channel_id=1, source_target_pairs={{0,2},{1,3},{2,0},{3,1},{4,6},{5,7},{6,4},{7,5},{8,10},{9,11},{10,... | collective-permute-start | bytes 3145736 | tf_op jit(solution)/shard_map/ppermute | solution.py:29
  43.5 33.7 %collective-permute-start.5 = (bf16[16,2,128,128]{3,2,1,0:T(8,128)(2,1)S(1)}, bf16[16,2,128,128]{3,2,1,0:T(8,128)(2,1)S(1)}, u32[]{:S(2)}, u32[]{:S(2)}) collective-permute-start(bf16[16,2,128,128]{3,2,1,0:T(8,128)(2,1)S(1)} %collective-permute-done.4.refs_3_), channel_id=1, source_target_pairs={{0,1},{1,0},{2,3},{3,2},{4,5},{5,4},{6,7},{7,6},{8,9},{9,8},{10,11... | collective-permute-start | bytes 3145736 | tf_op jit(solution)/shard_map/ppermute | solution.py:29
  43.5 1.0 copy-start.10
  44.5 54.3 %collective-permute-start.3 = (bf16[16,2,128,128]{3,2,1,0:T(8,128)(2,1)}, bf16[16,2,128,128]{3,2,1,0:T(8,128)(2,1)}, u32[]{:S(2)}, u32[]{:S(2)}) collective-permute-start(bf16[16,2,128,128]{3,2,1,0:T(8,128)(2,1)} %get-tuple-element.18.refs_1_), channel_id=1, source_target_pairs={{0,2},{1,3},{2,0},{3,1},{4,6},{5,7},{6,4},{7,5},{8,10},{9,11},{10,... | collective-permute-start | bytes 3145736 | tf_op jit(solution)/shard_map/ppermute | solution.py:29
  77.2 1.0 copy-start.12
  78.3 1.8 copy-start
  80.0 1.2 copy-start.5
  81.3 1.2 copy-start.11
  82.5 1.2 copy-start.13
  83.7 22.3 %copy-start.1 = (bf16[512,2688]{1,0:T(8,128)(2,1)S(1)}, bf16[512,2688]{1,0:T(8,128)(2,1)}, u32[]{:S(2)}) copy-start(bf16[512,2688]{1,0:T(8,128)(2,1)} %all-gather.3.cloned.1.call-done) | copy-start | bytes 8257540
  98.0 0.9 copy-start.7
  98.9 7.1 %collective-permute-start.6 = (bf16[16,2,128,128]{3,2,1,0:T(8,128)(2,1)}, bf16[16,2,128,128]{3,2,1,0:T(8,128)(2,1)}, u32[]{:S(2)}, u32[]{:S(2)}) collective-permute-start(bf16[16,2,128,128]{3,2,1,0:T(8,128)(2,1)} %collective-permute-done.3.refs_3_), channel_id=1, source_target_pairs={{0,1},{1,0},{2,3},{3,2},{4,5},{5,4},{6,7},{7,6},{8,9},{9,8},{10,11... | collective-permute-start | bytes 3145736 | tf_op jit(solution)/shard_map/ppermute | solution.py:29
  99.0 27.0 %collective-permute-start.2 = (bf16[16,2,128,128]{3,2,1,0:T(8,128)(2,1)}, bf16[16,2,128,128]{3,2,1,0:T(8,128)(2,1)}, u32[]{:S(2)}, u32[]{:S(2)}) collective-permute-start(bf16[16,2,128,128]{3,2,1,0:T(8,128)(2,1)} %get-tuple-element.16.refs_1_), channel_id=1, source_target_pairs={{0,2},{1,3},{2,0},{3,1},{4,6},{5,7},{6,4},{7,5},{8,10},{9,11},{10,... | collective-permute-start | bytes 3145736 | tf_op jit(solution)/shard_map/ppermute | solution.py:29
  101.8 25.9 %all-to-all-start.3 = ((bf16[4,672,128]{2,1,0:T(8,128)(2,1)}), bf16[4,672,128]{2,1,0:T(8,128)(2,1)}, u32[]{:S(2)}, u32[]{:S(2)}) async-start(bf16[4,672,128]{2,1,0:T(8,128)(2,1)} %copy-done.7), calls=%async_computation.3 | async-start | bytes 1376256 | tf_op jit(solution)/shard_map/all_to_all | solution.py:330
  117.4 0.9 copy-start.6
  126.0 5.9 %collective-permute-start.7 = (bf16[16,2,128,128]{3,2,1,0:T(8,128)(2,1)}, bf16[16,2,128,128]{3,2,1,0:T(8,128)(2,1)}, u32[]{:S(2)}, u32[]{:S(2)}) collective-permute-start(bf16[16,2,128,128]{3,2,1,0:T(8,128)(2,1)} %collective-permute-done.2.refs_3_), channel_id=1, source_target_pairs={{0,1},{1,0},{2,3},{3,2},{4,5},{5,4},{6,7},{7,6},{8,9},{9,8},{10,11... | collective-permute-start | bytes 3145736 | tf_op jit(solution)/shard_map/ppermute | solution.py:29
  126.0 25.9 %collective-permute-start.1 = (bf16[16,2,128,128]{3,2,1,0:T(8,128)(2,1)}, bf16[16,2,128,128]{3,2,1,0:T(8,128)(2,1)}, u32[]{:S(2)}, u32[]{:S(2)}) collective-permute-start(bf16[16,2,128,128]{3,2,1,0:T(8,128)(2,1)} %get-tuple-element.17.refs_1_), channel_id=1, source_target_pairs={{0,2},{1,3},{2,0},{3,1},{4,6},{5,7},{6,4},{7,5},{8,10},{9,11},{10,... | collective-permute-start | bytes 3145736 | tf_op jit(solution)/shard_map/ppermute | solution.py:29
  127.7 24.1 %all-to-all-start.2 = ((bf16[4,672,128]{2,1,0:T(8,128)(2,1)}), bf16[4,672,128]{2,1,0:T(8,128)(2,1)}, u32[]{:S(2)}, u32[]{:S(2)}) async-start(bf16[4,672,128]{2,1,0:T(8,128)(2,1)} %copy-done.6), calls=%async_computation.2 | async-start | bytes 1376256 | tf_op jit(solution)/shard_map/all_to_all | solution.py:330
  143.3 0.8 copy-start.9
  151.9 4.2 %collective-permute-start.8 = (bf16[16,2,128,128]{3,2,1,0:T(8,128)(2,1)}, bf16[16,2,128,128]{3,2,1,0:T(8,128)(2,1)}, u32[]{:S(2)}, u32[]{:S(2)}) collective-permute-start(bf16[16,2,128,128]{3,2,1,0:T(8,128)(2,1)} %collective-permute-done.1.refs_3_), channel_id=1, source_target_pairs={{0,1},{1,0},{2,3},{3,2},{4,5},{5,4},{6,7},{7,6},{8,9},{9,8},{10,11... | collective-permute-start | bytes 3145736 | tf_op jit(solution)/shard_map/ppermute | solution.py:29
  151.9 23.2 %all-to-all-start.1 = ((bf16[4,672,128]{2,1,0:T(8,128)(2,1)}), bf16[4,672,128]{2,1,0:T(8,128)(2,1)}, u32[]{:S(2)}, u32[]{:S(2)}) async-start(bf16[4,672,128]{2,1,0:T(8,128)(2,1)} %copy-done.9), calls=%async_computation.1 | async-start | bytes 1376256 | tf_op jit(solution)/shard_map/all_to_all | solution.py:330
  167.4 0.9 copy-start.8
  175.1 27.3 %all-to-all-start = ((bf16[4,672,128]{2,1,0:T(8,128)(2,1)}), bf16[4,672,128]{2,1,0:T(8,128)(2,1)S(1)}, u32[]{:S(2)}, u32[]{:S(2)}) async-start(bf16[4,672,128]{2,1,0:T(8,128)(2,1)} %copy-done.8), calls=%async_computation | async-start | bytes 1376256 | tf_op jit(solution)/shard_map/all_to_all | solution.py:330
  178.6 19.5 %collective-permute-start.9 = (bf16[1,2,128,512]{3,2,1,0:T(8,128)(2,1)S(1)}, bf16[1,2,128,512]{3,2,1,0:T(8,128)(2,1)S(1)}, u32[]{:S(2)}, u32[]{:S(2)}) collective-permute-start(bf16[1,2,128,512]{3,2,1,0:T(8,128)(2,1)S(1)} %bitcast.29), channel_id=1, source_target_pairs={{0,1},{1,2},{2,3},{3,4},{4,5},{5,6},{6,7},{7,8},{8,9},{9,10},{10,1... | collective-permute-start | bytes 786440 | tf_op jit(solution)/shard_map/ppermute | solution.py:34
  198.0 2.2 %copy-start.2 = (bf16[16,2,128,512]{3,2,1,0:T(8,128)(2,1)S(1)}, bf16[16,2,128,512]{3,2,1,0:T(8,128)(2,1)}, u32[]{:S(2)}) copy-start(bf16[16,2,128,512]{3,2,1,0:T(8,128)(2,1)} %pool.1) | copy-start | bytes 12582916
  202.4 0.8 copy-start.14
Sparse Core Ops, SparseCore 0:
  16.8 59.6 all-gather.2

commit v7 on v6

--- a/solution.py
+++ b/solution.py
@@ -34,56 +34,64 @@
     return lax.ppermute(array, axis, [(i, (i + by) % size) for i in range(size)])
 
 
-def attend_kernel(lines, head, limit, numbers, mine, *refs):
-    q_all, own, twin, side, both, fresh, out = refs[:7]
-    pages, queries, results, scores, tops, acc, q_sems, page_sems, out_sems = refs[7:]
-    slots = own.shape[0]
+def attend_kernel(lines, head, q_head, numbers, mine, *refs):
+    q_all, pair, other, fresh, out = refs[:5]
+    pages, queries, results, scores, tops, acc, found, q_sems, page_sems, out_sems = refs[5:]
+    slots = pair.shape[1]
     columns = pl.ds(head * HD, HD)
     extra = pages.shape[1] - 1
-
-    def number(request, place):
-        return numbers[request, mine[0] * (limit + 2) + place]
-
-    def count_of(t):
-        return number(request_of(t), limit)
+    cluster = mine[0]
+    core = mine[1]
 
     def request_of(t):
-        return lax.rem(mine[0] - t + lines, lines)
+        return lax.rem(cluster - t + lines, lines)
 
     def q_copy(t, h):
-        origin = q_all.at[request_of(t), pl.ds(0, PAGE), pl.ds((head * GQ + h) * HD, HD)]
+        origin = q_all.at[request_of(t), pl.ds(0, PAGE), pl.ds((q_head * GQ + h) * HD, HD)]
         return pltpu.make_async_copy(origin, queries.at[t, h], q_sems.at[t, h])
 
     def out_copy(t):
         return pltpu.make_async_copy(results.at[t], out.at[request_of(t)], out_sems.at[t])
 
-    def page_copy(source, slot, buffer, place):
-        if source.shape[-1] == HD:
-            origin = source.at[slot]
-        else:
-            origin = source.at[slot, :, :, columns]
-        return pltpu.make_async_copy(origin, pages.at[buffer, place], page_sems.at[buffer, place])
+    def page_copy(source, row, slot, buffer, place):
+        return pltpu.make_async_copy(source.at[row, slot], pages.at[buffer, place], page_sems.at[buffer, place])
 
     def fetch(t):
         request = request_of(t)
         buffer = lax.rem(t, 2)
 
-        @pl.loop(0, count_of(t))
-        def _(place):
-            code = number(request, place)
-            rank = lax.div(code, slots)
-            slot = lax.rem(code, slots)
-            for index, source in enumerate((own, twin, side, both)):
-                @pl.when(rank == index)
-                def _():
-                    page_copy(source, slot, buffer, place).start()
+        def look(j, place):
+            owner = numbers[request, j]
+            here = lax.div(owner, CLUSTER) == cluster
+            slot = numbers[request, MAXP + j]
+            local = lax.rem(owner, CLUSTER)
+            row = lax.div(local, 2)
+            same = lax.rem(local, 2) == core
+
+            @pl.when(here & same)
+            def _():
+                page_copy(pair, row, slot, buffer, place).start()
+
+            @pl.when(here & jnp.logical_not(same))
+            def _():
+                page_copy(other, row, slot, buffer, place).start()
+
+            return place + here.astype(jnp.int32)
+
+        found[t] = lax.fori_loop(0, numbers[request, 2 * MAXP], look, jnp.int32(0))
 
     def arrive(t):
         buffer = lax.rem(t, 2)
 
-        @pl.loop(0, count_of(t))
+        @pl.loop(0, found[t])
         def _(place):
-            page_copy(own, 0, buffer, place).wait()
+            page_copy(pair, 0, 0, buffer, place).wait()
+
+    def tokens_of(t):
+        request = request_of(t)
+        owner = numbers[request, numbers[request, 2 * MAXP] - 1]
+        last = jnp.where(lax.div(owner, CLUSTER) == cluster, numbers[request, 2 * MAXP + 1], PAGE)
+        return (found[t] - 1) * PAGE + last
 
     fresh_copy = pltpu.make_async_copy(fresh.at[:, :, columns], pages.at[0, extra], page_sems.at[0, extra])
     for t in range(lines):
@@ -127,14 +135,14 @@
         return with_ones(pages[lax.rem(t, 2), pl.ds(index * BLOCK, BLOCK), 1].reshape(BLOCK * PAGE, HD))
 
     def blocks_of(t):
-        return jnp.maximum(lax.div(count_of(t) + BLOCK - 1, BLOCK), 1)
+        return jnp.maximum(lax.div(found[t] + BLOCK - 1, BLOCK), 1)
 
     def reset():
         tops[...] = jnp.full(tops.shape, LOW, jnp.float32)
         acc[...] = jnp.zeros(acc.shape, jnp.float32)
 
     def finish(t):
-        some = (count_of(t) > 0) | (t == 0)
+        some = (found[t] > 0) | (t == 0)
         lane = lax.broadcasted_iota(jnp.int32, (PAGE, PAGE), 1)
         sums = jnp.ones((PAGE, PAGE), jnp.float32)
         heights = jnp.zeros((PAGE, PAGE), jnp.float32)
@@ -167,9 +175,8 @@
     for heads in HEADS:
         scores[heads[0]:heads[-1] + 1] = score(0, heads, first)
 
-    def step(_, carry):
+    def step(carry):
         t, index = carry
-        request = request_of(t)
         ends = index + 1 >= blocks_of(t)
         later_t = jnp.where(ends, t + 1, t)
         later_index = jnp.where(ends, 0, index + 1)
@@ -179,7 +186,7 @@
         def _():
             arrive(t + 1)
 
-        seen_here = (count_of(t) - 1 - index * BLOCK) * PAGE + number(request, limit + 1)
+        seen_here = tokens_of(t) - index * BLOCK * PAGE
         column = lax.broadcasted_iota(jnp.int32, (PAGE, BLOCK * PAGE), 1)
         values = values_of(t, index)
         keys = keys_of(ahead_t, later_index)
@@ -198,17 +205,14 @@
 
         return later_t, later_index
 
-    steps = blocks_of(0)
-    for t in range(1, lines):
-        steps += blocks_of(t)
-    lax.fori_loop(0, steps, step, (jnp.int32(0), jnp.int32(0)))
+    lax.while_loop(lambda carry: carry[0] < lines, step, (jnp.int32(0), jnp.int32(0)))
     for t in range(lines):
         out_copy(t).wait()
 
 
-def attend(head, limit, numbers, mine, q_all, pools, fresh):
+def attend(head, q_head, limit, numbers, mine, q_all, pair, other, fresh):
     lines = q_all.shape[0]
-    operands = [q_all, *pools, fresh]
+    operands = [q_all, pair, other, fresh]
     grid_spec = pltpu.PrefetchScalarGridSpec(
         num_scalar_prefetch=2,
         grid=(),
@@ -221,13 +225,14 @@
             pltpu.VMEM((GQ, PAGE, BLOCK * PAGE), jnp.float32),
             pltpu.VMEM((GQ, PAGE, PAGE), jnp.float32),
             pltpu.VMEM((GQ, PAGE, 2 * HD), jnp.float32),
+            pltpu.SMEM((lines,), jnp.int32),
             pltpu.SemaphoreType.DMA((lines, GQ)),
             pltpu.SemaphoreType.DMA((2, limit + 1)),
             pltpu.SemaphoreType.DMA((lines,)),
         ],
     )
     return pl.pallas_call(
-        functools.partial(attend_kernel, lines, head, limit),
+        functools.partial(attend_kernel, lines, head, q_head),
         grid_spec=grid_spec,
         out_shape=jax.ShapeDtypeStruct((lines, ROWS, HD), jnp.bfloat16),
         compiler_params=pltpu.CompilerParams(vmem_limit_bytes=16 * 2**20),
@@ -310,22 +315,6 @@
     )(parts, *before)
 
 
-def page_rows(me, lines, limit, slots, page_owner, page_slot, prefix_len):
-    owners = page_owner[0]
-    length = prefix_len[0]
-    used = (length + PAGE - 1) // PAGE
-    spot = jnp.arange(MAXP)
-    here = (spot < used)[None] & (owners[None] // CLUSTER == jnp.arange(lines)[:, None])
-    before = jnp.sum(here[:, None, :] & (spot[None, None, :] < spot[None, :, None]), axis=2)
-    local = ((owners % CLUSTER) ^ (me % CLUSTER)) * slots + page_slot[0]
-    chosen = here[:, :, None] & (before[:, :, None] == jnp.arange(limit)[None, None, :])
-    picks = jnp.sum(jnp.where(chosen, local[None, :, None], 0), axis=1)
-    counts = jnp.sum(here, axis=1)
-    tail = jnp.any(here & (spot == used - 1)[None], axis=1)
-    lasts = jnp.where(tail, length - (used - 1) * PAGE, PAGE)
-    return jnp.concatenate([picks, counts[:, None], lasts[:, None]], axis=1)
-
-
 def exchanged(array, groups):
     return lax.all_to_all(array, "serve", 0, 0, axis_index_groups=groups, tiled=True)
 
@@ -339,28 +328,31 @@
     lines = width // CLUSTER
     groups = [[c * CLUSTER + i for c in range(lines)] for i in range(CLUSTER)]
     me = lax.axis_index("serve")
-    slots = pool.shape[0]
     capacity = (MAXP + width - 2) // (width - 1)
     limit = min(MAXP, CLUSTER * capacity)
+    pairs = [[first, first + 2] for first in range(width) if first % 4 < 2]
+    used = (prefix_len + PAGE - 1) // PAGE
+    numbers = jnp.concatenate([page_owner[0], page_slot[0], used, prefix_len - (used - 1) * PAGE])
+    numbers = jnp.pad(numbers.astype(queries.dtype)[None], ((0, 15), (0, CHUNK - 2 * MAXP - 2)))
+    early = jnp.concatenate([queries[:, :CHUNK], numbers], axis=0)
+    early = exchanged(jnp.broadcast_to(early[None], (lines,) + early.shape), groups)
+    later = after(queries, early)[None, :, CHUNK:]
+    later = exchanged(jnp.broadcast_to(later, (lines, PAGE, (KVH - 1) * CHUNK)), groups)
+    numbers = early[:, PAGE, :2 * MAXP + 2].astype(jnp.int32)
+    mine = jnp.stack([me // CLUSTER, me % 2])
+    incoming = shifted(new_kv[0], "serve", 1)
     owns = [pool[:, :, :, :HD]]
     rest = after(pool, owns[0])
     owns += [rest[:, :, :, g * HD:(g + 1) * HD] for g in range(1, KVH)]
-    sides = [swapped(own, "serve", 2) for own in owns]
-    twin = swapped(rest, "serve", 1)
-    incoming = shifted(new_kv[0], "serve", 1)
-    numbers = page_rows(me, lines, limit, slots, page_owner, page_slot, prefix_len).astype(queries.dtype)
-    numbers = jnp.pad(numbers.reshape(1, -1), ((0, PAGE - 1), (0, PAGE - lines * (limit + 2))))
-    sent = jnp.concatenate([after(queries, owns[1]), numbers], axis=1)
-    q_all = lax.all_gather(sent, "serve", axis_index_groups=groups)
-    numbers = q_all[:, 0, KVH * CHUNK:].astype(jnp.int32)
-    mine = (me // CLUSTER)[None]
+    gathered = [lax.all_gather(own, "serve", axis_index_groups=pairs) for own in owns]
     fresh = new_kv[0, 0]
     attended = None
     parts = None
     for g in range(KVH):
-        side = sides[g] if g == 0 else after(sides[g], parts)
-        both = swapped(side, "serve", 1)
-        parts = attend(g, limit, numbers, mine, q_all, (owns[g], twin, side, both), fresh)
+        pair = gathered[g] if g == 0 else after(gathered[g], parts)
+        other = swapped(pair, "serve", 1)
+        q_all, q_head = (early, 0) if g == 0 else (later, g - 1)
+        parts = attend(g, q_head, limit, numbers, mine, q_all, pair, other, fresh)
         attended = merge(g, exchanged(parts, groups), attended)
     pool_out = store(store_slot[0], pool, after(incoming, parts))
     return (attended, pool_out)

time: 213 us -> 254 us (1.19)
  blocking collectives: 0 us -> 47.3 us
  Pallas kernels: 59.9 us -> 77.7 us
  waiting for transfers between devices: 87.9 us -> 76.2 us
  starting transfers between devices: 25.7 us -> 17.5 us
  other arithmetic: 3.63 us -> 0.19 us
    all_to_all x0 -> x2, blocking collectives: none -> 47.3 us  [exchanged(): lax.all_to_all(array, 'serve', 0, 0, axis_index_groups=groups, tiled=True)]
    ppermute x9 -> x4, waiting for transfers between devices: 39.2 us -> 0.28 us  [swapped(): return lax.ppermute(array, axis, [(i, i ^ bit) for i in range(size)])]
    all_to_all x4, waiting for transfers between devices: 6.78 us -> 26.9 us  [exchanged(): lax.all_to_all(array, 'serve', 0, 0, axis_index_groups=groups, tiled=True)]
    pallas_call x4, Pallas kernels: 48.4 us -> 66.1 us  [attend(): pl.pallas_call(functools.partial(attend_kernel, lines, head, q_head), gri...]
    all_gather x1 -> x4, waiting for transfers between devices: 30.2 us -> 40.3 us  [per_device(): lax.all_gather(own, 'serve', axis_index_groups=pairs)]
    ppermute x9 -> x4, starting transfers between devices: 9.6 us -> 0.15 us  [swapped(): return lax.ppermute(array, axis, [(i, i ^ bit) for i in range(size)])]
    unnamed x32 -> x22, local copies, waits for them, and re-layouts: 13.9 us -> 10.5 us
    ppermute x1, waiting for transfers between devices: 11.7 us -> 8.7 us  [shifted(): lax.ppermute(array, axis, [(i, (i + by) % size) for i in range(size)])]
  transfers between devices with their start and end apart: 15 -> 13, of which waited for: 6 -> 5; matrix products, arithmetic and copies ran while one was open for 0% -> 2% of each run, Pallas kernels for 27% -> 30%
where the time goes in v7:
time: 254 us; the launch traced here: 252 us
  Pallas kernels  77.7 us (31%)
  waiting for transfers between devices  76.2 us (30%)
  blocking collectives  47.3 us (19%)
  local copies, waits for them, and re-layouts  17.9 us (7%)
  starting transfers between devices  17.5 us (7%)
  between operations  15.5 us (6%)
    pallas_call x4, Pallas kernels, attend(): pl.pallas_call(functools.partial(attend_kernel, lines, head, q_head), gri...  66.1 us
    all_to_all x2, blocking collectives, exchanged(): lax.all_to_all(array, 'serve', 0, 0, axis_index_groups=groups, tiled=True)  47.3 us
    all_gather x4, waiting for transfers between devices, per_device(): lax.all_gather(own, 'serve', axis_index_groups=pairs)  40.3 us
    all_to_all x4, waiting for transfers between devices, exchanged(): lax.all_to_all(array, 'serve', 0, 0, axis_index_groups=groups, tiled=True)  26.9 us
    all_to_all x4, starting transfers between devices, exchanged(): lax.all_to_all(array, 'serve', 0, 0, axis_index_groups=groups, tiled=True)  17.2 us
    unnamed x22, local copies, waits for them, and re-layouts  10.5 us
    pallas_call x4, Pallas kernels, merge(): pl.pallas_call(functools.partial(merge_kernel, head), in_specs=[pl.BlockS...  9.41 us
    ppermute x1, waiting for transfers between devices, shifted(): lax.ppermute(array, axis, [(i, (i + by) % size) for i in range(size)])  8.7 us
  transfers between devices with their start and end apart: 13, of which 5 were waited for; matrix products, arithmetic and copies ran while one was open for 2% of the time, Pallas kernels for 30%

profile of v7, /device:TPU:0, one launch (start us, length us, event | category | flops | bytes accessed | tf_op | source)
XLA Modules:
  0.0 252.3 jit_solution(17083648090783758101)
XLA Ops:
  7.2 0.0 all-gather.15.cloned.1.call-start
  7.2 2.3 slice.24
  9.5 0.0 all-gather.15.cloned.1.call-update
  9.5 0.0 copy-start.9
  9.6 0.0 slice-start
  9.6 0.0 all-gather.13.cloned.1.call-start
  9.6 3.7 %fusion.13 = (bf16[16,2,128,128]{3,2,1,0:T(8,128)(2,1)}, bf16[16,2,128,128]{3,2,1,0:T(8,128)(2,1)}, bf16[16,2,128,128]{3,2,1,0:T(8,128)(2,1)}) fusion(bf16[16,2,128,512]{3,2,1,0:T(8,128)(2,1)} %pool.1), kind=kLoop, calls=%fused_computation.18 | loop fusion | bytes 6291456 | tf_op jit(solution)/shard_map/slice | solution.py:346
  13.3 0.0 all-gather.13.cloned.1.call-update
  13.3 0.0 slice-start.1
  14.1 31.8 %all-gather.15.cloned.1.call-done = bf16[32,2,128,128]{3,2,1,0:T(8,128)(2,1)} async-done(((bf16[16,2,128,128]{3,2,1,0:T(8,128)(2,1)}), bf16[32,2,128,128]{3,2,1,0:T(8,128)(2,1)}) %all-gather.15.cloned.1.call-update) | async-done | bytes 2097168 | tf_op jit(solution)/shard_map/all_gather | solution.py:347
  46.0 0.1 fusion.8
  46.1 0.1 broadcast_in_dim.4
  46.1 24.1 %all_to_all.30.refs_0_ = bf16[4,144,640]{2,1,0:T(8,128)(2,1)S(1)} all-to-all(bf16[4,144,640]{2,1,0:T(8,128)(2,1)S(1)} %broadcast_in_dim.4), channel_id=1, replica_groups={{0,4,8,12},{1,5,9,13},{2,6,10,14},{3,7,11,15},{16,20,24,28},{17,21,25,2..., dimensions={0} | all-to-all | bytes 1474560 | tf_op jit(solution)/shard_map/all_to_all | solution.py:319
  70.3 1.4 broadcast_in_dim.5
  71.7 3.7 %all-to-all-start.1 = ((bf16[4,128,1920]{2,1,0:T(8,128)(2,1)}), bf16[4,128,1920]{2,1,0:T(8,128)(2,1)S(1)}, u32[]{:S(2)}, u32[]{:S(2)}) async-start(bf16[4,128,1920]{2,1,0:T(8,128)(2,1)} %broadcast_in_dim.5), calls=%async_computation.1 | async-start | bytes 3932160 | tf_op jit(solution)/shard_map/all_to_all | solution.py:319
  75.4 0.0 all-gather.11.cloned.1.call-start
  75.5 0.1 pad_add_fusion.mine
  75.6 1.6 copy-done.3
  77.2 16.4 %shard_map.86 = bf16[4,672,128]{2,1,0:T(8,128)(2,1)} custom-call(s32[4,98]{1,0:T(4,128)S(1)} %fusion.12.numbers, s32[2]{0:T(128)S(1)} %pad_add_fusion.mine, bf16[4,144,640]{2,1,0:T(8,128)(2,1)S(1)} %all_to_all.30.refs_0_, bf16[2,16,2,128,128]{4,3,2,1,0:T(8,128)(2,1)S(1)} %bitcast.23, bf16[2,16,2,128,128]{4,3,2,1,0:T(8,128)(2,1)} %collective-permute-done.refs_2_, ...), custom_call_target="tpu_custom_call" | custom-call | flops 1 | bytes 1 | tf_op jit(solution)/shard_map/pallas_call | solution.py:234
  93.6 0.0 all-gather.13.cloned.1.call-done
  93.6 0.1 collective-permute-start.1
  93.7 0.0 all-gather.11.cloned.1.call-update
  93.7 0.0 all-gather.9.cloned.1.call-start
  93.7 26.9 %all-to-all-done.1.refs_0_ = bf16[4,128,1920]{2,1,0:T(8,128)(2,1)S(1)} async-done(((bf16[4,128,1920]{2,1,0:T(8,128)(2,1)}), bf16[4,128,1920]{2,1,0:T(8,128)(2,1)S(1)}, u32[]{:S(2)}, u32[]{:S(2)}) %all-to-all-start.1) | async-done | bytes 1966112 | tf_op jit(solution)/shard_map/all_to_all | solution.py:319
  120.6 1.6 copy-done.4
  122.2 16.7 %shard_map.87 = bf16[4,672,128]{2,1,0:T(8,128)(2,1)S(1)} custom-call(s32[4,98]{1,0:T(4,128)S(1)} %fusion.12.numbers, s32[2]{0:T(128)S(1)} %pad_add_fusion.mine, bf16[4,128,1920]{2,1,0:T(8,128)(2,1)S(1)} %all-to-all-done.1.refs_0_, bf16[2,16,2,128,128]{4,3,2,1,0:T(8,128)(2,1)S(1)} %bitcast.25, bf16[2,16,2,128,128]{4,3,2,1,0:T(8,128)(2,1)} %collective-permute-done.1.refs_2_, ...), custom_call_target="tpu_custom_call" | custom-call | flops 1 | bytes 1 | tf_op jit(solution)/shard_map/pallas_call | solution.py:234
  139.0 0.0 all-gather.11.cloned.1.call-done
  139.0 0.1 collective-permute-start.2
  139.1 0.0 all-gather.9.cloned.1.call-update
  139.1 4.2 %all-to-all-start.5 = ((bf16[4,672,128]{2,1,0:T(8,128)(2,1)}), bf16[4,672,128]{2,1,0:T(8,128)(2,1)}, u32[]{:S(2)}, u32[]{:S(2)}) async-start(bf16[4,672,128]{2,1,0:T(8,128)(2,1)} %shard_map.86), calls=%async_computation.5 | async-start | bytes 1376256 | tf_op jit(solution)/shard_map/all_to_all | solution.py:319
  143.3 0.3 collective-permute-done.2.refs_2_
  143.6 1.8 copy-done.5
  145.3 16.7 %shard_map.88 = bf16[4,672,128]{2,1,0:T(8,128)(2,1)S(1)} custom-call(s32[4,98]{1,0:T(4,128)S(1)} %fusion.12.numbers, s32[2]{0:T(128)S(1)} %pad_add_fusion.mine, bf16[4,128,1920]{2,1,0:T(8,128)(2,1)S(1)} %all-to-all-done.1.refs_0_, bf16[2,16,2,128,128]{4,3,2,1,0:T(8,128)(2,1)S(1)} %bitcast.27, bf16[2,16,2,128,128]{4,3,2,1,0:T(8,128)(2,1)} %collective-permute-done.2.refs_2_, ...), custom_call_target="tpu_custom_call" | custom-call | flops 1 | bytes 1 | tf_op jit(solution)/shard_map/pallas_call | solution.py:234
  162.1 0.8 copy-done.2
  162.9 8.4 %all-gather.9.cloned.1.call-done = bf16[32,2,128,128]{3,2,1,0:T(8,128)(2,1)} async-done(((bf16[16,2,128,128]{3,2,1,0:T(8,128)(2,1)}), bf16[32,2,128,128]{3,2,1,0:T(8,128)(2,1)}) %all-gather.9.cloned.1.call-update) | async-done | bytes 2097168 | tf_op jit(solution)/shard_map/all_gather | solution.py:347
  171.3 23.2 %all_to_all.31.parts = bf16[4,672,128]{2,1,0:T(8,128)(2,1)} all-to-all(bf16[4,672,128]{2,1,0:T(8,128)(2,1)S(1)} %shard_map.87), channel_id=1, replica_groups={{0,4,8,12},{1,5,9,13},{2,6,10,14},{3,7,11,15},{16,20,24,28},{17,21,25,2..., dimensions={0} | all-to-all | bytes 1376256 | tf_op jit(solution)/shard_map/all_to_all | solution.py:319
  194.5 3.5 %all-to-all-start.3 = ((bf16[4,672,128]{2,1,0:T(8,128)(2,1)}), bf16[4,672,128]{2,1,0:T(8,128)(2,1)S(1)}, u32[]{:S(2)}, u32[]{:S(2)}) async-start(bf16[4,672,128]{2,1,0:T(8,128)(2,1)} %copy-done.2), calls=%async_computation.3 | async-start | bytes 1376256 | tf_op jit(solution)/shard_map/all_to_all | solution.py:319
  198.0 1.6 copy-done.6
  199.6 16.4 %shard_map.89 = bf16[4,672,128]{2,1,0:T(8,128)(2,1)} custom-call(s32[4,98]{1,0:T(4,128)S(1)} %fusion.12.numbers, s32[2]{0:T(128)S(1)} %pad_add_fusion.mine, bf16[4,128,1920]{2,1,0:T(8,128)(2,1)S(1)} %all-to-all-done.1.refs_0_, bf16[2,16,2,128,128]{4,3,2,1,0:T(8,128)(2,1)S(1)} %bitcast.29, bf16[2,16,2,128,128]{4,3,2,1,0:T(8,128)(2,1)} %collective-permute-done.3.refs_2_, ...), custom_call_target="tpu_custom_call" | custom-call | flops 1 | bytes 1 | tf_op jit(solution)/shard_map/pallas_call | solution.py:234
  216.0 5.8 %all-to-all-start.2 = ((bf16[4,672,128]{2,1,0:T(8,128)(2,1)}), bf16[4,672,128]{2,1,0:T(8,128)(2,1)S(1)}, u32[]{:S(2)}, u32[]{:S(2)}) async-start(bf16[4,672,128]{2,1,0:T(8,128)(2,1)} %shard_map.89), calls=%async_computation.2 | async-start | bytes 1376256 | tf_op jit(solution)/shard_map/all_to_all | solution.py:319
  221.8 2.4 shard_map.90.refs_0_
  224.1 2.4 shard_map.91.refs_0_
  227.2 2.4 shard_map.92.refs_0_
  229.5 8.7 %collective-permute-done.4.incoming = bf16[1,2,128,512]{3,2,1,0:T(8,128)(2,1)S(1)} collective-permute-done((bf16[1,2,128,512]{3,2,1,0:T(8,128)(2,1)S(1)}, bf16[1,2,128,512]{3,2,1,0:T(8,128)(2,1)S(1)}, u32[]{:S(2)}, u32[]{:S(2)}) %collective-permute-start.4) | collective-permute-done | bytes 262176 | tf_op jit(solution)/shard_map/ppermute | solution.py:34
  238.2 2.2 copy-done
  240.4 2.1 shard_map.94
  242.6 0.9 copy-done.8
  243.4 2.4 shard_map.93
  (30 shorter events, 0.1 us)
Async XLA Ops:
  7.2 38.8 %all-gather.15.cloned.1.call-start = ((), (), s32[]{:S(2)}) async-start(), calls=%async_computation.9 | async-start | bytes 3145728 | tf_op jit(solution)/shard_map/all_gather | solution.py:347
  9.5 4.5 %copy-start.9 = (s32[1,48]{1,0:T(1,128)S(1)}, s32[1,48]{1,0:T(1,128)}, u32[]{:S(2)}) copy-start(s32[1,48]{1,0:T(1,128)} %param.10) | copy-start | bytes 580
  9.6 4.6 %copy-start.10 = (s32[1,48]{1,0:T(1,128)S(1)}, s32[1,48]{1,0:T(1,128)}, u32[]{:S(2)}) copy-start(s32[1,48]{1,0:T(1,128)} %param.11) | copy-start | bytes 580
  9.6 36.5 %slice-start = ((bf16[128,2560]{1,0:T(8,128)(2,1)}), bf16[128,640]{1,0:T(8,128)(2,1)S(1)}, s32[]{:S(2)}) async-start(bf16[128,2560]{1,0:T(8,128)(2,1)} %param.7), calls=%async_computation.10 | async-start | bytes 327680 | tf_op jit(solution)/shard_map/slice | solution.py:337
  9.6 84.0 %all-gather.13.cloned.1.call-start = ((), (), s32[]{:S(2)}) async-start(), calls=%async_computation.8 | async-start | bytes 3145728 | tf_op jit(solution)/shard_map/all_gather | solution.py:347
  13.3 56.9 %slice-start.1 = ((bf16[128,2560]{1,0:T(8,128)(2,1)}), bf16[128,1920]{1,0:T(8,128)(2,1)S(1)}, s32[]{:S(2)}) async-start(bf16[128,2560]{1,0:T(8,128)(2,1)} %param.7), calls=%async_computation.11 | async-start | bytes 983040 | tf_op jit(solution)/shard_map/slice | solution.py:339
  46.0 29.6 %collective-permute-start = (bf16[2,16,2,128,128]{4,3,2,1,0:T(8,128)(2,1)}, bf16[2,16,2,128,128]{4,3,2,1,0:T(8,128)(2,1)}, u32[]{:S(2)}, u32[]{:S(2)}) collective-permute-start(bf16[2,16,2,128,128]{4,3,2,1,0:T(8,128)(2,1)} %bitcast.22), channel_id=1, source_target_pairs={{0,1},{1,0},{2,3},{3,2},{4,5},{5,4},{6,7},{7,6},{8,9},{9,8},{10,11... | collective-permute-start | bytes 6291464 | tf_op jit(solution)/shard_map/ppermute | solution.py:29
  71.7 3.9 %copy-start.1 = (bf16[1,1,2,128,512]{4,3,2,1,0:T(8,128)(2,1)S(1)}, bf16[1,1,2,128,512]{4,3,2,1,0:T(8,128)(2,1)}, u32[]{:S(2)}) copy-start(bf16[1,1,2,128,512]{4,3,2,1,0:T(8,128)(2,1)} %param.8) | copy-start | bytes 786436
  71.7 48.9 %all-to-all-start.1 = ((bf16[4,128,1920]{2,1,0:T(8,128)(2,1)}), bf16[4,128,1920]{2,1,0:T(8,128)(2,1)S(1)}, u32[]{:S(2)}, u32[]{:S(2)}) async-start(bf16[4,128,1920]{2,1,0:T(8,128)(2,1)} %broadcast_in_dim.5), calls=%async_computation.1 | async-start | bytes 3932160 | tf_op jit(solution)/shard_map/all_to_all | solution.py:319
  75.4 63.5 %all-gather.11.cloned.1.call-start = ((), (), s32[]{:S(2)}) async-start(), calls=%async_computation.7 | async-start | bytes 3145728 | tf_op jit(solution)/shard_map/all_gather | solution.py:347
  75.6 1.6 copy-start.3
  93.6 27.0 %collective-permute-start.1 = (bf16[2,16,2,128,128]{4,3,2,1,0:T(8,128)(2,1)}, bf16[2,16,2,128,128]{4,3,2,1,0:T(8,128)(2,1)}, u32[]{:S(2)}, u32[]{:S(2)}) collective-permute-start(bf16[2,16,2,128,128]{4,3,2,1,0:T(8,128)(2,1)} %bitcast.24), channel_id=1, source_target_pairs={{0,1},{1,0},{2,3},{3,2},{4,5},{5,4},{6,7},{7,6},{8,9},{9,8},{10,11... | collective-permute-start | bytes 6291464 | tf_op jit(solution)/shard_map/ppermute | solution.py:29
  93.7 77.6 %all-gather.9.cloned.1.call-start = ((), (), s32[]{:S(2)}) async-start(), calls=%async_computation.6 | async-start | bytes 3145728 | tf_op jit(solution)/shard_map/all_gather | solution.py:347
  120.6 1.6 copy-start.4
  139.0 4.6 %collective-permute-start.2 = (bf16[2,16,2,128,128]{4,3,2,1,0:T(8,128)(2,1)}, bf16[2,16,2,128,128]{4,3,2,1,0:T(8,128)(2,1)}, u32[]{:S(2)}, u32[]{:S(2)}) collective-permute-start(bf16[2,16,2,128,128]{4,3,2,1,0:T(8,128)(2,1)} %bitcast.26), channel_id=1, source_target_pairs={{0,1},{1,0},{2,3},{3,2},{4,5},{5,4},{6,7},{7,6},{8,9},{9,8},{10,11... | collective-permute-start | bytes 6291464 | tf_op jit(solution)/shard_map/ppermute | solution.py:29
  139.1 32.2 %all-to-all-start.5 = ((bf16[4,672,128]{2,1,0:T(8,128)(2,1)}), bf16[4,672,128]{2,1,0:T(8,128)(2,1)}, u32[]{:S(2)}, u32[]{:S(2)}) async-start(bf16[4,672,128]{2,1,0:T(8,128)(2,1)} %shard_map.86), calls=%async_computation.5 | async-start | bytes 1376256 | tf_op jit(solution)/shard_map/all_to_all | solution.py:319
  143.5 1.8 copy-start.5
  162.1 0.8 copy-start.2
  171.3 26.7 %collective-permute-start.3 = (bf16[2,16,2,128,128]{4,3,2,1,0:T(8,128)(2,1)}, bf16[2,16,2,128,128]{4,3,2,1,0:T(8,128)(2,1)}, u32[]{:S(2)}, u32[]{:S(2)}) collective-permute-start(bf16[2,16,2,128,128]{4,3,2,1,0:T(8,128)(2,1)} %bitcast.28), channel_id=1, source_target_pairs={{0,1},{1,0},{2,3},{3,2},{4,5},{5,4},{6,7},{7,6},{8,9},{9,8},{10,11... | collective-permute-start | bytes 6291464 | tf_op jit(solution)/shard_map/ppermute | solution.py:29
  194.5 21.5 %all-to-all-start.3 = ((bf16[4,672,128]{2,1,0:T(8,128)(2,1)}), bf16[4,672,128]{2,1,0:T(8,128)(2,1)S(1)}, u32[]{:S(2)}, u32[]{:S(2)}) async-start(bf16[4,672,128]{2,1,0:T(8,128)(2,1)} %copy-done.2), calls=%async_computation.3 | async-start | bytes 1376256 | tf_op jit(solution)/shard_map/all_to_all | solution.py:319
  198.0 1.6 copy-start.6
  215.9 10.6 %copy-start.7 = (bf16[4,672,128]{2,1,0:T(8,128)(2,1)}, bf16[4,672,128]{2,1,0:T(8,128)(2,1)S(1)}, u32[]{:S(2)}) copy-start(bf16[4,672,128]{2,1,0:T(8,128)(2,1)S(1)} %all-to-all-done.3.parts) | copy-start | bytes 2064388
  216.0 26.6 %all-to-all-start.2 = ((bf16[4,672,128]{2,1,0:T(8,128)(2,1)}), bf16[4,672,128]{2,1,0:T(8,128)(2,1)S(1)}, u32[]{:S(2)}, u32[]{:S(2)}) async-start(bf16[4,672,128]{2,1,0:T(8,128)(2,1)} %shard_map.89), calls=%async_computation.2 | async-start | bytes 1376256 | tf_op jit(solution)/shard_map/all_to_all | solution.py:319
  221.8 16.4 %collective-permute-start.4 = (bf16[1,2,128,512]{3,2,1,0:T(8,128)(2,1)S(1)}, bf16[1,2,128,512]{3,2,1,0:T(8,128)(2,1)S(1)}, u32[]{:S(2)}, u32[]{:S(2)}) collective-permute-start(bf16[1,2,128,512]{3,2,1,0:T(8,128)(2,1)S(1)} %bitcast.21), channel_id=1, source_target_pairs={{0,1},{1,2},{2,3},{3,4},{4,5},{5,6},{6,7},{7,8},{8,9},{9,10},{10,1... | collective-permute-start | bytes 786440 | tf_op jit(solution)/shard_map/ppermute | solution.py:34
  238.2 2.2 copy-start
  242.6 0.9 copy-start.8
Sparse Core Ops, SparseCore 0:
  10.1 35.8 all-gather.14
  47.5 33.1 all-gather.12
  93.8 34.3 all-gather.10
  139.2 32.0 all-gather.8

commit v8 on v6

--- a/solution.py
+++ b/solution.py
@@ -34,7 +34,7 @@
     return lax.ppermute(array, axis, [(i, (i + by) % size) for i in range(size)])
 
 
-def attend_kernel(lines, head, limit, numbers, mine, *refs):
+def attend_kernel(lines, head, q_head, limit, numbers, mine, *refs):
     q_all, own, twin, side, both, fresh, out = refs[:7]
     pages, queries, results, scores, tops, acc, q_sems, page_sems, out_sems = refs[7:]
     slots = own.shape[0]
@@ -51,7 +51,7 @@
         return lax.rem(mine[0] - t + lines, lines)
 
     def q_copy(t, h):
-        origin = q_all.at[request_of(t), pl.ds(0, PAGE), pl.ds((head * GQ + h) * HD, HD)]
+        origin = q_all.at[request_of(t), pl.ds(0, PAGE), pl.ds((q_head * GQ + h) * HD, HD)]
         return pltpu.make_async_copy(origin, queries.at[t, h], q_sems.at[t, h])
 
     def out_copy(t):
@@ -206,7 +206,7 @@
         out_copy(t).wait()
 
 
-def attend(head, limit, numbers, mine, q_all, pools, fresh):
+def attend(head, q_head, limit, numbers, mine, q_all, pools, fresh):
     lines = q_all.shape[0]
     operands = [q_all, *pools, fresh]
     grid_spec = pltpu.PrefetchScalarGridSpec(
@@ -227,7 +227,7 @@
         ],
     )
     return pl.pallas_call(
-        functools.partial(attend_kernel, lines, head, limit),
+        functools.partial(attend_kernel, lines, head, q_head, limit),
         grid_spec=grid_spec,
         out_shape=jax.ShapeDtypeStruct((lines, ROWS, HD), jnp.bfloat16),
         compiler_params=pltpu.CompilerParams(vmem_limit_bytes=16 * 2**20),
@@ -266,7 +266,7 @@
         store_kernel,
         grid_spec=grid_spec,
         out_shape=jax.ShapeDtypeStruct(pool.shape, pool.dtype),
-        compiler_params=pltpu.CompilerParams(vmem_limit_bytes=16 * 2**20),
+        compiler_params=pltpu.CompilerParams(vmem_limit_bytes=60 * 2**20),
         cost_estimate=pl.CostEstimate(flops=1, bytes_accessed=1, transcendentals=0),
     )(slot, pool, incoming)
 
@@ -310,20 +310,38 @@
     )(parts, *before)
 
 
-def page_rows(me, lines, limit, slots, page_owner, page_slot, prefix_len):
-    owners = page_owner[0]
-    length = prefix_len[0]
-    used = (length + PAGE - 1) // PAGE
-    spot = jnp.arange(MAXP)
-    here = (spot < used)[None] & (owners[None] // CLUSTER == jnp.arange(lines)[:, None])
-    before = jnp.sum(here[:, None, :] & (spot[None, None, :] < spot[None, :, None]), axis=2)
-    local = ((owners % CLUSTER) ^ (me % CLUSTER)) * slots + page_slot[0]
-    chosen = here[:, :, None] & (before[:, :, None] == jnp.arange(limit)[None, None, :])
-    picks = jnp.sum(jnp.where(chosen, local[None, :, None], 0), axis=1)
-    counts = jnp.sum(here, axis=1)
-    tail = jnp.any(here & (spot == used - 1)[None], axis=1)
-    lasts = jnp.where(tail, length - (used - 1) * PAGE, PAGE)
-    return jnp.concatenate([picks, counts[:, None], lasts[:, None]], axis=1)
+def lists_kernel(lines, limit, slots, owners, places, length, mine, out):
+    step = limit + 2
+    used = lax.div(length[0] + PAGE - 1, PAGE)
+
+    @pl.loop(0, PAGE)
+    def _(i):
+        out[0, i] = 0
+
+    for d in range(lines):
+        out[0, d * step + limit + 1] = PAGE
+
+    @pl.loop(0, used)
+    def _(j):
+        owner = owners[0, j]
+        base = lax.div(owner, CLUSTER) * step
+        place = out[0, base + limit]
+        rank = lax.rem(owner, CLUSTER) ^ mine[1]
+        out[0, base + place] = rank * slots + places[0, j]
+        out[0, base + limit] = place + 1
+
+    final = lax.div(owners[0, used - 1], CLUSTER) * step
+    out[0, final + limit + 1] = length[0] - (used - 1) * PAGE
+
+
+def page_lists(lines, limit, slots, page_owner, page_slot, prefix_len, mine):
+    smem = pl.BlockSpec(memory_space=pltpu.SMEM)
+    return pl.pallas_call(
+        functools.partial(lists_kernel, lines, limit, slots),
+        in_specs=[smem] * 4,
+        out_specs=smem,
+        out_shape=jax.ShapeDtypeStruct((1, PAGE), jnp.int32),
+    )(page_owner, page_slot, prefix_len, mine)
 
 
 def exchanged(array, groups):
@@ -348,20 +366,31 @@
     sides = [swapped(own, "serve", 2) for own in owns]
     twin = swapped(rest, "serve", 1)
     incoming = shifted(new_kv[0], "serve", 1)
-    numbers = page_rows(me, lines, limit, slots, page_owner, page_slot, prefix_len).astype(queries.dtype)
-    numbers = jnp.pad(numbers.reshape(1, -1), ((0, PAGE - 1), (0, PAGE - lines * (limit + 2))))
-    sent = jnp.concatenate([after(queries, owns[1]), numbers], axis=1)
-    q_all = lax.all_gather(sent, "serve", axis_index_groups=groups)
-    numbers = q_all[:, 0, KVH * CHUNK:].astype(jnp.int32)
-    mine = (me // CLUSTER)[None]
+    mine = jnp.stack([me // CLUSTER, me % CLUSTER]).astype(jnp.int32)
+    numbers = page_lists(lines, limit, slots, page_owner, page_slot, prefix_len, mine)
+    numbers = jnp.pad(numbers.astype(queries.dtype), ((0, PAGE - 1), (0, 0)))
+    half = KVH // 2
+    early = jnp.concatenate([after(queries, owns[1])[:, :half * CHUNK], numbers], axis=1)
+    later = after(queries, early)[:, half * CHUNK:]
+    early = lax.all_gather(early, "serve", axis_index_groups=groups)
+    later = lax.all_gather(later, "serve", axis_index_groups=groups)
+    numbers = early[:, 0, half * CHUNK:].astype(jnp.int32)
     fresh = new_kv[0, 0]
     attended = None
+    done = None
+    arrived = []
     parts = None
     for g in range(KVH):
-        side = sides[g] if g == 0 else after(sides[g], parts)
+        side = sides[g]
+        if g > 0:
+            side = after(side, parts, *([incoming] if g == 1 else [done]))
         both = swapped(side, "serve", 1)
-        parts = attend(g, limit, numbers, mine, q_all, (owns[g], twin, side, both), fresh)
-        attended = merge(g, exchanged(parts, groups), attended)
+        q_all, q_head = (early, g) if g < half else (later, g - half)
+        parts = attend(g, q_head, limit, numbers, mine, q_all, (owns[g], twin, side, both), fresh)
+        if arrived:
+            attended = done = merge(g - 1, arrived.pop(), attended)
+        arrived.append(exchanged(parts, groups))
+    attended = merge(KVH - 1, arrived.pop(), attended)
     pool_out = store(store_slot[0], pool, after(incoming, parts))
     return (attended, pool_out)
 

time: 213 us -> 334 us (1.57)
  Pallas kernels: 59.9 us -> 197 us
  waiting for transfers between devices: 87.9 us -> 64.6 us
  blocking collectives: 0 us -> 22 us
  local copies, waits for them, and re-layouts: 19.7 us -> 13.3 us
  starting transfers between devices: 25.7 us -> 19.5 us
    pallas_call x1, Pallas kernels: 2.13 us -> 128 us  [store(): pl.pallas_call(store_kernel, grid_spec=grid_spec, out_shape=jax.ShapeDtyp...]
    all_to_all x4 -> x3, waiting for transfers between devices: 6.78 us -> 31.3 us  [exchanged(): lax.all_to_all(array, 'serve', 0, 0, axis_index_groups=groups, tiled=True)]
    all_to_all x0 -> x1, blocking collectives: none -> 22 us  [exchanged(): lax.all_to_all(array, 'serve', 0, 0, axis_index_groups=groups, tiled=True)]
    all_gather x1 -> x2, waiting for transfers between devices: 30.2 us -> 9.08 us  [the longest x1 9.06 us: per_device(): early = lax.all_gather(early, 'serve', axis_index_groups=groups)]
    ppermute x9, waiting for transfers between devices: 39.2 us -> 24.2 us  [swapped(): return lax.ppermute(array, axis, [(i, i ^ bit) for i in range(size)])]
    ppermute x1, waiting for transfers between devices: 11.7 us -> 0.01 us  [shifted(): lax.ppermute(array, axis, [(i, (i + by) % size) for i in range(size)])]
    pallas_call x4 -> x5, Pallas kernels: 48.4 us -> 59.5 us  [the longest x4 56.9 us: attend(): pl.pallas_call(functools.partial(attend_kernel, lines, head, q_head, limi...]
    unnamed x32 -> x20, local copies, waits for them, and re-layouts: 13.9 us -> 5.84 us
  transfers between devices with their start and end apart: 15 -> 15, of which waited for: 6 -> 5; matrix products, arithmetic and copies ran while one was open for 0% -> 2% of each run, Pallas kernels for 27% -> 58%
where the time goes in v8:
time: 334 us
  Pallas kernels  197 us (59%)
  waiting for transfers between devices  64.6 us (19%)
  blocking collectives  22 us (7%)
  starting transfers between devices  19.5 us (6%)
  between operations  15.6 us (5%)
  local copies, waits for them, and re-layouts  13.3 us (4%)
    pallas_call x1, Pallas kernels, store(): pl.pallas_call(store_kernel, grid_spec=grid_spec, out_shape=jax.ShapeDtyp...  128 us
    pallas_call x4, Pallas kernels, attend(): pl.pallas_call(functools.partial(attend_kernel, lines, head, q_head, limi...  56.9 us
    all_to_all x3, waiting for transfers between devices, exchanged(): lax.all_to_all(array, 'serve', 0, 0, axis_index_groups=groups, tiled=True)  31.3 us
    ppermute x9, waiting for transfers between devices, swapped(): return lax.ppermute(array, axis, [(i, i ^ bit) for i in range(size)])  24.2 us
    all_to_all x1, blocking collectives, exchanged(): lax.all_to_all(array, 'serve', 0, 0, axis_index_groups=groups, tiled=True)  22 us
    all_to_all x3, starting transfers between devices, exchanged(): lax.all_to_all(array, 'serve', 0, 0, axis_index_groups=groups, tiled=True)  11.2 us
    pallas_call x4, Pallas kernels, merge(): pl.pallas_call(functools.partial(merge_kernel, head), in_specs=[pl.BlockS...  9.41 us
    all_gather x1, waiting for transfers between devices, per_device(): early = lax.all_gather(early, 'serve', axis_index_groups=groups)  9.06 us
  transfers between devices with their start and end apart: 15, of which 5 were waited for; matrix products, arithmetic and copies ran while one was open for 2% of the time, Pallas kernels for 58%

profile of v8, /device:TPU:0, one launch (start us, length us, event | category | flops | bytes accessed | tf_op | source)
XLA Modules:
  0.0 334.4 jit_solution(3084753242421234442)
XLA Ops:
  7.2 0.0 slice-start
  7.2 0.0 all-gather.5.cloned.1.call-start
  7.2 1.3 slice.21.refs_1_
  8.6 0.0 copy-start.4
  8.6 0.5 collective-permute-start
  9.7 0.6 pad_add_fusion.mine
  10.3 2.7 shard_map.86
  13.0 0.7 convert_element_type.10
  13.7 3.7 %fusion.3 = (bf16[16,2,128,128]{3,2,1,0:T(8,128)(2,1)}, bf16[16,2,128,128]{3,2,1,0:T(8,128)(2,1)S(1)}, bf16[16,2,128,128]{3,2,1,0:T(8,128)(2,1)}) fusion(bf16[16,2,128,512]{3,2,1,0:T(8,128)(2,1)} %pool.1), kind=kLoop, calls=%fused_computation.6 | loop fusion | bytes 6291456 | tf_op jit(solution)/shard_map/slice | solution.py:365
  17.4 0.8 fusion.1
  18.2 0.0 all-gather.5.cloned.1.call-update
  18.2 2.5 collective-permute-start.4
  20.7 23.9 %collective-permute-done.4.refs_3_ = bf16[16,2,128,128]{3,2,1,0:T(8,128)(2,1)S(1)} collective-permute-done((bf16[16,2,128,128]{3,2,1,0:T(8,128)(2,1)S(1)}, bf16[16,2,128,128]{3,2,1,0:T(8,128)(2,1)S(1)}, u32[]{:S(2)}, u32[]{:S(2)}) %collective-permute-start.4) | collective-permute-done | bytes 1048608 | tf_op jit(solution)/shard_map/ppermute | solution.py:29
  44.7 0.1 collective-permute-start.5
  44.8 1.6 collective-permute-start.3
  46.4 0.2 collective-permute-start.6
  46.6 9.1 %all-gather.5.cloned.1.call-done = bf16[512,1408]{1,0:T(8,128)(2,1)} async-done(((bf16[128,1408]{1,0:T(8,128)(2,1)}), bf16[512,1408]{1,0:T(8,128)(2,1)}) %all-gather.5.cloned.1.call-update) | async-done | bytes 1441808 | tf_op jit(solution)/shard_map/all_gather | solution.py:375
  55.7 0.7 slice.28
  56.4 0.0 collective-permute-done.5.refs_4_
  56.4 1.4 copy-done
  57.8 15.2 %shard_map.87 = bf16[4,672,128]{2,1,0:T(8,128)(2,1)} custom-call(s32[4,128]{1,0:T(4,128)S(1)} %fusion.2.numbers, s32[2]{0:T(128)S(1)} %copy-done.7, bf16[4,128,1408]{2,1,0:T(8,128)(2,1)S(1)} %bitcast.14, bf16[16,2,128,128]{3,2,1,0:T(8,128)(2,1)S(1)} %slice.21.refs_1_, bf16[16,2,128,512]{3,2,1,0:T(8,128)(2,1)} %collective-permute-done.refs_2_, ...), custom_call_target="tpu_custom_call" | custom-call | flops 1 | bytes 1 | tf_op jit(solution)/shard_map/pallas_call | solution.py:229
  73.1 0.3 collective-permute-done.3.refs_3_
  73.4 3.0 collective-permute-start.2
  76.3 4.2 %all-to-all-start = ((bf16[4,672,128]{2,1,0:T(8,128)(2,1)}), bf16[4,672,128]{2,1,0:T(8,128)(2,1)}, u32[]{:S(2)}, u32[]{:S(2)}) async-start(bf16[4,672,128]{2,1,0:T(8,128)(2,1)} %shard_map.87), calls=%async_computation | async-start | bytes 1376256 | tf_op jit(solution)/shard_map/all_to_all | solution.py:348
  80.5 0.0 all-gather.7.cloned.1.call-start
  80.6 1.8 slice.25
  82.3 0.0 all-gather.7.cloned.1.call-update
  82.4 26.5 %all-to-all-done.parts = bf16[4,672,128]{2,1,0:T(8,128)(2,1)} async-done(((bf16[4,672,128]{2,1,0:T(8,128)(2,1)}), bf16[4,672,128]{2,1,0:T(8,128)(2,1)}, u32[]{:S(2)}, u32[]{:S(2)}) %all-to-all-start) | async-done | bytes 688160 | tf_op jit(solution)/shard_map/all_to_all | solution.py:348
  108.8 2.4 shard_map.89.refs_0_
  111.2 13.4 %shard_map.88 = bf16[4,672,128]{2,1,0:T(8,128)(2,1)S(1)} custom-call(s32[4,128]{1,0:T(4,128)S(1)} %fusion.2.numbers, s32[2]{0:T(128)S(1)} %copy-done.7, bf16[4,128,1408]{2,1,0:T(8,128)(2,1)S(1)} %bitcast.15, bf16[16,2,128,128]{3,2,1,0:T(8,128)(2,1)} %get-tuple-element.18.refs_1_, bf16[16,2,128,512]{3,2,1,0:T(8,128)(2,1)} %collective-permute-done.refs_2_, ...), custom_call_target="tpu_custom_call" | custom-call | flops 1 | bytes 1 | tf_op jit(solution)/shard_map/pallas_call | solution.py:229
  124.6 0.1 collective-permute-start.8
  124.7 0.1 collective-permute-start.1
  124.7 22.0 %all_to_all.20.parts = bf16[4,672,128]{2,1,0:T(8,128)(2,1)} all-to-all(bf16[4,672,128]{2,1,0:T(8,128)(2,1)S(1)} %shard_map.88), channel_id=1, replica_groups={{0,4,8,12},{1,5,9,13},{2,6,10,14},{3,7,11,15},{16,20,24,28},{17,21,25,2..., dimensions={0} | all-to-all | bytes 1376256 | tf_op jit(solution)/shard_map/all_to_all | solution.py:348
  146.8 2.4 shard_map.91.refs_0_
  149.1 0.0 all-gather.7.cloned.1.call-done
  149.2 1.1 copy-done.5
  150.2 1.3 copy-done.2
  151.5 1.2 copy-done.6
  152.8 14.2 %shard_map.90 = bf16[4,672,128]{2,1,0:T(8,128)(2,1)} custom-call(s32[4,128]{1,0:T(4,128)S(1)} %fusion.2.numbers, s32[2]{0:T(128)S(1)} %copy-done.7, bf16[4,128,1280]{2,1,0:T(8,128)(2,1)S(1)} %bitcast.16, bf16[16,2,128,128]{3,2,1,0:T(8,128)(2,1)} %get-tuple-element.16.refs_1_, bf16[16,2,128,512]{3,2,1,0:T(8,128)(2,1)} %collective-permute-done.refs_2_, ...), custom_call_target="tpu_custom_call" | custom-call | flops 1 | bytes 1 | tf_op jit(solution)/shard_map/pallas_call | solution.py:229
  167.0 0.1 collective-permute-start.9
  167.1 3.5 %all-to-all-start.3 = ((bf16[4,672,128]{2,1,0:T(8,128)(2,1)}), bf16[4,672,128]{2,1,0:T(8,128)(2,1)S(1)}, u32[]{:S(2)}, u32[]{:S(2)}) async-start(bf16[4,672,128]{2,1,0:T(8,128)(2,1)} %shard_map.90), calls=%async_computation.3 | async-start | bytes 1376256 | tf_op jit(solution)/shard_map/all_to_all | solution.py:348
  170.6 14.0 %shard_map.92 = bf16[4,672,128]{2,1,0:T(8,128)(2,1)} custom-call(s32[4,128]{1,0:T(4,128)S(1)} %fusion.2.numbers, s32[2]{0:T(128)S(1)} %copy-done.7, bf16[4,128,1280]{2,1,0:T(8,128)(2,1)S(1)} %bitcast.17, bf16[16,2,128,128]{3,2,1,0:T(8,128)(2,1)S(1)} %get-tuple-element.17.refs_1_, bf16[16,2,128,512]{3,2,1,0:T(8,128)(2,1)} %collective-permute-done.refs_2_, ...), custom_call_target="tpu_custom_call" | custom-call | flops 1 | bytes 1 | tf_op jit(solution)/shard_map/pallas_call | solution.py:229
  184.6 4.8 %all-to-all-done.3.parts = bf16[4,672,128]{2,1,0:T(8,128)(2,1)S(1)} async-done(((bf16[4,672,128]{2,1,0:T(8,128)(2,1)}), bf16[4,672,128]{2,1,0:T(8,128)(2,1)S(1)}, u32[]{:S(2)}, u32[]{:S(2)}) %all-to-all-start.3) | async-done | bytes 688160 | tf_op jit(solution)/shard_map/all_to_all | solution.py:348
  189.5 3.5 %all-to-all-start.2 = ((bf16[4,672,128]{2,1,0:T(8,128)(2,1)}), bf16[4,672,128]{2,1,0:T(8,128)(2,1)S(1)}, u32[]{:S(2)}, u32[]{:S(2)}) async-start(bf16[4,672,128]{2,1,0:T(8,128)(2,1)} %shard_map.92), calls=%async_computation.2 | async-start | bytes 1376256 | tf_op jit(solution)/shard_map/all_to_all | solution.py:348
  193.6 2.4 shard_map.93.refs_0_
  196.0 128.3 %shard_map.95 = bf16[16,2,128,512]{3,2,1,0:T(8,128)(2,1)} custom-call(s32[1]{0:T(128)} %bitcast.12.slot, bf16[16,2,128,512]{3,2,1,0:T(8,128)(2,1)} %pool.1, bf16[1,2,128,512]{3,2,1,0:T(8,128)(2,1)} %collective-permute-done.6.incoming), custom_call_target="tpu_custom_call" | custom-call | flops 1 | bytes 1 | tf_op jit(solution)/shard_map/pallas_call | solution.py:265
  324.3 0.9 copy-done.9
  325.2 2.4 shard_map.94
  (25 shorter events, 0.1 us)
Async XLA Ops:
  7.2 10.2 %slice-start = ((bf16[128,2560]{1,0:T(8,128)(2,1)}), bf16[128,1280]{1,0:T(8,128)(2,1)S(1)}, s32[]{:S(2)}) async-start(bf16[128,2560]{1,0:T(8,128)(2,1)} %param.7), calls=%async_computation.6 | async-start | bytes 655360 | tf_op jit(solution)/shard_map/slice | solution.py:373
  7.2 48.5 %all-gather.5.cloned.1.call-start = ((), (), s32[]{:S(2)}) async-start(), calls=%async_computation.4 | async-start | bytes 1802240 | tf_op jit(solution)/shard_map/all_gather | solution.py:375
  8.6 37.9 %copy-start.4 = (bf16[1,1,2,128,512]{4,3,2,1,0:T(8,128)(2,1)S(1)}, bf16[1,1,2,128,512]{4,3,2,1,0:T(8,128)(2,1)}, u32[]{:S(2)}) copy-start(bf16[1,1,2,128,512]{4,3,2,1,0:T(8,128)(2,1)} %param.8) | copy-start | bytes 786436
  8.6 47.8 %collective-permute-start = (bf16[16,2,128,512]{3,2,1,0:T(8,128)(2,1)}, bf16[16,2,128,512]{3,2,1,0:T(8,128)(2,1)}, u32[]{:S(2)}, u32[]{:S(2)}) collective-permute-start(bf16[16,2,128,512]{3,2,1,0:T(8,128)(2,1)} %pool.1), channel_id=1, source_target_pairs={{0,1},{1,0},{2,3},{3,2},{4,5},{5,4},{6,7},{7,6},{8,9},{9,8},{10,11... | collective-permute-start | bytes 12582920 | tf_op jit(solution)/shard_map/ppermute | solution.py:29
  10.3 46.1 %copy-start.7 = (s32[2]{0:T(128)S(1)}, s32[2]{0:T(128)}, u32[]{:S(2)}) copy-start(s32[2]{0:T(128)} %pad_add_fusion.mine) | copy-start | bytes 28
  18.2 26.5 %collective-permute-start.4 = (bf16[16,2,128,128]{3,2,1,0:T(8,128)(2,1)S(1)}, bf16[16,2,128,128]{3,2,1,0:T(8,128)(2,1)S(1)}, u32[]{:S(2)}, u32[]{:S(2)}) collective-permute-start(bf16[16,2,128,128]{3,2,1,0:T(8,128)(2,1)S(1)} %slice.21.refs_1_), channel_id=1, source_target_pairs={{0,2},{1,3},{2,0},{3,1},{4,6},{5,7},{6,4},{7,5},{8,10},{9,11},{10,... | collective-permute-start | bytes 3145736 | tf_op jit(solution)/shard_map/ppermute | solution.py:29
  44.7 11.7 %collective-permute-start.5 = (bf16[16,2,128,128]{3,2,1,0:T(8,128)(2,1)S(1)}, bf16[16,2,128,128]{3,2,1,0:T(8,128)(2,1)}, u32[]{:S(2)}, u32[]{:S(2)}) collective-permute-start(bf16[16,2,128,128]{3,2,1,0:T(8,128)(2,1)S(1)} %collective-permute-done.4.refs_3_), channel_id=1, source_target_pairs={{0,1},{1,0},{2,3},{3,2},{4,5},{5,4},{6,7},{7,6},{8,9},{9,8},{10,11... | collective-permute-start | bytes 3145736 | tf_op jit(solution)/shard_map/ppermute | solution.py:29
  44.8 28.6 %collective-permute-start.3 = (bf16[16,2,128,128]{3,2,1,0:T(8,128)(2,1)}, bf16[16,2,128,128]{3,2,1,0:T(8,128)(2,1)}, u32[]{:S(2)}, u32[]{:S(2)}) collective-permute-start(bf16[16,2,128,128]{3,2,1,0:T(8,128)(2,1)} %get-tuple-element.18.refs_1_), channel_id=1, source_target_pairs={{0,2},{1,3},{2,0},{3,1},{4,6},{5,7},{6,4},{7,5},{8,10},{9,11},{10,... | collective-permute-start | bytes 3145736 | tf_op jit(solution)/shard_map/ppermute | solution.py:29
  46.4 26.6 %collective-permute-start.6 = (bf16[1,2,128,512]{3,2,1,0:T(8,128)(2,1)S(1)}, bf16[1,2,128,512]{3,2,1,0:T(8,128)(2,1)}, u32[]{:S(2)}, u32[]{:S(2)}) collective-permute-start(bf16[1,2,128,512]{3,2,1,0:T(8,128)(2,1)S(1)} %bitcast.18), channel_id=1, source_target_pairs={{0,1},{1,2},{2,3},{3,4},{4,5},{5,6},{6,7},{7,8},{8,9},{9,10},{10,1... | collective-permute-start | bytes 786440 | tf_op jit(solution)/shard_map/ppermute | solution.py:34
  56.4 1.4 copy-start
  73.0 38.1 %copy-start.1 = (bf16[512,1408]{1,0:T(8,128)(2,1)S(1)}, bf16[512,1408]{1,0:T(8,128)(2,1)}, u32[]{:S(2)}) copy-start(bf16[512,1408]{1,0:T(8,128)(2,1)} %all-gather.5.cloned.1.call-done) | copy-start | bytes 4325380
  73.4 37.8 %collective-permute-start.7 = (bf16[16,2,128,128]{3,2,1,0:T(8,128)(2,1)}, bf16[16,2,128,128]{3,2,1,0:T(8,128)(2,1)}, u32[]{:S(2)}, u32[]{:S(2)}) collective-permute-start(bf16[16,2,128,128]{3,2,1,0:T(8,128)(2,1)} %collective-permute-done.3.refs_3_), channel_id=1, source_target_pairs={{0,1},{1,0},{2,3},{3,2},{4,5},{5,4},{6,7},{7,6},{8,9},{9,8},{10,11... | collective-permute-start | bytes 3145736 | tf_op jit(solution)/shard_map/ppermute | solution.py:29
  73.4 51.2 %collective-permute-start.2 = (bf16[16,2,128,128]{3,2,1,0:T(8,128)(2,1)}, bf16[16,2,128,128]{3,2,1,0:T(8,128)(2,1)}, u32[]{:S(2)}, u32[]{:S(2)}) collective-permute-start(bf16[16,2,128,128]{3,2,1,0:T(8,128)(2,1)} %get-tuple-element.16.refs_1_), channel_id=1, source_target_pairs={{0,2},{1,3},{2,0},{3,1},{4,6},{5,7},{6,4},{7,5},{8,10},{9,11},{10,... | collective-permute-start | bytes 3145736 | tf_op jit(solution)/shard_map/ppermute | solution.py:29
  76.3 32.5 %all-to-all-start = ((bf16[4,672,128]{2,1,0:T(8,128)(2,1)}), bf16[4,672,128]{2,1,0:T(8,128)(2,1)}, u32[]{:S(2)}, u32[]{:S(2)}) async-start(bf16[4,672,128]{2,1,0:T(8,128)(2,1)} %shard_map.87), calls=%async_computation | async-start | bytes 1376256 | tf_op jit(solution)/shard_map/all_to_all | solution.py:348
  80.5 68.6 %all-gather.7.cloned.1.call-start = ((), (), s32[]{:S(2)}) async-start(), calls=%async_computation.5 | async-start | bytes 1638400 | tf_op jit(solution)/shard_map/all_gather | solution.py:376
  124.6 24.6 %collective-permute-start.8 = (bf16[16,2,128,128]{3,2,1,0:T(8,128)(2,1)}, bf16[16,2,128,128]{3,2,1,0:T(8,128)(2,1)S(1)}, u32[]{:S(2)}, u32[]{:S(2)}) collective-permute-start(bf16[16,2,128,128]{3,2,1,0:T(8,128)(2,1)} %collective-permute-done.2.refs_3_), channel_id=1, source_target_pairs={{0,1},{1,0},{2,3},{3,2},{4,5},{5,4},{6,7},{7,6},{8,9},{9,8},{10,11... | collective-permute-start | bytes 3145736 | tf_op jit(solution)/shard_map/ppermute | solution.py:29
  124.7 42.3 %collective-permute-start.1 = (bf16[16,2,128,128]{3,2,1,0:T(8,128)(2,1)S(1)}, bf16[16,2,128,128]{3,2,1,0:T(8,128)(2,1)}, u32[]{:S(2)}, u32[]{:S(2)}) collective-permute-start(bf16[16,2,128,128]{3,2,1,0:T(8,128)(2,1)S(1)} %get-tuple-element.17.refs_1_), channel_id=1, source_target_pairs={{0,2},{1,3},{2,0},{3,1},{4,6},{5,7},{6,4},{7,5},{8,10},{9,11},{10,... | collective-permute-start | bytes 3145736 | tf_op jit(solution)/shard_map/ppermute | solution.py:29
  149.1 1.1 copy-start.5
  150.2 1.3 copy-start.2
  151.5 1.2 copy-start.6
  152.8 17.8 %copy-start.3 = (bf16[512,1280]{1,0:T(8,128)(2,1)S(1)}, bf16[512,1280]{1,0:T(8,128)(2,1)}, u32[]{:S(2)}) copy-start(bf16[512,1280]{1,0:T(8,128)(2,1)} %all-gather.7.cloned.1.call-done) | copy-start | bytes 3932164
  167.0 3.6 %collective-permute-start.9 = (bf16[16,2,128,128]{3,2,1,0:T(8,128)(2,1)}, bf16[16,2,128,128]{3,2,1,0:T(8,128)(2,1)}, u32[]{:S(2)}, u32[]{:S(2)}) collective-permute-start(bf16[16,2,128,128]{3,2,1,0:T(8,128)(2,1)} %collective-permute-done.1.refs_3_), channel_id=1, source_target_pairs={{0,1},{1,0},{2,3},{3,2},{4,5},{5,4},{6,7},{7,6},{8,9},{9,8},{10,11... | collective-permute-start | bytes 3145736 | tf_op jit(solution)/shard_map/ppermute | solution.py:29
  167.1 22.4 %all-to-all-start.3 = ((bf16[4,672,128]{2,1,0:T(8,128)(2,1)}), bf16[4,672,128]{2,1,0:T(8,128)(2,1)S(1)}, u32[]{:S(2)}, u32[]{:S(2)}) async-start(bf16[4,672,128]{2,1,0:T(8,128)(2,1)} %shard_map.90), calls=%async_computation.3 | async-start | bytes 1376256 | tf_op jit(solution)/shard_map/all_to_all | solution.py:348
  189.5 4.1 %copy-start.8 = (bf16[4,672,128]{2,1,0:T(8,128)(2,1)}, bf16[4,672,128]{2,1,0:T(8,128)(2,1)S(1)}, u32[]{:S(2)}) copy-start(bf16[4,672,128]{2,1,0:T(8,128)(2,1)S(1)} %all-to-all-done.3.parts) | copy-start | bytes 2064388
  189.5 134.8 %all-to-all-start.2 = ((bf16[4,672,128]{2,1,0:T(8,128)(2,1)}), bf16[4,672,128]{2,1,0:T(8,128)(2,1)S(1)}, u32[]{:S(2)}, u32[]{:S(2)}) async-start(bf16[4,672,128]{2,1,0:T(8,128)(2,1)} %shard_map.92), calls=%async_computation.2 | async-start | bytes 1376256 | tf_op jit(solution)/shard_map/all_to_all | solution.py:348
  324.3 0.9 copy-start.9
Sparse Core Ops, SparseCore 0:
  18.3 37.3 all-gather.4
  82.9 37.5 all-gather.6

commit v9 on v5

--- a/solution.py
+++ b/solution.py
@@ -249,14 +249,14 @@
         num_scalar_prefetch=5,
         grid=(),
         in_specs=[pl.BlockSpec(memory_space=pl.ANY)] * len(operands),
-        out_specs=[pl.BlockSpec(memory_space=pl.ANY), pl.BlockSpec(memory_space=pltpu.HBM)][:len(out_shape)],
+        out_specs=[pl.BlockSpec(memory_space=pltpu.HBM)] * len(out_shape),
         scratch_shapes=scratch,
     )
     return pl.pallas_call(
         functools.partial(attend_kernel, lines, head, q_head),
         grid_spec=grid_spec,
         out_shape=out_shape,
-        compiler_params=pltpu.CompilerParams(vmem_limit_bytes=24 * 2**20),
+        compiler_params=pltpu.CompilerParams(vmem_limit_bytes=16 * 2**20),
         cost_estimate=pl.CostEstimate(flops=1, bytes_accessed=1, transcendentals=0),
     )(picks, counts, lasts, mine, store, *operands)
 
@@ -340,7 +340,7 @@
     incoming = shifted(new_kv[0], "serve", 1)
     rows = page_rows(me, lines, limit, slots, page_owner, page_slot, prefix_len).astype(queries.dtype)
     rows = jnp.pad(rows[:, None], ((0, 0), (0, 15), (0, CHUNK - limit - 2)))
-    early = after(queries, owns[1])[:, :CHUNK]
+    early = after(queries, owns[1], twin)[:, :CHUNK]
     early = jnp.concatenate([jnp.broadcast_to(early[None], (lines, PAGE, CHUNK)), rows], axis=1)
     early = exchanged(early, groups)
     later = after(queries, sides[0], incoming)[None, :, CHUNK:]

time: 192 us -> 194 us (1.010)
  Pallas kernels: 67.6 us -> 63.6 us
  waiting for transfers between devices: 69.7 us -> 72.5 us
  starting transfers between devices: 31.7 us -> 33.8 us
    pallas_call x4, Pallas kernels: 58.2 us -> 54.2 us  [attend(): pl.pallas_call(functools.partial(attend_kernel, lines, head, q_head), gri...]
    ppermute x9, waiting for transfers between devices: 18.4 us -> 21.2 us  [swapped(): return lax.ppermute(array, axis, [(i, i ^ bit) for i in range(size)])]
    all_to_all x6, starting transfers between devices: 26.7 us -> 28.8 us  [exchanged(): lax.all_to_all(array, 'serve', 0, 0, axis_index_groups=groups, tiled=True)]
  transfers between devices with their start and end apart: 16 -> 16, of which waited for: 7 -> 8; matrix products, arithmetic and copies ran while one was open for 4% -> 3% of each run, Pallas kernels for 34% -> 32%
where the time goes in v9:
time: 194 us; the launch traced here: 193 us
  waiting for transfers between devices  72.5 us (37%)
  Pallas kernels  63.6 us (33%)
  starting transfers between devices  33.8 us (17%)
  local copies, waits for them, and re-layouts  18.3 us (9%)
  other arithmetic  2.31 us (1%)
  between operations  2.26 us (1%)
    pallas_call x4, Pallas kernels, attend(): pl.pallas_call(functools.partial(attend_kernel, lines, head, q_head), gri...  54.2 us
    all_to_all x6, waiting for transfers between devices, exchanged(): lax.all_to_all(array, 'serve', 0, 0, axis_index_groups=groups, tiled=True)  32.4 us
    all_to_all x6, starting transfers between devices, exchanged(): lax.all_to_all(array, 'serve', 0, 0, axis_index_groups=groups, tiled=True)  28.8 us
    ppermute x9, waiting for transfers between devices, swapped(): return lax.ppermute(array, axis, [(i, i ^ bit) for i in range(size)])  21.2 us
    ppermute x1, waiting for transfers between devices, shifted(): lax.ppermute(array, axis, [(i, (i + by) % size) for i in range(size)])  18.8 us
    unnamed x30, local copies, waits for them, and re-layouts  11.1 us
    pallas_call x4, Pallas kernels, merge(): pl.pallas_call(functools.partial(merge_kernel, head), in_specs=[pl.BlockS...  9.41 us
    ppermute x9, starting transfers between devices, swapped(): return lax.ppermute(array, axis, [(i, i ^ bit) for i in range(size)])  4.96 us
  transfers between devices with their start and end apart: 16, of which 8 were waited for; matrix products, arithmetic and copies ran while one was open for 3% of the time, Pallas kernels for 32%

profile of v9, /device:TPU:0, one launch (start us, length us, event | category | flops | bytes accessed | tf_op | source)
XLA Modules:
  0.0 192.7 jit_solution(8857087502809275610)
XLA Ops:
  0.6 1.3 slice.30.refs_1_
  2.0 0.5 collective-permute-start
  3.2 0.1 convert_reduce_fusion.1
  3.4 0.1 convert_reduce_fusion
  3.5 0.1 select_reduce_fusion
  3.7 0.1 and_reduce_fusion
  3.9 0.1 copy.20
  4.0 0.1 copy.19
  4.2 3.8 %fusion.17 = (bf16[16,2,128,128]{3,2,1,0:T(8,128)(2,1)}, bf16[16,2,128,128]{3,2,1,0:T(8,128)(2,1)}, bf16[16,2,128,128]{3,2,1,0:T(8,128)(2,1)}) fusion(bf16[16,2,128,512]{3,2,1,0:T(8,128)(2,1)} %refs_6_.1), kind=kLoop, calls=%fused_computation.41 | loop fusion | bytes 6291456 | tf_op jit(solution)/shard_map/slice | solution.py:337
  8.0 1.7 collective-permute-done.refs_2_
  9.7 0.9 pad_maximum_fusion
  10.6 6.2 %all-to-all-start = ((bf16[4,144,640]{2,1,0:T(8,128)(2,1)}), bf16[4,144,640]{2,1,0:T(8,128)(2,1)S(1)}, u32[]{:S(2)}, u32[]{:S(2)}) async-start(bf16[4,144,640]{2,1,0:T(8,128)(2,1)} %pad_maximum_fusion), calls=%async_computation | async-start | bytes 1474560 | tf_op jit(solution)/shard_map/all_to_all | solution.py:320
  16.9 1.5 collective-permute-start.1
  18.4 18.8 %collective-permute-done.2.refs_7_ = bf16[1,2,128,512]{3,2,1,0:T(8,128)(2,1)S(1)} collective-permute-done((bf16[1,2,128,512]{3,2,1,0:T(8,128)(2,1)S(1)}, bf16[1,2,128,512]{3,2,1,0:T(8,128)(2,1)S(1)}, u32[]{:S(2)}, u32[]{:S(2)}) %collective-permute-start.2) | collective-permute-done | bytes 262176 | tf_op jit(solution)/shard_map/ppermute | solution.py:34
  37.2 7.5 %collective-permute-done.1.refs_3_ = bf16[16,2,128,128]{3,2,1,0:T(8,128)(2,1)} collective-permute-done((bf16[16,2,128,128]{3,2,1,0:T(8,128)(2,1)S(1)}, bf16[16,2,128,128]{3,2,1,0:T(8,128)(2,1)}, u32[]{:S(2)}, u32[]{:S(2)}) %collective-permute-start.1) | collective-permute-done | bytes 1048608 | tf_op jit(solution)/shard_map/ppermute | solution.py:29
  44.7 1.6 broadcast_in_dim.32
  46.3 4.8 %all-to-all-start.1 = ((bf16[4,128,1920]{2,1,0:T(8,128)(2,1)}), bf16[4,128,1920]{2,1,0:T(8,128)(2,1)S(1)}, u32[]{:S(2)}, u32[]{:S(2)}) async-start(bf16[4,128,1920]{2,1,0:T(8,128)(2,1)} %broadcast_in_dim.32), calls=%async_computation.1 | async-start | bytes 3932160 | tf_op jit(solution)/shard_map/all_to_all | solution.py:320
  51.1 1.4 collective-permute-start.5
  53.2 0.7 slice_convert_fusion
  53.9 0.2 slice_reduce_fusion
  54.1 2.2 %copy-done = bf16[16,2,128,512]{3,2,1,0:T(8,128)(2,1)S(1)} copy-done((bf16[16,2,128,512]{3,2,1,0:T(8,128)(2,1)S(1)}, bf16[16,2,128,512]{3,2,1,0:T(8,128)(2,1)}, u32[]{:S(2)}) %copy-start) | copy-done | bytes 4194328
  56.3 1.1 copy-done.5
  57.4 13.8 %shard_map.86 = (bf16[4,672,128]{2,1,0:T(8,128)(2,1)S(1)}, bf16[16,2,128,512]{3,2,1,0:T(8,128)(2,1)}) custom-call(s32[4,16]{1,0:T(4,128)S(1)} %bitcast.31, s32[4]{0:T(128)S(1)} %get-tuple-element.19.counts, s32[4]{0:T(128)S(1)} %get-tuple-element.18.lasts, s32[1]{0:T(128)} %bitcast.8.mine, s32[1]{0:T(128)} %bitcast.21.store, ...), custom_call_target="tpu_custom_call" | custom-call | flops 1 | bytes 1 | tf_op jit(solution)/shard_map/pallas_call | solution.py:255
  71.3 0.9 copy-done.11
  72.2 4.8 %collective-permute-done.5.refs_3_ = bf16[16,2,128,128]{3,2,1,0:T(8,128)(2,1)} collective-permute-done((bf16[16,2,128,128]{3,2,1,0:T(8,128)(2,1)}, bf16[16,2,128,128]{3,2,1,0:T(8,128)(2,1)}, u32[]{:S(2)}, u32[]{:S(2)}) %collective-permute-start.5) | collective-permute-done | bytes 1048608 | tf_op jit(solution)/shard_map/ppermute | solution.py:29
  77.0 1.4 collective-permute-start.4
  78.4 17.3 %all-to-all-done.1.refs_0_ = bf16[4,128,1920]{2,1,0:T(8,128)(2,1)S(1)} async-done(((bf16[4,128,1920]{2,1,0:T(8,128)(2,1)}), bf16[4,128,1920]{2,1,0:T(8,128)(2,1)S(1)}, u32[]{:S(2)}, u32[]{:S(2)}) %all-to-all-start.1) | async-done | bytes 1966112 | tf_op jit(solution)/shard_map/all_to_all | solution.py:320
  95.7 4.2 %all-to-all-start.5 = ((bf16[4,672,128]{2,1,0:T(8,128)(2,1)}), bf16[4,672,128]{2,1,0:T(8,128)(2,1)}, u32[]{:S(2)}, u32[]{:S(2)}) async-start(bf16[4,672,128]{2,1,0:T(8,128)(2,1)} %copy-done.11), calls=%async_computation.5 | async-start | bytes 1376256 | tf_op jit(solution)/shard_map/all_to_all | solution.py:320
  99.9 1.0 copy-done.9
  100.9 1.2 copy-done.3
  102.1 1.2 copy-done.10
  103.3 14.4 %shard_map.87 = bf16[4,672,128]{2,1,0:T(8,128)(2,1)S(1)} custom-call(s32[4,16]{1,0:T(4,128)S(1)} %bitcast.32, s32[4]{0:T(128)S(1)} %get-tuple-element.19.counts, s32[4]{0:T(128)S(1)} %get-tuple-element.18.lasts, s32[1]{0:T(128)} %bitcast.8.mine, s32[1]{0:T(128)} %bitcast.22.store, bf16[4,128,1920]{2,1,0:T(8,128)(2,1)S(1)} %all-to-all-done.1.refs_0_, ...), custom_call_target="tpu_custom_call" | custom-call | flops 1 | bytes 1 | tf_op jit(solution)/shard_map/pallas_call | solution.py:255
  117.8 0.9 copy-done.6
  118.8 5.1 %all-to-all-start.4 = ((bf16[4,672,128]{2,1,0:T(8,128)(2,1)}), bf16[4,672,128]{2,1,0:T(8,128)(2,1)}, u32[]{:S(2)}, u32[]{:S(2)}) async-start(bf16[4,672,128]{2,1,0:T(8,128)(2,1)} %copy-done.6), calls=%async_computation.4 | async-start | bytes 1376256 | tf_op jit(solution)/shard_map/all_to_all | solution.py:320
  123.8 12.4 %shard_map.88 = bf16[4,672,128]{2,1,0:T(8,128)(2,1)S(1)} custom-call(s32[4,16]{1,0:T(4,128)S(1)} %bitcast.33, s32[4]{0:T(128)S(1)} %get-tuple-element.19.counts, s32[4]{0:T(128)S(1)} %get-tuple-element.18.lasts, s32[1]{0:T(128)} %bitcast.8.mine, s32[1]{0:T(128)} %bitcast.23.store, bf16[4,128,1920]{2,1,0:T(8,128)(2,1)S(1)} %all-to-all-done.1.refs_0_, ...), custom_call_target="tpu_custom_call" | custom-call | flops 1 | bytes 1 | tf_op jit(solution)/shard_map/pallas_call | solution.py:255
  136.3 0.9 copy-done.7
  137.2 7.2 %collective-permute-done.3.refs_3_ = bf16[16,2,128,128]{3,2,1,0:T(8,128)(2,1)} collective-permute-done((bf16[16,2,128,128]{3,2,1,0:T(8,128)(2,1)S(1)}, bf16[16,2,128,128]{3,2,1,0:T(8,128)(2,1)}, u32[]{:S(2)}, u32[]{:S(2)}) %collective-permute-start.3) | collective-permute-done | bytes 1048608 | tf_op jit(solution)/shard_map/ppermute | solution.py:29
  144.4 5.0 %all-to-all-start.3 = ((bf16[4,672,128]{2,1,0:T(8,128)(2,1)}), bf16[4,672,128]{2,1,0:T(8,128)(2,1)}, u32[]{:S(2)}, u32[]{:S(2)}) async-start(bf16[4,672,128]{2,1,0:T(8,128)(2,1)} %copy-done.7), calls=%async_computation.3 | async-start | bytes 1376256 | tf_op jit(solution)/shard_map/all_to_all | solution.py:320
  149.4 13.5 %shard_map.89 = bf16[4,672,128]{2,1,0:T(8,128)(2,1)S(1)} custom-call(s32[4,16]{1,0:T(4,128)S(1)} %bitcast.34, s32[4]{0:T(128)S(1)} %get-tuple-element.19.counts, s32[4]{0:T(128)S(1)} %get-tuple-element.18.lasts, s32[1]{0:T(128)} %bitcast.8.mine, s32[1]{0:T(128)} %bitcast.24.store, bf16[4,128,1920]{2,1,0:T(8,128)(2,1)S(1)} %all-to-all-done.1.refs_0_, ...), custom_call_target="tpu_custom_call" | custom-call | flops 1 | bytes 1 | tf_op jit(solution)/shard_map/pallas_call | solution.py:255
  162.9 0.9 copy-done.8
  163.8 4.4 %all-to-all-done.3.parts = bf16[4,672,128]{2,1,0:T(8,128)(2,1)} async-done(((bf16[4,672,128]{2,1,0:T(8,128)(2,1)}), bf16[4,672,128]{2,1,0:T(8,128)(2,1)}, u32[]{:S(2)}, u32[]{:S(2)}) %all-to-all-start.3) | async-done | bytes 688160 | tf_op jit(solution)/shard_map/all_to_all | solution.py:320
  168.2 3.5 %all-to-all-start.2 = ((bf16[4,672,128]{2,1,0:T(8,128)(2,1)}), bf16[4,672,128]{2,1,0:T(8,128)(2,1)S(1)}, u32[]{:S(2)}, u32[]{:S(2)}) async-start(bf16[4,672,128]{2,1,0:T(8,128)(2,1)} %copy-done.8), calls=%async_computation.2 | async-start | bytes 1376256 | tf_op jit(solution)/shard_map/all_to_all | solution.py:320
  171.7 2.4 %shard_map.90.refs_0_ = bf16[128,2560]{1,0:T(8,128)(2,1)} custom-call(bf16[4,672,128]{2,1,0:T(8,128)(2,1)} %all-to-all-done.5.parts), custom_call_target="tpu_custom_call" | custom-call | flops 1 | bytes 1 | tf_op jit(solution)/shard_map/pallas_call | solution.py:292
  174.0 2.4 %shard_map.91.refs_0_ = bf16[128,2560]{1,0:T(8,128)(2,1)} custom-call(bf16[4,672,128]{2,1,0:T(8,128)(2,1)} %all-to-all-done.4.parts, bf16[128,2560]{1,0:T(8,128)(2,1)} %shard_map.90.refs_0_), custom_call_target="tpu_custom_call", output_to_operand_aliasing={{}: (1, {})} | custom-call | flops 1 | bytes 1 | tf_op jit(solution)/shard_map/pallas_call | solution.py:292
  176.4 2.4 %shard_map.92.refs_0_ = bf16[128,2560]{1,0:T(8,128)(2,1)} custom-call(bf16[4,672,128]{2,1,0:T(8,128)(2,1)} %all-to-all-done.3.parts, bf16[128,2560]{1,0:T(8,128)(2,1)} %shard_map.91.refs_0_), custom_call_target="tpu_custom_call", output_to_operand_aliasing={{}: (1, {})} | custom-call | flops 1 | bytes 1 | tf_op jit(solution)/shard_map/pallas_call | solution.py:292
  178.8 10.7 %all-to-all-done.2.parts = bf16[4,672,128]{2,1,0:T(8,128)(2,1)S(1)} async-done(((bf16[4,672,128]{2,1,0:T(8,128)(2,1)}), bf16[4,672,128]{2,1,0:T(8,128)(2,1)S(1)}, u32[]{:S(2)}, u32[]{:S(2)}) %all-to-all-start.2) | async-done | bytes 688160 | tf_op jit(solution)/shard_map/all_to_all | solution.py:320
  189.5 0.8 copy-done.12
  190.3 2.4 %shard_map.93 = bf16[128,2560]{1,0:T(8,128)(2,1)} custom-call(bf16[4,672,128]{2,1,0:T(8,128)(2,1)} %copy-done.12, bf16[128,2560]{1,0:T(8,128)(2,1)} %shard_map.92.refs_0_), custom_call_target="tpu_custom_call", output_to_operand_aliasing={{}: (1, {})} | custom-call | flops 1 | bytes 1 | tf_op jit(solution)/shard_map/pallas_call | solution.py:292
  (49 shorter events, 0.4 us)
Async XLA Ops:
  0.6 2.6 %copy-start.13 = (s32[1,48]{1,0:T(1,128)S(1)}, s32[1,48]{1,0:T(1,128)}, u32[]{:S(2)}) copy-start(s32[1,48]{1,0:T(1,128)} %param.10) | copy-start | bytes 580
  0.6 2.9 %copy-start.14 = (s32[1,48]{1,0:T(1,128)S(1)}, s32[1,48]{1,0:T(1,128)}, u32[]{:S(2)}) copy-start(s32[1,48]{1,0:T(1,128)} %param.11) | copy-start | bytes 580
  2.0 7.6 %collective-permute-start = (bf16[16,2,128,512]{3,2,1,0:T(8,128)(2,1)}, bf16[16,2,128,512]{3,2,1,0:T(8,128)(2,1)}, u32[]{:S(2)}, u32[]{:S(2)}) collective-permute-start(bf16[16,2,128,512]{3,2,1,0:T(8,128)(2,1)} %refs_6_.1), channel_id=1, source_target_pairs={{0,1},{1,0},{2,3},{3,2},{4,5},{5,4},{6,7},{7,6},{8,9},{9,8},{10,11... | collective-permute-start | bytes 12582920 | tf_op jit(solution)/shard_map/ppermute | solution.py:29
  4.2 5.5 %slice-start = ((bf16[128,2560]{1,0:T(8,128)(2,1)}), bf16[128,640]{1,0:T(8,128)(2,1)S(1)}, s32[]{:S(2)}) async-start(bf16[128,2560]{1,0:T(8,128)(2,1)} %param.7), calls=%async_computation.6 | async-start | bytes 327680 | tf_op jit(solution)/shard_map/slice | solution.py:343
  9.6 8.8 %copy-start.1 = (bf16[1,1,2,128,512]{4,3,2,1,0:T(8,128)(2,1)S(1)}, bf16[1,1,2,128,512]{4,3,2,1,0:T(8,128)(2,1)}, u32[]{:S(2)}) copy-start(bf16[1,1,2,128,512]{4,3,2,1,0:T(8,128)(2,1)} %param.8) | copy-start | bytes 786436
  9.7 35.0 %slice-start.1 = ((bf16[128,2560]{1,0:T(8,128)(2,1)}), bf16[128,1920]{1,0:T(8,128)(2,1)S(1)}, s32[]{:S(2)}) async-start(bf16[128,2560]{1,0:T(8,128)(2,1)} %param.7), calls=%async_computation.7 | async-start | bytes 983040 | tf_op jit(solution)/shard_map/slice | solution.py:346
  10.6 34.1 %all-to-all-start = ((bf16[4,144,640]{2,1,0:T(8,128)(2,1)}), bf16[4,144,640]{2,1,0:T(8,128)(2,1)S(1)}, u32[]{:S(2)}, u32[]{:S(2)}) async-start(bf16[4,144,640]{2,1,0:T(8,128)(2,1)} %pad_maximum_fusion), calls=%async_computation | async-start | bytes 1474560 | tf_op jit(solution)/shard_map/all_to_all | solution.py:320
  16.9 27.8 %collective-permute-start.1 = (bf16[16,2,128,128]{3,2,1,0:T(8,128)(2,1)S(1)}, bf16[16,2,128,128]{3,2,1,0:T(8,128)(2,1)}, u32[]{:S(2)}, u32[]{:S(2)}) collective-permute-start(bf16[16,2,128,128]{3,2,1,0:T(8,128)(2,1)S(1)} %slice.30.refs_1_), channel_id=1, source_target_pairs={{0,2},{1,3},{2,0},{3,1},{4,6},{5,7},{6,4},{7,5},{8,10},{9,11},{10,... | collective-permute-start | bytes 3145736 | tf_op jit(solution)/shard_map/ppermute | solution.py:29
  18.4 18.8 %collective-permute-start.2 = (bf16[1,2,128,512]{3,2,1,0:T(8,128)(2,1)S(1)}, bf16[1,2,128,512]{3,2,1,0:T(8,128)(2,1)S(1)}, u32[]{:S(2)}, u32[]{:S(2)}) collective-permute-start(bf16[1,2,128,512]{3,2,1,0:T(8,128)(2,1)S(1)} %bitcast.25), channel_id=1, source_target_pairs={{0,1},{1,2},{2,3},{3,4},{4,5},{5,6},{6,7},{7,8},{8,9},{9,10},{10,1... | collective-permute-start | bytes 786440 | tf_op jit(solution)/shard_map/ppermute | solution.py:34
  44.7 1.6 copy-start.4
  46.3 49.4 %all-to-all-start.1 = ((bf16[4,128,1920]{2,1,0:T(8,128)(2,1)}), bf16[4,128,1920]{2,1,0:T(8,128)(2,1)S(1)}, u32[]{:S(2)}, u32[]{:S(2)}) async-start(bf16[4,128,1920]{2,1,0:T(8,128)(2,1)} %broadcast_in_dim.32), calls=%async_computation.1 | async-start | bytes 3932160 | tf_op jit(solution)/shard_map/all_to_all | solution.py:320
  51.1 3.0 %collective-permute-start.6 = (bf16[16,2,128,128]{3,2,1,0:T(8,128)(2,1)}, bf16[16,2,128,128]{3,2,1,0:T(8,128)(2,1)}, u32[]{:S(2)}, u32[]{:S(2)}) collective-permute-start(bf16[16,2,128,128]{3,2,1,0:T(8,128)(2,1)} %collective-permute-done.1.refs_3_), channel_id=1, source_target_pairs={{0,1},{1,0},{2,3},{3,2},{4,5},{5,4},{6,7},{7,6},{8,9},{9,8},{10,11... | collective-permute-start | bytes 3145736 | tf_op jit(solution)/shard_map/ppermute | solution.py:29
  51.1 25.9 %collective-permute-start.5 = (bf16[16,2,128,128]{3,2,1,0:T(8,128)(2,1)}, bf16[16,2,128,128]{3,2,1,0:T(8,128)(2,1)}, u32[]{:S(2)}, u32[]{:S(2)}) collective-permute-start(bf16[16,2,128,128]{3,2,1,0:T(8,128)(2,1)} %get-tuple-element.24.refs_1_), channel_id=1, source_target_pairs={{0,2},{1,3},{2,0},{3,1},{4,6},{5,7},{6,4},{7,5},{8,10},{9,11},{10,... | collective-permute-start | bytes 3145736 | tf_op jit(solution)/shard_map/ppermute | solution.py:29
  54.1 2.2 %copy-start = (bf16[16,2,128,512]{3,2,1,0:T(8,128)(2,1)S(1)}, bf16[16,2,128,512]{3,2,1,0:T(8,128)(2,1)}, u32[]{:S(2)}) copy-start(bf16[16,2,128,512]{3,2,1,0:T(8,128)(2,1)} %refs_6_.1) | copy-start | bytes 12582916
  56.3 1.1 copy-start.5
  71.3 0.9 copy-start.11
  77.0 22.9 %collective-permute-start.7 = (bf16[16,2,128,128]{3,2,1,0:T(8,128)(2,1)}, bf16[16,2,128,128]{3,2,1,0:T(8,128)(2,1)S(1)}, u32[]{:S(2)}, u32[]{:S(2)}) collective-permute-start(bf16[16,2,128,128]{3,2,1,0:T(8,128)(2,1)} %collective-permute-done.5.refs_3_), channel_id=1, source_target_pairs={{0,1},{1,0},{2,3},{3,2},{4,5},{5,4},{6,7},{7,6},{8,9},{9,8},{10,11... | collective-permute-start | bytes 3145736 | tf_op jit(solution)/shard_map/ppermute | solution.py:29
  77.0 41.7 %collective-permute-start.4 = (bf16[16,2,128,128]{3,2,1,0:T(8,128)(2,1)}, bf16[16,2,128,128]{3,2,1,0:T(8,128)(2,1)}, u32[]{:S(2)}, u32[]{:S(2)}) collective-permute-start(bf16[16,2,128,128]{3,2,1,0:T(8,128)(2,1)} %get-tuple-element.22.refs_1_), channel_id=1, source_target_pairs={{0,2},{1,3},{2,0},{3,1},{4,6},{5,7},{6,4},{7,5},{8,10},{9,11},{10,... | collective-permute-start | bytes 3145736 | tf_op jit(solution)/shard_map/ppermute | solution.py:29
  95.7 23.0 %all-to-all-start.5 = ((bf16[4,672,128]{2,1,0:T(8,128)(2,1)}), bf16[4,672,128]{2,1,0:T(8,128)(2,1)}, u32[]{:S(2)}, u32[]{:S(2)}) async-start(bf16[4,672,128]{2,1,0:T(8,128)(2,1)} %copy-done.11), calls=%async_computation.5 | async-start | bytes 1376256 | tf_op jit(solution)/shard_map/all_to_all | solution.py:320
  99.9 1.0 copy-start.9
  100.9 1.2 copy-start.3
  102.1 1.2 copy-start.10
  103.3 15.3 %copy-start.2 = (bf16[16,2,128,128]{3,2,1,0:T(8,128)(2,1)S(1)}, bf16[16,2,128,128]{3,2,1,0:T(8,128)(2,1)}, u32[]{:S(2)}) copy-start(bf16[16,2,128,128]{3,2,1,0:T(8,128)(2,1)} %get-tuple-element.23.refs_1_) | copy-start | bytes 3145732
  117.8 0.9 copy-start.6
  118.7 5.2 %collective-permute-start.8 = (bf16[16,2,128,128]{3,2,1,0:T(8,128)(2,1)}, bf16[16,2,128,128]{3,2,1,0:T(8,128)(2,1)}, u32[]{:S(2)}, u32[]{:S(2)}) collective-permute-start(bf16[16,2,128,128]{3,2,1,0:T(8,128)(2,1)} %collective-permute-done.4.refs_3_), channel_id=1, source_target_pairs={{0,1},{1,0},{2,3},{3,2},{4,5},{5,4},{6,7},{7,6},{8,9},{9,8},{10,11... | collective-permute-start | bytes 3145736 | tf_op jit(solution)/shard_map/ppermute | solution.py:29
  118.7 25.7 %collective-permute-start.3 = (bf16[16,2,128,128]{3,2,1,0:T(8,128)(2,1)S(1)}, bf16[16,2,128,128]{3,2,1,0:T(8,128)(2,1)}, u32[]{:S(2)}, u32[]{:S(2)}) collective-permute-start(bf16[16,2,128,128]{3,2,1,0:T(8,128)(2,1)S(1)} %copy-done.2), channel_id=1, source_target_pairs={{0,2},{1,3},{2,0},{3,1},{4,6},{5,7},{6,4},{7,5},{8,10},{9,11},{10,... | collective-permute-start | bytes 3145736 | tf_op jit(solution)/shard_map/ppermute | solution.py:29
  118.8 25.6 %all-to-all-start.4 = ((bf16[4,672,128]{2,1,0:T(8,128)(2,1)}), bf16[4,672,128]{2,1,0:T(8,128)(2,1)}, u32[]{:S(2)}, u32[]{:S(2)}) async-start(bf16[4,672,128]{2,1,0:T(8,128)(2,1)} %copy-done.6), calls=%async_computation.4 | async-start | bytes 1376256 | tf_op jit(solution)/shard_map/all_to_all | solution.py:320
  136.3 0.9 copy-start.7
  144.3 5.1 %collective-permute-start.9 = (bf16[16,2,128,128]{3,2,1,0:T(8,128)(2,1)}, bf16[16,2,128,128]{3,2,1,0:T(8,128)(2,1)}, u32[]{:S(2)}, u32[]{:S(2)}) collective-permute-start(bf16[16,2,128,128]{3,2,1,0:T(8,128)(2,1)} %collective-permute-done.3.refs_3_), channel_id=1, source_target_pairs={{0,1},{1,0},{2,3},{3,2},{4,5},{5,4},{6,7},{7,6},{8,9},{9,8},{10,11... | collective-permute-start | bytes 3145736 | tf_op jit(solution)/shard_map/ppermute | solution.py:29
  144.4 23.8 %all-to-all-start.3 = ((bf16[4,672,128]{2,1,0:T(8,128)(2,1)}), bf16[4,672,128]{2,1,0:T(8,128)(2,1)}, u32[]{:S(2)}, u32[]{:S(2)}) async-start(bf16[4,672,128]{2,1,0:T(8,128)(2,1)} %copy-done.7), calls=%async_computation.3 | async-start | bytes 1376256 | tf_op jit(solution)/shard_map/all_to_all | solution.py:320
  162.9 0.9 copy-start.8
  168.2 21.3 %all-to-all-start.2 = ((bf16[4,672,128]{2,1,0:T(8,128)(2,1)}), bf16[4,672,128]{2,1,0:T(8,128)(2,1)S(1)}, u32[]{:S(2)}, u32[]{:S(2)}) async-start(bf16[4,672,128]{2,1,0:T(8,128)(2,1)} %copy-done.8), calls=%async_computation.2 | async-start | bytes 1376256 | tf_op jit(solution)/shard_map/all_to_all | solution.py:320
  189.5 0.8 copy-start.12

commit v10 on v9

--- a/solution.py
+++ b/solution.py
@@ -339,26 +339,28 @@
     twin = swapped(rest, "serve", 1)
     incoming = shifted(new_kv[0], "serve", 1)
     rows = page_rows(me, lines, limit, slots, page_owner, page_slot, prefix_len).astype(queries.dtype)
-    rows = jnp.pad(rows[:, None], ((0, 0), (0, 15), (0, CHUNK - limit - 2)))
-    early = after(queries, owns[1], twin)[:, :CHUNK]
-    early = jnp.concatenate([jnp.broadcast_to(early[None], (lines, PAGE, CHUNK)), rows], axis=1)
-    early = exchanged(early, groups)
-    later = after(queries, sides[0], incoming)[None, :, CHUNK:]
-    later = exchanged(jnp.broadcast_to(later, (lines, PAGE, (KVH - 1) * CHUNK)), groups)
-    numbers = early[:, PAGE, :limit + 2].astype(jnp.int32)
+    rows = jnp.pad(rows[:, None], ((0, 0), (0, PAGE - 1), (0, PAGE - limit - 2)))
+    q_all = jnp.broadcast_to(queries[None], (lines, PAGE, KVH * CHUNK))
+    q_all = exchanged(jnp.concatenate([q_all, rows], axis=2), groups)
+    numbers = q_all[:, 0, KVH * CHUNK:KVH * CHUNK + limit + 2].astype(jnp.int32)
     tables = (numbers[:, :limit], numbers[:, limit], numbers[:, limit + 1], (me // CLUSTER)[None], store_slot[0])
     fresh = new_kv[0, 0]
     attended = None
-    parts = None
+    parts = []
     for g in range(KVH):
-        side = sides[g] if g == 0 else after(sides[g], parts)
+        side = sides[g]
+        if g == 1:
+            side = after(side, incoming)
+        if g > 1:
+            side = after(side, parts[g - 2])
         both = swapped(side, "serve", 1)
         pools = (owns[g], twin, side, both)
         if g == 0:
-            parts, pool_out = attend(g, 0, tables, early, pools, fresh, pool, incoming)
+            part, pool_out = attend(g, g, tables, q_all, pools, fresh, pool, incoming)
         else:
-            parts = attend(g, g - 1, tables, later, pools, fresh)[0]
-        attended = merge(g, exchanged(parts, groups), attended)
+            part = attend(g, g, tables, q_all, pools, fresh)[0]
+        parts.append(part)
+        attended = merge(g, exchanged(part, groups), attended)
     return (attended, pool_out)
 
 

time: 194 us -> 189 us (0.974)
  Pallas kernels: 63.6 us -> 56.9 us
  waiting for transfers between devices: 72.5 us -> 75.5 us
  local copies, waits for them, and re-layouts: 18.3 us -> 15.7 us
    pallas_call x4, Pallas kernels: 54.2 us -> 47.5 us  [attend(): pl.pallas_call(functools.partial(attend_kernel, lines, head, q_head), gri...]
    all_to_all x6 -> x5, starting transfers between devices: 28.8 us -> 23.8 us  [exchanged(): lax.all_to_all(array, 'serve', 0, 0, axis_index_groups=groups, tiled=True)]
    all_to_all x6 -> x5, waiting for transfers between devices: 32.4 us -> 28.6 us  [exchanged(): lax.all_to_all(array, 'serve', 0, 0, axis_index_groups=groups, tiled=True)]
    ppermute x9, waiting for transfers between devices: 21.2 us -> 24.8 us  [swapped(): return lax.ppermute(array, axis, [(i, i ^ bit) for i in range(size)])]
    ppermute x9, starting transfers between devices: 4.96 us -> 8.33 us  [swapped(): return lax.ppermute(array, axis, [(i, i ^ bit) for i in range(size)])]
    ppermute x1, waiting for transfers between devices: 18.8 us -> 22.1 us  [shifted(): lax.ppermute(array, axis, [(i, (i + by) % size) for i in range(size)])]
    unnamed x30 -> x20, local copies, waits for them, and re-layouts: 11.1 us -> 8.85 us
  transfers between devices with their start and end apart: 16 -> 15, of which waited for: 8 -> 9; matrix products, arithmetic and copies ran while one was open for 3% -> 3% of each run, Pallas kernels for 32% -> 29%
where the time goes in v10:
time: 189 us; the launch traced here: 187 us
  waiting for transfers between devices  75.5 us (40%)
  Pallas kernels  56.9 us (30%)
  starting transfers between devices  32.6 us (17%)
  local copies, waits for them, and re-layouts  15.7 us (8%)
  other arithmetic  3.76 us (2%)
  between operations  2.23 us (1%)
    pallas_call x4, Pallas kernels, attend(): pl.pallas_call(functools.partial(attend_kernel, lines, head, q_head), gri...  47.5 us
    all_to_all x5, waiting for transfers between devices, exchanged(): lax.all_to_all(array, 'serve', 0, 0, axis_index_groups=groups, tiled=True)  28.6 us
    ppermute x9, waiting for transfers between devices, swapped(): return lax.ppermute(array, axis, [(i, i ^ bit) for i in range(size)])  24.8 us
    all_to_all x5, starting transfers between devices, exchanged(): lax.all_to_all(array, 'serve', 0, 0, axis_index_groups=groups, tiled=True)  23.8 us
    ppermute x1, waiting for transfers between devices, shifted(): lax.ppermute(array, axis, [(i, (i + by) % size) for i in range(size)])  22.1 us
    pallas_call x4, Pallas kernels, merge(): pl.pallas_call(functools.partial(merge_kernel, head), in_specs=[pl.BlockS...  9.41 us
    unnamed x20, local copies, waits for them, and re-layouts  8.85 us
    ppermute x9, starting transfers between devices, swapped(): return lax.ppermute(array, axis, [(i, i ^ bit) for i in range(size)])  8.33 us
  transfers between devices with their start and end apart: 15, of which 9 were waited for; matrix products, arithmetic and copies ran while one was open for 3% of the time, Pallas kernels for 29%

profile of v10, /device:TPU:0, one launch (start us, length us, event | category | flops | bytes accessed | tf_op | source)
XLA Modules:
  0.0 186.7 jit_solution(7083797905516435150)
XLA Ops:
  1.3 0.7 fusion.15
  2.0 0.7 fusion.13
  2.7 0.1 convert_reduce_fusion.1
  2.8 0.1 convert_reduce_fusion
  3.0 0.1 select_reduce_fusion
  3.2 0.1 and_reduce_fusion
  3.4 0.1 copy.19
  3.6 1.3 broadcast_in_dim.24
  4.9 1.7 pad_maximum_fusion
  6.6 6.3 %all-to-all-start = ((bf16[4,128,2688]{2,1,0:T(8,128)(2,1)}), bf16[4,128,2688]{2,1,0:T(8,128)(2,1)S(1)}, u32[]{:S(2)}, u32[]{:S(2)}) async-start(bf16[4,128,2688]{2,1,0:T(8,128)(2,1)} %pad_maximum_fusion), calls=%async_computation | async-start | bytes 5505024 | tf_op jit(solution)/shard_map/all_to_all | solution.py:320
  12.9 1.3 slice.28.refs_1_
  14.4 1.6 collective-permute-start.7
  16.0 3.7 %fusion.17 = (bf16[16,2,128,128]{3,2,1,0:T(8,128)(2,1)}, bf16[16,2,128,128]{3,2,1,0:T(8,128)(2,1)}, bf16[16,2,128,128]{3,2,1,0:T(8,128)(2,1)}) fusion(bf16[16,2,128,512]{3,2,1,0:T(8,128)(2,1)} %refs_6_.1), kind=kLoop, calls=%fused_computation.41 | loop fusion | bytes 6291456 | tf_op jit(solution)/shard_map/slice | solution.py:337
  19.7 0.5 collective-permute-start.2
  20.2 20.3 %collective-permute-done.7.refs_3_ = bf16[16,2,128,128]{3,2,1,0:T(8,128)(2,1)} collective-permute-done((bf16[16,2,128,128]{3,2,1,0:T(8,128)(2,1)S(1)}, bf16[16,2,128,128]{3,2,1,0:T(8,128)(2,1)}, u32[]{:S(2)}, u32[]{:S(2)}) %collective-permute-start.7) | collective-permute-done | bytes 1048608 | tf_op jit(solution)/shard_map/ppermute | solution.py:29
  40.5 0.5 collective-permute-start.3
  41.0 1.5 collective-permute-start.6
  43.2 22.1 %collective-permute-done.3.refs_7_ = bf16[1,2,128,512]{3,2,1,0:T(8,128)(2,1)S(1)} collective-permute-done((bf16[1,2,128,512]{3,2,1,0:T(8,128)(2,1)S(1)}, bf16[1,2,128,512]{3,2,1,0:T(8,128)(2,1)S(1)}, u32[]{:S(2)}, u32[]{:S(2)}) %collective-permute-start.3) | collective-permute-done | bytes 262176 | tf_op jit(solution)/shard_map/ppermute | solution.py:34
  65.4 0.4 collective-permute-done.2.refs_3_
  65.8 0.9 collective-permute-start.4
  66.7 8.4 %all-to-all-done.refs_0_ = bf16[4,128,2688]{2,1,0:T(8,128)(2,1)S(1)} async-done(((bf16[4,128,2688]{2,1,0:T(8,128)(2,1)}), bf16[4,128,2688]{2,1,0:T(8,128)(2,1)S(1)}, u32[]{:S(2)}, u32[]{:S(2)}) %all-to-all-start) | async-done | bytes 2752544 | tf_op jit(solution)/shard_map/all_to_all | solution.py:320
  75.2 0.2 slice_reduce_fusion
  75.4 2.2 %copy-done = bf16[16,2,128,512]{3,2,1,0:T(8,128)(2,1)S(1)} copy-done((bf16[16,2,128,512]{3,2,1,0:T(8,128)(2,1)S(1)}, bf16[16,2,128,512]{3,2,1,0:T(8,128)(2,1)}, u32[]{:S(2)}) %copy-start) | copy-done | bytes 4194328
  77.6 1.2 copy-done.3
  78.8 12.6 %shard_map.88 = (bf16[4,672,128]{2,1,0:T(8,128)(2,1)S(1)}, bf16[16,2,128,512]{3,2,1,0:T(8,128)(2,1)}) custom-call(s32[4,16]{1,0:T(4,128)S(1)} %bitcast.31, s32[4]{0:T(128)S(1)} %get-tuple-element.15.counts, s32[4]{0:T(128)S(1)} %get-tuple-element.14.lasts, s32[1]{0:T(128)} %bitcast.8.mine, s32[1]{0:T(128)} %bitcast.23.store, ...), custom_call_target="tpu_custom_call" | custom-call | flops 1 | bytes 1 | tf_op jit(solution)/shard_map/pallas_call | solution.py:255
  91.4 0.8 copy-done.8
  92.2 5.6 %all-to-all-start.4 = ((bf16[4,672,128]{2,1,0:T(8,128)(2,1)}), bf16[4,672,128]{2,1,0:T(8,128)(2,1)}, u32[]{:S(2)}, u32[]{:S(2)}) async-start(bf16[4,672,128]{2,1,0:T(8,128)(2,1)} %copy-done.8), calls=%async_computation.4 | async-start | bytes 1376256 | tf_op jit(solution)/shard_map/all_to_all | solution.py:320
  97.9 3.7 %collective-permute-start.1 = (bf16[16,2,128,128]{3,2,1,0:T(8,128)(2,1)}, bf16[16,2,128,128]{3,2,1,0:T(8,128)(2,1)}, u32[]{:S(2)}, u32[]{:S(2)}) collective-permute-start(bf16[16,2,128,128]{3,2,1,0:T(8,128)(2,1)} %get-tuple-element.20.refs_1_), channel_id=1, source_target_pairs={{0,2},{1,3},{2,0},{3,1},{4,6},{5,7},{6,4},{7,5},{8,10},{9,11},{10,... | collective-permute-start | bytes 3145736 | tf_op jit(solution)/shard_map/ppermute | solution.py:29
  101.6 11.4 %shard_map.86 = bf16[4,672,128]{2,1,0:T(8,128)(2,1)S(1)} custom-call(s32[4,16]{1,0:T(4,128)S(1)} %bitcast.32, s32[4]{0:T(128)S(1)} %get-tuple-element.15.counts, s32[4]{0:T(128)S(1)} %get-tuple-element.14.lasts, s32[1]{0:T(128)} %bitcast.8.mine, s32[1]{0:T(128)} %bitcast.21.store, bf16[4,128,2688]{2,1,0:T(8,128)(2,1)S(1)} %all-to-all-done.refs_0_, ...), custom_call_target="tpu_custom_call" | custom-call | flops 1 | bytes 1 | tf_op jit(solution)/shard_map/pallas_call | solution.py:255
  113.0 0.8 copy-done.6
  113.8 2.8 %all-to-all-done.4.parts = bf16[4,672,128]{2,1,0:T(8,128)(2,1)} async-done(((bf16[4,672,128]{2,1,0:T(8,128)(2,1)}), bf16[4,672,128]{2,1,0:T(8,128)(2,1)}, u32[]{:S(2)}, u32[]{:S(2)}) %all-to-all-start.4) | async-done | bytes 688160 | tf_op jit(solution)/shard_map/all_to_all | solution.py:320
  116.6 4.2 %all-to-all-start.3 = ((bf16[4,672,128]{2,1,0:T(8,128)(2,1)}), bf16[4,672,128]{2,1,0:T(8,128)(2,1)}, u32[]{:S(2)}, u32[]{:S(2)}) async-start(bf16[4,672,128]{2,1,0:T(8,128)(2,1)} %copy-done.6), calls=%async_computation.3 | async-start | bytes 1376256 | tf_op jit(solution)/shard_map/all_to_all | solution.py:320
  120.8 4.0 %collective-permute-done.1.refs_3_ = bf16[16,2,128,128]{3,2,1,0:T(8,128)(2,1)} collective-permute-done((bf16[16,2,128,128]{3,2,1,0:T(8,128)(2,1)}, bf16[16,2,128,128]{3,2,1,0:T(8,128)(2,1)}, u32[]{:S(2)}, u32[]{:S(2)}) %collective-permute-start.1) | collective-permute-done | bytes 1048608 | tf_op jit(solution)/shard_map/ppermute | solution.py:29
  124.8 11.4 %shard_map.89 = bf16[4,672,128]{2,1,0:T(8,128)(2,1)S(1)} custom-call(s32[4,16]{1,0:T(4,128)S(1)} %bitcast.33, s32[4]{0:T(128)S(1)} %get-tuple-element.15.counts, s32[4]{0:T(128)S(1)} %get-tuple-element.14.lasts, s32[1]{0:T(128)} %bitcast.8.mine, s32[1]{0:T(128)} %bitcast.24.store, bf16[4,128,2688]{2,1,0:T(8,128)(2,1)S(1)} %all-to-all-done.refs_0_, ...), custom_call_target="tpu_custom_call" | custom-call | flops 1 | bytes 1 | tf_op jit(solution)/shard_map/pallas_call | solution.py:255
  136.2 0.9 copy-done.7
  137.0 2.9 %all-to-all-done.3.parts = bf16[4,672,128]{2,1,0:T(8,128)(2,1)} async-done(((bf16[4,672,128]{2,1,0:T(8,128)(2,1)}), bf16[4,672,128]{2,1,0:T(8,128)(2,1)}, u32[]{:S(2)}, u32[]{:S(2)}) %all-to-all-start.3) | async-done | bytes 688160 | tf_op jit(solution)/shard_map/all_to_all | solution.py:320
  139.9 4.2 %all-to-all-start.2 = ((bf16[4,672,128]{2,1,0:T(8,128)(2,1)}), bf16[4,672,128]{2,1,0:T(8,128)(2,1)}, u32[]{:S(2)}, u32[]{:S(2)}) async-start(bf16[4,672,128]{2,1,0:T(8,128)(2,1)} %copy-done.7), calls=%async_computation.2 | async-start | bytes 1376256 | tf_op jit(solution)/shard_map/all_to_all | solution.py:320
  144.1 1.2 copy-done.4
  145.3 12.2 %shard_map.87 = bf16[4,672,128]{2,1,0:T(8,128)(2,1)S(1)} custom-call(s32[4,16]{1,0:T(4,128)S(1)} %bitcast.34, s32[4]{0:T(128)S(1)} %get-tuple-element.15.counts, s32[4]{0:T(128)S(1)} %get-tuple-element.14.lasts, s32[1]{0:T(128)} %bitcast.8.mine, s32[1]{0:T(128)} %bitcast.22.store, bf16[4,128,2688]{2,1,0:T(8,128)(2,1)S(1)} %all-to-all-done.refs_0_, ...), custom_call_target="tpu_custom_call" | custom-call | flops 1 | bytes 1 | tf_op jit(solution)/shard_map/pallas_call | solution.py:255
  157.5 0.8 copy-done.5
  158.4 4.1 %all-to-all-done.2.parts = bf16[4,672,128]{2,1,0:T(8,128)(2,1)} async-done(((bf16[4,672,128]{2,1,0:T(8,128)(2,1)}), bf16[4,672,128]{2,1,0:T(8,128)(2,1)}, u32[]{:S(2)}, u32[]{:S(2)}) %all-to-all-start.2) | async-done | bytes 688160 | tf_op jit(solution)/shard_map/all_to_all | solution.py:320
  162.5 3.5 %all-to-all-start.1 = ((bf16[4,672,128]{2,1,0:T(8,128)(2,1)}), bf16[4,672,128]{2,1,0:T(8,128)(2,1)S(1)}, u32[]{:S(2)}, u32[]{:S(2)}) async-start(bf16[4,672,128]{2,1,0:T(8,128)(2,1)} %copy-done.5), calls=%async_computation.1 | async-start | bytes 1376256 | tf_op jit(solution)/shard_map/all_to_all | solution.py:320
  165.9 2.4 %shard_map.90.refs_0_ = bf16[128,2560]{1,0:T(8,128)(2,1)} custom-call(bf16[4,672,128]{2,1,0:T(8,128)(2,1)} %all-to-all-done.4.parts), custom_call_target="tpu_custom_call" | custom-call | flops 1 | bytes 1 | tf_op jit(solution)/shard_map/pallas_call | solution.py:292
  168.3 2.4 %shard_map.91.refs_0_ = bf16[128,2560]{1,0:T(8,128)(2,1)} custom-call(bf16[4,672,128]{2,1,0:T(8,128)(2,1)} %all-to-all-done.3.parts, bf16[128,2560]{1,0:T(8,128)(2,1)} %shard_map.90.refs_0_), custom_call_target="tpu_custom_call", output_to_operand_aliasing={{}: (1, {})} | custom-call | flops 1 | bytes 1 | tf_op jit(solution)/shard_map/pallas_call | solution.py:292
  170.7 2.4 %shard_map.92.refs_0_ = bf16[128,2560]{1,0:T(8,128)(2,1)} custom-call(bf16[4,672,128]{2,1,0:T(8,128)(2,1)} %all-to-all-done.2.parts, bf16[128,2560]{1,0:T(8,128)(2,1)} %shard_map.91.refs_0_), custom_call_target="tpu_custom_call", output_to_operand_aliasing={{}: (1, {})} | custom-call | flops 1 | bytes 1 | tf_op jit(solution)/shard_map/pallas_call | solution.py:292
  173.0 10.4 %all-to-all-done.1.parts = bf16[4,672,128]{2,1,0:T(8,128)(2,1)S(1)} async-done(((bf16[4,672,128]{2,1,0:T(8,128)(2,1)}), bf16[4,672,128]{2,1,0:T(8,128)(2,1)S(1)}, u32[]{:S(2)}, u32[]{:S(2)}) %all-to-all-start.1) | async-done | bytes 688160 | tf_op jit(solution)/shard_map/all_to_all | solution.py:320
  183.5 0.8 copy-done.9
  184.3 2.4 %shard_map.93 = bf16[128,2560]{1,0:T(8,128)(2,1)} custom-call(bf16[4,672,128]{2,1,0:T(8,128)(2,1)} %copy-done.9, bf16[128,2560]{1,0:T(8,128)(2,1)} %shard_map.92.refs_0_), custom_call_target="tpu_custom_call", output_to_operand_aliasing={{}: (1, {})} | custom-call | flops 1 | bytes 1 | tf_op jit(solution)/shard_map/pallas_call | solution.py:292
  (32 shorter events, 0.4 us)
Async XLA Ops:
  6.6 68.6 %all-to-all-start = ((bf16[4,128,2688]{2,1,0:T(8,128)(2,1)}), bf16[4,128,2688]{2,1,0:T(8,128)(2,1)S(1)}, u32[]{:S(2)}, u32[]{:S(2)}) async-start(bf16[4,128,2688]{2,1,0:T(8,128)(2,1)} %pad_maximum_fusion), calls=%async_computation | async-start | bytes 5505024 | tf_op jit(solution)/shard_map/all_to_all | solution.py:320
  14.3 5.4 %copy-start.2 = (bf16[16,2,128,128]{3,2,1,0:T(8,128)(2,1)}, bf16[16,2,128,128]{3,2,1,0:T(8,128)(2,1)S(1)}, u32[]{:S(2)}) copy-start(bf16[16,2,128,128]{3,2,1,0:T(8,128)(2,1)S(1)} %slice.28.refs_1_) | copy-start | bytes 3145732
  14.3 26.2 %copy-start.1 = (bf16[1,1,2,128,512]{4,3,2,1,0:T(8,128)(2,1)S(1)}, bf16[1,1,2,128,512]{4,3,2,1,0:T(8,128)(2,1)}, u32[]{:S(2)}) copy-start(bf16[1,1,2,128,512]{4,3,2,1,0:T(8,128)(2,1)} %param.8) | copy-start | bytes 786436
  14.3 61.1 %collective-permute-start = (bf16[16,2,128,512]{3,2,1,0:T(8,128)(2,1)}, bf16[16,2,128,512]{3,2,1,0:T(8,128)(2,1)}, u32[]{:S(2)}, u32[]{:S(2)}) collective-permute-start(bf16[16,2,128,512]{3,2,1,0:T(8,128)(2,1)} %refs_6_.1), channel_id=1, source_target_pairs={{0,1},{1,0},{2,3},{3,2},{4,5},{5,4},{6,7},{7,6},{8,9},{9,8},{10,11... | collective-permute-start | bytes 12582920 | tf_op jit(solution)/shard_map/ppermute | solution.py:29
  14.4 26.1 %collective-permute-start.7 = (bf16[16,2,128,128]{3,2,1,0:T(8,128)(2,1)S(1)}, bf16[16,2,128,128]{3,2,1,0:T(8,128)(2,1)}, u32[]{:S(2)}, u32[]{:S(2)}) collective-permute-start(bf16[16,2,128,128]{3,2,1,0:T(8,128)(2,1)S(1)} %slice.28.refs_1_), channel_id=1, source_target_pairs={{0,2},{1,3},{2,0},{3,1},{4,6},{5,7},{6,4},{7,5},{8,10},{9,11},{10,... | collective-permute-start | bytes 3145736 | tf_op jit(solution)/shard_map/ppermute | solution.py:29
  19.7 46.1 %collective-permute-start.2 = (bf16[16,2,128,128]{3,2,1,0:T(8,128)(2,1)}, bf16[16,2,128,128]{3,2,1,0:T(8,128)(2,1)}, u32[]{:S(2)}, u32[]{:S(2)}) collective-permute-start(bf16[16,2,128,128]{3,2,1,0:T(8,128)(2,1)} %get-tuple-element.19.refs_1_), channel_id=1, source_target_pairs={{0,2},{1,3},{2,0},{3,1},{4,6},{5,7},{6,4},{7,5},{8,10},{9,11},{10,... | collective-permute-start | bytes 3145736 | tf_op jit(solution)/shard_map/ppermute | solution.py:29
  40.5 34.9 %collective-permute-start.8 = (bf16[16,2,128,128]{3,2,1,0:T(8,128)(2,1)}, bf16[16,2,128,128]{3,2,1,0:T(8,128)(2,1)}, u32[]{:S(2)}, u32[]{:S(2)}) collective-permute-start(bf16[16,2,128,128]{3,2,1,0:T(8,128)(2,1)} %collective-permute-done.7.refs_3_), channel_id=1, source_target_pairs={{0,1},{1,0},{2,3},{3,2},{4,5},{5,4},{6,7},{7,6},{8,9},{9,8},{10,11... | collective-permute-start | bytes 3145736 | tf_op jit(solution)/shard_map/ppermute | solution.py:29
  40.5 24.8 %collective-permute-start.3 = (bf16[1,2,128,512]{3,2,1,0:T(8,128)(2,1)S(1)}, bf16[1,2,128,512]{3,2,1,0:T(8,128)(2,1)S(1)}, u32[]{:S(2)}, u32[]{:S(2)}) collective-permute-start(bf16[1,2,128,512]{3,2,1,0:T(8,128)(2,1)S(1)} %bitcast.25), channel_id=1, source_target_pairs={{0,1},{1,2},{2,3},{3,4},{4,5},{5,6},{6,7},{7,8},{8,9},{9,10},{10,1... | collective-permute-start | bytes 786440 | tf_op jit(solution)/shard_map/ppermute | solution.py:34
  41.0 60.5 %collective-permute-start.6 = (bf16[16,2,128,128]{3,2,1,0:T(8,128)(2,1)}, bf16[16,2,128,128]{3,2,1,0:T(8,128)(2,1)}, u32[]{:S(2)}, u32[]{:S(2)}) collective-permute-start(bf16[16,2,128,128]{3,2,1,0:T(8,128)(2,1)} %get-tuple-element.18.refs_1_), channel_id=1, source_target_pairs={{0,2},{1,3},{2,0},{3,1},{4,6},{5,7},{6,4},{7,5},{8,10},{9,11},{10,... | collective-permute-start | bytes 3145736 | tf_op jit(solution)/shard_map/ppermute | solution.py:29
  65.8 35.8 %collective-permute-start.4 = (bf16[16,2,128,128]{3,2,1,0:T(8,128)(2,1)}, bf16[16,2,128,128]{3,2,1,0:T(8,128)(2,1)}, u32[]{:S(2)}, u32[]{:S(2)}) collective-permute-start(bf16[16,2,128,128]{3,2,1,0:T(8,128)(2,1)} %collective-permute-done.2.refs_3_), channel_id=1, source_target_pairs={{0,1},{1,0},{2,3},{3,2},{4,5},{5,4},{6,7},{7,6},{8,9},{9,8},{10,11... | collective-permute-start | bytes 3145736 | tf_op jit(solution)/shard_map/ppermute | solution.py:29
  75.4 2.2 %copy-start = (bf16[16,2,128,512]{3,2,1,0:T(8,128)(2,1)S(1)}, bf16[16,2,128,512]{3,2,1,0:T(8,128)(2,1)}, u32[]{:S(2)}) copy-start(bf16[16,2,128,512]{3,2,1,0:T(8,128)(2,1)} %refs_6_.1) | copy-start | bytes 12582916
  77.6 1.2 copy-start.3
  91.4 0.8 copy-start.8
  92.2 24.3 %all-to-all-start.4 = ((bf16[4,672,128]{2,1,0:T(8,128)(2,1)}), bf16[4,672,128]{2,1,0:T(8,128)(2,1)}, u32[]{:S(2)}, u32[]{:S(2)}) async-start(bf16[4,672,128]{2,1,0:T(8,128)(2,1)} %copy-done.8), calls=%async_computation.4 | async-start | bytes 1376256 | tf_op jit(solution)/shard_map/all_to_all | solution.py:320
  97.9 26.9 %collective-permute-start.1 = (bf16[16,2,128,128]{3,2,1,0:T(8,128)(2,1)}, bf16[16,2,128,128]{3,2,1,0:T(8,128)(2,1)}, u32[]{:S(2)}, u32[]{:S(2)}) collective-permute-start(bf16[16,2,128,128]{3,2,1,0:T(8,128)(2,1)} %get-tuple-element.20.refs_1_), channel_id=1, source_target_pairs={{0,2},{1,3},{2,0},{3,1},{4,6},{5,7},{6,4},{7,5},{8,10},{9,11},{10,... | collective-permute-start | bytes 3145736 | tf_op jit(solution)/shard_map/ppermute | solution.py:29
  101.6 23.2 %collective-permute-start.9 = (bf16[16,2,128,128]{3,2,1,0:T(8,128)(2,1)}, bf16[16,2,128,128]{3,2,1,0:T(8,128)(2,1)}, u32[]{:S(2)}, u32[]{:S(2)}) collective-permute-start(bf16[16,2,128,128]{3,2,1,0:T(8,128)(2,1)} %collective-permute-done.6.refs_3_), channel_id=1, source_target_pairs={{0,1},{1,0},{2,3},{3,2},{4,5},{5,4},{6,7},{7,6},{8,9},{9,8},{10,11... | collective-permute-start | bytes 3145736 | tf_op jit(solution)/shard_map/ppermute | solution.py:29
  113.0 0.8 copy-start.6
  116.6 23.3 %all-to-all-start.3 = ((bf16[4,672,128]{2,1,0:T(8,128)(2,1)}), bf16[4,672,128]{2,1,0:T(8,128)(2,1)}, u32[]{:S(2)}, u32[]{:S(2)}) async-start(bf16[4,672,128]{2,1,0:T(8,128)(2,1)} %copy-done.6), calls=%async_computation.3 | async-start | bytes 1376256 | tf_op jit(solution)/shard_map/all_to_all | solution.py:320
  124.8 19.3 %collective-permute-start.5 = (bf16[16,2,128,128]{3,2,1,0:T(8,128)(2,1)}, bf16[16,2,128,128]{3,2,1,0:T(8,128)(2,1)}, u32[]{:S(2)}, u32[]{:S(2)}) collective-permute-start(bf16[16,2,128,128]{3,2,1,0:T(8,128)(2,1)} %collective-permute-done.1.refs_3_), channel_id=1, source_target_pairs={{0,1},{1,0},{2,3},{3,2},{4,5},{5,4},{6,7},{7,6},{8,9},{9,8},{10,11... | collective-permute-start | bytes 3145736 | tf_op jit(solution)/shard_map/ppermute | solution.py:29
  136.2 0.9 copy-start.7
  139.9 22.6 %all-to-all-start.2 = ((bf16[4,672,128]{2,1,0:T(8,128)(2,1)}), bf16[4,672,128]{2,1,0:T(8,128)(2,1)}, u32[]{:S(2)}, u32[]{:S(2)}) async-start(bf16[4,672,128]{2,1,0:T(8,128)(2,1)} %copy-done.7), calls=%async_computation.2 | async-start | bytes 1376256 | tf_op jit(solution)/shard_map/all_to_all | solution.py:320
  144.1 1.2 copy-start.4
  157.5 0.9 copy-start.5
  162.5 21.0 %all-to-all-start.1 = ((bf16[4,672,128]{2,1,0:T(8,128)(2,1)}), bf16[4,672,128]{2,1,0:T(8,128)(2,1)S(1)}, u32[]{:S(2)}, u32[]{:S(2)}) async-start(bf16[4,672,128]{2,1,0:T(8,128)(2,1)} %copy-done.5), calls=%async_computation.1 | async-start | bytes 1376256 | tf_op jit(solution)/shard_map/all_to_all | solution.py:320
  183.5 0.8 copy-start.9

commit v11 on v10

--- a/solution.py
+++ b/solution.py
@@ -256,7 +256,7 @@
         functools.partial(attend_kernel, lines, head, q_head),
         grid_spec=grid_spec,
         out_shape=out_shape,
-        compiler_params=pltpu.CompilerParams(vmem_limit_bytes=16 * 2**20),
+        compiler_params=pltpu.CompilerParams(vmem_limit_bytes=32 * 2**20),
         cost_estimate=pl.CostEstimate(flops=1, bytes_accessed=1, transcendentals=0),
     )(picks, counts, lasts, mine, store, *operands)
 
@@ -332,33 +332,33 @@
     slots = pool.shape[0]
     capacity = (MAXP + width - 2) // (width - 1)
     limit = min(MAXP, CLUSTER * capacity)
-    owns = [pool[:, :, :, :HD]]
+    incoming = shifted(new_kv[0], "serve", 1)
+    owns = [after(pool, incoming)[:, :, :, :HD]]
     rest = after(pool, owns[0])
     owns += [rest[:, :, :, g * HD:(g + 1) * HD] for g in range(1, KVH)]
     sides = [swapped(own, "serve", 2) for own in owns]
     twin = swapped(rest, "serve", 1)
-    incoming = shifted(new_kv[0], "serve", 1)
     rows = page_rows(me, lines, limit, slots, page_owner, page_slot, prefix_len).astype(queries.dtype)
     rows = jnp.pad(rows[:, None], ((0, 0), (0, PAGE - 1), (0, PAGE - limit - 2)))
-    q_all = jnp.broadcast_to(queries[None], (lines, PAGE, KVH * CHUNK))
-    q_all = exchanged(jnp.concatenate([q_all, rows], axis=2), groups)
-    numbers = q_all[:, 0, KVH * CHUNK:KVH * CHUNK + limit + 2].astype(jnp.int32)
+    early = jnp.broadcast_to(queries[None, :, :CHUNK], (lines, PAGE, CHUNK))
+    early = exchanged(jnp.concatenate([early, rows], axis=2), groups)
+    later = after(queries, early)[None, :, CHUNK:]
+    later = exchanged(jnp.broadcast_to(later, (lines, PAGE, (KVH - 1) * CHUNK)), groups)
+    numbers = early[:, 0, CHUNK:CHUNK + limit + 2].astype(jnp.int32)
     tables = (numbers[:, :limit], numbers[:, limit], numbers[:, limit + 1], (me // CLUSTER)[None], store_slot[0])
     fresh = new_kv[0, 0]
     attended = None
     parts = []
     for g in range(KVH):
         side = sides[g]
-        if g == 1:
-            side = after(side, incoming)
         if g > 1:
             side = after(side, parts[g - 2])
         both = swapped(side, "serve", 1)
         pools = (owns[g], twin, side, both)
         if g == 0:
-            part, pool_out = attend(g, g, tables, q_all, pools, fresh, pool, incoming)
+            part, pool_out = attend(g, 0, tables, early, pools, fresh, pool, incoming)
         else:
-            part = attend(g, g, tables, q_all, pools, fresh)[0]
+            part = attend(g, g - 1, tables, later, pools, fresh)[0]
         parts.append(part)
         attended = merge(g, exchanged(part, groups), attended)
     return (attended, pool_out)

time: 189 us -> 202 us (1.069)
  blocking collectives: 0 us -> 24.3 us
  starting transfers between devices: 32.6 us -> 24.1 us
  waiting for transfers between devices: 75.5 us -> 68.6 us
  Pallas kernels: 56.9 us -> 63.3 us
    all_to_all x0 -> x1, blocking collectives: none -> 24.3 us  [exchanged(): lax.all_to_all(array, 'serve', 0, 0, axis_index_groups=groups, tiled=True)]
    ppermute x9, waiting for transfers between devices: 24.8 us -> 43.6 us  [swapped(): return lax.ppermute(array, axis, [(i, i ^ bit) for i in range(size)])]
    ppermute x1, waiting for transfers between devices: 22.1 us -> 6.29 us  [shifted(): lax.ppermute(array, axis, [(i, (i + by) % size) for i in range(size)])]
    all_to_all x5, waiting for transfers between devices: 28.6 us -> 18.7 us  [exchanged(): lax.all_to_all(array, 'serve', 0, 0, axis_index_groups=groups, tiled=True)]
    pallas_call x4, Pallas kernels: 47.5 us -> 53.8 us  [attend(): pl.pallas_call(functools.partial(attend_kernel, lines, head, q_head), gri...]
    ppermute x9, starting transfers between devices: 8.33 us -> 3.94 us  [swapped(): return lax.ppermute(array, axis, [(i, i ^ bit) for i in range(size)])]
    all_to_all x5, starting transfers between devices: 23.8 us -> 19.7 us  [exchanged(): lax.all_to_all(array, 'serve', 0, 0, axis_index_groups=groups, tiled=True)]
  transfers between devices with their start and end apart: 15 -> 15, of which waited for: 9 -> 8; matrix products, arithmetic and copies ran while one was open for 3% -> 4% of each run, Pallas kernels for 29% -> 30%
where the time goes in v11:
time: 202 us; the launch traced here: 200 us
  waiting for transfers between devices  68.6 us (34%)
  Pallas kernels  63.3 us (31%)
  blocking collectives  24.3 us (12%)
  starting transfers between devices  24.1 us (12%)
  local copies, waits for them, and re-layouts  14.5 us (7%)
  other arithmetic  2.78 us (1%)
  between operations  2.26 us (1%)
    pallas_call x4, Pallas kernels, attend(): pl.pallas_call(functools.partial(attend_kernel, lines, head, q_head), gri...  53.8 us
    ppermute x9, waiting for transfers between devices, swapped(): return lax.ppermute(array, axis, [(i, i ^ bit) for i in range(size)])  43.6 us
    all_to_all x1, blocking collectives, exchanged(): lax.all_to_all(array, 'serve', 0, 0, axis_index_groups=groups, tiled=True)  24.3 us
    all_to_all x5, starting transfers between devices, exchanged(): lax.all_to_all(array, 'serve', 0, 0, axis_index_groups=groups, tiled=True)  19.7 us
    all_to_all x5, waiting for transfers between devices, exchanged(): lax.all_to_all(array, 'serve', 0, 0, axis_index_groups=groups, tiled=True)  18.7 us
    pallas_call x4, Pallas kernels, merge(): pl.pallas_call(functools.partial(merge_kernel, head), in_specs=[pl.BlockS...  9.41 us
    unnamed x20, local copies, waits for them, and re-layouts  7.65 us
    ppermute x1, waiting for transfers between devices, shifted(): lax.ppermute(array, axis, [(i, (i + by) % size) for i in range(size)])  6.29 us
  transfers between devices with their start and end apart: 15, of which 8 were waited for; matrix products, arithmetic and copies ran while one was open for 4% of the time, Pallas kernels for 30%

profile of v11, /device:TPU:0, one launch (start us, length us, event | category | flops | bytes accessed | tf_op | source)
XLA Modules:
  0.0 199.8 jit_solution(2313195605522221121)
XLA Ops:
  0.6 0.5 collective-permute-start
  1.9 0.7 fusion.15
  2.5 0.7 fusion.13
  3.2 0.1 convert_reduce_fusion.1
  3.3 0.1 convert_reduce_fusion
  3.5 0.1 select_reduce_fusion
  3.7 0.1 and_reduce_fusion
  3.8 0.1 copy.20
  3.9 0.1 copy.19
  4.0 0.1 fusion.8
  4.1 6.3 %collective-permute-done.refs_7_ = bf16[1,2,128,512]{3,2,1,0:T(8,128)(2,1)S(1)} collective-permute-done((bf16[1,2,128,512]{3,2,1,0:T(8,128)(2,1)}, bf16[1,2,128,512]{3,2,1,0:T(8,128)(2,1)S(1)}, u32[]{:S(2)}, u32[]{:S(2)}) %collective-permute-start) | collective-permute-done | bytes 262176 | tf_op jit(solution)/shard_map/ppermute | solution.py:34
  10.4 1.3 slice.36.refs_1_
  11.9 24.3 %all_to_all.30.refs_0_ = bf16[4,128,768]{2,1,0:T(8,128)(2,1)} all-to-all(bf16[4,128,768]{2,1,0:T(8,128)(2,1)S(1)} %pad_maximum_fusion), channel_id=1, replica_groups={{0,4,8,12},{1,5,9,13},{2,6,10,14},{3,7,11,15},{16,20,24,28},{17,21,25,2..., dimensions={0} | all-to-all | bytes 1572864 | tf_op jit(solution)/shard_map/all_to_all | solution.py:320
  36.3 1.4 broadcast_in_dim.32
  37.7 3.6 %all-to-all-start.1 = ((bf16[4,128,1920]{2,1,0:T(8,128)(2,1)}), bf16[4,128,1920]{2,1,0:T(8,128)(2,1)S(1)}, u32[]{:S(2)}, u32[]{:S(2)}) async-start(bf16[4,128,1920]{2,1,0:T(8,128)(2,1)} %broadcast_in_dim.32), calls=%async_computation.1 | async-start | bytes 3932160 | tf_op jit(solution)/shard_map/all_to_all | solution.py:320
  41.3 0.7 collective-permute-start.7
  42.0 3.7 %fusion.17 = (bf16[16,2,128,128]{3,2,1,0:T(8,128)(2,1)}, bf16[16,2,128,128]{3,2,1,0:T(8,128)(2,1)}, bf16[16,2,128,128]{3,2,1,0:T(8,128)(2,1)}) fusion(bf16[16,2,128,512]{3,2,1,0:T(8,128)(2,1)} %refs_6_.1), kind=kLoop, calls=%fused_computation.41 | loop fusion | bytes 6291456 | tf_op jit(solution)/shard_map/slice | solution.py:338
  45.6 1.4 collective-permute-start.3
  47.0 20.5 %collective-permute-done.7.refs_3_ = bf16[16,2,128,128]{3,2,1,0:T(8,128)(2,1)} collective-permute-done((bf16[16,2,128,128]{3,2,1,0:T(8,128)(2,1)S(1)}, bf16[16,2,128,128]{3,2,1,0:T(8,128)(2,1)}, u32[]{:S(2)}, u32[]{:S(2)}) %collective-permute-start.7) | collective-permute-done | bytes 1048608 | tf_op jit(solution)/shard_map/ppermute | solution.py:29
  68.2 0.7 collective-permute-start.6
  68.9 0.7 slice_convert_fusion
  69.6 20.4 %collective-permute-done.3.refs_3_ = bf16[16,2,128,128]{3,2,1,0:T(8,128)(2,1)} collective-permute-done((bf16[16,2,128,128]{3,2,1,0:T(8,128)(2,1)}, bf16[16,2,128,128]{3,2,1,0:T(8,128)(2,1)}, u32[]{:S(2)}, u32[]{:S(2)}) %collective-permute-start.3) | collective-permute-done | bytes 1048608 | tf_op jit(solution)/shard_map/ppermute | solution.py:29
  90.0 0.2 slice_reduce_fusion
  90.3 2.2 %copy-done = bf16[16,2,128,512]{3,2,1,0:T(8,128)(2,1)S(1)} copy-done((bf16[16,2,128,512]{3,2,1,0:T(8,128)(2,1)S(1)}, bf16[16,2,128,512]{3,2,1,0:T(8,128)(2,1)}, u32[]{:S(2)}) %copy-start) | copy-done | bytes 4194328
  92.5 1.1 copy-done.4
  93.6 14.0 %shard_map.88 = (bf16[4,672,128]{2,1,0:T(8,128)(2,1)S(1)}, bf16[16,2,128,512]{3,2,1,0:T(8,128)(2,1)}) custom-call(s32[4,16]{1,0:T(4,128)S(1)} %bitcast.31, s32[4]{0:T(128)S(1)} %get-tuple-element.17.counts, s32[4]{0:T(128)S(1)} %get-tuple-element.16.lasts, s32[1]{0:T(128)} %bitcast.8.mine, s32[1]{0:T(128)} %bitcast.23.store, ...), custom_call_target="tpu_custom_call" | custom-call | flops 1 | bytes 1 | tf_op jit(solution)/shard_map/pallas_call | solution.py:255
  107.6 0.8 copy-done.8
  108.5 4.3 %all-to-all-start.5 = ((bf16[4,672,128]{2,1,0:T(8,128)(2,1)}), bf16[4,672,128]{2,1,0:T(8,128)(2,1)}, u32[]{:S(2)}, u32[]{:S(2)}) async-start(bf16[4,672,128]{2,1,0:T(8,128)(2,1)} %copy-done.8), calls=%async_computation.5 | async-start | bytes 1376256 | tf_op jit(solution)/shard_map/all_to_all | solution.py:320
  112.8 1.1 collective-permute-start.2
  113.8 12.5 %shard_map.86 = bf16[4,672,128]{2,1,0:T(8,128)(2,1)S(1)} custom-call(s32[4,16]{1,0:T(4,128)S(1)} %bitcast.32, s32[4]{0:T(128)S(1)} %get-tuple-element.17.counts, s32[4]{0:T(128)S(1)} %get-tuple-element.16.lasts, s32[1]{0:T(128)} %bitcast.8.mine, s32[1]{0:T(128)} %bitcast.21.store, bf16[4,128,1920]{2,1,0:T(8,128)(2,1)S(1)} %all-to-all-done.1.refs_0_, ...), custom_call_target="tpu_custom_call" | custom-call | flops 1 | bytes 1 | tf_op jit(solution)/shard_map/pallas_call | solution.py:255
  126.4 0.8 copy-done.6
  127.2 4.2 %all-to-all-done.5.parts = bf16[4,672,128]{2,1,0:T(8,128)(2,1)} async-done(((bf16[4,672,128]{2,1,0:T(8,128)(2,1)}), bf16[4,672,128]{2,1,0:T(8,128)(2,1)}, u32[]{:S(2)}, u32[]{:S(2)}) %all-to-all-start.5) | async-done | bytes 688160 | tf_op jit(solution)/shard_map/all_to_all | solution.py:320
  131.4 4.2 %all-to-all-start.4 = ((bf16[4,672,128]{2,1,0:T(8,128)(2,1)}), bf16[4,672,128]{2,1,0:T(8,128)(2,1)}, u32[]{:S(2)}, u32[]{:S(2)}) async-start(bf16[4,672,128]{2,1,0:T(8,128)(2,1)} %copy-done.6), calls=%async_computation.4 | async-start | bytes 1376256 | tf_op jit(solution)/shard_map/all_to_all | solution.py:320
  135.6 2.6 %collective-permute-done.2.refs_3_ = bf16[16,2,128,128]{3,2,1,0:T(8,128)(2,1)} collective-permute-done((bf16[16,2,128,128]{3,2,1,0:T(8,128)(2,1)}, bf16[16,2,128,128]{3,2,1,0:T(8,128)(2,1)}, u32[]{:S(2)}, u32[]{:S(2)}) %collective-permute-start.2) | collective-permute-done | bytes 1048608 | tf_op jit(solution)/shard_map/ppermute | solution.py:29
  138.2 13.7 %shard_map.89 = bf16[4,672,128]{2,1,0:T(8,128)(2,1)S(1)} custom-call(s32[4,16]{1,0:T(4,128)S(1)} %bitcast.33, s32[4]{0:T(128)S(1)} %get-tuple-element.17.counts, s32[4]{0:T(128)S(1)} %get-tuple-element.16.lasts, s32[1]{0:T(128)} %bitcast.8.mine, s32[1]{0:T(128)} %bitcast.24.store, bf16[4,128,1920]{2,1,0:T(8,128)(2,1)S(1)} %all-to-all-done.1.refs_0_, ...), custom_call_target="tpu_custom_call" | custom-call | flops 1 | bytes 1 | tf_op jit(solution)/shard_map/pallas_call | solution.py:255
  151.9 0.9 copy-done.7
  152.8 0.5 all-to-all-done.4.parts
  153.3 4.2 %all-to-all-start.3 = ((bf16[4,672,128]{2,1,0:T(8,128)(2,1)}), bf16[4,672,128]{2,1,0:T(8,128)(2,1)}, u32[]{:S(2)}, u32[]{:S(2)}) async-start(bf16[4,672,128]{2,1,0:T(8,128)(2,1)} %copy-done.7), calls=%async_computation.3 | async-start | bytes 1376256 | tf_op jit(solution)/shard_map/all_to_all | solution.py:320
  157.5 13.7 %shard_map.87 = bf16[4,672,128]{2,1,0:T(8,128)(2,1)S(1)} custom-call(s32[4,16]{1,0:T(4,128)S(1)} %bitcast.34, s32[4]{0:T(128)S(1)} %get-tuple-element.17.counts, s32[4]{0:T(128)S(1)} %get-tuple-element.16.lasts, s32[1]{0:T(128)} %bitcast.8.mine, s32[1]{0:T(128)} %bitcast.22.store, bf16[4,128,1920]{2,1,0:T(8,128)(2,1)S(1)} %all-to-all-done.1.refs_0_, ...), custom_call_target="tpu_custom_call" | custom-call | flops 1 | bytes 1 | tf_op jit(solution)/shard_map/pallas_call | solution.py:255
  171.2 0.8 copy-done.5
  172.0 3.6 %all-to-all-done.3.parts = bf16[4,672,128]{2,1,0:T(8,128)(2,1)} async-done(((bf16[4,672,128]{2,1,0:T(8,128)(2,1)}), bf16[4,672,128]{2,1,0:T(8,128)(2,1)}, u32[]{:S(2)}, u32[]{:S(2)}) %all-to-all-start.3) | async-done | bytes 688160 | tf_op jit(solution)/shard_map/all_to_all | solution.py:320
  175.6 3.5 %all-to-all-start.2 = ((bf16[4,672,128]{2,1,0:T(8,128)(2,1)}), bf16[4,672,128]{2,1,0:T(8,128)(2,1)S(1)}, u32[]{:S(2)}, u32[]{:S(2)}) async-start(bf16[4,672,128]{2,1,0:T(8,128)(2,1)} %copy-done.5), calls=%async_computation.2 | async-start | bytes 1376256 | tf_op jit(solution)/shard_map/all_to_all | solution.py:320
  179.1 2.4 %shard_map.90.refs_0_ = bf16[128,2560]{1,0:T(8,128)(2,1)} custom-call(bf16[4,672,128]{2,1,0:T(8,128)(2,1)} %all-to-all-done.5.parts), custom_call_target="tpu_custom_call" | custom-call | flops 1 | bytes 1 | tf_op jit(solution)/shard_map/pallas_call | solution.py:292
  181.5 2.4 %shard_map.91.refs_0_ = bf16[128,2560]{1,0:T(8,128)(2,1)} custom-call(bf16[4,672,128]{2,1,0:T(8,128)(2,1)} %all-to-all-done.4.parts, bf16[128,2560]{1,0:T(8,128)(2,1)} %shard_map.90.refs_0_), custom_call_target="tpu_custom_call", output_to_operand_aliasing={{}: (1, {})} | custom-call | flops 1 | bytes 1 | tf_op jit(solution)/shard_map/pallas_call | solution.py:292
  183.8 2.4 %shard_map.92.refs_0_ = bf16[128,2560]{1,0:T(8,128)(2,1)} custom-call(bf16[4,672,128]{2,1,0:T(8,128)(2,1)} %all-to-all-done.3.parts, bf16[128,2560]{1,0:T(8,128)(2,1)} %shard_map.91.refs_0_), custom_call_target="tpu_custom_call", output_to_operand_aliasing={{}: (1, {})} | custom-call | flops 1 | bytes 1 | tf_op jit(solution)/shard_map/pallas_call | solution.py:292
  186.2 10.4 %all-to-all-done.2.parts = bf16[4,672,128]{2,1,0:T(8,128)(2,1)S(1)} async-done(((bf16[4,672,128]{2,1,0:T(8,128)(2,1)}), bf16[4,672,128]{2,1,0:T(8,128)(2,1)S(1)}, u32[]{:S(2)}, u32[]{:S(2)}) %all-to-all-start.2) | async-done | bytes 688160 | tf_op jit(solution)/shard_map/all_to_all | solution.py:320
  196.6 0.9 copy-done.9
  197.5 2.4 %shard_map.93 = bf16[128,2560]{1,0:T(8,128)(2,1)} custom-call(bf16[4,672,128]{2,1,0:T(8,128)(2,1)} %copy-done.9, bf16[128,2560]{1,0:T(8,128)(2,1)} %shard_map.92.refs_0_), custom_call_target="tpu_custom_call", output_to_operand_aliasing={{}: (1, {})} | custom-call | flops 1 | bytes 1 | tf_op jit(solution)/shard_map/pallas_call | solution.py:292
  (38 shorter events, 0.3 us)
Async XLA Ops:
  0.6 11.2 %slice-start = ((bf16[128,2560]{1,0:T(8,128)(2,1)}), bf16[128,640]{1,0:T(8,128)(2,1)S(1)}, s32[]{:S(2)}) async-start(bf16[128,2560]{1,0:T(8,128)(2,1)} %param.7), calls=%async_computation.6 | async-start | bytes 327680 | tf_op jit(solution)/shard_map/slice | solution.py:343
  0.6 9.8 %collective-permute-start = (bf16[1,2,128,512]{3,2,1,0:T(8,128)(2,1)}, bf16[1,2,128,512]{3,2,1,0:T(8,128)(2,1)S(1)}, u32[]{:S(2)}, u32[]{:S(2)}) collective-permute-start(bf16[1,2,128,512]{3,2,1,0:T(8,128)(2,1)} %bitcast.25), channel_id=1, source_target_pairs={{0,1},{1,2},{2,3},{3,4},{4,5},{5,6},{6,7},{7,8},{8,9},{9,10},{10,1... | collective-permute-start | bytes 786440 | tf_op jit(solution)/shard_map/ppermute | solution.py:34
  11.7 78.6 %collective-permute-start.1 = (bf16[16,2,128,512]{3,2,1,0:T(8,128)(2,1)}, bf16[16,2,128,512]{3,2,1,0:T(8,128)(2,1)}, u32[]{:S(2)}, u32[]{:S(2)}) collective-permute-start(bf16[16,2,128,512]{3,2,1,0:T(8,128)(2,1)} %refs_6_.1), channel_id=1, source_target_pairs={{0,1},{1,0},{2,3},{3,2},{4,5},{5,4},{6,7},{7,6},{8,9},{9,8},{10,11... | collective-permute-start | bytes 12582920 | tf_op jit(solution)/shard_map/ppermute | solution.py:29
  11.9 24.4 %slice-start.1 = ((bf16[128,2560]{1,0:T(8,128)(2,1)}), bf16[128,1920]{1,0:T(8,128)(2,1)S(1)}, s32[]{:S(2)}) async-start(bf16[128,2560]{1,0:T(8,128)(2,1)} %param.7), calls=%async_computation.7 | async-start | bytes 983040 | tf_op jit(solution)/shard_map/slice | solution.py:345
  37.7 70.8 %all-to-all-start.1 = ((bf16[4,128,1920]{2,1,0:T(8,128)(2,1)}), bf16[4,128,1920]{2,1,0:T(8,128)(2,1)S(1)}, u32[]{:S(2)}, u32[]{:S(2)}) async-start(bf16[4,128,1920]{2,1,0:T(8,128)(2,1)} %broadcast_in_dim.32), calls=%async_computation.1 | async-start | bytes 3932160 | tf_op jit(solution)/shard_map/all_to_all | solution.py:320
  41.3 49.0 %copy-start.1 = (bf16[1,1,2,128,512]{4,3,2,1,0:T(8,128)(2,1)S(1)}, bf16[1,1,2,128,512]{4,3,2,1,0:T(8,128)(2,1)}, u32[]{:S(2)}) copy-start(bf16[1,1,2,128,512]{4,3,2,1,0:T(8,128)(2,1)} %param.8) | copy-start | bytes 786436
  41.3 26.3 %collective-permute-start.7 = (bf16[16,2,128,128]{3,2,1,0:T(8,128)(2,1)S(1)}, bf16[16,2,128,128]{3,2,1,0:T(8,128)(2,1)}, u32[]{:S(2)}, u32[]{:S(2)}) collective-permute-start(bf16[16,2,128,128]{3,2,1,0:T(8,128)(2,1)S(1)} %slice.36.refs_1_), channel_id=1, source_target_pairs={{0,2},{1,3},{2,0},{3,1},{4,6},{5,7},{6,4},{7,5},{8,10},{9,11},{10,... | collective-permute-start | bytes 3145736 | tf_op jit(solution)/shard_map/ppermute | solution.py:29
  45.6 44.4 %collective-permute-start.3 = (bf16[16,2,128,128]{3,2,1,0:T(8,128)(2,1)}, bf16[16,2,128,128]{3,2,1,0:T(8,128)(2,1)}, u32[]{:S(2)}, u32[]{:S(2)}) collective-permute-start(bf16[16,2,128,128]{3,2,1,0:T(8,128)(2,1)} %get-tuple-element.21.refs_1_), channel_id=1, source_target_pairs={{0,2},{1,3},{2,0},{3,1},{4,6},{5,7},{6,4},{7,5},{8,10},{9,11},{10,... | collective-permute-start | bytes 3145736 | tf_op jit(solution)/shard_map/ppermute | solution.py:29
  67.6 22.7 %collective-permute-start.8 = (bf16[16,2,128,128]{3,2,1,0:T(8,128)(2,1)}, bf16[16,2,128,128]{3,2,1,0:T(8,128)(2,1)}, u32[]{:S(2)}, u32[]{:S(2)}) collective-permute-start(bf16[16,2,128,128]{3,2,1,0:T(8,128)(2,1)} %collective-permute-done.7.refs_3_), channel_id=1, source_target_pairs={{0,1},{1,0},{2,3},{3,2},{4,5},{5,4},{6,7},{7,6},{8,9},{9,8},{10,11... | collective-permute-start | bytes 3145736 | tf_op jit(solution)/shard_map/ppermute | solution.py:29
  68.2 45.6 %collective-permute-start.6 = (bf16[16,2,128,128]{3,2,1,0:T(8,128)(2,1)}, bf16[16,2,128,128]{3,2,1,0:T(8,128)(2,1)}, u32[]{:S(2)}, u32[]{:S(2)}) collective-permute-start(bf16[16,2,128,128]{3,2,1,0:T(8,128)(2,1)} %get-tuple-element.20.refs_1_), channel_id=1, source_target_pairs={{0,2},{1,3},{2,0},{3,1},{4,6},{5,7},{6,4},{7,5},{8,10},{9,11},{10,... | collective-permute-start | bytes 3145736 | tf_op jit(solution)/shard_map/ppermute | solution.py:29
  90.0 23.8 %collective-permute-start.4 = (bf16[16,2,128,128]{3,2,1,0:T(8,128)(2,1)}, bf16[16,2,128,128]{3,2,1,0:T(8,128)(2,1)}, u32[]{:S(2)}, u32[]{:S(2)}) collective-permute-start(bf16[16,2,128,128]{3,2,1,0:T(8,128)(2,1)} %collective-permute-done.3.refs_3_), channel_id=1, source_target_pairs={{0,1},{1,0},{2,3},{3,2},{4,5},{5,4},{6,7},{7,6},{8,9},{9,8},{10,11... | collective-permute-start | bytes 3145736 | tf_op jit(solution)/shard_map/ppermute | solution.py:29
  90.3 2.2 %copy-start = (bf16[16,2,128,512]{3,2,1,0:T(8,128)(2,1)S(1)}, bf16[16,2,128,512]{3,2,1,0:T(8,128)(2,1)}, u32[]{:S(2)}) copy-start(bf16[16,2,128,512]{3,2,1,0:T(8,128)(2,1)} %refs_6_.1) | copy-start | bytes 12582916
  92.5 1.1 copy-start.4
  107.6 0.9 copy-start.8
  108.5 22.9 %all-to-all-start.5 = ((bf16[4,672,128]{2,1,0:T(8,128)(2,1)}), bf16[4,672,128]{2,1,0:T(8,128)(2,1)}, u32[]{:S(2)}, u32[]{:S(2)}) async-start(bf16[4,672,128]{2,1,0:T(8,128)(2,1)} %copy-done.8), calls=%async_computation.5 | async-start | bytes 1376256 | tf_op jit(solution)/shard_map/all_to_all | solution.py:320
  112.8 25.4 %collective-permute-start.2 = (bf16[16,2,128,128]{3,2,1,0:T(8,128)(2,1)}, bf16[16,2,128,128]{3,2,1,0:T(8,128)(2,1)}, u32[]{:S(2)}, u32[]{:S(2)}) collective-permute-start(bf16[16,2,128,128]{3,2,1,0:T(8,128)(2,1)} %get-tuple-element.22.refs_1_), channel_id=1, source_target_pairs={{0,2},{1,3},{2,0},{3,1},{4,6},{5,7},{6,4},{7,5},{8,10},{9,11},{10,... | collective-permute-start | bytes 3145736 | tf_op jit(solution)/shard_map/ppermute | solution.py:29
  113.8 24.4 %collective-permute-start.9 = (bf16[16,2,128,128]{3,2,1,0:T(8,128)(2,1)}, bf16[16,2,128,128]{3,2,1,0:T(8,128)(2,1)}, u32[]{:S(2)}, u32[]{:S(2)}) collective-permute-start(bf16[16,2,128,128]{3,2,1,0:T(8,128)(2,1)} %collective-permute-done.6.refs_3_), channel_id=1, source_target_pairs={{0,1},{1,0},{2,3},{3,2},{4,5},{5,4},{6,7},{7,6},{8,9},{9,8},{10,11... | collective-permute-start | bytes 3145736 | tf_op jit(solution)/shard_map/ppermute | solution.py:29
  126.4 0.8 copy-start.6
  127.2 11.0 %copy-start.3 = (bf16[16,2,128,128]{3,2,1,0:T(8,128)(2,1)S(1)}, bf16[16,2,128,128]{3,2,1,0:T(8,128)(2,1)}, u32[]{:S(2)}) copy-start(bf16[16,2,128,128]{3,2,1,0:T(8,128)(2,1)} %get-tuple-element.20.refs_1_) | copy-start | bytes 3145732
  131.4 21.9 %all-to-all-start.4 = ((bf16[4,672,128]{2,1,0:T(8,128)(2,1)}), bf16[4,672,128]{2,1,0:T(8,128)(2,1)}, u32[]{:S(2)}, u32[]{:S(2)}) async-start(bf16[4,672,128]{2,1,0:T(8,128)(2,1)} %copy-done.6), calls=%async_computation.4 | async-start | bytes 1376256 | tf_op jit(solution)/shard_map/all_to_all | solution.py:320
  138.2 19.3 %collective-permute-start.5 = (bf16[16,2,128,128]{3,2,1,0:T(8,128)(2,1)}, bf16[16,2,128,128]{3,2,1,0:T(8,128)(2,1)}, u32[]{:S(2)}, u32[]{:S(2)}) collective-permute-start(bf16[16,2,128,128]{3,2,1,0:T(8,128)(2,1)} %collective-permute-done.2.refs_3_), channel_id=1, source_target_pairs={{0,1},{1,0},{2,3},{3,2},{4,5},{5,4},{6,7},{7,6},{8,9},{9,8},{10,11... | collective-permute-start | bytes 3145736 | tf_op jit(solution)/shard_map/ppermute | solution.py:29
  151.9 0.9 copy-start.7
  152.8 4.7 %copy-start.2 = (bf16[16,2,128,128]{3,2,1,0:T(8,128)(2,1)S(1)}, bf16[16,2,128,128]{3,2,1,0:T(8,128)(2,1)}, u32[]{:S(2)}) copy-start(bf16[16,2,128,128]{3,2,1,0:T(8,128)(2,1)} %get-tuple-element.22.refs_1_) | copy-start | bytes 3145732
  153.3 22.3 %all-to-all-start.3 = ((bf16[4,672,128]{2,1,0:T(8,128)(2,1)}), bf16[4,672,128]{2,1,0:T(8,128)(2,1)}, u32[]{:S(2)}, u32[]{:S(2)}) async-start(bf16[4,672,128]{2,1,0:T(8,128)(2,1)} %copy-done.7), calls=%async_computation.3 | async-start | bytes 1376256 | tf_op jit(solution)/shard_map/all_to_all | solution.py:320
  171.1 0.9 copy-start.5
  175.6 21.0 %all-to-all-start.2 = ((bf16[4,672,128]{2,1,0:T(8,128)(2,1)}), bf16[4,672,128]{2,1,0:T(8,128)(2,1)S(1)}, u32[]{:S(2)}, u32[]{:S(2)}) async-start(bf16[4,672,128]{2,1,0:T(8,128)(2,1)} %copy-done.5), calls=%async_computation.2 | async-start | bytes 1376256 | tf_op jit(solution)/shard_map/all_to_all | solution.py:320
  196.6 0.9 copy-start.9

commit v12 on v10

--- a/solution.py
+++ b/solution.py
@@ -18,7 +18,6 @@
 CLUSTER = 4
 BLOCK = 4
 STAT = 32
-HEADS = ((0, 1, 2), (3, 4))
 ROWS = GQ * PAGE + STAT
 CHUNK = GQ * HD
 CONTRACT_LAST = (((1,), (1,)), ((), ()))
@@ -109,30 +108,31 @@
 
         pltpu.make_async_copy(incoming.at[0], pool_out.at[store[0]], store_sems.at[store[0]]).start()
 
-    def soften(heads, scored, values):
+    def soften(h, scored, values):
         factor = SCALE * LOG2E
-        expos = []
-        fades = []
-        for h in heads:
-            s = scored(h)
-            old = tops[h]
-            new = jnp.maximum(old, jnp.max(s, axis=1, keepdims=True))
-            tops[h] = new
-            fades.append(jnp.exp2((old - new) * factor))
-            wide = jnp.concatenate([new] * (s.shape[1] // PAGE), axis=1)
-            expos.append(jnp.exp2((s - wide) * factor).astype(jnp.bfloat16))
-        added = jnp.dot(jnp.concatenate(expos, axis=0), values, preferred_element_type=jnp.float32)
-        for i, h in enumerate(heads):
-            fade = fades[i]
-            acc[h] = acc[h] * jnp.concatenate([fade, fade], axis=1) + added[i * PAGE:(i + 1) * PAGE]
+        old = tops[h]
+        new = jnp.maximum(old, jnp.max(scored(), axis=1, keepdims=True))
+        tops[h] = new
+        fade = jnp.exp2((old - new) * factor)
+        s = scored()
+        wide = jnp.concatenate([new] * (s.shape[1] // PAGE), axis=1)
+        expo = jnp.exp2((s - wide) * factor).astype(jnp.bfloat16)
+        added = jnp.dot(expo, values, preferred_element_type=jnp.float32)
+        acc[h] = acc[h] * jnp.concatenate([fade, fade], axis=1) + added
 
     def with_ones(values):
         return jnp.concatenate([values, jnp.ones_like(values)], axis=1)
 
-    def score(t, heads, keys):
-        query = queries[t, heads[0]:heads[-1] + 1].reshape(len(heads) * PAGE, HD)
-        s = lax.dot_general(query, keys, CONTRACT_LAST, preferred_element_type=jnp.float32)
-        return s.reshape(len(heads), PAGE, keys.shape[0])
+    def score(t, h, keys):
+        return lax.dot_general(queries[t, h], keys, CONTRACT_LAST, preferred_element_type=jnp.float32)
+
+    def seen_of(t, index):
+        request = request_of(t)
+        return (counts[request] - 1 - index * BLOCK) * PAGE + lasts[request]
+
+    def score_block(t, index, h, keys):
+        column = lax.broadcasted_iota(jnp.int32, (PAGE, BLOCK * PAGE), 1)
+        scores[h] = jnp.where(column < seen_of(t, index), score(t, h, keys), LOW)
 
     def keys_of(t, index):
         return pages[lax.rem(t, 2), pl.ds(index * BLOCK, BLOCK), 0].reshape(BLOCK * PAGE, HD)
@@ -173,17 +173,16 @@
     reset()
     span_values = with_ones(pages[0, extra, 1])
     seen = lax.broadcasted_iota(jnp.int32, (PAGE, PAGE), 1) <= lax.broadcasted_iota(jnp.int32, (PAGE, PAGE), 0)
-    for heads in HEADS:
-        s = score(0, heads, pages[0, extra, 0])
-        soften(heads, lambda h: jnp.where(seen, s[h - heads[0]], LOW), span_values)
+    for h in range(GQ):
+        s = jnp.where(seen, score(0, h, pages[0, extra, 0]), LOW)
+        soften(h, lambda: s, span_values)
     arrive(0)
     first = keys_of(0, 0)
-    for heads in HEADS:
-        scores[heads[0]:heads[-1] + 1] = score(0, heads, first)
+    for h in range(GQ):
+        score_block(0, 0, h, first)
 
     def step(_, carry):
         t, index = carry
-        request = request_of(t)
         ends = index + 1 >= blocks_of(t)
         later_t = jnp.where(ends, t + 1, t)
         later_index = jnp.where(ends, 0, index + 1)
@@ -193,13 +192,11 @@
         def _():
             arrive(t + 1)
 
-        limit = (counts[request] - 1 - index * BLOCK) * PAGE + lasts[request]
-        column = lax.broadcasted_iota(jnp.int32, (PAGE, BLOCK * PAGE), 1)
         values = values_of(t, index)
         keys = keys_of(ahead_t, later_index)
-        for heads in HEADS:
-            soften(heads, lambda h: jnp.where(column < limit, scores[h], LOW), values)
-            scores[heads[0]:heads[-1] + 1] = score(ahead_t, heads, keys)
+        for h in range(GQ):
+            soften(h, lambda: scores[h], values)
+            score_block(ahead_t, later_index, h, keys)
 
         @pl.when(ends)
         def _():
@@ -256,7 +253,7 @@
         functools.partial(attend_kernel, lines, head, q_head),
         grid_spec=grid_spec,
         out_shape=out_shape,
-        compiler_params=pltpu.CompilerParams(vmem_limit_bytes=16 * 2**20),
+        compiler_params=pltpu.CompilerParams(vmem_limit_bytes=24 * 2**20),
         cost_estimate=pl.CostEstimate(flops=1, bytes_accessed=1, transcendentals=0),
     )(picks, counts, lasts, mine, store, *operands)
 
@@ -332,12 +329,12 @@
     slots = pool.shape[0]
     capacity = (MAXP + width - 2) // (width - 1)
     limit = min(MAXP, CLUSTER * capacity)
-    owns = [pool[:, :, :, :HD]]
+    incoming = shifted(new_kv[0], "serve", 1)
+    owns = [after(pool, incoming)[:, :, :, :HD]]
     rest = after(pool, owns[0])
     owns += [rest[:, :, :, g * HD:(g + 1) * HD] for g in range(1, KVH)]
     sides = [swapped(own, "serve", 2) for own in owns]
     twin = swapped(rest, "serve", 1)
-    incoming = shifted(new_kv[0], "serve", 1)
     rows = page_rows(me, lines, limit, slots, page_owner, page_slot, prefix_len).astype(queries.dtype)
     rows = jnp.pad(rows[:, None], ((0, 0), (0, PAGE - 1), (0, PAGE - limit - 2)))
     q_all = jnp.broadcast_to(queries[None], (lines, PAGE, KVH * CHUNK))
@@ -349,8 +346,6 @@
     parts = []
     for g in range(KVH):
         side = sides[g]
-        if g == 1:
-            side = after(side, incoming)
         if g > 1:
             side = after(side, parts[g - 2])
         both = swapped(side, "serve", 1)

time: 189 us -> 240 us (1.27)
  waiting for transfers between devices: 75.5 us -> 116 us
  Pallas kernels: 56.9 us -> 62.2 us
  starting transfers between devices: 32.6 us -> 37.9 us
    ppermute x1, waiting for transfers between devices: 22.1 us -> 52.3 us  [shifted(): lax.ppermute(array, axis, [(i, (i + by) % size) for i in range(size)])]
    ppermute x9, waiting for transfers between devices: 24.8 us -> 45.1 us  [swapped(): return lax.ppermute(array, axis, [(i, i ^ bit) for i in range(size)])]
    all_to_all x5, starting transfers between devices: 23.8 us -> 33.9 us  [exchanged(): lax.all_to_all(array, 'serve', 0, 0, axis_index_groups=groups, tiled=True)]
    all_to_all x5, waiting for transfers between devices: 28.6 us -> 18.9 us  [exchanged(): lax.all_to_all(array, 'serve', 0, 0, axis_index_groups=groups, tiled=True)]
    pallas_call x4, Pallas kernels: 47.5 us -> 52.8 us  [attend(): pl.pallas_call(functools.partial(attend_kernel, lines, head, q_head), gri...]
    ppermute x9, starting transfers between devices: 8.33 us -> 4.06 us  [swapped(): return lax.ppermute(array, axis, [(i, i ^ bit) for i in range(size)])]
    unnamed x20 -> x22, local copies, waits for them, and re-layouts: 8.85 us -> 10.1 us
  transfers between devices with their start and end apart: 15 -> 15, of which waited for: 9 -> 8; matrix products, arithmetic and copies ran while one was open for 3% -> 2% of each run, Pallas kernels for 29% -> 25%
where the time goes in v12:
time: 240 us
  waiting for transfers between devices  116 us (48%)
  Pallas kernels  62.2 us (26%)
  starting transfers between devices  37.9 us (16%)
  local copies, waits for them, and re-layouts  17.1 us (7%)
  other arithmetic  3.76 us (2%)
    pallas_call x4, Pallas kernels, attend(): pl.pallas_call(functools.partial(attend_kernel, lines, head, q_head), gri...  52.8 us
    ppermute x1, waiting for transfers between devices, shifted(): lax.ppermute(array, axis, [(i, (i + by) % size) for i in range(size)])  52.3 us
    ppermute x9, waiting for transfers between devices, swapped(): return lax.ppermute(array, axis, [(i, i ^ bit) for i in range(size)])  45.1 us
    all_to_all x5, starting transfers between devices, exchanged(): lax.all_to_all(array, 'serve', 0, 0, axis_index_groups=groups, tiled=True)  33.9 us
    all_to_all x5, waiting for transfers between devices, exchanged(): lax.all_to_all(array, 'serve', 0, 0, axis_index_groups=groups, tiled=True)  18.9 us
    unnamed x22, local copies, waits for them, and re-layouts  10.1 us
    pallas_call x4, Pallas kernels, merge(): pl.pallas_call(functools.partial(merge_kernel, head), in_specs=[pl.BlockS...  9.41 us
  transfers between devices with their start and end apart: 15, of which 8 were waited for; matrix products, arithmetic and copies ran while one was open for 2% of the time, Pallas kernels for 25%

profile of v12, /device:TPU:0, one launch (start us, length us, event | category | flops | bytes accessed | tf_op | source)
XLA Modules:
  0.0 239.5 jit_solution(7317040996784854667)
XLA Ops:
  1.3 0.7 fusion.15
  2.0 0.7 fusion.13
  2.7 0.1 convert_reduce_fusion.1
  2.8 0.1 convert_reduce_fusion
  3.0 0.1 select_reduce_fusion
  3.2 0.1 and_reduce_fusion
  3.3 0.1 copy.20
  3.4 0.1 copy.19
  3.5 0.1 fusion.8
  3.6 1.3 broadcast_in_dim.24
  4.9 1.7 pad_maximum_fusion
  6.6 6.4 %all-to-all-start = ((bf16[4,128,2688]{2,1,0:T(8,128)(2,1)}), bf16[4,128,2688]{2,1,0:T(8,128)(2,1)S(1)}, u32[]{:S(2)}, u32[]{:S(2)}) async-start(bf16[4,128,2688]{2,1,0:T(8,128)(2,1)} %pad_maximum_fusion), calls=%async_computation | async-start | bytes 5505024 | tf_op jit(solution)/shard_map/all_to_all | solution.py:317
  13.1 52.3 %collective-permute-done.refs_7_ = bf16[1,2,128,512]{3,2,1,0:T(8,128)(2,1)S(1)} collective-permute-done((bf16[1,2,128,512]{3,2,1,0:T(8,128)(2,1)S(1)}, bf16[1,2,128,512]{3,2,1,0:T(8,128)(2,1)S(1)}, u32[]{:S(2)}, u32[]{:S(2)}) %collective-permute-start) | collective-permute-done | bytes 262176 | tf_op jit(solution)/shard_map/ppermute | solution.py:33
  65.4 1.3 slice.28.refs_1_
  66.9 4.0 %fusion.17 = (bf16[16,2,128,128]{3,2,1,0:T(8,128)(2,1)}, bf16[16,2,128,128]{3,2,1,0:T(8,128)(2,1)}, bf16[16,2,128,128]{3,2,1,0:T(8,128)(2,1)}) fusion(bf16[16,2,128,512]{3,2,1,0:T(8,128)(2,1)} %refs_6_.1), kind=kLoop, calls=%fused_computation.41 | loop fusion | bytes 6291456 | tf_op jit(solution)/shard_map/slice | solution.py:335
  70.9 1.8 collective-permute-start.3
  72.6 20.3 %collective-permute-done.7.refs_3_ = bf16[16,2,128,128]{3,2,1,0:T(8,128)(2,1)} collective-permute-done((bf16[16,2,128,128]{3,2,1,0:T(8,128)(2,1)S(1)}, bf16[16,2,128,128]{3,2,1,0:T(8,128)(2,1)}, u32[]{:S(2)}, u32[]{:S(2)}) %collective-permute-start.7) | collective-permute-done | bytes 1048608 | tf_op jit(solution)/shard_map/ppermute | solution.py:28
  93.6 0.1 collective-permute-start.6
  93.7 21.7 %collective-permute-done.3.refs_3_ = bf16[16,2,128,128]{3,2,1,0:T(8,128)(2,1)} collective-permute-done((bf16[16,2,128,128]{3,2,1,0:T(8,128)(2,1)}, bf16[16,2,128,128]{3,2,1,0:T(8,128)(2,1)}, u32[]{:S(2)}, u32[]{:S(2)}) %collective-permute-start.3) | collective-permute-done | bytes 1048608 | tf_op jit(solution)/shard_map/ppermute | solution.py:28
  115.4 0.2 slice_reduce_fusion
  115.7 2.2 copy-done
  117.9 1.2 copy-done.3
  119.1 13.7 %shard_map.88 = (bf16[4,672,128]{2,1,0:T(8,128)(2,1)S(1)}, bf16[16,2,128,512]{3,2,1,0:T(8,128)(2,1)}) custom-call(s32[4,16]{1,0:T(4,128)S(1)} %bitcast.31, s32[4]{0:T(128)S(1)} %get-tuple-element.15.counts, s32[4]{0:T(128)S(1)} %get-tuple-element.14.lasts, s32[1]{0:T(128)} %bitcast.8.mine, s32[1]{0:T(128)} %bitcast.23.store, ...), custom_call_target="tpu_custom_call" | custom-call | flops 1 | bytes 1 | tf_op jit(solution)/shard_map/pallas_call | solution.py:252
  132.8 0.8 copy-done.9
  133.7 14.9 %all-to-all-start.4 = ((bf16[4,672,128]{2,1,0:T(8,128)(2,1)}), bf16[4,672,128]{2,1,0:T(8,128)(2,1)}, u32[]{:S(2)}, u32[]{:S(2)}) async-start(bf16[4,672,128]{2,1,0:T(8,128)(2,1)} %copy-done.9), calls=%async_computation.4 | async-start | bytes 1376256 | tf_op jit(solution)/shard_map/all_to_all | solution.py:317
  148.5 1.6 collective-permute-start.9
  150.2 12.3 %shard_map.86 = bf16[4,672,128]{2,1,0:T(8,128)(2,1)S(1)} custom-call(s32[4,16]{1,0:T(4,128)S(1)} %bitcast.32, s32[4]{0:T(128)S(1)} %get-tuple-element.15.counts, s32[4]{0:T(128)S(1)} %get-tuple-element.14.lasts, s32[1]{0:T(128)} %bitcast.8.mine, s32[1]{0:T(128)} %bitcast.21.store, bf16[4,128,2688]{2,1,0:T(8,128)(2,1)S(1)} %all-to-all-done.refs_0_, ...), custom_call_target="tpu_custom_call" | custom-call | flops 1 | bytes 1 | tf_op jit(solution)/shard_map/pallas_call | solution.py:252
  162.5 0.9 copy-done.7
  163.4 3.7 %all-to-all-done.4.parts = bf16[4,672,128]{2,1,0:T(8,128)(2,1)} async-done(((bf16[4,672,128]{2,1,0:T(8,128)(2,1)}), bf16[4,672,128]{2,1,0:T(8,128)(2,1)}, u32[]{:S(2)}, u32[]{:S(2)}) %all-to-all-start.4) | async-done | bytes 688160 | tf_op jit(solution)/shard_map/all_to_all | solution.py:317
  167.0 4.2 %all-to-all-start.3 = ((bf16[4,672,128]{2,1,0:T(8,128)(2,1)}), bf16[4,672,128]{2,1,0:T(8,128)(2,1)}, u32[]{:S(2)}, u32[]{:S(2)}) async-start(bf16[4,672,128]{2,1,0:T(8,128)(2,1)} %copy-done.7), calls=%async_computation.3 | async-start | bytes 1376256 | tf_op jit(solution)/shard_map/all_to_all | solution.py:317
  171.2 3.1 %collective-permute-done.2.refs_3_ = bf16[16,2,128,128]{3,2,1,0:T(8,128)(2,1)} collective-permute-done((bf16[16,2,128,128]{3,2,1,0:T(8,128)(2,1)}, bf16[16,2,128,128]{3,2,1,0:T(8,128)(2,1)}, u32[]{:S(2)}, u32[]{:S(2)}) %collective-permute-start.2) | collective-permute-done | bytes 1048608 | tf_op jit(solution)/shard_map/ppermute | solution.py:28
  174.4 0.4 collective-permute-start.5
  174.7 1.2 copy-done.5
  175.9 13.4 %shard_map.89 = bf16[4,672,128]{2,1,0:T(8,128)(2,1)S(1)} custom-call(s32[4,16]{1,0:T(4,128)S(1)} %bitcast.33, s32[4]{0:T(128)S(1)} %get-tuple-element.15.counts, s32[4]{0:T(128)S(1)} %get-tuple-element.14.lasts, s32[1]{0:T(128)} %bitcast.8.mine, s32[1]{0:T(128)} %bitcast.24.store, bf16[4,128,2688]{2,1,0:T(8,128)(2,1)S(1)} %all-to-all-done.refs_0_, ...), custom_call_target="tpu_custom_call" | custom-call | flops 1 | bytes 1 | tf_op jit(solution)/shard_map/pallas_call | solution.py:252
  189.3 0.8 copy-done.8
  190.2 0.4 all-to-all-done.3.parts
  190.6 4.9 %all-to-all-start.2 = ((bf16[4,672,128]{2,1,0:T(8,128)(2,1)}), bf16[4,672,128]{2,1,0:T(8,128)(2,1)}, u32[]{:S(2)}, u32[]{:S(2)}) async-start(bf16[4,672,128]{2,1,0:T(8,128)(2,1)} %copy-done.8), calls=%async_computation.2 | async-start | bytes 1376256 | tf_op jit(solution)/shard_map/all_to_all | solution.py:317
  195.5 1.2 copy-done.4
  196.7 13.4 %shard_map.87 = bf16[4,672,128]{2,1,0:T(8,128)(2,1)S(1)} custom-call(s32[4,16]{1,0:T(4,128)S(1)} %bitcast.34, s32[4]{0:T(128)S(1)} %get-tuple-element.15.counts, s32[4]{0:T(128)S(1)} %get-tuple-element.14.lasts, s32[1]{0:T(128)} %bitcast.8.mine, s32[1]{0:T(128)} %bitcast.22.store, bf16[4,128,2688]{2,1,0:T(8,128)(2,1)S(1)} %all-to-all-done.refs_0_, ...), custom_call_target="tpu_custom_call" | custom-call | flops 1 | bytes 1 | tf_op jit(solution)/shard_map/pallas_call | solution.py:252
  210.1 0.8 copy-done.6
  210.9 3.7 %all-to-all-done.2.parts = bf16[4,672,128]{2,1,0:T(8,128)(2,1)} async-done(((bf16[4,672,128]{2,1,0:T(8,128)(2,1)}), bf16[4,672,128]{2,1,0:T(8,128)(2,1)}, u32[]{:S(2)}, u32[]{:S(2)}) %all-to-all-start.2) | async-done | bytes 688160 | tf_op jit(solution)/shard_map/all_to_all | solution.py:317
  214.6 3.5 %all-to-all-start.1 = ((bf16[4,672,128]{2,1,0:T(8,128)(2,1)}), bf16[4,672,128]{2,1,0:T(8,128)(2,1)S(1)}, u32[]{:S(2)}, u32[]{:S(2)}) async-start(bf16[4,672,128]{2,1,0:T(8,128)(2,1)} %copy-done.6), calls=%async_computation.1 | async-start | bytes 1376256 | tf_op jit(solution)/shard_map/all_to_all | solution.py:317
  218.1 2.4 shard_map.90.refs_0_
  220.5 2.4 shard_map.91.refs_0_
  222.8 2.4 shard_map.92.refs_0_
  225.2 11.1 %all-to-all-done.1.parts = bf16[4,672,128]{2,1,0:T(8,128)(2,1)S(1)} async-done(((bf16[4,672,128]{2,1,0:T(8,128)(2,1)}), bf16[4,672,128]{2,1,0:T(8,128)(2,1)S(1)}, u32[]{:S(2)}, u32[]{:S(2)}) %all-to-all-start.1) | async-done | bytes 688160 | tf_op jit(solution)/shard_map/all_to_all | solution.py:317
  236.3 0.9 copy-done.10
  237.2 2.4 shard_map.93
  (34 shorter events, 0.3 us)
Async XLA Ops:
  6.6 6.5 %copy-start.1 = (bf16[1,1,2,128,512]{4,3,2,1,0:T(8,128)(2,1)S(1)}, bf16[1,1,2,128,512]{4,3,2,1,0:T(8,128)(2,1)}, u32[]{:S(2)}) copy-start(bf16[1,1,2,128,512]{4,3,2,1,0:T(8,128)(2,1)} %param.8) | copy-start | bytes 786436
  6.6 108.8 %all-to-all-start = ((bf16[4,128,2688]{2,1,0:T(8,128)(2,1)}), bf16[4,128,2688]{2,1,0:T(8,128)(2,1)S(1)}, u32[]{:S(2)}, u32[]{:S(2)}) async-start(bf16[4,128,2688]{2,1,0:T(8,128)(2,1)} %pad_maximum_fusion), calls=%async_computation | async-start | bytes 5505024 | tf_op jit(solution)/shard_map/all_to_all | solution.py:317
  13.1 52.3 %collective-permute-start = (bf16[1,2,128,512]{3,2,1,0:T(8,128)(2,1)S(1)}, bf16[1,2,128,512]{3,2,1,0:T(8,128)(2,1)S(1)}, u32[]{:S(2)}, u32[]{:S(2)}) collective-permute-start(bf16[1,2,128,512]{3,2,1,0:T(8,128)(2,1)S(1)} %bitcast.25), channel_id=1, source_target_pairs={{0,1},{1,2},{2,3},{3,4},{4,5},{5,6},{6,7},{7,8},{8,9},{9,10},{10,1... | collective-permute-start | bytes 786440 | tf_op jit(solution)/shard_map/ppermute | solution.py:33
  66.7 4.1 %copy-start.2 = (bf16[16,2,128,128]{3,2,1,0:T(8,128)(2,1)}, bf16[16,2,128,128]{3,2,1,0:T(8,128)(2,1)S(1)}, u32[]{:S(2)}) copy-start(bf16[16,2,128,128]{3,2,1,0:T(8,128)(2,1)S(1)} %slice.28.refs_1_) | copy-start | bytes 3145732
  66.7 48.9 %collective-permute-start.1 = (bf16[16,2,128,512]{3,2,1,0:T(8,128)(2,1)}, bf16[16,2,128,512]{3,2,1,0:T(8,128)(2,1)}, u32[]{:S(2)}, u32[]{:S(2)}) collective-permute-start(bf16[16,2,128,512]{3,2,1,0:T(8,128)(2,1)} %refs_6_.1), channel_id=1, source_target_pairs={{0,1},{1,0},{2,3},{3,2},{4,5},{5,4},{6,7},{7,6},{8,9},{9,8},{10,11... | collective-permute-start | bytes 12582920 | tf_op jit(solution)/shard_map/ppermute | solution.py:28
  66.8 26.1 %collective-permute-start.7 = (bf16[16,2,128,128]{3,2,1,0:T(8,128)(2,1)S(1)}, bf16[16,2,128,128]{3,2,1,0:T(8,128)(2,1)}, u32[]{:S(2)}, u32[]{:S(2)}) collective-permute-start(bf16[16,2,128,128]{3,2,1,0:T(8,128)(2,1)S(1)} %slice.28.refs_1_), channel_id=1, source_target_pairs={{0,2},{1,3},{2,0},{3,1},{4,6},{5,7},{6,4},{7,5},{8,10},{9,11},{10,... | collective-permute-start | bytes 3145736 | tf_op jit(solution)/shard_map/ppermute | solution.py:28
  70.9 44.6 %collective-permute-start.3 = (bf16[16,2,128,128]{3,2,1,0:T(8,128)(2,1)}, bf16[16,2,128,128]{3,2,1,0:T(8,128)(2,1)}, u32[]{:S(2)}, u32[]{:S(2)}) collective-permute-start(bf16[16,2,128,128]{3,2,1,0:T(8,128)(2,1)} %get-tuple-element.19.refs_1_), channel_id=1, source_target_pairs={{0,2},{1,3},{2,0},{3,1},{4,6},{5,7},{6,4},{7,5},{8,10},{9,11},{10,... | collective-permute-start | bytes 3145736 | tf_op jit(solution)/shard_map/ppermute | solution.py:28
  92.9 22.7 %collective-permute-start.8 = (bf16[16,2,128,128]{3,2,1,0:T(8,128)(2,1)}, bf16[16,2,128,128]{3,2,1,0:T(8,128)(2,1)}, u32[]{:S(2)}, u32[]{:S(2)}) collective-permute-start(bf16[16,2,128,128]{3,2,1,0:T(8,128)(2,1)} %collective-permute-done.7.refs_3_), channel_id=1, source_target_pairs={{0,1},{1,0},{2,3},{3,2},{4,5},{5,4},{6,7},{7,6},{8,9},{9,8},{10,11... | collective-permute-start | bytes 3145736 | tf_op jit(solution)/shard_map/ppermute | solution.py:28
  93.6 54.9 %collective-permute-start.6 = (bf16[16,2,128,128]{3,2,1,0:T(8,128)(2,1)}, bf16[16,2,128,128]{3,2,1,0:T(8,128)(2,1)}, u32[]{:S(2)}, u32[]{:S(2)}) collective-permute-start(bf16[16,2,128,128]{3,2,1,0:T(8,128)(2,1)} %get-tuple-element.18.refs_1_), channel_id=1, source_target_pairs={{0,2},{1,3},{2,0},{3,1},{4,6},{5,7},{6,4},{7,5},{8,10},{9,11},{10,... | collective-permute-start | bytes 3145736 | tf_op jit(solution)/shard_map/ppermute | solution.py:28
  115.4 34.8 %collective-permute-start.4 = (bf16[16,2,128,128]{3,2,1,0:T(8,128)(2,1)}, bf16[16,2,128,128]{3,2,1,0:T(8,128)(2,1)}, u32[]{:S(2)}, u32[]{:S(2)}) collective-permute-start(bf16[16,2,128,128]{3,2,1,0:T(8,128)(2,1)} %collective-permute-done.3.refs_3_), channel_id=1, source_target_pairs={{0,1},{1,0},{2,3},{3,2},{4,5},{5,4},{6,7},{7,6},{8,9},{9,8},{10,11... | collective-permute-start | bytes 3145736 | tf_op jit(solution)/shard_map/ppermute | solution.py:28
  115.7 2.2 copy-start
  117.9 1.2 copy-start.3
  132.8 0.8 copy-start.9
  133.7 33.4 %all-to-all-start.4 = ((bf16[4,672,128]{2,1,0:T(8,128)(2,1)}), bf16[4,672,128]{2,1,0:T(8,128)(2,1)}, u32[]{:S(2)}, u32[]{:S(2)}) async-start(bf16[4,672,128]{2,1,0:T(8,128)(2,1)} %copy-done.9), calls=%async_computation.4 | async-start | bytes 1376256 | tf_op jit(solution)/shard_map/all_to_all | solution.py:317
  148.5 25.8 %collective-permute-start.2 = (bf16[16,2,128,128]{3,2,1,0:T(8,128)(2,1)}, bf16[16,2,128,128]{3,2,1,0:T(8,128)(2,1)}, u32[]{:S(2)}, u32[]{:S(2)}) collective-permute-start(bf16[16,2,128,128]{3,2,1,0:T(8,128)(2,1)} %get-tuple-element.20.refs_1_), channel_id=1, source_target_pairs={{0,2},{1,3},{2,0},{3,1},{4,6},{5,7},{6,4},{7,5},{8,10},{9,11},{10,... | collective-permute-start | bytes 3145736 | tf_op jit(solution)/shard_map/ppermute | solution.py:28
  148.5 26.2 %collective-permute-start.9 = (bf16[16,2,128,128]{3,2,1,0:T(8,128)(2,1)}, bf16[16,2,128,128]{3,2,1,0:T(8,128)(2,1)}, u32[]{:S(2)}, u32[]{:S(2)}) collective-permute-start(bf16[16,2,128,128]{3,2,1,0:T(8,128)(2,1)} %collective-permute-done.6.refs_3_), channel_id=1, source_target_pairs={{0,1},{1,0},{2,3},{3,2},{4,5},{5,4},{6,7},{7,6},{8,9},{9,8},{10,11... | collective-permute-start | bytes 3145736 | tf_op jit(solution)/shard_map/ppermute | solution.py:28
  162.5 0.9 copy-start.7
  167.0 23.5 %all-to-all-start.3 = ((bf16[4,672,128]{2,1,0:T(8,128)(2,1)}), bf16[4,672,128]{2,1,0:T(8,128)(2,1)}, u32[]{:S(2)}, u32[]{:S(2)}) async-start(bf16[4,672,128]{2,1,0:T(8,128)(2,1)} %copy-done.7), calls=%async_computation.3 | async-start | bytes 1376256 | tf_op jit(solution)/shard_map/all_to_all | solution.py:317
  174.4 21.1 %collective-permute-start.5 = (bf16[16,2,128,128]{3,2,1,0:T(8,128)(2,1)}, bf16[16,2,128,128]{3,2,1,0:T(8,128)(2,1)}, u32[]{:S(2)}, u32[]{:S(2)}) collective-permute-start(bf16[16,2,128,128]{3,2,1,0:T(8,128)(2,1)} %collective-permute-done.2.refs_3_), channel_id=1, source_target_pairs={{0,1},{1,0},{2,3},{3,2},{4,5},{5,4},{6,7},{7,6},{8,9},{9,8},{10,11... | collective-permute-start | bytes 3145736 | tf_op jit(solution)/shard_map/ppermute | solution.py:28
  174.7 1.2 copy-start.5
  189.3 0.9 copy-start.8
  190.6 24.0 %all-to-all-start.2 = ((bf16[4,672,128]{2,1,0:T(8,128)(2,1)}), bf16[4,672,128]{2,1,0:T(8,128)(2,1)}, u32[]{:S(2)}, u32[]{:S(2)}) async-start(bf16[4,672,128]{2,1,0:T(8,128)(2,1)} %copy-done.8), calls=%async_computation.2 | async-start | bytes 1376256 | tf_op jit(solution)/shard_map/all_to_all | solution.py:317
  195.5 1.2 copy-start.4
  210.1 0.9 copy-start.6
  214.6 21.7 %all-to-all-start.1 = ((bf16[4,672,128]{2,1,0:T(8,128)(2,1)}), bf16[4,672,128]{2,1,0:T(8,128)(2,1)S(1)}, u32[]{:S(2)}, u32[]{:S(2)}) async-start(bf16[4,672,128]{2,1,0:T(8,128)(2,1)} %copy-done.6), calls=%async_computation.1 | async-start | bytes 1376256 | tf_op jit(solution)/shard_map/all_to_all | solution.py:317
  236.3 0.9 copy-start.10

commit v13 on v12

--- a/solution.py
+++ b/solution.py
@@ -330,14 +330,14 @@
     capacity = (MAXP + width - 2) // (width - 1)
     limit = min(MAXP, CLUSTER * capacity)
     incoming = shifted(new_kv[0], "serve", 1)
-    owns = [after(pool, incoming)[:, :, :, :HD]]
+    owns = [pool[:, :, :, :HD]]
     rest = after(pool, owns[0])
     owns += [rest[:, :, :, g * HD:(g + 1) * HD] for g in range(1, KVH)]
     sides = [swapped(own, "serve", 2) for own in owns]
     twin = swapped(rest, "serve", 1)
     rows = page_rows(me, lines, limit, slots, page_owner, page_slot, prefix_len).astype(queries.dtype)
     rows = jnp.pad(rows[:, None], ((0, 0), (0, PAGE - 1), (0, PAGE - limit - 2)))
-    q_all = jnp.broadcast_to(queries[None], (lines, PAGE, KVH * CHUNK))
+    q_all = jnp.broadcast_to(after(queries, incoming)[None], (lines, PAGE, KVH * CHUNK))
     q_all = exchanged(jnp.concatenate([q_all, rows], axis=2), groups)
     numbers = q_all[:, 0, KVH * CHUNK:KVH * CHUNK + limit + 2].astype(jnp.int32)
     tables = (numbers[:, :limit], numbers[:, limit], numbers[:, limit + 1], (me // CLUSTER)[None], store_slot[0])

time: 240 us -> 188 us (0.78)
  waiting for transfers between devices: 116 us -> 82.7 us
  starting transfers between devices: 37.9 us -> 24.4 us
  Pallas kernels: 62.2 us -> 58.8 us
    ppermute x1, waiting for transfers between devices: 52.3 us -> 6.29 us  [shifted(): lax.ppermute(array, axis, [(i, (i + by) % size) for i in range(size)])]
    all_to_all x5, starting transfers between devices: 33.9 us -> 19.7 us  [exchanged(): lax.all_to_all(array, 'serve', 0, 0, axis_index_groups=groups, tiled=True)]
    all_to_all x5, waiting for transfers between devices: 18.9 us -> 32 us  [exchanged(): lax.all_to_all(array, 'serve', 0, 0, axis_index_groups=groups, tiled=True)]
    pallas_call x4, Pallas kernels: 52.8 us -> 49.4 us  [attend(): pl.pallas_call(functools.partial(attend_kernel, lines, head, q_head), gri...]
    unnamed x22 -> x20, local copies, waits for them, and re-layouts: 10.1 us -> 8.85 us
  transfers between devices with their start and end apart: 15 -> 15, of which waited for: 8 -> 9; matrix products, arithmetic and copies ran while one was open for 2% -> 4% of each run, Pallas kernels for 25% -> 30%
where the time goes in v13:
time: 188 us
  waiting for transfers between devices  82.7 us (44%)
  Pallas kernels  58.8 us (31%)
  starting transfers between devices  24.4 us (13%)
  local copies, waits for them, and re-layouts  15.7 us (8%)
  other arithmetic  3.76 us (2%)
  between operations  2.24 us (1%)
    pallas_call x4, Pallas kernels, attend(): pl.pallas_call(functools.partial(attend_kernel, lines, head, q_head), gri...  49.4 us
    ppermute x9, waiting for transfers between devices, swapped(): return lax.ppermute(array, axis, [(i, i ^ bit) for i in range(size)])  44.4 us
    all_to_all x5, waiting for transfers between devices, exchanged(): lax.all_to_all(array, 'serve', 0, 0, axis_index_groups=groups, tiled=True)  32 us
    all_to_all x5, starting transfers between devices, exchanged(): lax.all_to_all(array, 'serve', 0, 0, axis_index_groups=groups, tiled=True)  19.7 us
    pallas_call x4, Pallas kernels, merge(): pl.pallas_call(functools.partial(merge_kernel, head), in_specs=[pl.BlockS...  9.41 us
    unnamed x20, local copies, waits for them, and re-layouts  8.85 us
    ppermute x1, waiting for transfers between devices, shifted(): lax.ppermute(array, axis, [(i, (i + by) % size) for i in range(size)])  6.29 us
    ppermute x9, starting transfers between devices, swapped(): return lax.ppermute(array, axis, [(i, i ^ bit) for i in range(size)])  4.17 us
  transfers between devices with their start and end apart: 15, of which 9 were waited for; matrix products, arithmetic and copies ran while one was open for 4% of the time, Pallas kernels for 30%

profile of v13, /device:TPU:0, one launch (start us, length us, event | category | flops | bytes accessed | tf_op | source)
XLA Modules:
  0.0 187.6 jit_solution(3789842640236143304)
XLA Ops:
  0.6 0.5 collective-permute-start
  1.8 0.7 fusion.15
  2.5 0.7 fusion.13
  3.2 0.1 convert_reduce_fusion.1
  3.3 0.1 convert_reduce_fusion
  3.5 0.1 select_reduce_fusion
  3.7 0.1 and_reduce_fusion
  3.9 0.1 copy.19
  4.1 6.3 %collective-permute-done.refs_7_ = bf16[1,2,128,512]{3,2,1,0:T(8,128)(2,1)S(1)} collective-permute-done((bf16[1,2,128,512]{3,2,1,0:T(8,128)(2,1)}, bf16[1,2,128,512]{3,2,1,0:T(8,128)(2,1)S(1)}, u32[]{:S(2)}, u32[]{:S(2)}) %collective-permute-start) | collective-permute-done | bytes 262176 | tf_op jit(solution)/shard_map/ppermute | solution.py:33
  10.4 1.3 broadcast_in_dim.24
  11.7 1.7 pad_maximum_fusion
  13.4 3.7 %all-to-all-start = ((bf16[4,128,2688]{2,1,0:T(8,128)(2,1)}), bf16[4,128,2688]{2,1,0:T(8,128)(2,1)S(1)}, u32[]{:S(2)}, u32[]{:S(2)}) async-start(bf16[4,128,2688]{2,1,0:T(8,128)(2,1)} %pad_maximum_fusion), calls=%async_computation | async-start | bytes 5505024 | tf_op jit(solution)/shard_map/all_to_all | solution.py:317
  17.1 1.3 slice.28.refs_1_
  18.5 0.5 collective-permute-start.7
  19.1 3.7 %fusion.17 = (bf16[16,2,128,128]{3,2,1,0:T(8,128)(2,1)}, bf16[16,2,128,128]{3,2,1,0:T(8,128)(2,1)}, bf16[16,2,128,128]{3,2,1,0:T(8,128)(2,1)}) fusion(bf16[16,2,128,512]{3,2,1,0:T(8,128)(2,1)} %refs_6_.1), kind=kLoop, calls=%fused_computation.41 | loop fusion | bytes 6291456 | tf_op jit(solution)/shard_map/slice | solution.py:335
  22.8 1.6 collective-permute-start.3
  24.4 20.3 %collective-permute-done.7.refs_3_ = bf16[16,2,128,128]{3,2,1,0:T(8,128)(2,1)} collective-permute-done((bf16[16,2,128,128]{3,2,1,0:T(8,128)(2,1)S(1)}, bf16[16,2,128,128]{3,2,1,0:T(8,128)(2,1)}, u32[]{:S(2)}, u32[]{:S(2)}) %collective-permute-start.7) | collective-permute-done | bytes 1048608 | tf_op jit(solution)/shard_map/ppermute | solution.py:28
  44.7 0.5 collective-permute-start.6
  45.8 21.4 %collective-permute-done.3.refs_3_ = bf16[16,2,128,128]{3,2,1,0:T(8,128)(2,1)} collective-permute-done((bf16[16,2,128,128]{3,2,1,0:T(8,128)(2,1)}, bf16[16,2,128,128]{3,2,1,0:T(8,128)(2,1)}, u32[]{:S(2)}, u32[]{:S(2)}) %collective-permute-start.3) | collective-permute-done | bytes 1048608 | tf_op jit(solution)/shard_map/ppermute | solution.py:28
  67.2 10.6 %all-to-all-done.refs_0_ = bf16[4,128,2688]{2,1,0:T(8,128)(2,1)S(1)} async-done(((bf16[4,128,2688]{2,1,0:T(8,128)(2,1)}), bf16[4,128,2688]{2,1,0:T(8,128)(2,1)S(1)}, u32[]{:S(2)}, u32[]{:S(2)}) %all-to-all-start) | async-done | bytes 2752544 | tf_op jit(solution)/shard_map/all_to_all | solution.py:317
  77.7 0.2 slice_reduce_fusion
  78.0 2.2 %copy-done = bf16[16,2,128,512]{3,2,1,0:T(8,128)(2,1)S(1)} copy-done((bf16[16,2,128,512]{3,2,1,0:T(8,128)(2,1)S(1)}, bf16[16,2,128,512]{3,2,1,0:T(8,128)(2,1)}, u32[]{:S(2)}) %copy-start) | copy-done | bytes 4194328
  80.1 1.2 copy-done.3
  81.4 13.0 %shard_map.88 = (bf16[4,672,128]{2,1,0:T(8,128)(2,1)S(1)}, bf16[16,2,128,512]{3,2,1,0:T(8,128)(2,1)}) custom-call(s32[4,16]{1,0:T(4,128)S(1)} %bitcast.31, s32[4]{0:T(128)S(1)} %get-tuple-element.15.counts, s32[4]{0:T(128)S(1)} %get-tuple-element.14.lasts, s32[1]{0:T(128)} %bitcast.9.mine, s32[1]{0:T(128)} %bitcast.23.store, ...), custom_call_target="tpu_custom_call" | custom-call | flops 1 | bytes 1 | tf_op jit(solution)/shard_map/pallas_call | solution.py:252
  94.3 0.8 copy-done.8
  95.2 4.2 %all-to-all-start.4 = ((bf16[4,672,128]{2,1,0:T(8,128)(2,1)}), bf16[4,672,128]{2,1,0:T(8,128)(2,1)}, u32[]{:S(2)}, u32[]{:S(2)}) async-start(bf16[4,672,128]{2,1,0:T(8,128)(2,1)} %copy-done.8), calls=%async_computation.4 | async-start | bytes 1376256 | tf_op jit(solution)/shard_map/all_to_all | solution.py:317
  99.3 1.4 collective-permute-start.2
  100.8 11.9 %shard_map.86 = bf16[4,672,128]{2,1,0:T(8,128)(2,1)S(1)} custom-call(s32[4,16]{1,0:T(4,128)S(1)} %bitcast.32, s32[4]{0:T(128)S(1)} %get-tuple-element.15.counts, s32[4]{0:T(128)S(1)} %get-tuple-element.14.lasts, s32[1]{0:T(128)} %bitcast.9.mine, s32[1]{0:T(128)} %bitcast.21.store, bf16[4,128,2688]{2,1,0:T(8,128)(2,1)S(1)} %all-to-all-done.refs_0_, ...), custom_call_target="tpu_custom_call" | custom-call | flops 1 | bytes 1 | tf_op jit(solution)/shard_map/pallas_call | solution.py:252
  112.7 0.8 copy-done.6
  113.6 5.0 %all-to-all-done.4.parts = bf16[4,672,128]{2,1,0:T(8,128)(2,1)} async-done(((bf16[4,672,128]{2,1,0:T(8,128)(2,1)}), bf16[4,672,128]{2,1,0:T(8,128)(2,1)}, u32[]{:S(2)}, u32[]{:S(2)}) %all-to-all-start.4) | async-done | bytes 688160 | tf_op jit(solution)/shard_map/all_to_all | solution.py:317
  118.6 4.2 %all-to-all-start.3 = ((bf16[4,672,128]{2,1,0:T(8,128)(2,1)}), bf16[4,672,128]{2,1,0:T(8,128)(2,1)}, u32[]{:S(2)}, u32[]{:S(2)}) async-start(bf16[4,672,128]{2,1,0:T(8,128)(2,1)} %copy-done.6), calls=%async_computation.3 | async-start | bytes 1376256 | tf_op jit(solution)/shard_map/all_to_all | solution.py:317
  122.8 2.8 %collective-permute-done.2.refs_3_ = bf16[16,2,128,128]{3,2,1,0:T(8,128)(2,1)} collective-permute-done((bf16[16,2,128,128]{3,2,1,0:T(8,128)(2,1)}, bf16[16,2,128,128]{3,2,1,0:T(8,128)(2,1)}, u32[]{:S(2)}, u32[]{:S(2)}) %collective-permute-start.2) | collective-permute-done | bytes 1048608 | tf_op jit(solution)/shard_map/ppermute | solution.py:28
  125.5 0.1 collective-permute-start.5
  125.6 11.9 %shard_map.89 = bf16[4,672,128]{2,1,0:T(8,128)(2,1)S(1)} custom-call(s32[4,16]{1,0:T(4,128)S(1)} %bitcast.33, s32[4]{0:T(128)S(1)} %get-tuple-element.15.counts, s32[4]{0:T(128)S(1)} %get-tuple-element.14.lasts, s32[1]{0:T(128)} %bitcast.9.mine, s32[1]{0:T(128)} %bitcast.24.store, bf16[4,128,2688]{2,1,0:T(8,128)(2,1)S(1)} %all-to-all-done.refs_0_, ...), custom_call_target="tpu_custom_call" | custom-call | flops 1 | bytes 1 | tf_op jit(solution)/shard_map/pallas_call | solution.py:252
  137.6 0.9 copy-done.7
  138.4 2.9 %all-to-all-done.3.parts = bf16[4,672,128]{2,1,0:T(8,128)(2,1)} async-done(((bf16[4,672,128]{2,1,0:T(8,128)(2,1)}), bf16[4,672,128]{2,1,0:T(8,128)(2,1)}, u32[]{:S(2)}, u32[]{:S(2)}) %all-to-all-start.3) | async-done | bytes 688160 | tf_op jit(solution)/shard_map/all_to_all | solution.py:317
  141.4 4.2 %all-to-all-start.2 = ((bf16[4,672,128]{2,1,0:T(8,128)(2,1)}), bf16[4,672,128]{2,1,0:T(8,128)(2,1)}, u32[]{:S(2)}, u32[]{:S(2)}) async-start(bf16[4,672,128]{2,1,0:T(8,128)(2,1)} %copy-done.7), calls=%async_computation.2 | async-start | bytes 1376256 | tf_op jit(solution)/shard_map/all_to_all | solution.py:317
  145.6 1.2 copy-done.4
  146.8 12.6 %shard_map.87 = bf16[4,672,128]{2,1,0:T(8,128)(2,1)S(1)} custom-call(s32[4,16]{1,0:T(4,128)S(1)} %bitcast.34, s32[4]{0:T(128)S(1)} %get-tuple-element.15.counts, s32[4]{0:T(128)S(1)} %get-tuple-element.14.lasts, s32[1]{0:T(128)} %bitcast.9.mine, s32[1]{0:T(128)} %bitcast.22.store, bf16[4,128,2688]{2,1,0:T(8,128)(2,1)S(1)} %all-to-all-done.refs_0_, ...), custom_call_target="tpu_custom_call" | custom-call | flops 1 | bytes 1 | tf_op jit(solution)/shard_map/pallas_call | solution.py:252
  159.4 0.8 copy-done.5
  160.3 3.1 %all-to-all-done.2.parts = bf16[4,672,128]{2,1,0:T(8,128)(2,1)} async-done(((bf16[4,672,128]{2,1,0:T(8,128)(2,1)}), bf16[4,672,128]{2,1,0:T(8,128)(2,1)}, u32[]{:S(2)}, u32[]{:S(2)}) %all-to-all-start.2) | async-done | bytes 688160 | tf_op jit(solution)/shard_map/all_to_all | solution.py:317
  163.4 3.5 %all-to-all-start.1 = ((bf16[4,672,128]{2,1,0:T(8,128)(2,1)}), bf16[4,672,128]{2,1,0:T(8,128)(2,1)S(1)}, u32[]{:S(2)}, u32[]{:S(2)}) async-start(bf16[4,672,128]{2,1,0:T(8,128)(2,1)} %copy-done.5), calls=%async_computation.1 | async-start | bytes 1376256 | tf_op jit(solution)/shard_map/all_to_all | solution.py:317
  166.9 2.4 %shard_map.90.refs_0_ = bf16[128,2560]{1,0:T(8,128)(2,1)} custom-call(bf16[4,672,128]{2,1,0:T(8,128)(2,1)} %all-to-all-done.4.parts), custom_call_target="tpu_custom_call" | custom-call | flops 1 | bytes 1 | tf_op jit(solution)/shard_map/pallas_call | solution.py:289
  169.3 2.4 %shard_map.91.refs_0_ = bf16[128,2560]{1,0:T(8,128)(2,1)} custom-call(bf16[4,672,128]{2,1,0:T(8,128)(2,1)} %all-to-all-done.3.parts, bf16[128,2560]{1,0:T(8,128)(2,1)} %shard_map.90.refs_0_), custom_call_target="tpu_custom_call", output_to_operand_aliasing={{}: (1, {})} | custom-call | flops 1 | bytes 1 | tf_op jit(solution)/shard_map/pallas_call | solution.py:289
  171.6 2.4 %shard_map.92.refs_0_ = bf16[128,2560]{1,0:T(8,128)(2,1)} custom-call(bf16[4,672,128]{2,1,0:T(8,128)(2,1)} %all-to-all-done.2.parts, bf16[128,2560]{1,0:T(8,128)(2,1)} %shard_map.91.refs_0_), custom_call_target="tpu_custom_call", output_to_operand_aliasing={{}: (1, {})} | custom-call | flops 1 | bytes 1 | tf_op jit(solution)/shard_map/pallas_call | solution.py:289
  174.0 10.4 %all-to-all-done.1.parts = bf16[4,672,128]{2,1,0:T(8,128)(2,1)S(1)} async-done(((bf16[4,672,128]{2,1,0:T(8,128)(2,1)}), bf16[4,672,128]{2,1,0:T(8,128)(2,1)S(1)}, u32[]{:S(2)}, u32[]{:S(2)}) %all-to-all-start.1) | async-done | bytes 688160 | tf_op jit(solution)/shard_map/all_to_all | solution.py:317
  184.4 0.8 copy-done.9
  185.2 2.4 %shard_map.93 = bf16[128,2560]{1,0:T(8,128)(2,1)} custom-call(bf16[4,672,128]{2,1,0:T(8,128)(2,1)} %copy-done.9, bf16[128,2560]{1,0:T(8,128)(2,1)} %shard_map.92.refs_0_), custom_call_target="tpu_custom_call", output_to_operand_aliasing={{}: (1, {})} | custom-call | flops 1 | bytes 1 | tf_op jit(solution)/shard_map/pallas_call | solution.py:289
  (32 shorter events, 0.4 us)
Async XLA Ops:
  0.6 9.8 %collective-permute-start = (bf16[1,2,128,512]{3,2,1,0:T(8,128)(2,1)}, bf16[1,2,128,512]{3,2,1,0:T(8,128)(2,1)S(1)}, u32[]{:S(2)}, u32[]{:S(2)}) collective-permute-start(bf16[1,2,128,512]{3,2,1,0:T(8,128)(2,1)} %bitcast.25), channel_id=1, source_target_pairs={{0,1},{1,2},{2,3},{3,4},{4,5},{5,6},{6,7},{7,8},{8,9},{9,10},{10,1... | collective-permute-start | bytes 786440 | tf_op jit(solution)/shard_map/ppermute | solution.py:33
  13.4 64.3 %all-to-all-start = ((bf16[4,128,2688]{2,1,0:T(8,128)(2,1)}), bf16[4,128,2688]{2,1,0:T(8,128)(2,1)S(1)}, u32[]{:S(2)}, u32[]{:S(2)}) async-start(bf16[4,128,2688]{2,1,0:T(8,128)(2,1)} %pad_maximum_fusion), calls=%async_computation | async-start | bytes 5505024 | tf_op jit(solution)/shard_map/all_to_all | solution.py:317
  18.4 4.4 %copy-start.2 = (bf16[16,2,128,128]{3,2,1,0:T(8,128)(2,1)}, bf16[16,2,128,128]{3,2,1,0:T(8,128)(2,1)S(1)}, u32[]{:S(2)}) copy-start(bf16[16,2,128,128]{3,2,1,0:T(8,128)(2,1)S(1)} %slice.28.refs_1_) | copy-start | bytes 3145732
  18.4 59.5 %copy-start.1 = (bf16[1,1,2,128,512]{4,3,2,1,0:T(8,128)(2,1)S(1)}, bf16[1,1,2,128,512]{4,3,2,1,0:T(8,128)(2,1)}, u32[]{:S(2)}) copy-start(bf16[1,1,2,128,512]{4,3,2,1,0:T(8,128)(2,1)} %param.8) | copy-start | bytes 786436
  18.5 59.5 %collective-permute-start.1 = (bf16[16,2,128,512]{3,2,1,0:T(8,128)(2,1)}, bf16[16,2,128,512]{3,2,1,0:T(8,128)(2,1)}, u32[]{:S(2)}, u32[]{:S(2)}) collective-permute-start(bf16[16,2,128,512]{3,2,1,0:T(8,128)(2,1)} %refs_6_.1), channel_id=1, source_target_pairs={{0,1},{1,0},{2,3},{3,2},{4,5},{5,4},{6,7},{7,6},{8,9},{9,8},{10,11... | collective-permute-start | bytes 12582920 | tf_op jit(solution)/shard_map/ppermute | solution.py:28
  18.5 26.1 %collective-permute-start.7 = (bf16[16,2,128,128]{3,2,1,0:T(8,128)(2,1)S(1)}, bf16[16,2,128,128]{3,2,1,0:T(8,128)(2,1)}, u32[]{:S(2)}, u32[]{:S(2)}) collective-permute-start(bf16[16,2,128,128]{3,2,1,0:T(8,128)(2,1)S(1)} %slice.28.refs_1_), channel_id=1, source_target_pairs={{0,2},{1,3},{2,0},{3,1},{4,6},{5,7},{6,4},{7,5},{8,10},{9,11},{10,... | collective-permute-start | bytes 3145736 | tf_op jit(solution)/shard_map/ppermute | solution.py:28
  22.8 44.3 %collective-permute-start.3 = (bf16[16,2,128,128]{3,2,1,0:T(8,128)(2,1)}, bf16[16,2,128,128]{3,2,1,0:T(8,128)(2,1)}, u32[]{:S(2)}, u32[]{:S(2)}) collective-permute-start(bf16[16,2,128,128]{3,2,1,0:T(8,128)(2,1)} %get-tuple-element.19.refs_1_), channel_id=1, source_target_pairs={{0,2},{1,3},{2,0},{3,1},{4,6},{5,7},{6,4},{7,5},{8,10},{9,11},{10,... | collective-permute-start | bytes 3145736 | tf_op jit(solution)/shard_map/ppermute | solution.py:28
  44.7 33.2 %collective-permute-start.8 = (bf16[16,2,128,128]{3,2,1,0:T(8,128)(2,1)}, bf16[16,2,128,128]{3,2,1,0:T(8,128)(2,1)}, u32[]{:S(2)}, u32[]{:S(2)}) collective-permute-start(bf16[16,2,128,128]{3,2,1,0:T(8,128)(2,1)} %collective-permute-done.7.refs_3_), channel_id=1, source_target_pairs={{0,1},{1,0},{2,3},{3,2},{4,5},{5,4},{6,7},{7,6},{8,9},{9,8},{10,11... | collective-permute-start | bytes 3145736 | tf_op jit(solution)/shard_map/ppermute | solution.py:28
  44.7 56.1 %collective-permute-start.6 = (bf16[16,2,128,128]{3,2,1,0:T(8,128)(2,1)}, bf16[16,2,128,128]{3,2,1,0:T(8,128)(2,1)}, u32[]{:S(2)}, u32[]{:S(2)}) collective-permute-start(bf16[16,2,128,128]{3,2,1,0:T(8,128)(2,1)} %get-tuple-element.18.refs_1_), channel_id=1, source_target_pairs={{0,2},{1,3},{2,0},{3,1},{4,6},{5,7},{6,4},{7,5},{8,10},{9,11},{10,... | collective-permute-start | bytes 3145736 | tf_op jit(solution)/shard_map/ppermute | solution.py:28
  67.1 33.6 %collective-permute-start.4 = (bf16[16,2,128,128]{3,2,1,0:T(8,128)(2,1)}, bf16[16,2,128,128]{3,2,1,0:T(8,128)(2,1)}, u32[]{:S(2)}, u32[]{:S(2)}) collective-permute-start(bf16[16,2,128,128]{3,2,1,0:T(8,128)(2,1)} %collective-permute-done.3.refs_3_), channel_id=1, source_target_pairs={{0,1},{1,0},{2,3},{3,2},{4,5},{5,4},{6,7},{7,6},{8,9},{9,8},{10,11... | collective-permute-start | bytes 3145736 | tf_op jit(solution)/shard_map/ppermute | solution.py:28
  78.0 2.2 %copy-start = (bf16[16,2,128,512]{3,2,1,0:T(8,128)(2,1)S(1)}, bf16[16,2,128,512]{3,2,1,0:T(8,128)(2,1)}, u32[]{:S(2)}) copy-start(bf16[16,2,128,512]{3,2,1,0:T(8,128)(2,1)} %refs_6_.1) | copy-start | bytes 12582916
  80.1 1.2 copy-start.3
  94.3 0.8 copy-start.8
  95.2 23.4 %all-to-all-start.4 = ((bf16[4,672,128]{2,1,0:T(8,128)(2,1)}), bf16[4,672,128]{2,1,0:T(8,128)(2,1)}, u32[]{:S(2)}, u32[]{:S(2)}) async-start(bf16[4,672,128]{2,1,0:T(8,128)(2,1)} %copy-done.8), calls=%async_computation.4 | async-start | bytes 1376256 | tf_op jit(solution)/shard_map/all_to_all | solution.py:317
  99.3 26.2 %collective-permute-start.2 = (bf16[16,2,128,128]{3,2,1,0:T(8,128)(2,1)}, bf16[16,2,128,128]{3,2,1,0:T(8,128)(2,1)}, u32[]{:S(2)}, u32[]{:S(2)}) collective-permute-start(bf16[16,2,128,128]{3,2,1,0:T(8,128)(2,1)} %get-tuple-element.20.refs_1_), channel_id=1, source_target_pairs={{0,2},{1,3},{2,0},{3,1},{4,6},{5,7},{6,4},{7,5},{8,10},{9,11},{10,... | collective-permute-start | bytes 3145736 | tf_op jit(solution)/shard_map/ppermute | solution.py:28
  100.8 24.9 %collective-permute-start.9 = (bf16[16,2,128,128]{3,2,1,0:T(8,128)(2,1)}, bf16[16,2,128,128]{3,2,1,0:T(8,128)(2,1)}, u32[]{:S(2)}, u32[]{:S(2)}) collective-permute-start(bf16[16,2,128,128]{3,2,1,0:T(8,128)(2,1)} %collective-permute-done.6.refs_3_), channel_id=1, source_target_pairs={{0,1},{1,0},{2,3},{3,2},{4,5},{5,4},{6,7},{7,6},{8,9},{9,8},{10,11... | collective-permute-start | bytes 3145736 | tf_op jit(solution)/shard_map/ppermute | solution.py:28
  112.7 0.8 copy-start.6
  118.6 22.8 %all-to-all-start.3 = ((bf16[4,672,128]{2,1,0:T(8,128)(2,1)}), bf16[4,672,128]{2,1,0:T(8,128)(2,1)}, u32[]{:S(2)}, u32[]{:S(2)}) async-start(bf16[4,672,128]{2,1,0:T(8,128)(2,1)} %copy-done.6), calls=%async_computation.3 | async-start | bytes 1376256 | tf_op jit(solution)/shard_map/all_to_all | solution.py:317
  125.5 20.1 %collective-permute-start.5 = (bf16[16,2,128,128]{3,2,1,0:T(8,128)(2,1)}, bf16[16,2,128,128]{3,2,1,0:T(8,128)(2,1)}, u32[]{:S(2)}, u32[]{:S(2)}) collective-permute-start(bf16[16,2,128,128]{3,2,1,0:T(8,128)(2,1)} %collective-permute-done.2.refs_3_), channel_id=1, source_target_pairs={{0,1},{1,0},{2,3},{3,2},{4,5},{5,4},{6,7},{7,6},{8,9},{9,8},{10,11... | collective-permute-start | bytes 3145736 | tf_op jit(solution)/shard_map/ppermute | solution.py:28
  137.6 0.9 copy-start.7
  141.4 22.0 %all-to-all-start.2 = ((bf16[4,672,128]{2,1,0:T(8,128)(2,1)}), bf16[4,672,128]{2,1,0:T(8,128)(2,1)}, u32[]{:S(2)}, u32[]{:S(2)}) async-start(bf16[4,672,128]{2,1,0:T(8,128)(2,1)} %copy-done.7), calls=%async_computation.2 | async-start | bytes 1376256 | tf_op jit(solution)/shard_map/all_to_all | solution.py:317
  145.6 1.2 copy-start.4
  159.4 0.9 copy-start.5
  163.4 21.0 %all-to-all-start.1 = ((bf16[4,672,128]{2,1,0:T(8,128)(2,1)}), bf16[4,672,128]{2,1,0:T(8,128)(2,1)S(1)}, u32[]{:S(2)}, u32[]{:S(2)}) async-start(bf16[4,672,128]{2,1,0:T(8,128)(2,1)} %copy-done.5), calls=%async_computation.1 | async-start | bytes 1376256 | tf_op jit(solution)/shard_map/all_to_all | solution.py:317
  184.4 0.8 copy-start.9

commit v14 on v13

--- a/solution.py
+++ b/solution.py
@@ -337,23 +337,27 @@
     twin = swapped(rest, "serve", 1)
     rows = page_rows(me, lines, limit, slots, page_owner, page_slot, prefix_len).astype(queries.dtype)
     rows = jnp.pad(rows[:, None], ((0, 0), (0, PAGE - 1), (0, PAGE - limit - 2)))
-    q_all = jnp.broadcast_to(after(queries, incoming)[None], (lines, PAGE, KVH * CHUNK))
-    q_all = exchanged(jnp.concatenate([q_all, rows], axis=2), groups)
-    numbers = q_all[:, 0, KVH * CHUNK:KVH * CHUNK + limit + 2].astype(jnp.int32)
+    half = KVH // 2 * CHUNK
+    early = jnp.broadcast_to(after(queries, incoming)[None, :, :half], (lines, PAGE, half))
+    early = exchanged(jnp.concatenate([early, rows], axis=2), groups)
+    later = after(queries, sides[0])[None, :, half:]
+    later = exchanged(jnp.broadcast_to(later, (lines, PAGE, KVH * CHUNK - half)), groups)
+    numbers = early[:, 0, half:half + limit + 2].astype(jnp.int32)
     tables = (numbers[:, :limit], numbers[:, limit], numbers[:, limit + 1], (me // CLUSTER)[None], store_slot[0])
     fresh = new_kv[0, 0]
     attended = None
     parts = []
     for g in range(KVH):
         side = sides[g]
-        if g > 1:
-            side = after(side, parts[g - 2])
+        if g > 0:
+            side = after(side, parts[g - 1])
+        q_all, q_head = (early, g) if g < KVH // 2 else (later, g - KVH // 2)
         both = swapped(side, "serve", 1)
         pools = (owns[g], twin, side, both)
         if g == 0:
-            part, pool_out = attend(g, g, tables, q_all, pools, fresh, pool, incoming)
+            part, pool_out = attend(g, q_head, tables, q_all, pools, fresh, pool, incoming)
         else:
-            part = attend(g, g, tables, q_all, pools, fresh)[0]
+            part = attend(g, q_head, tables, q_all, pools, fresh)[0]
         parts.append(part)
         attended = merge(g, exchanged(part, groups), attended)
     return (attended, pool_out)

time: 188 us -> 184 us (0.979)
  waiting for transfers between devices: 82.7 us -> 75 us
  starting transfers between devices: 24.4 us -> 30.4 us
  local copies, waits for them, and re-layouts: 15.7 us -> 12.8 us
    all_to_all x5 -> x6, waiting for transfers between devices: 32 us -> 26.5 us  [exchanged(): lax.all_to_all(array, 'serve', 0, 0, axis_index_groups=groups, tiled=True)]
    all_to_all x5 -> x6, starting transfers between devices: 19.7 us -> 25.1 us  [exchanged(): lax.all_to_all(array, 'serve', 0, 0, axis_index_groups=groups, tiled=True)]
    unnamed x20 -> x18, local copies, waits for them, and re-layouts: 8.85 us -> 6.05 us
    ppermute x1, waiting for transfers between devices: 6.29 us -> 3.58 us  [shifted(): lax.ppermute(array, axis, [(i, (i + by) % size) for i in range(size)])]
  transfers between devices with their start and end apart: 15 -> 16, of which waited for: 9 -> 9; matrix products, arithmetic and copies ran while one was open for 4% -> 5% of each run, Pallas kernels for 30% -> 32%
where the time goes in v14:
time: 184 us; the launch traced here: 182 us
  waiting for transfers between devices  75 us (41%)
  Pallas kernels  60.1 us (33%)
  starting transfers between devices  30.4 us (17%)
  local copies, waits for them, and re-layouts  12.8 us (7%)
  between operations  2.26 us (1%)
  other arithmetic  1.91 us (1%)
    pallas_call x4, Pallas kernels, attend(): pl.pallas_call(functools.partial(attend_kernel, lines, head, q_head), gri...  50.7 us
    ppermute x9, waiting for transfers between devices, swapped(): return lax.ppermute(array, axis, [(i, i ^ bit) for i in range(size)])  44.9 us
    all_to_all x6, waiting for transfers between devices, exchanged(): lax.all_to_all(array, 'serve', 0, 0, axis_index_groups=groups, tiled=True)  26.5 us
    all_to_all x6, starting transfers between devices, exchanged(): lax.all_to_all(array, 'serve', 0, 0, axis_index_groups=groups, tiled=True)  25.1 us
    pallas_call x4, Pallas kernels, merge(): pl.pallas_call(functools.partial(merge_kernel, head), in_specs=[pl.BlockS...  9.41 us
    unnamed x18, local copies, waits for them, and re-layouts  6.05 us
    ppermute x9, starting transfers between devices, swapped(): return lax.ppermute(array, axis, [(i, i ^ bit) for i in range(size)])  4.86 us
    slice x1, local copies, waits for them, and re-layouts, per_device(): owns += [rest[:, :, :, g * HD:(g + 1) * HD] for g in range(1, KVH)]  3.75 us
  transfers between devices with their start and end apart: 16, of which 9 were waited for; matrix products, arithmetic and copies ran while one was open for 5% of the time, Pallas kernels for 32%

profile of v14, /device:TPU:0, one launch (start us, length us, event | category | flops | bytes accessed | tf_op | source)
XLA Modules:
  0.0 182.5 jit_solution(5461814120502806377)
XLA Ops:
  0.7 0.5 collective-permute-start
  1.2 1.3 slice.35.refs_1_
  2.5 2.7 %collective-permute-start.2 = (bf16[16,2,128,512]{3,2,1,0:T(8,128)(2,1)}, bf16[16,2,128,512]{3,2,1,0:T(8,128)(2,1)}, u32[]{:S(2)}, u32[]{:S(2)}) collective-permute-start(bf16[16,2,128,512]{3,2,1,0:T(8,128)(2,1)} %refs_6_.1), channel_id=1, source_target_pairs={{0,1},{1,0},{2,3},{3,2},{4,5},{5,4},{6,7},{7,6},{8,9},{9,8},{10,11... | collective-permute-start | bytes 12582920 | tf_op jit(solution)/shard_map/ppermute | solution.py:28
  5.9 0.1 convert_reduce_fusion.1
  6.1 0.1 convert_reduce_fusion
  6.2 0.1 select_reduce_fusion
  6.4 0.1 and_reduce_fusion
  6.5 0.1 copy.20
  6.7 0.1 copy.19
  6.8 0.1 fusion.8
  6.8 3.6 %collective-permute-done.refs_7_ = bf16[1,2,128,512]{3,2,1,0:T(8,128)(2,1)S(1)} collective-permute-done((bf16[1,2,128,512]{3,2,1,0:T(8,128)(2,1)}, bf16[1,2,128,512]{3,2,1,0:T(8,128)(2,1)S(1)}, u32[]{:S(2)}, u32[]{:S(2)}) %collective-permute-start) | collective-permute-done | bytes 262176 | tf_op jit(solution)/shard_map/ppermute | solution.py:33
  10.4 0.1 broadcast_in_dim.26
  10.5 1.2 pad_maximum_fusion
  11.7 3.7 %all-to-all-start = ((bf16[4,128,1408]{2,1,0:T(8,128)(2,1)}), bf16[4,128,1408]{2,1,0:T(8,128)(2,1)S(1)}, u32[]{:S(2)}, u32[]{:S(2)}) async-start(bf16[4,128,1408]{2,1,0:T(8,128)(2,1)} %pad_maximum_fusion), calls=%async_computation | async-start | bytes 2883584 | tf_op jit(solution)/shard_map/all_to_all | solution.py:317
  15.4 0.6 collective-permute-start.1
  16.0 22.6 %collective-permute-done.1.refs_3_ = bf16[16,2,128,128]{3,2,1,0:T(8,128)(2,1)} collective-permute-done((bf16[16,2,128,128]{3,2,1,0:T(8,128)(2,1)S(1)}, bf16[16,2,128,128]{3,2,1,0:T(8,128)(2,1)}, u32[]{:S(2)}, u32[]{:S(2)}) %collective-permute-start.1) | collective-permute-done | bytes 1048608 | tf_op jit(solution)/shard_map/ppermute | solution.py:28
  38.6 9.4 %all-to-all-done.refs_0_ = bf16[4,128,1408]{2,1,0:T(8,128)(2,1)S(1)} async-done(((bf16[4,128,1408]{2,1,0:T(8,128)(2,1)}), bf16[4,128,1408]{2,1,0:T(8,128)(2,1)S(1)}, u32[]{:S(2)}, u32[]{:S(2)}) %all-to-all-start) | async-done | bytes 1441824 | tf_op jit(solution)/shard_map/all_to_all | solution.py:317
  48.1 1.2 broadcast_in_dim.32
  49.2 3.5 %all-to-all-start.1 = ((bf16[4,128,1280]{2,1,0:T(8,128)(2,1)}), bf16[4,128,1280]{2,1,0:T(8,128)(2,1)S(1)}, u32[]{:S(2)}, u32[]{:S(2)}) async-start(bf16[4,128,1280]{2,1,0:T(8,128)(2,1)} %broadcast_in_dim.32), calls=%async_computation.1 | async-start | bytes 2621440 | tf_op jit(solution)/shard_map/all_to_all | solution.py:317
  52.8 0.1 collective-permute-start.6
  52.9 3.7 %fusion.17 = (bf16[16,2,128,128]{3,2,1,0:T(8,128)(2,1)}, bf16[16,2,128,128]{3,2,1,0:T(8,128)(2,1)}, bf16[16,2,128,128]{3,2,1,0:T(8,128)(2,1)}) fusion(bf16[16,2,128,512]{3,2,1,0:T(8,128)(2,1)} %refs_6_.1), kind=kLoop, calls=%fused_computation.41 | loop fusion | bytes 6291456 | tf_op jit(solution)/shard_map/slice | solution.py:335
  56.6 0.5 collective-permute-start.5
  57.8 0.2 slice_reduce_fusion
  58.1 2.2 %copy-done = bf16[16,2,128,512]{3,2,1,0:T(8,128)(2,1)S(1)} copy-done((bf16[16,2,128,512]{3,2,1,0:T(8,128)(2,1)S(1)}, bf16[16,2,128,512]{3,2,1,0:T(8,128)(2,1)}, u32[]{:S(2)}) %copy-start) | copy-done | bytes 4194328
  60.2 1.2 copy-done.3
  61.5 13.4 %shard_map.86 = (bf16[4,672,128]{2,1,0:T(8,128)(2,1)S(1)}, bf16[16,2,128,512]{3,2,1,0:T(8,128)(2,1)}) custom-call(s32[4,16]{1,0:T(4,128)S(1)} %bitcast.31, s32[4]{0:T(128)S(1)} %get-tuple-element.19.counts, s32[4]{0:T(128)S(1)} %get-tuple-element.18.lasts, s32[1]{0:T(128)} %bitcast.9.mine, s32[1]{0:T(128)} %bitcast.21.store, ...), custom_call_target="tpu_custom_call" | custom-call | flops 1 | bytes 1 | tf_op jit(solution)/shard_map/pallas_call | solution.py:252
  74.9 0.9 copy-done.5
  75.8 6.7 %collective-permute-done.5.refs_3_ = bf16[16,2,128,128]{3,2,1,0:T(8,128)(2,1)} collective-permute-done((bf16[16,2,128,128]{3,2,1,0:T(8,128)(2,1)}, bf16[16,2,128,128]{3,2,1,0:T(8,128)(2,1)}, u32[]{:S(2)}, u32[]{:S(2)}) %collective-permute-start.5) | collective-permute-done | bytes 1048608 | tf_op jit(solution)/shard_map/ppermute | solution.py:28
  82.5 0.5 collective-permute-start.4
  83.0 0.6 all-to-all-done.1.refs_0_
  83.6 4.4 %all-to-all-start.5 = ((bf16[4,672,128]{2,1,0:T(8,128)(2,1)}), bf16[4,672,128]{2,1,0:T(8,128)(2,1)}, u32[]{:S(2)}, u32[]{:S(2)}) async-start(bf16[4,672,128]{2,1,0:T(8,128)(2,1)} %copy-done.5), calls=%async_computation.5 | async-start | bytes 1376256 | tf_op jit(solution)/shard_map/all_to_all | solution.py:317
  88.0 12.3 %shard_map.87 = bf16[4,672,128]{2,1,0:T(8,128)(2,1)S(1)} custom-call(s32[4,16]{1,0:T(4,128)S(1)} %bitcast.32, s32[4]{0:T(128)S(1)} %get-tuple-element.19.counts, s32[4]{0:T(128)S(1)} %get-tuple-element.18.lasts, s32[1]{0:T(128)} %bitcast.9.mine, s32[1]{0:T(128)} %bitcast.22.store, bf16[4,128,1408]{2,1,0:T(8,128)(2,1)S(1)} %all-to-all-done.refs_0_, ...), custom_call_target="tpu_custom_call" | custom-call | flops 1 | bytes 1 | tf_op jit(solution)/shard_map/pallas_call | solution.py:252
  100.3 0.8 copy-done.4
  101.1 7.3 %collective-permute-done.4.refs_3_ = bf16[16,2,128,128]{3,2,1,0:T(8,128)(2,1)} collective-permute-done((bf16[16,2,128,128]{3,2,1,0:T(8,128)(2,1)}, bf16[16,2,128,128]{3,2,1,0:T(8,128)(2,1)}, u32[]{:S(2)}, u32[]{:S(2)}) %collective-permute-start.4) | collective-permute-done | bytes 1048608 | tf_op jit(solution)/shard_map/ppermute | solution.py:28
  108.4 0.5 collective-permute-start.3
  108.9 5.0 %all-to-all-start.4 = ((bf16[4,672,128]{2,1,0:T(8,128)(2,1)}), bf16[4,672,128]{2,1,0:T(8,128)(2,1)}, u32[]{:S(2)}, u32[]{:S(2)}) async-start(bf16[4,672,128]{2,1,0:T(8,128)(2,1)} %copy-done.4), calls=%async_computation.4 | async-start | bytes 1376256 | tf_op jit(solution)/shard_map/all_to_all | solution.py:317
  113.9 11.9 %shard_map.88 = bf16[4,672,128]{2,1,0:T(8,128)(2,1)} custom-call(s32[4,16]{1,0:T(4,128)S(1)} %bitcast.33, s32[4]{0:T(128)S(1)} %get-tuple-element.19.counts, s32[4]{0:T(128)S(1)} %get-tuple-element.18.lasts, s32[1]{0:T(128)} %bitcast.9.mine, s32[1]{0:T(128)} %bitcast.23.store, bf16[4,128,1280]{2,1,0:T(8,128)(2,1)S(1)} %all-to-all-done.1.refs_0_, ...), custom_call_target="tpu_custom_call" | custom-call | flops 1 | bytes 1 | tf_op jit(solution)/shard_map/pallas_call | solution.py:252
  125.8 8.4 %collective-permute-done.3.refs_3_ = bf16[16,2,128,128]{3,2,1,0:T(8,128)(2,1)S(1)} collective-permute-done((bf16[16,2,128,128]{3,2,1,0:T(8,128)(2,1)}, bf16[16,2,128,128]{3,2,1,0:T(8,128)(2,1)S(1)}, u32[]{:S(2)}, u32[]{:S(2)}) %collective-permute-start.3) | collective-permute-done | bytes 1048608 | tf_op jit(solution)/shard_map/ppermute | solution.py:28
  134.2 5.0 %all-to-all-start.3 = ((bf16[4,672,128]{2,1,0:T(8,128)(2,1)}), bf16[4,672,128]{2,1,0:T(8,128)(2,1)}, u32[]{:S(2)}, u32[]{:S(2)}) async-start(bf16[4,672,128]{2,1,0:T(8,128)(2,1)} %shard_map.88), calls=%async_computation.3 | async-start | bytes 1376256 | tf_op jit(solution)/shard_map/all_to_all | solution.py:317
  139.2 13.0 %shard_map.89 = bf16[4,672,128]{2,1,0:T(8,128)(2,1)} custom-call(s32[4,16]{1,0:T(4,128)S(1)} %bitcast.34, s32[4]{0:T(128)S(1)} %get-tuple-element.19.counts, s32[4]{0:T(128)S(1)} %get-tuple-element.18.lasts, s32[1]{0:T(128)} %bitcast.9.mine, s32[1]{0:T(128)} %bitcast.24.store, bf16[4,128,1280]{2,1,0:T(8,128)(2,1)S(1)} %all-to-all-done.1.refs_0_, ...), custom_call_target="tpu_custom_call" | custom-call | flops 1 | bytes 1 | tf_op jit(solution)/shard_map/pallas_call | solution.py:252
  152.2 5.8 %all-to-all-done.3.parts = bf16[4,672,128]{2,1,0:T(8,128)(2,1)} async-done(((bf16[4,672,128]{2,1,0:T(8,128)(2,1)}), bf16[4,672,128]{2,1,0:T(8,128)(2,1)}, u32[]{:S(2)}, u32[]{:S(2)}) %all-to-all-start.3) | async-done | bytes 688160 | tf_op jit(solution)/shard_map/all_to_all | solution.py:317
  158.0 3.5 %all-to-all-start.2 = ((bf16[4,672,128]{2,1,0:T(8,128)(2,1)}), bf16[4,672,128]{2,1,0:T(8,128)(2,1)S(1)}, u32[]{:S(2)}, u32[]{:S(2)}) async-start(bf16[4,672,128]{2,1,0:T(8,128)(2,1)} %shard_map.89), calls=%async_computation.2 | async-start | bytes 1376256 | tf_op jit(solution)/shard_map/all_to_all | solution.py:317
  161.4 2.4 %shard_map.90.refs_0_ = bf16[128,2560]{1,0:T(8,128)(2,1)} custom-call(bf16[4,672,128]{2,1,0:T(8,128)(2,1)} %all-to-all-done.5.parts), custom_call_target="tpu_custom_call" | custom-call | flops 1 | bytes 1 | tf_op jit(solution)/shard_map/pallas_call | solution.py:289
  163.8 2.4 %shard_map.91.refs_0_ = bf16[128,2560]{1,0:T(8,128)(2,1)} custom-call(bf16[4,672,128]{2,1,0:T(8,128)(2,1)} %all-to-all-done.4.parts, bf16[128,2560]{1,0:T(8,128)(2,1)} %shard_map.90.refs_0_), custom_call_target="tpu_custom_call", output_to_operand_aliasing={{}: (1, {})} | custom-call | flops 1 | bytes 1 | tf_op jit(solution)/shard_map/pallas_call | solution.py:289
  166.2 2.4 %shard_map.92.refs_0_ = bf16[128,2560]{1,0:T(8,128)(2,1)} custom-call(bf16[4,672,128]{2,1,0:T(8,128)(2,1)} %all-to-all-done.3.parts, bf16[128,2560]{1,0:T(8,128)(2,1)} %shard_map.91.refs_0_), custom_call_target="tpu_custom_call", output_to_operand_aliasing={{}: (1, {})} | custom-call | flops 1 | bytes 1 | tf_op jit(solution)/shard_map/pallas_call | solution.py:289
  168.5 10.7 %all-to-all-done.2.parts = bf16[4,672,128]{2,1,0:T(8,128)(2,1)S(1)} async-done(((bf16[4,672,128]{2,1,0:T(8,128)(2,1)}), bf16[4,672,128]{2,1,0:T(8,128)(2,1)S(1)}, u32[]{:S(2)}, u32[]{:S(2)}) %all-to-all-start.2) | async-done | bytes 688160 | tf_op jit(solution)/shard_map/all_to_all | solution.py:317
  179.3 0.9 copy-done.6
  180.1 2.4 %shard_map.93 = bf16[128,2560]{1,0:T(8,128)(2,1)} custom-call(bf16[4,672,128]{2,1,0:T(8,128)(2,1)} %copy-done.6, bf16[128,2560]{1,0:T(8,128)(2,1)} %shard_map.92.refs_0_), custom_call_target="tpu_custom_call", output_to_operand_aliasing={{}: (1, {})} | custom-call | flops 1 | bytes 1 | tf_op jit(solution)/shard_map/pallas_call | solution.py:289
  (37 shorter events, 0.1 us)
Async XLA Ops:
  0.6 5.3 %copy-start.7 = (s32[1,48]{1,0:T(1,128)S(1)}, s32[1,48]{1,0:T(1,128)}, u32[]{:S(2)}) copy-start(s32[1,48]{1,0:T(1,128)} %param.10) | copy-start | bytes 580
  0.6 5.3 %copy-start.8 = (s32[1,48]{1,0:T(1,128)S(1)}, s32[1,48]{1,0:T(1,128)}, u32[]{:S(2)}) copy-start(s32[1,48]{1,0:T(1,128)} %param.11) | copy-start | bytes 580
  0.6 9.8 %slice-start = ((bf16[128,2560]{1,0:T(8,128)(2,1)}), bf16[128,1280]{1,0:T(8,128)(2,1)S(1)}, s32[]{:S(2)}) async-start(bf16[128,2560]{1,0:T(8,128)(2,1)} %param.7), calls=%async_computation.6 | async-start | bytes 655360 | tf_op jit(solution)/shard_map/slice | solution.py:341
  0.7 9.8 %collective-permute-start = (bf16[1,2,128,512]{3,2,1,0:T(8,128)(2,1)}, bf16[1,2,128,512]{3,2,1,0:T(8,128)(2,1)S(1)}, u32[]{:S(2)}, u32[]{:S(2)}) collective-permute-start(bf16[1,2,128,512]{3,2,1,0:T(8,128)(2,1)} %bitcast.25), channel_id=1, source_target_pairs={{0,1},{1,2},{2,3},{3,4},{4,5},{5,6},{6,7},{7,8},{8,9},{9,10},{10,1... | collective-permute-start | bytes 786440 | tf_op jit(solution)/shard_map/ppermute | solution.py:33
  2.5 13.0 %copy-start.2 = (bf16[16,2,128,128]{3,2,1,0:T(8,128)(2,1)}, bf16[16,2,128,128]{3,2,1,0:T(8,128)(2,1)S(1)}, u32[]{:S(2)}) copy-start(bf16[16,2,128,128]{3,2,1,0:T(8,128)(2,1)S(1)} %slice.35.refs_1_) | copy-start | bytes 3145732
  2.5 55.6 %collective-permute-start.2 = (bf16[16,2,128,512]{3,2,1,0:T(8,128)(2,1)}, bf16[16,2,128,512]{3,2,1,0:T(8,128)(2,1)}, u32[]{:S(2)}, u32[]{:S(2)}) collective-permute-start(bf16[16,2,128,512]{3,2,1,0:T(8,128)(2,1)} %refs_6_.1), channel_id=1, source_target_pairs={{0,1},{1,0},{2,3},{3,2},{4,5},{5,4},{6,7},{7,6},{8,9},{9,8},{10,11... | collective-permute-start | bytes 12582920 | tf_op jit(solution)/shard_map/ppermute | solution.py:28
  11.7 36.3 %slice-start.1 = ((bf16[128,2560]{1,0:T(8,128)(2,1)}), bf16[128,1280]{1,0:T(8,128)(2,1)S(1)}, s32[]{:S(2)}) async-start(bf16[128,2560]{1,0:T(8,128)(2,1)} %param.7), calls=%async_computation.7 | async-start | bytes 655360 | tf_op jit(solution)/shard_map/slice | solution.py:343
  11.7 36.3 %all-to-all-start = ((bf16[4,128,1408]{2,1,0:T(8,128)(2,1)}), bf16[4,128,1408]{2,1,0:T(8,128)(2,1)S(1)}, u32[]{:S(2)}, u32[]{:S(2)}) async-start(bf16[4,128,1408]{2,1,0:T(8,128)(2,1)} %pad_maximum_fusion), calls=%async_computation | async-start | bytes 2883584 | tf_op jit(solution)/shard_map/all_to_all | solution.py:317
  15.4 23.2 %collective-permute-start.1 = (bf16[16,2,128,128]{3,2,1,0:T(8,128)(2,1)S(1)}, bf16[16,2,128,128]{3,2,1,0:T(8,128)(2,1)}, u32[]{:S(2)}, u32[]{:S(2)}) collective-permute-start(bf16[16,2,128,128]{3,2,1,0:T(8,128)(2,1)S(1)} %slice.35.refs_1_), channel_id=1, source_target_pairs={{0,2},{1,3},{2,0},{3,1},{4,6},{5,7},{6,4},{7,5},{8,10},{9,11},{10,... | collective-permute-start | bytes 3145736 | tf_op jit(solution)/shard_map/ppermute | solution.py:28
  49.2 34.4 %all-to-all-start.1 = ((bf16[4,128,1280]{2,1,0:T(8,128)(2,1)}), bf16[4,128,1280]{2,1,0:T(8,128)(2,1)S(1)}, u32[]{:S(2)}, u32[]{:S(2)}) async-start(bf16[4,128,1280]{2,1,0:T(8,128)(2,1)} %broadcast_in_dim.32), calls=%async_computation.1 | async-start | bytes 2621440 | tf_op jit(solution)/shard_map/all_to_all | solution.py:317
  52.8 5.3 %copy-start.1 = (bf16[1,1,2,128,512]{4,3,2,1,0:T(8,128)(2,1)S(1)}, bf16[1,1,2,128,512]{4,3,2,1,0:T(8,128)(2,1)}, u32[]{:S(2)}) copy-start(bf16[1,1,2,128,512]{4,3,2,1,0:T(8,128)(2,1)} %param.8) | copy-start | bytes 786436
  52.8 5.2 %collective-permute-start.6 = (bf16[16,2,128,128]{3,2,1,0:T(8,128)(2,1)}, bf16[16,2,128,128]{3,2,1,0:T(8,128)(2,1)}, u32[]{:S(2)}, u32[]{:S(2)}) collective-permute-start(bf16[16,2,128,128]{3,2,1,0:T(8,128)(2,1)} %collective-permute-done.1.refs_3_), channel_id=1, source_target_pairs={{0,1},{1,0},{2,3},{3,2},{4,5},{5,4},{6,7},{7,6},{8,9},{9,8},{10,11... | collective-permute-start | bytes 3145736 | tf_op jit(solution)/shard_map/ppermute | solution.py:28
  56.6 25.9 %collective-permute-start.5 = (bf16[16,2,128,128]{3,2,1,0:T(8,128)(2,1)}, bf16[16,2,128,128]{3,2,1,0:T(8,128)(2,1)}, u32[]{:S(2)}, u32[]{:S(2)}) collective-permute-start(bf16[16,2,128,128]{3,2,1,0:T(8,128)(2,1)} %get-tuple-element.22.refs_1_), channel_id=1, source_target_pairs={{0,2},{1,3},{2,0},{3,1},{4,6},{5,7},{6,4},{7,5},{8,10},{9,11},{10,... | collective-permute-start | bytes 3145736 | tf_op jit(solution)/shard_map/ppermute | solution.py:28
  58.1 2.2 %copy-start = (bf16[16,2,128,512]{3,2,1,0:T(8,128)(2,1)S(1)}, bf16[16,2,128,512]{3,2,1,0:T(8,128)(2,1)}, u32[]{:S(2)}) copy-start(bf16[16,2,128,512]{3,2,1,0:T(8,128)(2,1)} %refs_6_.1) | copy-start | bytes 12582916
  60.2 1.2 copy-start.3
  74.9 0.9 copy-start.5
  82.5 5.5 %collective-permute-start.7 = (bf16[16,2,128,128]{3,2,1,0:T(8,128)(2,1)}, bf16[16,2,128,128]{3,2,1,0:T(8,128)(2,1)}, u32[]{:S(2)}, u32[]{:S(2)}) collective-permute-start(bf16[16,2,128,128]{3,2,1,0:T(8,128)(2,1)} %collective-permute-done.5.refs_3_), channel_id=1, source_target_pairs={{0,1},{1,0},{2,3},{3,2},{4,5},{5,4},{6,7},{7,6},{8,9},{9,8},{10,11... | collective-permute-start | bytes 3145736 | tf_op jit(solution)/shard_map/ppermute | solution.py:28
  82.5 25.9 %collective-permute-start.4 = (bf16[16,2,128,128]{3,2,1,0:T(8,128)(2,1)}, bf16[16,2,128,128]{3,2,1,0:T(8,128)(2,1)}, u32[]{:S(2)}, u32[]{:S(2)}) collective-permute-start(bf16[16,2,128,128]{3,2,1,0:T(8,128)(2,1)} %get-tuple-element.23.refs_1_), channel_id=1, source_target_pairs={{0,2},{1,3},{2,0},{3,1},{4,6},{5,7},{6,4},{7,5},{8,10},{9,11},{10,... | collective-permute-start | bytes 3145736 | tf_op jit(solution)/shard_map/ppermute | solution.py:28
  83.6 25.3 %all-to-all-start.5 = ((bf16[4,672,128]{2,1,0:T(8,128)(2,1)}), bf16[4,672,128]{2,1,0:T(8,128)(2,1)}, u32[]{:S(2)}, u32[]{:S(2)}) async-start(bf16[4,672,128]{2,1,0:T(8,128)(2,1)} %copy-done.5), calls=%async_computation.5 | async-start | bytes 1376256 | tf_op jit(solution)/shard_map/all_to_all | solution.py:317
  100.3 0.8 copy-start.4
  108.4 5.5 %collective-permute-start.8 = (bf16[16,2,128,128]{3,2,1,0:T(8,128)(2,1)}, bf16[16,2,128,128]{3,2,1,0:T(8,128)(2,1)}, u32[]{:S(2)}, u32[]{:S(2)}) collective-permute-start(bf16[16,2,128,128]{3,2,1,0:T(8,128)(2,1)} %collective-permute-done.4.refs_3_), channel_id=1, source_target_pairs={{0,1},{1,0},{2,3},{3,2},{4,5},{5,4},{6,7},{7,6},{8,9},{9,8},{10,11... | collective-permute-start | bytes 3145736 | tf_op jit(solution)/shard_map/ppermute | solution.py:28
  108.4 25.8 %collective-permute-start.3 = (bf16[16,2,128,128]{3,2,1,0:T(8,128)(2,1)}, bf16[16,2,128,128]{3,2,1,0:T(8,128)(2,1)S(1)}, u32[]{:S(2)}, u32[]{:S(2)}) collective-permute-start(bf16[16,2,128,128]{3,2,1,0:T(8,128)(2,1)} %get-tuple-element.24.refs_1_), channel_id=1, source_target_pairs={{0,2},{1,3},{2,0},{3,1},{4,6},{5,7},{6,4},{7,5},{8,10},{9,11},{10,... | collective-permute-start | bytes 3145736 | tf_op jit(solution)/shard_map/ppermute | solution.py:28
  108.9 25.3 %all-to-all-start.4 = ((bf16[4,672,128]{2,1,0:T(8,128)(2,1)}), bf16[4,672,128]{2,1,0:T(8,128)(2,1)}, u32[]{:S(2)}, u32[]{:S(2)}) async-start(bf16[4,672,128]{2,1,0:T(8,128)(2,1)} %copy-done.4), calls=%async_computation.4 | async-start | bytes 1376256 | tf_op jit(solution)/shard_map/all_to_all | solution.py:317
  134.2 5.0 %collective-permute-start.9 = (bf16[16,2,128,128]{3,2,1,0:T(8,128)(2,1)S(1)}, bf16[16,2,128,128]{3,2,1,0:T(8,128)(2,1)}, u32[]{:S(2)}, u32[]{:S(2)}) collective-permute-start(bf16[16,2,128,128]{3,2,1,0:T(8,128)(2,1)S(1)} %collective-permute-done.3.refs_3_), channel_id=1, source_target_pairs={{0,1},{1,0},{2,3},{3,2},{4,5},{5,4},{6,7},{7,6},{8,9},{9,8},{10,11... | collective-permute-start | bytes 3145736 | tf_op jit(solution)/shard_map/ppermute | solution.py:28
  134.2 23.8 %all-to-all-start.3 = ((bf16[4,672,128]{2,1,0:T(8,128)(2,1)}), bf16[4,672,128]{2,1,0:T(8,128)(2,1)}, u32[]{:S(2)}, u32[]{:S(2)}) async-start(bf16[4,672,128]{2,1,0:T(8,128)(2,1)} %shard_map.88), calls=%async_computation.3 | async-start | bytes 1376256 | tf_op jit(solution)/shard_map/all_to_all | solution.py:317
  158.0 21.3 %all-to-all-start.2 = ((bf16[4,672,128]{2,1,0:T(8,128)(2,1)}), bf16[4,672,128]{2,1,0:T(8,128)(2,1)S(1)}, u32[]{:S(2)}, u32[]{:S(2)}) async-start(bf16[4,672,128]{2,1,0:T(8,128)(2,1)} %shard_map.89), calls=%async_computation.2 | async-start | bytes 1376256 | tf_op jit(solution)/shard_map/all_to_all | solution.py:317
  179.3 0.9 copy-start.6

commit v15 on v14

--- a/solution.py
+++ b/solution.py
@@ -340,7 +340,7 @@
     half = KVH // 2 * CHUNK
     early = jnp.broadcast_to(after(queries, incoming)[None, :, :half], (lines, PAGE, half))
     early = exchanged(jnp.concatenate([early, rows], axis=2), groups)
-    later = after(queries, sides[0])[None, :, half:]
+    later = after(queries, sides[0], owns[1])[None, :, half:]
     later = exchanged(jnp.broadcast_to(later, (lines, PAGE, KVH * CHUNK - half)), groups)
     numbers = early[:, 0, half:half + limit + 2].astype(jnp.int32)
     tables = (numbers[:, :limit], numbers[:, limit], numbers[:, limit + 1], (me // CLUSTER)[None], store_slot[0])

time: 184 us -> 180 us (0.978)
  waiting for transfers between devices: 75 us -> 59.7 us
  Pallas kernels: 60.1 us -> 68.8 us
  local copies, waits for them, and re-layouts: 12.8 us -> 16.2 us
    ppermute x9, waiting for transfers between devices: 44.9 us -> 28.3 us  [swapped(): return lax.ppermute(array, axis, [(i, i ^ bit) for i in range(size)])]
    pallas_call x4, Pallas kernels: 50.7 us -> 59.4 us  [attend(): pl.pallas_call(functools.partial(attend_kernel, lines, head, q_head), gri...]
    unnamed x18 -> x24, local copies, waits for them, and re-layouts: 6.05 us -> 9.45 us
  transfers between devices with their start and end apart: 16 -> 16, of which waited for: 9 -> 10; matrix products, arithmetic and copies ran while one was open for 5% -> 5% of each run, Pallas kernels for 32% -> 37%
where the time goes in v15:
time: 180 us; the launch traced here: 179 us
  Pallas kernels  68.8 us (38%)
  waiting for transfers between devices  59.7 us (33%)
  starting transfers between devices  29.9 us (17%)
  local copies, waits for them, and re-layouts  16.2 us (9%)
  between operations  2.26 us (1%)
  other arithmetic  1.91 us (1%)
    pallas_call x4, Pallas kernels, attend(): pl.pallas_call(functools.partial(attend_kernel, lines, head, q_head), gri...  59.4 us
    ppermute x9, waiting for transfers between devices, swapped(): return lax.ppermute(array, axis, [(i, i ^ bit) for i in range(size)])  28.3 us
    all_to_all x6, waiting for transfers between devices, exchanged(): lax.all_to_all(array, 'serve', 0, 0, axis_index_groups=groups, tiled=True)  27.8 us
    all_to_all x6, starting transfers between devices, exchanged(): lax.all_to_all(array, 'serve', 0, 0, axis_index_groups=groups, tiled=True)  24.6 us
    unnamed x24, local copies, waits for them, and re-layouts  9.45 us
    pallas_call x4, Pallas kernels, merge(): pl.pallas_call(functools.partial(merge_kernel, head), in_specs=[pl.BlockS...  9.41 us
    ppermute x9, starting transfers between devices, swapped(): return lax.ppermute(array, axis, [(i, i ^ bit) for i in range(size)])  4.82 us
    slice x1, local copies, waits for them, and re-layouts, per_device(): owns += [rest[:, :, :, g * HD:(g + 1) * HD] for g in range(1, KVH)]  3.72 us
  transfers between devices with their start and end apart: 16, of which 10 were waited for; matrix products, arithmetic and copies ran while one was open for 5% of the time, Pallas kernels for 37%

profile of v15, /device:TPU:0, one launch (start us, length us, event | category | flops | bytes accessed | tf_op | source)
XLA Modules:
  0.0 178.7 jit_solution(14992384875131292279)
XLA Ops:
  0.7 0.5 collective-permute-start
  1.2 1.3 slice.35.refs_1_
  2.5 2.7 %collective-permute-start.2 = (bf16[16,2,128,512]{3,2,1,0:T(8,128)(2,1)}, bf16[16,2,128,512]{3,2,1,0:T(8,128)(2,1)}, u32[]{:S(2)}, u32[]{:S(2)}) collective-permute-start(bf16[16,2,128,512]{3,2,1,0:T(8,128)(2,1)} %refs_6_.1), channel_id=1, source_target_pairs={{0,1},{1,0},{2,3},{3,2},{4,5},{5,4},{6,7},{7,6},{8,9},{9,8},{10,11... | collective-permute-start | bytes 12582920 | tf_op jit(solution)/shard_map/ppermute | solution.py:28
  5.9 0.1 convert_reduce_fusion.1
  6.1 0.1 convert_reduce_fusion
  6.2 0.1 select_reduce_fusion
  6.4 0.1 and_reduce_fusion
  6.7 0.1 copy.19
  6.8 3.6 %collective-permute-done.refs_7_ = bf16[1,2,128,512]{3,2,1,0:T(8,128)(2,1)S(1)} collective-permute-done((bf16[1,2,128,512]{3,2,1,0:T(8,128)(2,1)}, bf16[1,2,128,512]{3,2,1,0:T(8,128)(2,1)S(1)}, u32[]{:S(2)}, u32[]{:S(2)}) %collective-permute-start) | collective-permute-done | bytes 262176 | tf_op jit(solution)/shard_map/ppermute | solution.py:33
  10.5 1.2 pad_maximum_fusion
  11.7 3.6 %all-to-all-start = ((bf16[4,128,1408]{2,1,0:T(8,128)(2,1)}), bf16[4,128,1408]{2,1,0:T(8,128)(2,1)S(1)}, u32[]{:S(2)}, u32[]{:S(2)}) async-start(bf16[4,128,1408]{2,1,0:T(8,128)(2,1)} %pad_maximum_fusion), calls=%async_computation | async-start | bytes 2883584 | tf_op jit(solution)/shard_map/all_to_all | solution.py:317
  15.3 0.6 collective-permute-start.1
  15.9 3.7 %fusion.17 = (bf16[16,2,128,128]{3,2,1,0:T(8,128)(2,1)}, bf16[16,2,128,128]{3,2,1,0:T(8,128)(2,1)}, bf16[16,2,128,128]{3,2,1,0:T(8,128)(2,1)}) fusion(bf16[16,2,128,512]{3,2,1,0:T(8,128)(2,1)} %refs_6_.1), kind=kLoop, calls=%fused_computation.41 | loop fusion | bytes 6291456 | tf_op jit(solution)/shard_map/slice | solution.py:335
  19.6 18.8 %collective-permute-done.1.refs_3_ = bf16[16,2,128,128]{3,2,1,0:T(8,128)(2,1)S(1)} collective-permute-done((bf16[16,2,128,128]{3,2,1,0:T(8,128)(2,1)S(1)}, bf16[16,2,128,128]{3,2,1,0:T(8,128)(2,1)S(1)}, u32[]{:S(2)}, u32[]{:S(2)}) %collective-permute-start.1) | collective-permute-done | bytes 1048608 | tf_op jit(solution)/shard_map/ppermute | solution.py:28
  38.4 1.0 copy-done.6
  39.4 8.5 %all-to-all-done.refs_0_ = bf16[4,128,1408]{2,1,0:T(8,128)(2,1)S(1)} async-done(((bf16[4,128,1408]{2,1,0:T(8,128)(2,1)}), bf16[4,128,1408]{2,1,0:T(8,128)(2,1)S(1)}, u32[]{:S(2)}, u32[]{:S(2)}) %all-to-all-start) | async-done | bytes 1441824 | tf_op jit(solution)/shard_map/all_to_all | solution.py:317
  47.9 1.2 broadcast_in_dim.32
  49.1 3.7 %all-to-all-start.1 = ((bf16[4,128,1280]{2,1,0:T(8,128)(2,1)}), bf16[4,128,1280]{2,1,0:T(8,128)(2,1)S(1)}, u32[]{:S(2)}, u32[]{:S(2)}) async-start(bf16[4,128,1280]{2,1,0:T(8,128)(2,1)} %broadcast_in_dim.32), calls=%async_computation.1 | async-start | bytes 2621440 | tf_op jit(solution)/shard_map/all_to_all | solution.py:317
  52.9 0.6 collective-permute-start.5
  54.1 0.2 slice_reduce_fusion
  54.3 1.5 collective-permute-done.6.refs_4_
  55.9 2.2 %copy-done = bf16[16,2,128,512]{3,2,1,0:T(8,128)(2,1)S(1)} copy-done((bf16[16,2,128,512]{3,2,1,0:T(8,128)(2,1)S(1)}, bf16[16,2,128,512]{3,2,1,0:T(8,128)(2,1)}, u32[]{:S(2)}) %copy-start) | copy-done | bytes 4194328
  58.0 1.2 copy-done.3
  59.3 1.2 copy-done.7
  60.5 16.4 %shard_map.86 = (bf16[4,672,128]{2,1,0:T(8,128)(2,1)S(1)}, bf16[16,2,128,512]{3,2,1,0:T(8,128)(2,1)}) custom-call(s32[4,16]{1,0:T(4,128)S(1)} %bitcast.31, s32[4]{0:T(128)S(1)} %get-tuple-element.19.counts, s32[4]{0:T(128)S(1)} %get-tuple-element.18.lasts, s32[1]{0:T(128)} %bitcast.9.mine, s32[1]{0:T(128)} %bitcast.21.store, ...), custom_call_target="tpu_custom_call" | custom-call | flops 1 | bytes 1 | tf_op jit(solution)/shard_map/pallas_call | solution.py:252
  76.9 0.9 copy-done.8
  77.8 0.9 collective-permute-done.5.refs_3_
  78.8 0.5 collective-permute-start.4
  79.3 4.3 %all-to-all-done.1.refs_0_ = bf16[4,128,1280]{2,1,0:T(8,128)(2,1)S(1)} async-done(((bf16[4,128,1280]{2,1,0:T(8,128)(2,1)}), bf16[4,128,1280]{2,1,0:T(8,128)(2,1)S(1)}, u32[]{:S(2)}, u32[]{:S(2)}) %all-to-all-start.1) | async-done | bytes 1310752 | tf_op jit(solution)/shard_map/all_to_all | solution.py:317
  83.6 4.2 %all-to-all-start.5 = ((bf16[4,672,128]{2,1,0:T(8,128)(2,1)}), bf16[4,672,128]{2,1,0:T(8,128)(2,1)}, u32[]{:S(2)}, u32[]{:S(2)}) async-start(bf16[4,672,128]{2,1,0:T(8,128)(2,1)} %copy-done.8), calls=%async_computation.5 | async-start | bytes 1376256 | tf_op jit(solution)/shard_map/all_to_all | solution.py:317
  87.8 1.2 copy-done.4
  89.0 14.9 %shard_map.87 = bf16[4,672,128]{2,1,0:T(8,128)(2,1)S(1)} custom-call(s32[4,16]{1,0:T(4,128)S(1)} %bitcast.32, s32[4]{0:T(128)S(1)} %get-tuple-element.19.counts, s32[4]{0:T(128)S(1)} %get-tuple-element.18.lasts, s32[1]{0:T(128)} %bitcast.9.mine, s32[1]{0:T(128)} %bitcast.22.store, bf16[4,128,1408]{2,1,0:T(8,128)(2,1)S(1)} %all-to-all-done.refs_0_, ...), custom_call_target="tpu_custom_call" | custom-call | flops 1 | bytes 1 | tf_op jit(solution)/shard_map/pallas_call | solution.py:252
  103.9 0.8 copy-done.5
  104.7 0.4 collective-permute-start.3
  105.2 0.2 all-to-all-done.5.parts
  105.3 4.8 %all-to-all-start.4 = ((bf16[4,672,128]{2,1,0:T(8,128)(2,1)}), bf16[4,672,128]{2,1,0:T(8,128)(2,1)}, u32[]{:S(2)}, u32[]{:S(2)}) async-start(bf16[4,672,128]{2,1,0:T(8,128)(2,1)} %copy-done.5), calls=%async_computation.4 | async-start | bytes 1376256 | tf_op jit(solution)/shard_map/all_to_all | solution.py:317
  110.1 13.4 %shard_map.88 = bf16[4,672,128]{2,1,0:T(8,128)(2,1)} custom-call(s32[4,16]{1,0:T(4,128)S(1)} %bitcast.33, s32[4]{0:T(128)S(1)} %get-tuple-element.19.counts, s32[4]{0:T(128)S(1)} %get-tuple-element.18.lasts, s32[1]{0:T(128)} %bitcast.9.mine, s32[1]{0:T(128)} %bitcast.23.store, bf16[4,128,1280]{2,1,0:T(8,128)(2,1)S(1)} %all-to-all-done.1.refs_0_, ...), custom_call_target="tpu_custom_call" | custom-call | flops 1 | bytes 1 | tf_op jit(solution)/shard_map/pallas_call | solution.py:252
  123.5 7.0 %collective-permute-done.3.refs_3_ = bf16[16,2,128,128]{3,2,1,0:T(8,128)(2,1)S(1)} collective-permute-done((bf16[16,2,128,128]{3,2,1,0:T(8,128)(2,1)}, bf16[16,2,128,128]{3,2,1,0:T(8,128)(2,1)S(1)}, u32[]{:S(2)}, u32[]{:S(2)}) %collective-permute-start.3) | collective-permute-done | bytes 1048608 | tf_op jit(solution)/shard_map/ppermute | solution.py:28
  130.5 4.9 %all-to-all-start.3 = ((bf16[4,672,128]{2,1,0:T(8,128)(2,1)}), bf16[4,672,128]{2,1,0:T(8,128)(2,1)}, u32[]{:S(2)}, u32[]{:S(2)}) async-start(bf16[4,672,128]{2,1,0:T(8,128)(2,1)} %shard_map.88), calls=%async_computation.3 | async-start | bytes 1376256 | tf_op jit(solution)/shard_map/all_to_all | solution.py:317
  135.4 14.7 %shard_map.89 = bf16[4,672,128]{2,1,0:T(8,128)(2,1)} custom-call(s32[4,16]{1,0:T(4,128)S(1)} %bitcast.34, s32[4]{0:T(128)S(1)} %get-tuple-element.19.counts, s32[4]{0:T(128)S(1)} %get-tuple-element.18.lasts, s32[1]{0:T(128)} %bitcast.9.mine, s32[1]{0:T(128)} %bitcast.24.store, bf16[4,128,1280]{2,1,0:T(8,128)(2,1)S(1)} %all-to-all-done.1.refs_0_, ...), custom_call_target="tpu_custom_call" | custom-call | flops 1 | bytes 1 | tf_op jit(solution)/shard_map/pallas_call | solution.py:252
  150.1 4.1 %all-to-all-done.3.parts = bf16[4,672,128]{2,1,0:T(8,128)(2,1)} async-done(((bf16[4,672,128]{2,1,0:T(8,128)(2,1)}), bf16[4,672,128]{2,1,0:T(8,128)(2,1)}, u32[]{:S(2)}, u32[]{:S(2)}) %all-to-all-start.3) | async-done | bytes 688160 | tf_op jit(solution)/shard_map/all_to_all | solution.py:317
  154.2 3.5 %all-to-all-start.2 = ((bf16[4,672,128]{2,1,0:T(8,128)(2,1)}), bf16[4,672,128]{2,1,0:T(8,128)(2,1)S(1)}, u32[]{:S(2)}, u32[]{:S(2)}) async-start(bf16[4,672,128]{2,1,0:T(8,128)(2,1)} %shard_map.89), calls=%async_computation.2 | async-start | bytes 1376256 | tf_op jit(solution)/shard_map/all_to_all | solution.py:317
  157.7 2.4 %shard_map.90.refs_0_ = bf16[128,2560]{1,0:T(8,128)(2,1)} custom-call(bf16[4,672,128]{2,1,0:T(8,128)(2,1)} %all-to-all-done.5.parts), custom_call_target="tpu_custom_call" | custom-call | flops 1 | bytes 1 | tf_op jit(solution)/shard_map/pallas_call | solution.py:289
  160.0 2.4 %shard_map.91.refs_0_ = bf16[128,2560]{1,0:T(8,128)(2,1)} custom-call(bf16[4,672,128]{2,1,0:T(8,128)(2,1)} %all-to-all-done.4.parts, bf16[128,2560]{1,0:T(8,128)(2,1)} %shard_map.90.refs_0_), custom_call_target="tpu_custom_call", output_to_operand_aliasing={{}: (1, {})} | custom-call | flops 1 | bytes 1 | tf_op jit(solution)/shard_map/pallas_call | solution.py:289
  162.4 2.4 %shard_map.92.refs_0_ = bf16[128,2560]{1,0:T(8,128)(2,1)} custom-call(bf16[4,672,128]{2,1,0:T(8,128)(2,1)} %all-to-all-done.3.parts, bf16[128,2560]{1,0:T(8,128)(2,1)} %shard_map.91.refs_0_), custom_call_target="tpu_custom_call", output_to_operand_aliasing={{}: (1, {})} | custom-call | flops 1 | bytes 1 | tf_op jit(solution)/shard_map/pallas_call | solution.py:289
  164.8 10.7 %all-to-all-done.2.parts = bf16[4,672,128]{2,1,0:T(8,128)(2,1)S(1)} async-done(((bf16[4,672,128]{2,1,0:T(8,128)(2,1)}), bf16[4,672,128]{2,1,0:T(8,128)(2,1)S(1)}, u32[]{:S(2)}, u32[]{:S(2)}) %all-to-all-start.2) | async-done | bytes 688160 | tf_op jit(solution)/shard_map/all_to_all | solution.py:317
  175.5 0.9 copy-done.9
  176.4 2.4 %shard_map.93 = bf16[128,2560]{1,0:T(8,128)(2,1)} custom-call(bf16[4,672,128]{2,1,0:T(8,128)(2,1)} %copy-done.9, bf16[128,2560]{1,0:T(8,128)(2,1)} %shard_map.92.refs_0_), custom_call_target="tpu_custom_call", output_to_operand_aliasing={{}: (1, {})} | custom-call | flops 1 | bytes 1 | tf_op jit(solution)/shard_map/pallas_call | solution.py:289
  (43 shorter events, 0.5 us)
Async XLA Ops:
  0.6 5.3 %copy-start.10 = (s32[1,48]{1,0:T(1,128)S(1)}, s32[1,48]{1,0:T(1,128)}, u32[]{:S(2)}) copy-start(s32[1,48]{1,0:T(1,128)} %param.10) | copy-start | bytes 580
  0.6 5.3 %copy-start.11 = (s32[1,48]{1,0:T(1,128)S(1)}, s32[1,48]{1,0:T(1,128)}, u32[]{:S(2)}) copy-start(s32[1,48]{1,0:T(1,128)} %param.11) | copy-start | bytes 580
  0.6 9.8 %slice-start = ((bf16[128,2560]{1,0:T(8,128)(2,1)}), bf16[128,1280]{1,0:T(8,128)(2,1)S(1)}, s32[]{:S(2)}) async-start(bf16[128,2560]{1,0:T(8,128)(2,1)} %param.7), calls=%async_computation.6 | async-start | bytes 655360 | tf_op jit(solution)/shard_map/slice | solution.py:341
  0.7 9.8 %collective-permute-start = (bf16[1,2,128,512]{3,2,1,0:T(8,128)(2,1)}, bf16[1,2,128,512]{3,2,1,0:T(8,128)(2,1)S(1)}, u32[]{:S(2)}, u32[]{:S(2)}) collective-permute-start(bf16[1,2,128,512]{3,2,1,0:T(8,128)(2,1)} %bitcast.25), channel_id=1, source_target_pairs={{0,1},{1,2},{2,3},{3,4},{4,5},{5,6},{6,7},{7,8},{8,9},{9,10},{10,1... | collective-permute-start | bytes 786440 | tf_op jit(solution)/shard_map/ppermute | solution.py:33
  2.5 12.8 %copy-start.2 = (bf16[16,2,128,128]{3,2,1,0:T(8,128)(2,1)}, bf16[16,2,128,128]{3,2,1,0:T(8,128)(2,1)S(1)}, u32[]{:S(2)}) copy-start(bf16[16,2,128,128]{3,2,1,0:T(8,128)(2,1)S(1)} %slice.35.refs_1_) | copy-start | bytes 3145732
  2.5 53.4 %collective-permute-start.2 = (bf16[16,2,128,512]{3,2,1,0:T(8,128)(2,1)}, bf16[16,2,128,512]{3,2,1,0:T(8,128)(2,1)}, u32[]{:S(2)}, u32[]{:S(2)}) collective-permute-start(bf16[16,2,128,512]{3,2,1,0:T(8,128)(2,1)} %refs_6_.1), channel_id=1, source_target_pairs={{0,1},{1,0},{2,3},{3,2},{4,5},{5,4},{6,7},{7,6},{8,9},{9,8},{10,11... | collective-permute-start | bytes 12582920 | tf_op jit(solution)/shard_map/ppermute | solution.py:28
  11.7 36.2 %all-to-all-start = ((bf16[4,128,1408]{2,1,0:T(8,128)(2,1)}), bf16[4,128,1408]{2,1,0:T(8,128)(2,1)S(1)}, u32[]{:S(2)}, u32[]{:S(2)}) async-start(bf16[4,128,1408]{2,1,0:T(8,128)(2,1)} %pad_maximum_fusion), calls=%async_computation | async-start | bytes 2883584 | tf_op jit(solution)/shard_map/all_to_all | solution.py:317
  15.3 32.6 %slice-start.1 = ((bf16[128,2560]{1,0:T(8,128)(2,1)}), bf16[128,1280]{1,0:T(8,128)(2,1)S(1)}, s32[]{:S(2)}) async-start(bf16[128,2560]{1,0:T(8,128)(2,1)} %param.7), calls=%async_computation.7 | async-start | bytes 655360 | tf_op jit(solution)/shard_map/slice | solution.py:343
  15.3 23.1 %collective-permute-start.1 = (bf16[16,2,128,128]{3,2,1,0:T(8,128)(2,1)S(1)}, bf16[16,2,128,128]{3,2,1,0:T(8,128)(2,1)S(1)}, u32[]{:S(2)}, u32[]{:S(2)}) collective-permute-start(bf16[16,2,128,128]{3,2,1,0:T(8,128)(2,1)S(1)} %slice.35.refs_1_), channel_id=1, source_target_pairs={{0,2},{1,3},{2,0},{3,1},{4,6},{5,7},{6,4},{7,5},{8,10},{9,11},{10,... | collective-permute-start | bytes 3145736 | tf_op jit(solution)/shard_map/ppermute | solution.py:28
  38.4 1.0 copy-start.6
  49.1 6.8 %copy-start.1 = (bf16[1,1,2,128,512]{4,3,2,1,0:T(8,128)(2,1)S(1)}, bf16[1,1,2,128,512]{4,3,2,1,0:T(8,128)(2,1)}, u32[]{:S(2)}) copy-start(bf16[1,1,2,128,512]{4,3,2,1,0:T(8,128)(2,1)} %param.8) | copy-start | bytes 786436
  49.1 34.5 %all-to-all-start.1 = ((bf16[4,128,1280]{2,1,0:T(8,128)(2,1)}), bf16[4,128,1280]{2,1,0:T(8,128)(2,1)S(1)}, u32[]{:S(2)}, u32[]{:S(2)}) async-start(bf16[4,128,1280]{2,1,0:T(8,128)(2,1)} %broadcast_in_dim.32), calls=%async_computation.1 | async-start | bytes 2621440 | tf_op jit(solution)/shard_map/all_to_all | solution.py:317
  52.8 3.1 %collective-permute-start.6 = (bf16[16,2,128,128]{3,2,1,0:T(8,128)(2,1)}, bf16[16,2,128,128]{3,2,1,0:T(8,128)(2,1)}, u32[]{:S(2)}, u32[]{:S(2)}) collective-permute-start(bf16[16,2,128,128]{3,2,1,0:T(8,128)(2,1)} %copy-done.6), channel_id=1, source_target_pairs={{0,1},{1,0},{2,3},{3,2},{4,5},{5,4},{6,7},{7,6},{8,9},{9,8},{10,11... | collective-permute-start | bytes 3145736 | tf_op jit(solution)/shard_map/ppermute | solution.py:28
  52.9 25.9 %collective-permute-start.5 = (bf16[16,2,128,128]{3,2,1,0:T(8,128)(2,1)}, bf16[16,2,128,128]{3,2,1,0:T(8,128)(2,1)}, u32[]{:S(2)}, u32[]{:S(2)}) collective-permute-start(bf16[16,2,128,128]{3,2,1,0:T(8,128)(2,1)} %get-tuple-element.24.refs_1_), channel_id=1, source_target_pairs={{0,2},{1,3},{2,0},{3,1},{4,6},{5,7},{6,4},{7,5},{8,10},{9,11},{10,... | collective-permute-start | bytes 3145736 | tf_op jit(solution)/shard_map/ppermute | solution.py:28
  55.9 2.2 %copy-start = (bf16[16,2,128,512]{3,2,1,0:T(8,128)(2,1)S(1)}, bf16[16,2,128,512]{3,2,1,0:T(8,128)(2,1)}, u32[]{:S(2)}) copy-start(bf16[16,2,128,512]{3,2,1,0:T(8,128)(2,1)} %refs_6_.1) | copy-start | bytes 12582916
  58.0 1.2 copy-start.3
  59.3 1.2 copy-start.7
  76.9 0.9 copy-start.8
  78.8 9.0 %collective-permute-start.7 = (bf16[16,2,128,128]{3,2,1,0:T(8,128)(2,1)}, bf16[16,2,128,128]{3,2,1,0:T(8,128)(2,1)}, u32[]{:S(2)}, u32[]{:S(2)}) collective-permute-start(bf16[16,2,128,128]{3,2,1,0:T(8,128)(2,1)} %collective-permute-done.5.refs_3_), channel_id=1, source_target_pairs={{0,1},{1,0},{2,3},{3,2},{4,5},{5,4},{6,7},{7,6},{8,9},{9,8},{10,11... | collective-permute-start | bytes 3145736 | tf_op jit(solution)/shard_map/ppermute | solution.py:28
  78.8 26.0 %collective-permute-start.4 = (bf16[16,2,128,128]{3,2,1,0:T(8,128)(2,1)}, bf16[16,2,128,128]{3,2,1,0:T(8,128)(2,1)}, u32[]{:S(2)}, u32[]{:S(2)}) collective-permute-start(bf16[16,2,128,128]{3,2,1,0:T(8,128)(2,1)} %get-tuple-element.22.refs_1_), channel_id=1, source_target_pairs={{0,2},{1,3},{2,0},{3,1},{4,6},{5,7},{6,4},{7,5},{8,10},{9,11},{10,... | collective-permute-start | bytes 3145736 | tf_op jit(solution)/shard_map/ppermute | solution.py:28
  83.6 21.7 %all-to-all-start.5 = ((bf16[4,672,128]{2,1,0:T(8,128)(2,1)}), bf16[4,672,128]{2,1,0:T(8,128)(2,1)}, u32[]{:S(2)}, u32[]{:S(2)}) async-start(bf16[4,672,128]{2,1,0:T(8,128)(2,1)} %copy-done.8), calls=%async_computation.5 | async-start | bytes 1376256 | tf_op jit(solution)/shard_map/all_to_all | solution.py:317
  87.8 1.2 copy-start.4
  103.9 0.8 copy-start.5
  104.7 5.4 %collective-permute-start.8 = (bf16[16,2,128,128]{3,2,1,0:T(8,128)(2,1)}, bf16[16,2,128,128]{3,2,1,0:T(8,128)(2,1)}, u32[]{:S(2)}, u32[]{:S(2)}) collective-permute-start(bf16[16,2,128,128]{3,2,1,0:T(8,128)(2,1)} %collective-permute-done.4.refs_3_), channel_id=1, source_target_pairs={{0,1},{1,0},{2,3},{3,2},{4,5},{5,4},{6,7},{7,6},{8,9},{9,8},{10,11... | collective-permute-start | bytes 3145736 | tf_op jit(solution)/shard_map/ppermute | solution.py:28
  104.7 25.8 %collective-permute-start.3 = (bf16[16,2,128,128]{3,2,1,0:T(8,128)(2,1)}, bf16[16,2,128,128]{3,2,1,0:T(8,128)(2,1)S(1)}, u32[]{:S(2)}, u32[]{:S(2)}) collective-permute-start(bf16[16,2,128,128]{3,2,1,0:T(8,128)(2,1)} %get-tuple-element.23.refs_1_), channel_id=1, source_target_pairs={{0,2},{1,3},{2,0},{3,1},{4,6},{5,7},{6,4},{7,5},{8,10},{9,11},{10,... | collective-permute-start | bytes 3145736 | tf_op jit(solution)/shard_map/ppermute | solution.py:28
  105.3 25.2 %all-to-all-start.4 = ((bf16[4,672,128]{2,1,0:T(8,128)(2,1)}), bf16[4,672,128]{2,1,0:T(8,128)(2,1)}, u32[]{:S(2)}, u32[]{:S(2)}) async-start(bf16[4,672,128]{2,1,0:T(8,128)(2,1)} %copy-done.5), calls=%async_computation.4 | async-start | bytes 1376256 | tf_op jit(solution)/shard_map/all_to_all | solution.py:317
  130.5 4.9 %collective-permute-start.9 = (bf16[16,2,128,128]{3,2,1,0:T(8,128)(2,1)S(1)}, bf16[16,2,128,128]{3,2,1,0:T(8,128)(2,1)}, u32[]{:S(2)}, u32[]{:S(2)}) collective-permute-start(bf16[16,2,128,128]{3,2,1,0:T(8,128)(2,1)S(1)} %collective-permute-done.3.refs_3_), channel_id=1, source_target_pairs={{0,1},{1,0},{2,3},{3,2},{4,5},{5,4},{6,7},{7,6},{8,9},{9,8},{10,11... | collective-permute-start | bytes 3145736 | tf_op jit(solution)/shard_map/ppermute | solution.py:28
  130.5 23.7 %all-to-all-start.3 = ((bf16[4,672,128]{2,1,0:T(8,128)(2,1)}), bf16[4,672,128]{2,1,0:T(8,128)(2,1)}, u32[]{:S(2)}, u32[]{:S(2)}) async-start(bf16[4,672,128]{2,1,0:T(8,128)(2,1)} %shard_map.88), calls=%async_computation.3 | async-start | bytes 1376256 | tf_op jit(solution)/shard_map/all_to_all | solution.py:317
  154.2 21.3 %all-to-all-start.2 = ((bf16[4,672,128]{2,1,0:T(8,128)(2,1)}), bf16[4,672,128]{2,1,0:T(8,128)(2,1)S(1)}, u32[]{:S(2)}, u32[]{:S(2)}) async-start(bf16[4,672,128]{2,1,0:T(8,128)(2,1)} %shard_map.89), calls=%async_computation.2 | async-start | bytes 1376256 | tf_op jit(solution)/shard_map/all_to_all | solution.py:317
  175.5 0.9 copy-start.9

commit v16 on v15

--- a/solution.py
+++ b/solution.py
@@ -337,7 +337,7 @@
     twin = swapped(rest, "serve", 1)
     rows = page_rows(me, lines, limit, slots, page_owner, page_slot, prefix_len).astype(queries.dtype)
     rows = jnp.pad(rows[:, None], ((0, 0), (0, PAGE - 1), (0, PAGE - limit - 2)))
-    half = KVH // 2 * CHUNK
+    half = CHUNK
     early = jnp.broadcast_to(after(queries, incoming)[None, :, :half], (lines, PAGE, half))
     early = exchanged(jnp.concatenate([early, rows], axis=2), groups)
     later = after(queries, sides[0], owns[1])[None, :, half:]
@@ -351,7 +351,7 @@
         side = sides[g]
         if g > 0:
             side = after(side, parts[g - 1])
-        q_all, q_head = (early, g) if g < KVH // 2 else (later, g - KVH // 2)
+        q_all, q_head = (early, 0) if g == 0 else (later, g - 1)
         both = swapped(side, "serve", 1)
         pools = (owns[g], twin, side, both)
         if g == 0:

time: 180 us -> 186 us (1.033)
  Pallas kernels: 68.8 us -> 61.5 us
  waiting for transfers between devices: 59.7 us -> 65.6 us
  local copies, waits for them, and re-layouts: 16.2 us -> 21.3 us
  starting transfers between devices: 29.9 us -> 31.8 us
    pallas_call x4, Pallas kernels: 59.4 us -> 52.1 us  [attend(): pl.pallas_call(functools.partial(attend_kernel, lines, head, q_head), gri...]
    unnamed x24 -> x34, local copies, waits for them, and re-layouts: 9.45 us -> 14.3 us
    all_to_all x6, waiting for transfers between devices: 27.8 us -> 31.9 us  [exchanged(): lax.all_to_all(array, 'serve', 0, 0, axis_index_groups=groups, tiled=True)]
  transfers between devices with their start and end apart: 16 -> 16, of which waited for: 10 -> 8; matrix products, arithmetic and copies ran while one was open for 5% -> 5% of each run, Pallas kernels for 37% -> 32%
where the time goes in v16:
time: 186 us; the launch traced here: 185 us
  waiting for transfers between devices  65.6 us (35%)
  Pallas kernels  61.5 us (33%)
  starting transfers between devices  31.8 us (17%)
  local copies, waits for them, and re-layouts  21.3 us (11%)
  other arithmetic  2.34 us (1%)
  between operations  2.24 us (1%)
    pallas_call x4, Pallas kernels, attend(): pl.pallas_call(functools.partial(attend_kernel, lines, head, q_head), gri...  52.1 us
    all_to_all x6, waiting for transfers between devices, exchanged(): lax.all_to_all(array, 'serve', 0, 0, axis_index_groups=groups, tiled=True)  31.9 us
    ppermute x9, waiting for transfers between devices, swapped(): return lax.ppermute(array, axis, [(i, i ^ bit) for i in range(size)])  30.1 us
    all_to_all x6, starting transfers between devices, exchanged(): lax.all_to_all(array, 'serve', 0, 0, axis_index_groups=groups, tiled=True)  24.8 us
    unnamed x34, local copies, waits for them, and re-layouts  14.3 us
    pallas_call x4, Pallas kernels, merge(): pl.pallas_call(functools.partial(merge_kernel, head), in_specs=[pl.BlockS...  9.41 us
    ppermute x9, starting transfers between devices, swapped(): return lax.ppermute(array, axis, [(i, i ^ bit) for i in range(size)])  6.46 us
    slice x1, local copies, waits for them, and re-layouts, per_device(): owns += [rest[:, :, :, g * HD:(g + 1) * HD] for g in range(1, KVH)]  3.74 us
  transfers between devices with their start and end apart: 16, of which 8 were waited for; matrix products, arithmetic and copies ran while one was open for 5% of the time, Pallas kernels for 32%

profile of v16, /device:TPU:0, one launch (start us, length us, event | category | flops | bytes accessed | tf_op | source)
XLA Modules:
  0.0 184.7 jit_solution(8890715273441949955)
XLA Ops:
  0.7 0.5 collective-permute-start
  1.2 1.3 slice.35.refs_1_
  2.5 2.7 %collective-permute-start.2 = (bf16[16,2,128,512]{3,2,1,0:T(8,128)(2,1)}, bf16[16,2,128,512]{3,2,1,0:T(8,128)(2,1)}, u32[]{:S(2)}, u32[]{:S(2)}) collective-permute-start(bf16[16,2,128,512]{3,2,1,0:T(8,128)(2,1)} %refs_6_.1), channel_id=1, source_target_pairs={{0,1},{1,0},{2,3},{3,2},{4,5},{5,4},{6,7},{7,6},{8,9},{9,8},{10,11... | collective-permute-start | bytes 12582920 | tf_op jit(solution)/shard_map/ppermute | solution.py:28
  6.1 0.1 convert_reduce_fusion
  6.9 3.6 %collective-permute-done.refs_7_ = bf16[1,2,128,512]{3,2,1,0:T(8,128)(2,1)S(1)} collective-permute-done((bf16[1,2,128,512]{3,2,1,0:T(8,128)(2,1)}, bf16[1,2,128,512]{3,2,1,0:T(8,128)(2,1)S(1)}, u32[]{:S(2)}, u32[]{:S(2)}) %collective-permute-start) | collective-permute-done | bytes 262176 | tf_op jit(solution)/shard_map/ppermute | solution.py:33
  10.5 1.0 pad_maximum_fusion
  11.4 3.5 %all-to-all-start = ((bf16[4,128,768]{2,1,0:T(8,128)(2,1)}), bf16[4,128,768]{2,1,0:T(8,128)(2,1)S(1)}, u32[]{:S(2)}, u32[]{:S(2)}) async-start(bf16[4,128,768]{2,1,0:T(8,128)(2,1)} %pad_maximum_fusion), calls=%async_computation | async-start | bytes 1572864 | tf_op jit(solution)/shard_map/all_to_all | solution.py:317
  15.0 0.6 collective-permute-start.1
  15.6 3.7 %fusion.17 = (bf16[16,2,128,128]{3,2,1,0:T(8,128)(2,1)}, bf16[16,2,128,128]{3,2,1,0:T(8,128)(2,1)}, bf16[16,2,128,128]{3,2,1,0:T(8,128)(2,1)}) fusion(bf16[16,2,128,512]{3,2,1,0:T(8,128)(2,1)} %refs_6_.1), kind=kLoop, calls=%fused_computation.41 | loop fusion | bytes 6291456 | tf_op jit(solution)/shard_map/slice | solution.py:335
  19.3 18.8 %collective-permute-done.1.refs_3_ = bf16[16,2,128,128]{3,2,1,0:T(8,128)(2,1)S(1)} collective-permute-done((bf16[16,2,128,128]{3,2,1,0:T(8,128)(2,1)S(1)}, bf16[16,2,128,128]{3,2,1,0:T(8,128)(2,1)S(1)}, u32[]{:S(2)}, u32[]{:S(2)}) %collective-permute-start.1) | collective-permute-done | bytes 1048608 | tf_op jit(solution)/shard_map/ppermute | solution.py:28
  38.1 1.0 copy-done.9
  39.1 0.9 copy-done.4
  40.0 1.5 broadcast_in_dim.32
  41.4 4.9 %all-to-all-start.1 = ((bf16[4,128,1920]{2,1,0:T(8,128)(2,1)}), bf16[4,128,1920]{2,1,0:T(8,128)(2,1)S(1)}, u32[]{:S(2)}, u32[]{:S(2)}) async-start(bf16[4,128,1920]{2,1,0:T(8,128)(2,1)} %broadcast_in_dim.32), calls=%async_computation.1 | async-start | bytes 3932160 | tf_op jit(solution)/shard_map/all_to_all | solution.py:317
  46.4 0.5 collective-permute-start.5
  47.6 0.7 slice_convert_fusion
  48.3 0.2 slice_reduce_fusion
  48.5 0.9 collective-permute-done.6.refs_4_
  49.4 2.2 %copy-done = bf16[16,2,128,512]{3,2,1,0:T(8,128)(2,1)S(1)} copy-done((bf16[16,2,128,512]{3,2,1,0:T(8,128)(2,1)S(1)}, bf16[16,2,128,512]{3,2,1,0:T(8,128)(2,1)}, u32[]{:S(2)}) %copy-start) | copy-done | bytes 4194328
  51.6 1.1 copy-done.5
  52.7 1.2 copy-done.10
  54.0 13.8 %shard_map.86 = (bf16[4,672,128]{2,1,0:T(8,128)(2,1)S(1)}, bf16[16,2,128,512]{3,2,1,0:T(8,128)(2,1)}) custom-call(s32[4,16]{1,0:T(4,128)S(1)} %bitcast.31, s32[4]{0:T(128)S(1)} %get-tuple-element.19.counts, s32[4]{0:T(128)S(1)} %get-tuple-element.18.lasts, s32[1]{0:T(128)} %bitcast.9.mine, s32[1]{0:T(128)} %bitcast.21.store, ...), custom_call_target="tpu_custom_call" | custom-call | flops 1 | bytes 1 | tf_op jit(solution)/shard_map/pallas_call | solution.py:252
  67.8 0.9 copy-done.13
  68.6 3.6 %collective-permute-done.5.refs_3_ = bf16[16,2,128,128]{3,2,1,0:T(8,128)(2,1)} collective-permute-done((bf16[16,2,128,128]{3,2,1,0:T(8,128)(2,1)}, bf16[16,2,128,128]{3,2,1,0:T(8,128)(2,1)}, u32[]{:S(2)}, u32[]{:S(2)}) %collective-permute-start.5) | collective-permute-done | bytes 1048608 | tf_op jit(solution)/shard_map/ppermute | solution.py:28
  72.3 0.5 collective-permute-start.4
  72.8 16.0 %all-to-all-done.1.refs_0_ = bf16[4,128,1920]{2,1,0:T(8,128)(2,1)S(1)} async-done(((bf16[4,128,1920]{2,1,0:T(8,128)(2,1)}), bf16[4,128,1920]{2,1,0:T(8,128)(2,1)S(1)}, u32[]{:S(2)}, u32[]{:S(2)}) %all-to-all-start.1) | async-done | bytes 1966112 | tf_op jit(solution)/shard_map/all_to_all | solution.py:317
  88.8 4.2 %all-to-all-start.5 = ((bf16[4,672,128]{2,1,0:T(8,128)(2,1)}), bf16[4,672,128]{2,1,0:T(8,128)(2,1)}, u32[]{:S(2)}, u32[]{:S(2)}) async-start(bf16[4,672,128]{2,1,0:T(8,128)(2,1)} %copy-done.13), calls=%async_computation.5 | async-start | bytes 1376256 | tf_op jit(solution)/shard_map/all_to_all | solution.py:317
  93.0 1.0 copy-done.11
  94.0 1.2 copy-done.3
  95.2 1.2 copy-done.12
  96.5 13.6 %shard_map.87 = bf16[4,672,128]{2,1,0:T(8,128)(2,1)S(1)} custom-call(s32[4,16]{1,0:T(4,128)S(1)} %bitcast.32, s32[4]{0:T(128)S(1)} %get-tuple-element.19.counts, s32[4]{0:T(128)S(1)} %get-tuple-element.18.lasts, s32[1]{0:T(128)} %bitcast.9.mine, s32[1]{0:T(128)} %bitcast.22.store, bf16[4,128,1920]{2,1,0:T(8,128)(2,1)S(1)} %all-to-all-done.1.refs_0_, ...), custom_call_target="tpu_custom_call" | custom-call | flops 1 | bytes 1 | tf_op jit(solution)/shard_map/pallas_call | solution.py:252
  110.1 0.9 copy-done.6
  110.9 2.1 %collective-permute-start.3 = (bf16[16,2,128,128]{3,2,1,0:T(8,128)(2,1)S(1)}, bf16[16,2,128,128]{3,2,1,0:T(8,128)(2,1)}, u32[]{:S(2)}, u32[]{:S(2)}) collective-permute-start(bf16[16,2,128,128]{3,2,1,0:T(8,128)(2,1)S(1)} %copy-done.2), channel_id=1, source_target_pairs={{0,2},{1,3},{2,0},{3,1},{4,6},{5,7},{6,4},{7,5},{8,10},{9,11},{10,... | collective-permute-start | bytes 3145736 | tf_op jit(solution)/shard_map/ppermute | solution.py:28
  113.0 4.2 %all-to-all-start.4 = ((bf16[4,672,128]{2,1,0:T(8,128)(2,1)}), bf16[4,672,128]{2,1,0:T(8,128)(2,1)}, u32[]{:S(2)}, u32[]{:S(2)}) async-start(bf16[4,672,128]{2,1,0:T(8,128)(2,1)} %copy-done.6), calls=%async_computation.4 | async-start | bytes 1376256 | tf_op jit(solution)/shard_map/all_to_all | solution.py:317
  117.3 11.9 %shard_map.88 = bf16[4,672,128]{2,1,0:T(8,128)(2,1)S(1)} custom-call(s32[4,16]{1,0:T(4,128)S(1)} %bitcast.33, s32[4]{0:T(128)S(1)} %get-tuple-element.19.counts, s32[4]{0:T(128)S(1)} %get-tuple-element.18.lasts, s32[1]{0:T(128)} %bitcast.9.mine, s32[1]{0:T(128)} %bitcast.23.store, bf16[4,128,1920]{2,1,0:T(8,128)(2,1)S(1)} %all-to-all-done.1.refs_0_, ...), custom_call_target="tpu_custom_call" | custom-call | flops 1 | bytes 1 | tf_op jit(solution)/shard_map/pallas_call | solution.py:252
  129.2 0.9 copy-done.7
  130.1 6.8 %collective-permute-done.3.refs_3_ = bf16[16,2,128,128]{3,2,1,0:T(8,128)(2,1)} collective-permute-done((bf16[16,2,128,128]{3,2,1,0:T(8,128)(2,1)S(1)}, bf16[16,2,128,128]{3,2,1,0:T(8,128)(2,1)}, u32[]{:S(2)}, u32[]{:S(2)}) %collective-permute-start.3) | collective-permute-done | bytes 1048608 | tf_op jit(solution)/shard_map/ppermute | solution.py:28
  136.9 4.5 %all-to-all-start.3 = ((bf16[4,672,128]{2,1,0:T(8,128)(2,1)}), bf16[4,672,128]{2,1,0:T(8,128)(2,1)}, u32[]{:S(2)}, u32[]{:S(2)}) async-start(bf16[4,672,128]{2,1,0:T(8,128)(2,1)} %copy-done.7), calls=%async_computation.3 | async-start | bytes 1376256 | tf_op jit(solution)/shard_map/all_to_all | solution.py:317
  141.4 12.8 %shard_map.89 = bf16[4,672,128]{2,1,0:T(8,128)(2,1)S(1)} custom-call(s32[4,16]{1,0:T(4,128)S(1)} %bitcast.34, s32[4]{0:T(128)S(1)} %get-tuple-element.19.counts, s32[4]{0:T(128)S(1)} %get-tuple-element.18.lasts, s32[1]{0:T(128)} %bitcast.9.mine, s32[1]{0:T(128)} %bitcast.24.store, bf16[4,128,1920]{2,1,0:T(8,128)(2,1)S(1)} %all-to-all-done.1.refs_0_, ...), custom_call_target="tpu_custom_call" | custom-call | flops 1 | bytes 1 | tf_op jit(solution)/shard_map/pallas_call | solution.py:252
  154.2 0.9 copy-done.8
  155.1 5.1 %all-to-all-done.3.parts = bf16[4,672,128]{2,1,0:T(8,128)(2,1)} async-done(((bf16[4,672,128]{2,1,0:T(8,128)(2,1)}), bf16[4,672,128]{2,1,0:T(8,128)(2,1)}, u32[]{:S(2)}, u32[]{:S(2)}) %all-to-all-start.3) | async-done | bytes 688160 | tf_op jit(solution)/shard_map/all_to_all | solution.py:317
  160.2 3.5 %all-to-all-start.2 = ((bf16[4,672,128]{2,1,0:T(8,128)(2,1)}), bf16[4,672,128]{2,1,0:T(8,128)(2,1)S(1)}, u32[]{:S(2)}, u32[]{:S(2)}) async-start(bf16[4,672,128]{2,1,0:T(8,128)(2,1)} %copy-done.8), calls=%async_computation.2 | async-start | bytes 1376256 | tf_op jit(solution)/shard_map/all_to_all | solution.py:317
  163.7 2.4 %shard_map.90.refs_0_ = bf16[128,2560]{1,0:T(8,128)(2,1)} custom-call(bf16[4,672,128]{2,1,0:T(8,128)(2,1)} %all-to-all-done.5.parts), custom_call_target="tpu_custom_call" | custom-call | flops 1 | bytes 1 | tf_op jit(solution)/shard_map/pallas_call | solution.py:289
  166.0 2.4 %shard_map.91.refs_0_ = bf16[128,2560]{1,0:T(8,128)(2,1)} custom-call(bf16[4,672,128]{2,1,0:T(8,128)(2,1)} %all-to-all-done.4.parts, bf16[128,2560]{1,0:T(8,128)(2,1)} %shard_map.90.refs_0_), custom_call_target="tpu_custom_call", output_to_operand_aliasing={{}: (1, {})} | custom-call | flops 1 | bytes 1 | tf_op jit(solution)/shard_map/pallas_call | solution.py:289
  168.4 2.4 %shard_map.92.refs_0_ = bf16[128,2560]{1,0:T(8,128)(2,1)} custom-call(bf16[4,672,128]{2,1,0:T(8,128)(2,1)} %all-to-all-done.3.parts, bf16[128,2560]{1,0:T(8,128)(2,1)} %shard_map.91.refs_0_), custom_call_target="tpu_custom_call", output_to_operand_aliasing={{}: (1, {})} | custom-call | flops 1 | bytes 1 | tf_op jit(solution)/shard_map/pallas_call | solution.py:289
  170.8 10.7 %all-to-all-done.2.parts = bf16[4,672,128]{2,1,0:T(8,128)(2,1)S(1)} async-done(((bf16[4,672,128]{2,1,0:T(8,128)(2,1)}), bf16[4,672,128]{2,1,0:T(8,128)(2,1)S(1)}, u32[]{:S(2)}, u32[]{:S(2)}) %all-to-all-start.2) | async-done | bytes 688160 | tf_op jit(solution)/shard_map/all_to_all | solution.py:317
  181.5 0.8 copy-done.14
  182.3 2.4 %shard_map.93 = bf16[128,2560]{1,0:T(8,128)(2,1)} custom-call(bf16[4,672,128]{2,1,0:T(8,128)(2,1)} %copy-done.14, bf16[128,2560]{1,0:T(8,128)(2,1)} %shard_map.92.refs_0_), custom_call_target="tpu_custom_call", output_to_operand_aliasing={{}: (1, {})} | custom-call | flops 1 | bytes 1 | tf_op jit(solution)/shard_map/pallas_call | solution.py:289
  (53 shorter events, 0.9 us)
Async XLA Ops:
  0.6 5.3 %copy-start.15 = (s32[1,48]{1,0:T(1,128)S(1)}, s32[1,48]{1,0:T(1,128)}, u32[]{:S(2)}) copy-start(s32[1,48]{1,0:T(1,128)} %param.10) | copy-start | bytes 580
  0.6 5.3 %copy-start.16 = (s32[1,48]{1,0:T(1,128)S(1)}, s32[1,48]{1,0:T(1,128)}, u32[]{:S(2)}) copy-start(s32[1,48]{1,0:T(1,128)} %param.11) | copy-start | bytes 580
  0.6 9.8 %slice-start = ((bf16[128,2560]{1,0:T(8,128)(2,1)}), bf16[128,640]{1,0:T(8,128)(2,1)S(1)}, s32[]{:S(2)}) async-start(bf16[128,2560]{1,0:T(8,128)(2,1)} %param.7), calls=%async_computation.6 | async-start | bytes 327680 | tf_op jit(solution)/shard_map/slice | solution.py:341
  0.7 9.8 %collective-permute-start = (bf16[1,2,128,512]{3,2,1,0:T(8,128)(2,1)}, bf16[1,2,128,512]{3,2,1,0:T(8,128)(2,1)S(1)}, u32[]{:S(2)}, u32[]{:S(2)}) collective-permute-start(bf16[1,2,128,512]{3,2,1,0:T(8,128)(2,1)} %bitcast.25), channel_id=1, source_target_pairs={{0,1},{1,2},{2,3},{3,4},{4,5},{5,6},{6,7},{7,8},{8,9},{9,10},{10,1... | collective-permute-start | bytes 786440 | tf_op jit(solution)/shard_map/ppermute | solution.py:33
  2.5 46.9 %collective-permute-start.2 = (bf16[16,2,128,512]{3,2,1,0:T(8,128)(2,1)}, bf16[16,2,128,512]{3,2,1,0:T(8,128)(2,1)}, u32[]{:S(2)}, u32[]{:S(2)}) collective-permute-start(bf16[16,2,128,512]{3,2,1,0:T(8,128)(2,1)} %refs_6_.1), channel_id=1, source_target_pairs={{0,1},{1,0},{2,3},{3,2},{4,5},{5,4},{6,7},{7,6},{8,9},{9,8},{10,11... | collective-permute-start | bytes 12582920 | tf_op jit(solution)/shard_map/ppermute | solution.py:28
  11.4 27.6 %all-to-all-start = ((bf16[4,128,768]{2,1,0:T(8,128)(2,1)}), bf16[4,128,768]{2,1,0:T(8,128)(2,1)S(1)}, u32[]{:S(2)}, u32[]{:S(2)}) async-start(bf16[4,128,768]{2,1,0:T(8,128)(2,1)} %pad_maximum_fusion), calls=%async_computation | async-start | bytes 1572864 | tf_op jit(solution)/shard_map/all_to_all | solution.py:317
  15.0 25.0 %slice-start.1 = ((bf16[128,2560]{1,0:T(8,128)(2,1)}), bf16[128,1920]{1,0:T(8,128)(2,1)S(1)}, s32[]{:S(2)}) async-start(bf16[128,2560]{1,0:T(8,128)(2,1)} %param.7), calls=%async_computation.7 | async-start | bytes 983040 | tf_op jit(solution)/shard_map/slice | solution.py:343
  15.0 23.1 %collective-permute-start.1 = (bf16[16,2,128,128]{3,2,1,0:T(8,128)(2,1)S(1)}, bf16[16,2,128,128]{3,2,1,0:T(8,128)(2,1)S(1)}, u32[]{:S(2)}, u32[]{:S(2)}) collective-permute-start(bf16[16,2,128,128]{3,2,1,0:T(8,128)(2,1)S(1)} %slice.35.refs_1_), channel_id=1, source_target_pairs={{0,2},{1,3},{2,0},{3,1},{4,6},{5,7},{6,4},{7,5},{8,10},{9,11},{10,... | collective-permute-start | bytes 3145736 | tf_op jit(solution)/shard_map/ppermute | solution.py:28
  38.1 1.0 copy-start.9
  39.1 0.9 copy-start.4
  41.4 8.0 %copy-start.1 = (bf16[1,1,2,128,512]{4,3,2,1,0:T(8,128)(2,1)S(1)}, bf16[1,1,2,128,512]{4,3,2,1,0:T(8,128)(2,1)}, u32[]{:S(2)}) copy-start(bf16[1,1,2,128,512]{4,3,2,1,0:T(8,128)(2,1)} %param.8) | copy-start | bytes 786436
  41.4 47.4 %all-to-all-start.1 = ((bf16[4,128,1920]{2,1,0:T(8,128)(2,1)}), bf16[4,128,1920]{2,1,0:T(8,128)(2,1)S(1)}, u32[]{:S(2)}, u32[]{:S(2)}) async-start(bf16[4,128,1920]{2,1,0:T(8,128)(2,1)} %broadcast_in_dim.32), calls=%async_computation.1 | async-start | bytes 3932160 | tf_op jit(solution)/shard_map/all_to_all | solution.py:317
  46.4 3.0 %collective-permute-start.6 = (bf16[16,2,128,128]{3,2,1,0:T(8,128)(2,1)}, bf16[16,2,128,128]{3,2,1,0:T(8,128)(2,1)}, u32[]{:S(2)}, u32[]{:S(2)}) collective-permute-start(bf16[16,2,128,128]{3,2,1,0:T(8,128)(2,1)} %copy-done.9), channel_id=1, source_target_pairs={{0,1},{1,0},{2,3},{3,2},{4,5},{5,4},{6,7},{7,6},{8,9},{9,8},{10,11... | collective-permute-start | bytes 3145736 | tf_op jit(solution)/shard_map/ppermute | solution.py:28
  46.4 25.9 %collective-permute-start.5 = (bf16[16,2,128,128]{3,2,1,0:T(8,128)(2,1)}, bf16[16,2,128,128]{3,2,1,0:T(8,128)(2,1)}, u32[]{:S(2)}, u32[]{:S(2)}) collective-permute-start(bf16[16,2,128,128]{3,2,1,0:T(8,128)(2,1)} %get-tuple-element.24.refs_1_), channel_id=1, source_target_pairs={{0,2},{1,3},{2,0},{3,1},{4,6},{5,7},{6,4},{7,5},{8,10},{9,11},{10,... | collective-permute-start | bytes 3145736 | tf_op jit(solution)/shard_map/ppermute | solution.py:28
  49.4 2.2 %copy-start = (bf16[16,2,128,512]{3,2,1,0:T(8,128)(2,1)S(1)}, bf16[16,2,128,512]{3,2,1,0:T(8,128)(2,1)}, u32[]{:S(2)}) copy-start(bf16[16,2,128,512]{3,2,1,0:T(8,128)(2,1)} %refs_6_.1) | copy-start | bytes 12582916
  51.6 1.1 copy-start.5
  52.7 1.2 copy-start.10
  67.8 0.9 copy-start.13
  72.3 20.7 %collective-permute-start.7 = (bf16[16,2,128,128]{3,2,1,0:T(8,128)(2,1)}, bf16[16,2,128,128]{3,2,1,0:T(8,128)(2,1)S(1)}, u32[]{:S(2)}, u32[]{:S(2)}) collective-permute-start(bf16[16,2,128,128]{3,2,1,0:T(8,128)(2,1)} %collective-permute-done.5.refs_3_), channel_id=1, source_target_pairs={{0,1},{1,0},{2,3},{3,2},{4,5},{5,4},{6,7},{7,6},{8,9},{9,8},{10,11... | collective-permute-start | bytes 3145736 | tf_op jit(solution)/shard_map/ppermute | solution.py:28
  72.3 38.6 %collective-permute-start.4 = (bf16[16,2,128,128]{3,2,1,0:T(8,128)(2,1)}, bf16[16,2,128,128]{3,2,1,0:T(8,128)(2,1)}, u32[]{:S(2)}, u32[]{:S(2)}) collective-permute-start(bf16[16,2,128,128]{3,2,1,0:T(8,128)(2,1)} %get-tuple-element.22.refs_1_), channel_id=1, source_target_pairs={{0,2},{1,3},{2,0},{3,1},{4,6},{5,7},{6,4},{7,5},{8,10},{9,11},{10,... | collective-permute-start | bytes 3145736 | tf_op jit(solution)/shard_map/ppermute | solution.py:28
  88.8 24.2 %all-to-all-start.5 = ((bf16[4,672,128]{2,1,0:T(8,128)(2,1)}), bf16[4,672,128]{2,1,0:T(8,128)(2,1)}, u32[]{:S(2)}, u32[]{:S(2)}) async-start(bf16[4,672,128]{2,1,0:T(8,128)(2,1)} %copy-done.13), calls=%async_computation.5 | async-start | bytes 1376256 | tf_op jit(solution)/shard_map/all_to_all | solution.py:317
  93.0 1.0 copy-start.11
  94.0 1.2 copy-start.3
  95.2 1.2 copy-start.12
  96.5 14.5 %copy-start.2 = (bf16[16,2,128,128]{3,2,1,0:T(8,128)(2,1)S(1)}, bf16[16,2,128,128]{3,2,1,0:T(8,128)(2,1)}, u32[]{:S(2)}) copy-start(bf16[16,2,128,128]{3,2,1,0:T(8,128)(2,1)} %get-tuple-element.23.refs_1_) | copy-start | bytes 3145732
  110.1 0.9 copy-start.6
  110.9 6.4 %collective-permute-start.8 = (bf16[16,2,128,128]{3,2,1,0:T(8,128)(2,1)}, bf16[16,2,128,128]{3,2,1,0:T(8,128)(2,1)}, u32[]{:S(2)}, u32[]{:S(2)}) collective-permute-start(bf16[16,2,128,128]{3,2,1,0:T(8,128)(2,1)} %collective-permute-done.4.refs_3_), channel_id=1, source_target_pairs={{0,1},{1,0},{2,3},{3,2},{4,5},{5,4},{6,7},{7,6},{8,9},{9,8},{10,11... | collective-permute-start | bytes 3145736 | tf_op jit(solution)/shard_map/ppermute | solution.py:28
  110.9 26.0 %collective-permute-start.3 = (bf16[16,2,128,128]{3,2,1,0:T(8,128)(2,1)S(1)}, bf16[16,2,128,128]{3,2,1,0:T(8,128)(2,1)}, u32[]{:S(2)}, u32[]{:S(2)}) collective-permute-start(bf16[16,2,128,128]{3,2,1,0:T(8,128)(2,1)S(1)} %copy-done.2), channel_id=1, source_target_pairs={{0,2},{1,3},{2,0},{3,1},{4,6},{5,7},{6,4},{7,5},{8,10},{9,11},{10,... | collective-permute-start | bytes 3145736 | tf_op jit(solution)/shard_map/ppermute | solution.py:28
  113.0 23.9 %all-to-all-start.4 = ((bf16[4,672,128]{2,1,0:T(8,128)(2,1)}), bf16[4,672,128]{2,1,0:T(8,128)(2,1)}, u32[]{:S(2)}, u32[]{:S(2)}) async-start(bf16[4,672,128]{2,1,0:T(8,128)(2,1)} %copy-done.6), calls=%async_computation.4 | async-start | bytes 1376256 | tf_op jit(solution)/shard_map/all_to_all | solution.py:317
  129.2 0.9 copy-start.7
  136.9 4.5 %collective-permute-start.9 = (bf16[16,2,128,128]{3,2,1,0:T(8,128)(2,1)}, bf16[16,2,128,128]{3,2,1,0:T(8,128)(2,1)}, u32[]{:S(2)}, u32[]{:S(2)}) collective-permute-start(bf16[16,2,128,128]{3,2,1,0:T(8,128)(2,1)} %collective-permute-done.3.refs_3_), channel_id=1, source_target_pairs={{0,1},{1,0},{2,3},{3,2},{4,5},{5,4},{6,7},{7,6},{8,9},{9,8},{10,11... | collective-permute-start | bytes 3145736 | tf_op jit(solution)/shard_map/ppermute | solution.py:28
  136.9 23.3 %all-to-all-start.3 = ((bf16[4,672,128]{2,1,0:T(8,128)(2,1)}), bf16[4,672,128]{2,1,0:T(8,128)(2,1)}, u32[]{:S(2)}, u32[]{:S(2)}) async-start(bf16[4,672,128]{2,1,0:T(8,128)(2,1)} %copy-done.7), calls=%async_computation.3 | async-start | bytes 1376256 | tf_op jit(solution)/shard_map/all_to_all | solution.py:317
  154.2 0.9 copy-start.8
  160.2 21.3 %all-to-all-start.2 = ((bf16[4,672,128]{2,1,0:T(8,128)(2,1)}), bf16[4,672,128]{2,1,0:T(8,128)(2,1)S(1)}, u32[]{:S(2)}, u32[]{:S(2)}) async-start(bf16[4,672,128]{2,1,0:T(8,128)(2,1)} %copy-done.8), calls=%async_computation.2 | async-start | bytes 1376256 | tf_op jit(solution)/shard_map/all_to_all | solution.py:317
  181.5 0.8 copy-start.14
